TPU v7x, 32 devices: a whole 2x2x4 slice. The times are simulated.
32 devices in a mesh: gz: 4 (over z), xy: 8 (over y, x, core).
Axes of the slice: x: 2, y: 2, z: 4, core: 2. Of those that a mesh axis runs over, the one named last changes fastest.
Arguments:
- source_inner: float32 [8, 2, 16, 4096], P('gz', None, None, 'xy'), may hold values from -6 to 6
- source_front: float32 [8, 2, 16, 4096], P('gz', None, None, 'xy'), may hold values from -6 to 6
- inner_inverse: bfloat16 [8, 8, 2, 512, 512], P('gz', 'xy'), may hold values from -0.1875 to 0.1875
- coupling: bfloat16 [8, 8, 2, 512, 256], P('gz', 'xy'), may hold values from -0.1875 to 0.1875
- schur_inverse: bfloat16 [8, 2, 4096, 4096], P('gz', None, None, 'xy'), may hold values from -0.046875 to 0.046875
- front_rows: int32 [8, 2048], P('gz', 'xy'), may hold values from 0 to 4095, as said below
- link: float32 [8, 4096], P('gz', 'xy'), may hold values from 0.5 to 1.5
- front_size: int32 [8], P('gz'), may hold values from 2048 to 4096, as said below
Outputs:
- inner_field: float32 [8, 2, 16, 4096], P('gz', None, None, 'xy')
- front_field: float32 [8, 2, 16, 4096], P('gz', None, None, 'xy')
Inputs may be any that keep to these rules, and one draw needn't show every extreme that they name: `front_rows`: within one local front of one panel the 256 entries are distinct. `front_size`: some panel has exactly 4096 live unknowns and some exactly half of 4096.
All inputs are finite; a program needn't handle non-finite values.
Results may differ from a plain program's by a relative error of at most 0.0075.
Values may be sent and summed in bfloat16 or wider, within the bound.
No kernel may reach another device: no remote copies, remote signals or barrier semaphores. Data moves between devices by JAX's collectives and lax.ppermute only.
A program may use at most 64 MiB of HBM per device.

v0:
```python
import jax
import jax.numpy as jnp
from jax import lax
from jax.sharding import PartitionSpec as P


def passed_along(shard, axis, by):
    peers = lax.axis_size(axis)
    pairs = [(i, i + by) for i in range(peers) if 0 <= i + by < peers]
    return lax.ppermute(shard, axis, pairs)


def complex_product(field, matrix):
    row_count = field.shape[1]
    flattened = field.astype(jnp.bfloat16).reshape(2 * row_count, field.shape[2])
    first_part = jnp.dot(flattened, matrix[0], preferred_element_type=jnp.float32)
    second = jnp.dot(flattened, matrix[1], preferred_element_type=jnp.float32)
    return jnp.stack(
        [first_part[:row_count] - second[row_count:], second[:row_count] + first_part[row_count:]]
    )


def complex_product_t(field, matrix):
    row_count = field.shape[1]
    flattened = field.reshape(2 * row_count, field.shape[2])
    contract = (((1,), (1,)), ((), ()))
    first_part = lax.dot_general(flattened, matrix[0], contract, preferred_element_type=jnp.float32)
    second = lax.dot_general(flattened, matrix[1], contract, preferred_element_type=jnp.float32)
    return jnp.stack(
        [first_part[:row_count] - second[row_count:], second[:row_count] + first_part[row_count:]]
    )


def schur_apply(rhs_front, matrix):
    outgoing = rhs_front.astype(jnp.bfloat16)
    return complex_product(lax.all_gather(outgoing, "xy", axis=2, tiled=True), matrix)


def on_device(
    source_inner, source_front, inner_inverse, coupling, schur_inverse, front_rows, link, front_size
):
    chain_length = lax.axis_size("gz")
    panel_count = source_inner.shape[0]
    side_count = source_inner.shape[2]
    share_rows = source_front.shape[3]
    bound_rows = front_rows.shape[1]
    own_start = lax.axis_index("xy") * share_rows
    own_rows = own_start + jnp.arange(share_rows, dtype=jnp.int32)
    masks = [
        (own_rows < front_size[panel_index]).astype(jnp.float32)
        for panel_index in range(panel_count)
    ]
    solved_all = []
    bases = []
    for panel_index in range(panel_count):
        solved = complex_product(source_inner[panel_index], inner_inverse[panel_index, 0])
        pushed = complex_product(solved, coupling[panel_index, 0])
        flat_values = pushed.reshape(2 * side_count, bound_rows)
        positions = front_rows[panel_index].astype(jnp.float32).reshape(1, bound_rows)
        values = lax.all_gather(flat_values, "xy", axis=1, tiled=True)
        add_positions = lax.all_gather(positions, "xy", axis=1, tiled=True)
        local_rows = add_positions[0] - own_start.astype(jnp.float32)
        hit_table = (
            local_rows[:, None] == jnp.arange(share_rows, dtype=jnp.float32)[None, :]
        ).astype(jnp.float32)
        summed = jnp.dot(
            values, hit_table, precision=lax.Precision.HIGHEST, preferred_element_type=jnp.float32
        )
        contrib = summed.reshape(2, side_count, share_rows)
        solved_all.append(solved)
        bases.append(source_front[panel_index] - contrib)
    incoming = jnp.zeros((2, side_count, share_rows), jnp.float32)
    for turn_index in range(chain_length):
        if turn_index > 0:
            incoming = passed_along(outgoing, "gz", 1)
        forward_incoming = incoming
        forward_results = []
        for forward_panel_index in range(panel_count):
            base_rhs = bases[forward_panel_index]
            rhs_front = masks[forward_panel_index] * (
                base_rhs + link[forward_panel_index] * forward_incoming
            )
            forward_incoming = masks[forward_panel_index] * schur_apply(
                rhs_front, schur_inverse[forward_panel_index]
            )
            forward_results.append(forward_incoming)
        fronts = forward_results
        outgoing = fronts[-1]
    incoming = jnp.zeros((2, side_count, share_rows), jnp.float32)
    for turn_index in range(chain_length):
        if turn_index > 0:
            incoming = passed_along(outgoing, "gz", -1)
        backward_incoming = incoming
        results = [None] * panel_count
        for backward_panel_index in reversed(range(panel_count)):
            change = masks[backward_panel_index] * schur_apply(
                masks[backward_panel_index] * backward_incoming, schur_inverse[backward_panel_index]
            )
            results[backward_panel_index] = change
            backward_incoming = link[backward_panel_index] * (fronts[backward_panel_index] + change)
        changes = results
        outgoing = backward_incoming
    totals = [fronts[panel_index] + changes[panel_index] for panel_index in range(panel_count)]
    stacked = jnp.stack(totals)
    everywhere = lax.all_gather(stacked.astype(jnp.bfloat16), "xy", axis=3, tiled=True)
    inner_out = []
    for panel_index in range(panel_count):
        picked = jnp.take(everywhere[panel_index], front_rows[panel_index], axis=2)
        lifted = complex_product_t(picked, coupling[panel_index, 0])
        inner_out.append(
            solved_all[panel_index] - complex_product(lifted, inner_inverse[panel_index, 0])
        )
    return (jnp.stack(inner_out), stacked)


def solution(mesh):
    placed = (
        P("gz", None, None, "xy"),
        P("gz", None, None, "xy"),
        P("gz", "xy", None, None, None),
        P("gz", "xy", None, None, None),
        P("gz", None, None, "xy"),
        P("gz", "xy"),
        P("gz", "xy"),
        P("gz"),
    )
    return jax.shard_map(
        on_device,
        mesh=mesh,
        in_specs=placed,
        out_specs=(P("gz", None, None, "xy"), P("gz", None, None, "xy")),
        check_vma=False,
    )
```

profile of v0, /device:TPU:0, one launch (start us, length us, event | category | flops | bytes accessed | tf_op | source)
XLA Modules:
  0.0 291.9 jit_solution(5210203549175184782)
XLA Ops:
  0.6 1.0 convert.36
  1.6 1.2 fusion.102
  2.8 1.2 fusion.106
  4.1 1.2 fusion.110
  5.3 1.2 fusion.114
  7.2 1.1 fusion.134
  8.3 1.1 fusion.138
  10.2 1.3 fusion.256
  12.2 10.8 %all_gather.61 = f32[32,2048]{1,0:T(8,128)S(1)} all-gather(f32[32,256]{1,0:T(8,128)S(1)} %bitcast.382), channel_id=1, replica_groups=mesh['gz'=4,'xy'=8] {'xy'}, dimensions={1}, use_global_device_ids=true | all-gather | bytes 294912 | tf_op jit(solution)/shard_map/all_gather | solution.py:60
  23.0 8.9 %all_gather.62 = f32[1,2048]{1,0:T(1,128)S(1)} all-gather(f32[1,256]{1,0:T(1,128)S(1)} %get-tuple-element.74), channel_id=1, replica_groups=mesh['gz'=4,'xy'=8] {'xy'}, dimensions={1}, use_global_device_ids=true | all-gather | bytes 9216 | tf_op jit(solution)/shard_map/all_gather | solution.py:61
  31.8 1.5 fusion.64
  33.4 8.3 %all_gather.65 = bf16[2,16,4096]{2,1,0:T(8,128)(2,1)S(1)} all-gather(bf16[2,16,512]{2,1,0:T(8,128)(2,1)S(1)} %get-tuple-element.7), channel_id=1, replica_groups=mesh['gz'=4,'xy'=8] {'xy'}, dimensions={2}, use_global_device_ids=true | all-gather | bytes 294912 | tf_op jit(solution)/shard_map/all_gather | solution.py:36
  41.7 3.1 %fusion.46 = f32[32,512]{1,0:T(8,128)S(1)} fusion(bf16[32,4096]{1,0:T(8,128)(2,1)S(1)} %bitcast.333, bf16[2,2,4096,512]{3,2,1,0:T(8,128)(2,1)} %param.14), kind=kOutput, calls=%fused_computation.48 | convolution fusion | flops 134217728 | bytes 4521984 | tf_op jit(solution)/shard_map/dot_general | solution.py:17
  44.8 3.2 %fusion.62 = f32[32,512]{1,0:T(8,128)S(1)} fusion(bf16[32,4096]{1,0:T(8,128)(2,1)S(1)} %bitcast.334, bf16[2,2,4096,512]{3,2,1,0:T(8,128)(2,1)} %param.14), kind=kOutput, calls=%fused_computation.64 | convolution fusion | flops 134217728 | bytes 4521984 | tf_op jit(solution)/shard_map/dot_general | solution.py:16
  48.9 1.4 fusion.249
  50.4 9.4 %all_gather.63 = f32[32,2048]{1,0:T(8,128)S(1)} all-gather(f32[32,256]{1,0:T(8,128)S(1)} %bitcast.383), channel_id=1, replica_groups=mesh['gz'=4,'xy'=8] {'xy'}, dimensions={1}, use_global_device_ids=true | all-gather | bytes 294912 | tf_op jit(solution)/shard_map/all_gather | solution.py:60
  59.8 7.9 %all_gather.64 = f32[1,2048]{1,0:T(1,128)S(1)} all-gather(f32[1,256]{1,0:T(1,128)S(1)} %get-tuple-element.75), channel_id=1, replica_groups=mesh['gz'=4,'xy'=8] {'xy'}, dimensions={1}, use_global_device_ids=true | all-gather | bytes 9216 | tf_op jit(solution)/shard_map/all_gather | solution.py:61
  67.7 1.5 fusion.65
  69.3 9.3 %all_gather.66 = bf16[2,16,4096]{2,1,0:T(8,128)(2,1)S(1)} all-gather(bf16[2,16,512]{2,1,0:T(8,128)(2,1)S(1)} %get-tuple-element.5), channel_id=1, replica_groups=mesh['gz'=4,'xy'=8] {'xy'}, dimensions={2}, use_global_device_ids=true | all-gather | bytes 294912 | tf_op jit(solution)/shard_map/all_gather | solution.py:36
  78.6 3.0 %fusion.14 = f32[32,512]{1,0:T(8,128)S(1)} fusion(bf16[32,4096]{1,0:T(8,128)(2,1)S(1)} %bitcast.335, bf16[2,2,4096,512]{3,2,1,0:T(8,128)(2,1)} %param.14), kind=kOutput, calls=%fused_computation.16 | convolution fusion | flops 134217728 | bytes 4521984 | tf_op jit(solution)/shard_map/dot_general | solution.py:17
  81.6 3.0 %fusion.30 = f32[32,512]{1,0:T(8,128)S(1)} fusion(bf16[32,4096]{1,0:T(8,128)(2,1)S(1)} %bitcast.336, bf16[2,2,4096,512]{3,2,1,0:T(8,128)(2,1)} %param.14), kind=kOutput, calls=%fused_computation.32 | convolution fusion | flops 134217728 | bytes 4521984 | tf_op jit(solution)/shard_map/dot_general | solution.py:16
  84.6 3.5 %collective-permute-start = (f32[2,16,512]{2,1,0:T(8,128)S(1)}, f32[2,16,512]{2,1,0:T(8,128)S(1)}, u32[]{:S(2)}, u32[]{:S(2)}) collective-permute-start(f32[2,16,512]{2,1,0:T(8,128)S(1)} %maximum_multiply_fusion.1), channel_id=1, source_target_pairs={{0,8},{8,16},{16,24},{1,9},{9,17},{17,25},{2,10},{10,18},{18,26},{... | collective-permute-start | bytes 196616 | tf_op jit(solution)/shard_map/ppermute | solution.py:10
  88.9 0.8 fusion.22
  90.0 8.3 %all_gather.67 = bf16[2,16,4096]{2,1,0:T(8,128)(2,1)S(1)} all-gather(bf16[2,16,512]{2,1,0:T(8,128)(2,1)S(1)} %multiply_convert_fusion.6), channel_id=1, replica_groups=mesh['gz'=4,'xy'=8] {'xy'}, dimensions={2}, use_global_device_ids=true | all-gather | bytes 294912 | tf_op jit(solution)/shard_map/all_gather | solution.py:36
  99.2 0.8 fusion.60
  100.0 9.3 %all_gather.68 = bf16[2,16,4096]{2,1,0:T(8,128)(2,1)S(1)} all-gather(bf16[2,16,512]{2,1,0:T(8,128)(2,1)S(1)} %fusion.159), channel_id=1, replica_groups=mesh['gz'=4,'xy'=8] {'xy'}, dimensions={2}, use_global_device_ids=true | all-gather | bytes 294912 | tf_op jit(solution)/shard_map/all_gather | solution.py:36
  110.1 0.8 fusion.28
  111.0 4.4 %collective-permute-start.1 = (f32[2,16,512]{2,1,0:T(8,128)S(1)}, f32[2,16,512]{2,1,0:T(8,128)S(1)}, u32[]{:S(2)}, u32[]{:S(2)}) collective-permute-start(f32[2,16,512]{2,1,0:T(8,128)S(1)} %maximum_multiply_fusion.3), channel_id=1, source_target_pairs={{0,8},{8,16},{16,24},{1,9},{9,17},{17,25},{2,10},{10,18},{18,26},{... | collective-permute-start | bytes 196616 | tf_op jit(solution)/shard_map/ppermute | solution.py:10
  115.4 1.9 collective-permute-done.1
  117.3 8.5 %all_gather.69 = bf16[2,16,4096]{2,1,0:T(8,128)(2,1)S(1)} all-gather(bf16[2,16,512]{2,1,0:T(8,128)(2,1)S(1)} %multiply_convert_fusion.5), channel_id=1, replica_groups=mesh['gz'=4,'xy'=8] {'xy'}, dimensions={2}, use_global_device_ids=true | all-gather | bytes 294912 | tf_op jit(solution)/shard_map/all_gather | solution.py:36
  126.6 0.8 fusion.58
  127.5 9.3 %all_gather.70 = bf16[2,16,4096]{2,1,0:T(8,128)(2,1)S(1)} all-gather(bf16[2,16,512]{2,1,0:T(8,128)(2,1)S(1)} %fusion.163), channel_id=1, replica_groups=mesh['gz'=4,'xy'=8] {'xy'}, dimensions={2}, use_global_device_ids=true | all-gather | bytes 294912 | tf_op jit(solution)/shard_map/all_gather | solution.py:36
  137.6 0.8 fusion.26
  138.4 4.3 %collective-permute-start.2 = (f32[2,16,512]{2,1,0:T(8,128)S(1)}, f32[2,16,512]{2,1,0:T(8,128)S(1)}, u32[]{:S(2)}, u32[]{:S(2)}) collective-permute-start(f32[2,16,512]{2,1,0:T(8,128)S(1)} %maximum_multiply_fusion.5), channel_id=1, source_target_pairs={{0,8},{8,16},{16,24},{1,9},{9,17},{17,25},{2,10},{10,18},{18,26},{... | collective-permute-start | bytes 196616 | tf_op jit(solution)/shard_map/ppermute | solution.py:10
  143.4 1.3 collective-permute-done.2
  144.7 8.3 %all_gather.71 = bf16[2,16,4096]{2,1,0:T(8,128)(2,1)S(1)} all-gather(bf16[2,16,512]{2,1,0:T(8,128)(2,1)S(1)} %multiply_convert_fusion.4), channel_id=1, replica_groups=mesh['gz'=4,'xy'=8] {'xy'}, dimensions={2}, use_global_device_ids=true | all-gather | bytes 294912 | tf_op jit(solution)/shard_map/all_gather | solution.py:36
  153.8 0.8 fusion.56
  154.7 9.3 %all_gather.72 = bf16[2,16,4096]{2,1,0:T(8,128)(2,1)S(1)} all-gather(bf16[2,16,512]{2,1,0:T(8,128)(2,1)S(1)} %multiply_convert_fusion.3), channel_id=1, replica_groups=mesh['gz'=4,'xy'=8] {'xy'}, dimensions={2}, use_global_device_ids=true | all-gather | bytes 294912 | tf_op jit(solution)/shard_map/all_gather | solution.py:36
  164.8 0.8 fusion.8
  165.7 8.3 %all_gather.73 = bf16[2,16,4096]{2,1,0:T(8,128)(2,1)S(1)} all-gather(bf16[2,16,512]{2,1,0:T(8,128)(2,1)S(1)} %fusion.168), channel_id=1, replica_groups=mesh['gz'=4,'xy'=8] {'xy'}, dimensions={2}, use_global_device_ids=true | all-gather | bytes 294912 | tf_op jit(solution)/shard_map/all_gather | solution.py:36
  174.8 0.8 fusion.54
  175.7 1.3 collective-permute-start.3
  177.5 5.2 %collective-permute-done.3 = f32[2,16,512]{2,1,0:T(8,128)S(1)} collective-permute-done((f32[2,16,512]{2,1,0:T(8,128)S(1)}, f32[2,16,512]{2,1,0:T(8,128)S(1)}, u32[]{:S(2)}, u32[]{:S(2)}) %collective-permute-start.3) | collective-permute-done | bytes 65568 | tf_op jit(solution)/shard_map/ppermute | solution.py:10
  182.7 9.3 %all_gather.74 = bf16[2,16,4096]{2,1,0:T(8,128)(2,1)S(1)} all-gather(bf16[2,16,512]{2,1,0:T(8,128)(2,1)S(1)} %multiply_convert_fusion.2), channel_id=1, replica_groups=mesh['gz'=4,'xy'=8] {'xy'}, dimensions={2}, use_global_device_ids=true | all-gather | bytes 294912 | tf_op jit(solution)/shard_map/all_gather | solution.py:36
  193.7 8.3 %all_gather.75 = bf16[2,16,4096]{2,1,0:T(8,128)(2,1)S(1)} all-gather(bf16[2,16,512]{2,1,0:T(8,128)(2,1)S(1)} %fusion.174), channel_id=1, replica_groups=mesh['gz'=4,'xy'=8] {'xy'}, dimensions={2}, use_global_device_ids=true | all-gather | bytes 294912 | tf_op jit(solution)/shard_map/all_gather | solution.py:36
  203.7 1.3 collective-permute-start.4
  205.0 4.9 %collective-permute-done.4 = f32[2,16,512]{2,1,0:T(8,128)S(1)} collective-permute-done((f32[2,16,512]{2,1,0:T(8,128)S(1)}, f32[2,16,512]{2,1,0:T(8,128)S(1)}, u32[]{:S(2)}, u32[]{:S(2)}) %collective-permute-start.4) | collective-permute-done | bytes 65568 | tf_op jit(solution)/shard_map/ppermute | solution.py:10
  209.9 9.5 %all_gather.76 = bf16[2,16,4096]{2,1,0:T(8,128)(2,1)S(1)} all-gather(bf16[2,16,512]{2,1,0:T(8,128)(2,1)S(1)} %multiply_convert_fusion.1), channel_id=1, replica_groups=mesh['gz'=4,'xy'=8] {'xy'}, dimensions={2}, use_global_device_ids=true | all-gather | bytes 294912 | tf_op jit(solution)/shard_map/all_gather | solution.py:36
  220.3 0.8 fusion.18
  221.1 8.3 %all_gather.77 = bf16[2,16,4096]{2,1,0:T(8,128)(2,1)S(1)} all-gather(bf16[2,16,512]{2,1,0:T(8,128)(2,1)S(1)} %fusion.180), channel_id=1, replica_groups=mesh['gz'=4,'xy'=8] {'xy'}, dimensions={2}, use_global_device_ids=true | all-gather | bytes 294912 | tf_op jit(solution)/shard_map/all_gather | solution.py:36
  230.3 0.8 fusion.50
  231.2 1.3 collective-permute-start.5
  232.5 4.9 %collective-permute-done.5 = f32[2,16,512]{2,1,0:T(8,128)S(1)} collective-permute-done((f32[2,16,512]{2,1,0:T(8,128)S(1)}, f32[2,16,512]{2,1,0:T(8,128)S(1)}, u32[]{:S(2)}, u32[]{:S(2)}) %collective-permute-start.5) | collective-permute-done | bytes 65568 | tf_op jit(solution)/shard_map/ppermute | solution.py:10
  237.4 9.3 %all_gather.78 = bf16[2,16,4096]{2,1,0:T(8,128)(2,1)S(1)} all-gather(bf16[2,16,512]{2,1,0:T(8,128)(2,1)S(1)} %multiply_convert_fusion), channel_id=1, replica_groups=mesh['gz'=4,'xy'=8] {'xy'}, dimensions={2}, use_global_device_ids=true | all-gather | bytes 294912 | tf_op jit(solution)/shard_map/all_gather | solution.py:36
  248.4 8.3 %all_gather.79 = bf16[2,16,4096]{2,1,0:T(8,128)(2,1)S(1)} all-gather(bf16[2,16,512]{2,1,0:T(8,128)(2,1)S(1)} %fusion.186), channel_id=1, replica_groups=mesh['gz'=4,'xy'=8] {'xy'}, dimensions={2}, use_global_device_ids=true | all-gather | bytes 294912 | tf_op jit(solution)/shard_map/all_gather | solution.py:36
  257.5 0.8 fusion.48
  259.1 9.8 %all_gather.80 = bf16[2,2,16,4096]{3,2,1,0:T(8,128)(2,1)S(1)} all-gather(bf16[2,2,16,512]{3,2,1,0:T(8,128)(2,1)S(1)} %get-tuple-element.3), channel_id=1, replica_groups=mesh['gz'=4,'xy'=8] {'xy'}, dimensions={3}, use_global_device_ids=true | all-gather | bytes 589824 | tf_op jit(solution)/shard_map/all_gather | solution.py:105
  269.7 5.0 %copy.14 = bf16[2,16,4096]{1,0,2:T(2,128)(2,1)} copy(bf16[2,16,4096]{2,1,0:T(8,128)(2,1)} %get-tuple-element.10) | data formatting | bytes 524288 | tf_op jit(solution)/shard_map/squeeze | solution.py:108
  274.7 3.2 %gather_fusion.1 = bf16[256,2,16]{2,1,0:T(2,128)(2,1)} fusion(bf16[2,16,4096]{1,0,2:T(2,128)(2,1)} %copy.14, s32[1024]{0:T(1024)S(1)} %pad_clamp_fusion), kind=kCustom, calls=%fused_computation.1.clone | custom fusion | bytes 33792 | tf_op jit(solution)/shard_map/jit(_take)/gather | solution.py:108
  277.9 1.2 fusion.151
  279.8 0.9 fusion.124
  280.7 0.9 fusion.128
  282.0 3.8 %copy.12 = bf16[2,16,4096]{1,0,2:T(2,128)(2,1)} copy(bf16[2,16,4096]{2,1,0:T(8,128)(2,1)S(1)} %get-tuple-element.9) | data formatting | bytes 524288 | tf_op jit(solution)/shard_map/squeeze | solution.py:108
  285.9 2.5 gather_fusion
  (113 shorter events, 24.9 us)
Async XLA Ops:
  0.6 22.3 %copy-start.3 = (s32[2,256]{1,0:T(2,128)S(1)}, s32[2,256]{1,0:T(2,128)}, u32[]{:S(2)}) copy-start(s32[2,256]{1,0:T(2,128)} %param.15) | copy-start | bytes 6148
  0.6 32.7 %copy-start.2 = (f32[2,2,16,512]{3,2,1,0:T(8,128)S(1)}, f32[2,2,16,512]{3,2,1,0:T(8,128)}, u32[]{:S(2)}) copy-start(f32[2,2,16,512]{3,2,1,0:T(8,128)} %param.11) | copy-start | bytes 393220
  41.7 6.9 %copy-start.1 = (bf16[2,1,2,512,256]{4,3,2,1,0:T(8,128)(2,1)S(1)}, bf16[2,1,2,512,256]{4,3,2,1,0:T(8,128)(2,1)}, u32[]{:S(2)}) copy-start(bf16[2,1,2,512,256]{4,3,2,1,0:T(8,128)(2,1)} %param.13) | copy-start | bytes 3145732
  44.8 43.3 %copy-start.6 = (bf16[2,2,4096,512]{3,2,1,0:T(8,128)(2,1)S(1)}, bf16[2,2,4096,512]{3,2,1,0:T(8,128)(2,1)}, u32[]{:S(2)}) copy-start(bf16[2,2,4096,512]{3,2,1,0:T(8,128)(2,1)} %param.14) | copy-start | bytes 50331652
  84.6 5.4 %collective-permute-start = (f32[2,16,512]{2,1,0:T(8,128)S(1)}, f32[2,16,512]{2,1,0:T(8,128)S(1)}, u32[]{:S(2)}, u32[]{:S(2)}) collective-permute-start(f32[2,16,512]{2,1,0:T(8,128)S(1)} %maximum_multiply_fusion.1), channel_id=1, source_target_pairs={{0,8},{8,16},{16,24},{1,9},{9,17},{17,25},{2,10},{10,18},{18,26},{... | collective-permute-start | bytes 196616 | tf_op jit(solution)/shard_map/ppermute | solution.py:10
  111.0 6.2 %collective-permute-start.1 = (f32[2,16,512]{2,1,0:T(8,128)S(1)}, f32[2,16,512]{2,1,0:T(8,128)S(1)}, u32[]{:S(2)}, u32[]{:S(2)}) collective-permute-start(f32[2,16,512]{2,1,0:T(8,128)S(1)} %maximum_multiply_fusion.3), channel_id=1, source_target_pairs={{0,8},{8,16},{16,24},{1,9},{9,17},{17,25},{2,10},{10,18},{18,26},{... | collective-permute-start | bytes 196616 | tf_op jit(solution)/shard_map/ppermute | solution.py:10
  138.4 6.2 %collective-permute-start.2 = (f32[2,16,512]{2,1,0:T(8,128)S(1)}, f32[2,16,512]{2,1,0:T(8,128)S(1)}, u32[]{:S(2)}, u32[]{:S(2)}) collective-permute-start(f32[2,16,512]{2,1,0:T(8,128)S(1)} %maximum_multiply_fusion.5), channel_id=1, source_target_pairs={{0,8},{8,16},{16,24},{1,9},{9,17},{17,25},{2,10},{10,18},{18,26},{... | collective-permute-start | bytes 196616 | tf_op jit(solution)/shard_map/ppermute | solution.py:10
  175.7 7.0 %collective-permute-start.3 = (f32[2,16,512]{2,1,0:T(8,128)S(1)}, f32[2,16,512]{2,1,0:T(8,128)S(1)}, u32[]{:S(2)}, u32[]{:S(2)}) collective-permute-start(f32[2,16,512]{2,1,0:T(8,128)S(1)} %fusion.170), channel_id=1, source_target_pairs={{8,0},{16,8},{24,16},{9,1},{17,9},{25,17},{10,2},{18,10},{26,18},{... | collective-permute-start | bytes 196616 | tf_op jit(solution)/shard_map/ppermute | solution.py:10
  203.7 6.2 %collective-permute-start.4 = (f32[2,16,512]{2,1,0:T(8,128)S(1)}, f32[2,16,512]{2,1,0:T(8,128)S(1)}, u32[]{:S(2)}, u32[]{:S(2)}) collective-permute-start(f32[2,16,512]{2,1,0:T(8,128)S(1)} %fusion.176), channel_id=1, source_target_pairs={{8,0},{16,8},{24,16},{9,1},{17,9},{25,17},{10,2},{18,10},{26,18},{... | collective-permute-start | bytes 196616 | tf_op jit(solution)/shard_map/ppermute | solution.py:10
  231.2 6.2 %collective-permute-start.5 = (f32[2,16,512]{2,1,0:T(8,128)S(1)}, f32[2,16,512]{2,1,0:T(8,128)S(1)}, u32[]{:S(2)}, u32[]{:S(2)}) collective-permute-start(f32[2,16,512]{2,1,0:T(8,128)S(1)} %fusion.182), channel_id=1, source_target_pairs={{8,0},{16,8},{24,16},{9,1},{17,9},{25,17},{10,2},{18,10},{26,18},{... | collective-permute-start | bytes 196616 | tf_op jit(solution)/shard_map/ppermute | solution.py:10
  257.5 20.3 %copy-start.4 = (pred[256]{0:T(512)(128)(4,1)S(1)}, pred[256]{0:T(512)(128)(4,1)}, u32[]{:S(2)}) copy-start(pred[256]{0:T(512)(128)(4,1)} %compare_and_fusion) | copy-start | bytes 772
  258.4 23.3 %copy-start = (bf16[2,1,2,512,512]{4,3,2,1,0:T(8,128)(2,1)S(1)}, bf16[2,1,2,512,512]{4,3,2,1,0:T(8,128)(2,1)}, u32[]{:S(2)}) copy-start(bf16[2,1,2,512,512]{4,3,2,1,0:T(8,128)(2,1)} %param.12) | copy-start | bytes 6291460
  268.9 19.5 %copy-start.5 = (pred[256]{0:T(512)(128)(4,1)S(1)}, pred[256]{0:T(512)(128)(4,1)}, u32[]{:S(2)}) copy-start(pred[256]{0:T(512)(128)(4,1)} %compare_and_fusion.1) | copy-start | bytes 772
where the time goes:
time: 294 us; the launch traced here: 292 us
  blocking collectives  179 us (61%)
  matrix products  48.4 us (16%)
  waiting for transfers between devices  18.4 us (6%)
  local copies, waits for them, and re-layouts  18.2 us (6%)
  starting transfers between devices  16.1 us (5%)
  other arithmetic  10.7 us (4%)
    all_gather x15, blocking collectives, schur_apply(): lax.all_gather(outgoing, 'xy', axis=2, tiled=True)  132 us
    dot_general x22, matrix products, complex_product(): jnp.dot(flattened, matrix[0], preferred_element_type=jnp.float32)  21.8 us
    dot_general x22, matrix products, complex_product(): second = jnp.dot(flattened, matrix[1], preferred_element_type=jnp.float32)  21.4 us
    all_gather x2, blocking collectives, on_device(): values = lax.all_gather(flat_values, 'xy', axis=1, tiled=True)  20.2 us
    ppermute x6, waiting for transfers between devices, passed_along(): return lax.ppermute(shard, axis, pairs)  18.4 us
    all_gather x2, blocking collectives, on_device(): add_positions = lax.all_gather(positions, 'xy', axis=1, tiled=True)  16.8 us
    ppermute x6, starting transfers between devices, passed_along(): return lax.ppermute(shard, axis, pairs)  16.1 us
    all_gather x1, blocking collectives, on_device(): lax.all_gather(stacked.astype(jnp.bfloat16), 'xy', axis=3, tiled=True)  9.82 us
  transfers between devices with their start and end apart: 6, of which 6 were waited for; matrix products, arithmetic and copies ran while one was open for 1% of the time, Pallas kernels for 0%

commit v1 on v0

v1 whole, which is shorter than its diff:
```python
import functools

import jax
import jax.numpy as jnp
from jax import lax
from jax.experimental import pallas as pl
from jax.experimental.pallas import tpu as pltpu
from jax.sharding import PartitionSpec as P

IN_VMEM = pl.BlockSpec(memory_space=pltpu.VMEM)


def resident(array):
    return pltpu.with_memory_space_constraint(array, pltpu.VMEM)


def complex_product(field, matrix):
    row_count = field.shape[1]
    flattened = field.astype(jnp.bfloat16).reshape(2 * row_count, field.shape[2])
    first_part = jnp.dot(flattened, matrix[0], preferred_element_type=jnp.float32)
    second = jnp.dot(flattened, matrix[1], preferred_element_type=jnp.float32)
    return jnp.stack(
        [first_part[:row_count] - second[row_count:], second[:row_count] + first_part[row_count:]]
    )


def complex_product_t(field, matrix):
    row_count = field.shape[1]
    flattened = field.astype(jnp.bfloat16).reshape(2 * row_count, field.shape[2])
    contract = (((1,), (1,)), ((), ()))
    first_part = lax.dot_general(flattened, matrix[0], contract, preferred_element_type=jnp.float32)
    second = lax.dot_general(flattened, matrix[1], contract, preferred_element_type=jnp.float32)
    return jnp.stack(
        [first_part[:row_count] - second[row_count:], second[:row_count] + first_part[row_count:]]
    )


def swapped(shard, mask):
    peers = lax.axis_size("xy")
    return lax.ppermute(shard, "xy", [(i, i ^ mask) for i in range(peers)])


def gathered_within(message):
    peers = lax.axis_size("xy")
    mine = jnp.stack([message] + [swapped(message, mask) for mask in range(2, peers, 2)])
    return mine, swapped(mine, 1)


def sources_within(peers):
    def sources(me):
        mine = [me ^ mask for mask in range(0, peers, 2)]
        return mine, [peer ^ 1 for peer in mine]

    return sources


def crossed(message, by, keep_mask):
    peers, groups = lax.axis_size("xy"), lax.axis_size("gz")
    half = peers // 4
    pair = jnp.stack([message, swapped(message, 1)])
    parts = []
    for turn in range(half):
        pairs = []
        for group in range(groups):
            for peer in range(peers):
                target = peer ^ (2 * (turn + (peer % 2) * half))
                pairs.append((group * peers + peer, (group + by) % groups * peers + target))
        parts.append(lax.ppermute(pair, ("gz", "xy"), pairs))
    mine = jnp.concatenate(parts)
    if keep_mask is not None:
        mine = jnp.where(keep_mask, mine, jnp.zeros_like(mine))
    return mine, swapped(mine, 1)


def sources_crossed(peers):
    half = peers // 4

    def half_of(me):
        return [
            (me ^ (2 * turn) ^ (me % 2 * (2 * half))) ^ core
            for turn in range(half)
            for core in range(2)
        ]

    def sources(me):
        return half_of(me), half_of(me ^ 1)

    return sources


def step_kernel(panel, turn, sources, has_addend, keeps, *refs):
    mine_ref, other_ref, schur_ref, mask_ref, link_ref = refs[:5]
    addend_ref = refs[5] if has_addend else None
    kept_in, kept_ref, message_ref = refs[-4], refs[-2], refs[-1]

    @pl.when(lax.axis_index("gz") == turn)
    def _():
        row_count, share = mine_ref.shape[2], mine_ref.shape[3]
        mine_from, other_from = sources(lax.axis_index("xy"))
        first = jnp.zeros((2 * row_count, share), jnp.float32)
        second = jnp.zeros((2 * row_count, share), jnp.float32)
        for ref, origins in ((mine_ref, mine_from), (other_ref, other_from)):
            for place, origin in enumerate(origins):
                rows = pl.ds(pl.multiple_of(origin * share, share), share)
                field = ref[place].reshape(2 * row_count, share)
                first += jnp.dot(
                    field, schur_ref[panel, 0, rows, :], preferred_element_type=jnp.float32
                )
                second += jnp.dot(
                    field, schur_ref[panel, 1, rows, :], preferred_element_type=jnp.float32
                )
        mask = mask_ref[...]
        link = link_ref[...]
        values = (
            mask * (first[:row_count] - second[row_count:]),
            mask * (second[:row_count] + first[row_count:]),
        )
        for part, value in enumerate(values):
            if keeps:
                value = kept_in[part] + value
            kept_ref[part] = value
            outgoing = link * value
            if has_addend:
                outgoing = addend_ref[part] + outgoing
            message_ref[part] = outgoing.astype(jnp.bfloat16)


def sweep_step(panel, turn, sources, pieces, schur, mask, link, addend, kept, message, keeps):
    operands = [resident(pieces[0]), resident(pieces[1]), schur, mask, link]
    if addend is not None:
        operands.append(addend)
    count = len(operands)
    return pl.pallas_call(
        functools.partial(step_kernel, panel, turn, sources, addend is not None, keeps),
        out_shape=(
            pltpu.VMEM(kept.shape, kept.dtype),
            pltpu.VMEM(message.shape, message.dtype),
        ),
        in_specs=[IN_VMEM] * (count + 2),
        out_specs=(IN_VMEM, IN_VMEM),
        input_output_aliases={count: 0, count + 1: 1},
        compiler_params=pltpu.CompilerParams(vmem_limit_bytes=40 * 2**20),
    )(*operands, resident(kept), resident(message))


def on_device(
    source_inner, source_front, inner_inverse, coupling, schur_inverse, front_rows, link, front_size
):
    peers, groups = lax.axis_size("xy"), lax.axis_size("gz")
    me = lax.axis_index("xy")
    panel_count, _, side_count, share = source_front.shape
    bound = front_rows.shape[1]
    half = peers // 4
    schur = resident(schur_inverse)
    own_rows = me * share + jnp.arange(share, dtype=jnp.int32)
    masks = [
        (own_rows < front_size[panel]).astype(jnp.float32)[None, :] for panel in range(panel_count)
    ]
    links = [link[panel][None, :] for panel in range(panel_count)]

    solved = [
        complex_product(source_inner[panel], inner_inverse[panel, 0])
        for panel in range(panel_count)
    ]
    pushed = [
        complex_product(solved[panel], coupling[panel, 0]).reshape(2 * side_count, bound)
        for panel in range(panel_count)
    ]
    sent = jnp.concatenate(pushed + [front_rows.astype(jnp.float32)])
    sent = jnp.pad(sent, ((0, -sent.shape[0] % 8), (0, 0)))
    received = lax.all_gather(sent, "xy", axis=1, tiled=True)
    bases = []
    for panel in range(panel_count):
        values = received[2 * side_count * panel : 2 * side_count * (panel + 1)]
        positions = received[2 * side_count * panel_count + panel].astype(jnp.int32)
        hits = (positions[:, None] == own_rows[None, :]).astype(jnp.bfloat16)
        high = values.astype(jnp.bfloat16)
        low = (values - high.astype(jnp.float32)).astype(jnp.bfloat16)
        summed = jnp.dot(jnp.concatenate([high, low]), hits, preferred_element_type=jnp.float32)
        summed = summed[: 2 * side_count] + summed[2 * side_count :]
        contrib = summed.reshape(2, side_count, share)
        bases.append(masks[panel] * (source_front[panel] - contrib))

    forward_links = [masks[panel] * links[panel] for panel in range(panel_count)]
    packed = jnp.concatenate(
        [bases[0].reshape(2 * side_count, share), jnp.tile(forward_links[0], (8, 1))]
    )
    packed = lax.ppermute(packed, "gz", [(g, (g - 1) % groups) for g in range(groups)])
    next_base = packed[: 2 * side_count].reshape(2, side_count, share)
    next_link = packed[2 * side_count : 2 * side_count + 1]
    backward_links = [
        links[panel] * masks[panel - 1] if panel else links[0] for panel in range(panel_count)
    ]
    own_masks = [resident(mask) for mask in masks]
    forward_addends = [resident(base) for base in bases[1:] + [next_base]]
    forward_scales = [resident(scale) for scale in forward_links[1:] + [next_link]]
    backward_scales = [resident(scale) for scale in backward_links]
    arriving = jnp.stack(sources_crossed(peers)(me)[0]).reshape(2 * half, 1, 1, 1)
    arriving_rows = arriving * share + jnp.arange(share, dtype=jnp.int32)
    arriving_mask = arriving_rows < front_size[panel_count - 1]

    kept = [jnp.zeros((2, side_count, share), jnp.float32) for _ in range(panel_count)]
    message = bases[0].astype(jnp.bfloat16)
    within, across = sources_within(peers), sources_crossed(peers)
    pieces, sources = gathered_within(message), within
    for turn in range(groups):
        for panel in range(panel_count):
            last = turn == groups - 1 and panel == panel_count - 1
            kept[panel], message = sweep_step(
                panel, turn, sources, pieces, schur, own_masks[panel],
                backward_scales[panel] if last else forward_scales[panel],
                None if last else forward_addends[panel],
                kept[panel], message, False,
            )
            if panel < panel_count - 1 or last:
                pieces, sources = gathered_within(message), within
            else:
                pieces, sources = crossed(message, 1, None), across
    if panel_count == 1 and groups > 1:
        pieces, sources = crossed(message, -1, arriving_mask), across
    for turn in reversed(range(groups)):
        for panel in reversed(range(panel_count)):
            if turn == groups - 1 and panel == panel_count - 1:
                continue
            kept[panel], message = sweep_step(
                panel, turn, sources, pieces, schur, own_masks[panel],
                backward_scales[panel], None, kept[panel], message, True,
            )
            if panel > 0:
                pieces, sources = gathered_within(message), within
            elif turn > 0:
                pieces, sources = crossed(message, -1, arriving_mask), across

    fronts = jnp.stack(kept)
    everywhere = lax.all_gather(fronts.astype(jnp.bfloat16), "xy", axis=3, tiled=True)
    all_rows = jnp.arange(everywhere.shape[3], dtype=jnp.int32)
    inner_out = []
    for panel in range(panel_count):
        chosen = (all_rows[:, None] == front_rows[panel][None, :]).astype(jnp.bfloat16)
        flat = everywhere[panel].reshape(2 * side_count, everywhere.shape[3])
        picked = jnp.dot(flat, chosen, preferred_element_type=jnp.float32)
        picked = picked.reshape(2, side_count, bound)
        lifted = complex_product_t(picked, coupling[panel, 0])
        inner_out.append(solved[panel] - complex_product(lifted, inner_inverse[panel, 0]))
    return (jnp.stack(inner_out), fronts)


def solution(mesh):
    placed = (
        P("gz", None, None, "xy"),
        P("gz", None, None, "xy"),
        P("gz", "xy", None, None, None),
        P("gz", "xy", None, None, None),
        P("gz", None, None, "xy"),
        P("gz", "xy"),
        P("gz", "xy"),
        P("gz"),
    )
    return jax.shard_map(
        on_device,
        mesh=mesh,
        in_specs=placed,
        out_specs=(P("gz", None, None, "xy"), P("gz", None, None, "xy")),
        check_vma=False,
    )
```

time: 294 us -> 210 us (0.71)
  blocking collectives: 179 us -> 21.1 us
  waiting for transfers between devices: 18.4 us -> 89.1 us
  starting transfers between devices: 16.1 us -> 56.1 us
  matrix products: 48.4 us -> 10.2 us
  Pallas kernels: 0 us -> 6.15 us
    all_gather x20 -> x2, blocking collectives: 179 us -> 21.1 us  [the longest x1 11.5 us: on_device(): received = lax.all_gather(sent, 'xy', axis=1, tiled=True)]
    ppermute x6 -> x61, waiting for transfers between devices: 18.4 us -> 89.1 us  [the longest x48 53.2 us: swapped(): return lax.ppermute(shard, 'xy', [(i, i ^ mask) for i in range(peers)])]
    ppermute x6 -> x61, starting transfers between devices: 16.1 us -> 56.1 us  [the longest x48 34.1 us: swapped(): return lax.ppermute(shard, 'xy', [(i, i ^ mask) for i in range(peers)])]
    dot_general x22 -> x6, matrix products: 21.8 us -> 3.1 us  [complex_product(): jnp.dot(flattened, matrix[0], preferred_element_type=jnp.float32)]
    dot_general x22 -> x6, matrix products: 21.4 us -> 3.03 us  [complex_product(): second = jnp.dot(flattened, matrix[1], preferred_element_type=jnp.float32)]
    unnamed x14 -> x23, local copies, waits for them, and re-layouts: 0.04 us -> 17.4 us
    squeeze x3 -> x0, local copies, waits for them, and re-layouts: 9.59 us -> none  [on_device(): picked = jnp.take(everywhere[panel_index], front_rows[panel_index], axis=2)]
    pallas_call x0 -> x15, Pallas kernels: none -> 6.15 us  [sweep_step(): pl.pallas_call(functools.partial(step_kernel, panel, turn, sources, adden...]
  transfers between devices with their start and end apart: 6 -> 61, of which waited for: 6 -> 59; matrix products, arithmetic and copies ran while one was open for 1% -> 2% of each run, Pallas kernels for 0% -> 0%
where the time goes in v1:
time: 210 us
  waiting for transfers between devices  89.1 us (42%)
  starting transfers between devices  56.1 us (27%)
  blocking collectives  21.1 us (10%)
  local copies, waits for them, and re-layouts  18 us (9%)
  matrix products  10.2 us (5%)
  other arithmetic  7.76 us (4%)
  Pallas kernels  6.15 us (3%)
    ppermute x48, waiting for transfers between devices, swapped(): return lax.ppermute(shard, 'xy', [(i, i ^ mask) for i in range(peers)])  53.2 us
    ppermute x48, starting transfers between devices, swapped(): return lax.ppermute(shard, 'xy', [(i, i ^ mask) for i in range(peers)])  34.1 us
    ppermute x12, waiting for transfers between devices, crossed(): parts.append(lax.ppermute(pair, ('gz', 'xy'), pairs))  33.8 us
    ppermute x12, starting transfers between devices, crossed(): parts.append(lax.ppermute(pair, ('gz', 'xy'), pairs))  19.9 us
    unnamed x23, local copies, waits for them, and re-layouts  17.4 us
    all_gather x1, blocking collectives, on_device(): received = lax.all_gather(sent, 'xy', axis=1, tiled=True)  11.5 us
    all_gather x1, blocking collectives, on_device(): lax.all_gather(fronts.astype(jnp.bfloat16), 'xy', axis=3, tiled=True)  9.63 us
    pallas_call x15, Pallas kernels, sweep_step(): pl.pallas_call(functools.partial(step_kernel, panel, turn, sources, adden...  6.15 us
  transfers between devices with their start and end apart: 61, of which 59 were waited for; matrix products, arithmetic and copies ran while one was open for 2% of the time, Pallas kernels for 0%

profile of v1, /device:TPU:0, one launch (start us, length us, event | category | flops | bytes accessed | tf_op | source)
XLA Modules:
  0.0 209.8 jit_solution(4142646508732632161)
XLA Ops:
  7.3 11.5 %all_gather.6 = f32[72,2048]{1,0:T(8,128)S(1)} all-gather(f32[72,256]{1,0:T(8,128)S(1)} %select_maximum_fusion), channel_id=1, replica_groups=mesh['gz'=4,'xy'=8] {'xy'}, dimensions={1}, use_global_device_ids=true | all-gather | bytes 663552 | tf_op jit(solution)/shard_map/all_gather | solution.py:171
  20.4 1.3 compare_convert_fusion.1
  22.6 1.6 collective-permute-start
  24.7 1.5 collective-permute-start.2
  26.6 1.5 collective-permute-done.1
  28.1 1.4 collective-permute-done.2
  29.6 1.3 fusion.106
  31.7 5.8 %copy-done = bf16[2,2,4096,512]{3,2,1,0:T(8,128)(2,1)S(1)} copy-done((bf16[2,2,4096,512]{3,2,1,0:T(8,128)(2,1)S(1)}, bf16[2,2,4096,512]{3,2,1,0:T(8,128)(2,1)}, u32[]{:S(2)}) %copy-start) | copy-done | bytes 16777240
  37.4 1.5 shard_map.95
  39.0 1.6 collective-permute-start.4
  41.0 1.5 collective-permute-start.6
  42.9 1.5 collective-permute-done.5
  44.4 1.4 collective-permute-done.6
  46.0 2.0 collective-permute-start.8
  48.7 2.2 %collective-permute-done.8 = f32[40,512]{1,0:T(8,128)S(1)} collective-permute-done((f32[40,512]{1,0:T(8,128)S(1)}, f32[40,512]{1,0:T(8,128)S(1)}, u32[]{:S(2)}, u32[]{:S(2)}) %collective-permute-start.8) | collective-permute-done | bytes 81952 | tf_op jit(solution)/shard_map/ppermute | solution.py:188
  50.9 5.8 %copy-done.1 = bf16[2,2,4096,512]{3,2,1,0:T(8,128)(2,1)S(1)} copy-done((bf16[2,2,4096,512]{3,2,1,0:T(8,128)(2,1)S(1)}, bf16[2,2,4096,512]{3,2,1,0:T(8,128)(2,1)}, u32[]{:S(2)}) %copy-start.1) | copy-done | bytes 16777240
  56.7 1.5 shard_map.96
  60.4 5.8 %collective-permute-done.10 = bf16[2,2,16,512]{3,2,1,0:T(8,128)(2,1)S(1)} collective-permute-done((bf16[2,2,16,512]{3,2,1,0:T(8,128)(2,1)S(1)}, bf16[2,2,16,512]{3,2,1,0:T(8,128)(2,1)S(1)}, u32[]{:S(2)}, u32[]{:S(2)}) %collective-permute-start.10) | collective-permute-done | bytes 65568 | tf_op jit(solution)/shard_map/ppermute | solution.py:68
  66.3 1.7 collective-permute-done.11
  71.5 1.5 collective-permute-start.15
  74.4 1.9 collective-permute-done.15
  76.4 1.3 collective-permute-done.16.refs_1_
  79.0 1.5 collective-permute-start.18
  80.5 5.0 %collective-permute-done.18 = bf16[2,2,16,512]{3,2,1,0:T(8,128)(2,1)S(1)} collective-permute-done((bf16[2,2,16,512]{3,2,1,0:T(8,128)(2,1)S(1)}, bf16[2,2,16,512]{3,2,1,0:T(8,128)(2,1)S(1)}, u32[]{:S(2)}, u32[]{:S(2)}) %collective-permute-start.18) | collective-permute-done | bytes 65568 | tf_op jit(solution)/shard_map/ppermute | solution.py:68
  85.4 2.5 %collective-permute-done.19 = bf16[2,2,16,512]{3,2,1,0:T(8,128)(2,1)S(1)} collective-permute-done((bf16[2,2,16,512]{3,2,1,0:T(8,128)(2,1)S(1)}, bf16[2,2,16,512]{3,2,1,0:T(8,128)(2,1)S(1)}, u32[]{:S(2)}, u32[]{:S(2)}) %collective-permute-start.19) | collective-permute-done | bytes 65568 | tf_op jit(solution)/shard_map/ppermute | solution.py:68
  87.9 1.3 collective-permute-done.20.refs_1_
  91.3 1.5 collective-permute-start.23
  93.9 2.2 %collective-permute-done.23 = bf16[2,16,512]{2,1,0:T(8,128)(2,1)S(1)} collective-permute-done((bf16[2,16,512]{2,1,0:T(8,128)(2,1)S(1)}, bf16[2,16,512]{2,1,0:T(8,128)(2,1)S(1)}, u32[]{:S(2)}, u32[]{:S(2)}) %collective-permute-start.23) | collective-permute-done | bytes 32800 | tf_op jit(solution)/shard_map/ppermute | solution.py:40
  96.2 1.3 collective-permute-done.24.refs_1_
  98.8 3.0 %collective-permute-start.27 = (bf16[2,2,16,512]{3,2,1,0:T(8,128)(2,1)S(1)}, bf16[2,2,16,512]{3,2,1,0:T(8,128)(2,1)S(1)}, u32[]{:S(2)}, u32[]{:S(2)}) collective-permute-start(bf16[2,2,16,512]{3,2,1,0:T(8,128)(2,1)S(1)} %pad_maximum_fusion.14), channel_id=1, source_target_pairs={{0,10},{1,15},{2,8},{3,13},{4,14},{5,11},{6,12},{7,9},{8,18},{9,23... | collective-permute-start | bytes 196616 | tf_op jit(solution)/shard_map/ppermute | solution.py:68
  101.8 3.7 %collective-permute-done.26 = bf16[2,2,16,512]{3,2,1,0:T(8,128)(2,1)S(1)} collective-permute-done((bf16[2,2,16,512]{3,2,1,0:T(8,128)(2,1)S(1)}, bf16[2,2,16,512]{3,2,1,0:T(8,128)(2,1)S(1)}, u32[]{:S(2)}, u32[]{:S(2)}) %collective-permute-start.26) | collective-permute-done | bytes 65568 | tf_op jit(solution)/shard_map/ppermute | solution.py:68
  105.5 1.5 collective-permute-done.27
  107.1 1.3 collective-permute-done.28.refs_1_
  110.4 1.5 collective-permute-start.31
  113.2 2.1 collective-permute-done.31
  115.3 1.3 collective-permute-done.32.refs_1_
  118.7 1.5 collective-permute-start.35
  121.4 2.1 collective-permute-done.35
  123.6 1.3 collective-permute-done.36.refs_1_
  125.0 5.8 %copy-done.2 = bf16[2,2,4096,512]{3,2,1,0:T(8,128)(2,1)S(1)} copy-done((bf16[2,2,4096,512]{3,2,1,0:T(8,128)(2,1)S(1)}, bf16[2,2,4096,512]{3,2,1,0:T(8,128)(2,1)}, u32[]{:S(2)}) %copy-start.2) | copy-done | bytes 16777240
  132.0 6.3 %collective-permute-start.38 = (bf16[2,2,16,512]{3,2,1,0:T(8,128)(2,1)S(1)}, bf16[2,2,16,512]{3,2,1,0:T(8,128)(2,1)S(1)}, u32[]{:S(2)}, u32[]{:S(2)}) collective-permute-start(bf16[2,2,16,512]{3,2,1,0:T(8,128)(2,1)S(1)} %pad_maximum_fusion.15), channel_id=1, source_target_pairs={{0,24},{1,29},{2,26},{3,31},{4,28},{5,25},{6,30},{7,27},{8,0},{9,5... | collective-permute-start | bytes 196616 | tf_op jit(solution)/shard_map/ppermute | solution.py:68
  139.2 1.5 collective-permute-done.38
  140.7 3.2 %collective-permute-done.39 = bf16[2,2,16,512]{3,2,1,0:T(8,128)(2,1)S(1)} collective-permute-done((bf16[2,2,16,512]{3,2,1,0:T(8,128)(2,1)S(1)}, bf16[2,2,16,512]{3,2,1,0:T(8,128)(2,1)S(1)}, u32[]{:S(2)}, u32[]{:S(2)}) %collective-permute-start.39) | collective-permute-done | bytes 65568 | tf_op jit(solution)/shard_map/ppermute | solution.py:68
  144.0 1.3 collective-permute-done.40.refs_1_
  147.4 1.5 collective-permute-start.43
  150.0 2.2 %collective-permute-done.43 = bf16[2,16,512]{2,1,0:T(8,128)(2,1)S(1)} collective-permute-done((bf16[2,16,512]{2,1,0:T(8,128)(2,1)S(1)}, bf16[2,16,512]{2,1,0:T(8,128)(2,1)S(1)}, u32[]{:S(2)}, u32[]{:S(2)}) %collective-permute-start.43) | collective-permute-done | bytes 32800 | tf_op jit(solution)/shard_map/ppermute | solution.py:40
  152.3 1.3 collective-permute-done.44.refs_1_
  154.9 2.6 %collective-permute-start.46 = (bf16[2,2,16,512]{3,2,1,0:T(8,128)(2,1)S(1)}, bf16[2,2,16,512]{3,2,1,0:T(8,128)(2,1)S(1)}, u32[]{:S(2)}, u32[]{:S(2)}) collective-permute-start(bf16[2,2,16,512]{3,2,1,0:T(8,128)(2,1)S(1)} %pad_maximum_fusion.16), channel_id=1, source_target_pairs={{0,24},{1,29},{2,26},{3,31},{4,28},{5,25},{6,30},{7,27},{8,0},{9,5... | collective-permute-start | bytes 196616 | tf_op jit(solution)/shard_map/ppermute | solution.py:68
  157.5 1.7 collective-permute-start.47
  159.4 3.7 %collective-permute-done.47 = bf16[2,2,16,512]{3,2,1,0:T(8,128)(2,1)S(1)} collective-permute-done((bf16[2,2,16,512]{3,2,1,0:T(8,128)(2,1)S(1)}, bf16[2,2,16,512]{3,2,1,0:T(8,128)(2,1)S(1)}, u32[]{:S(2)}, u32[]{:S(2)}) %collective-permute-start.47) | collective-permute-done | bytes 65568 | tf_op jit(solution)/shard_map/ppermute | solution.py:68
  163.3 1.3 collective-permute-done.48.refs_1_
  166.6 1.5 collective-permute-start.51
  169.4 2.1 collective-permute-done.51
  171.5 1.3 collective-permute-done.52.refs_1_
  174.1 2.8 %collective-permute-start.54 = (bf16[2,2,16,512]{3,2,1,0:T(8,128)(2,1)S(1)}, bf16[2,2,16,512]{3,2,1,0:T(8,128)(2,1)S(1)}, u32[]{:S(2)}, u32[]{:S(2)}) collective-permute-start(bf16[2,2,16,512]{3,2,1,0:T(8,128)(2,1)S(1)} %pad_maximum_fusion.17), channel_id=1, source_target_pairs={{0,24},{1,29},{2,26},{3,31},{4,28},{5,25},{6,30},{7,27},{8,0},{9,5... | collective-permute-start | bytes 196616 | tf_op jit(solution)/shard_map/ppermute | solution.py:68
  177.7 1.7 collective-permute-done.54
  179.4 3.2 %collective-permute-done.55 = bf16[2,2,16,512]{3,2,1,0:T(8,128)(2,1)S(1)} collective-permute-done((bf16[2,2,16,512]{3,2,1,0:T(8,128)(2,1)S(1)}, bf16[2,2,16,512]{3,2,1,0:T(8,128)(2,1)S(1)}, u32[]{:S(2)}, u32[]{:S(2)}) %collective-permute-start.55) | collective-permute-done | bytes 65568 | tf_op jit(solution)/shard_map/ppermute | solution.py:68
  184.0 1.5 shard_map.108
  185.6 1.4 collective-permute-start.57
  187.7 1.5 collective-permute-start.59
  190.9 1.6 collective-permute-done.59
  192.6 1.3 collective-permute-done.60.refs_1_
  193.9 1.5 shard_map.109
  196.1 9.6 %all_gather.7 = bf16[2,2,16,4096]{3,2,1,0:T(8,128)(2,1)S(1)} all-gather(bf16[2,2,16,512]{3,2,1,0:T(8,128)(2,1)S(1)} %get-tuple-element.60), channel_id=1, replica_groups=mesh['gz'=4,'xy'=8] {'xy'}, dimensions={3}, use_global_device_ids=true | all-gather | bytes 589824 | tf_op jit(solution)/shard_map/all_gather | solution.py:235
  (184 shorter events, 53.4 us)
Async XLA Ops:
  6.7 12.2 %copy-start.9 = (s32[2]{0:T(128)S(1)}, s32[2]{0:T(128)}, u32[]{:S(2)}) copy-start(s32[2]{0:T(128)} %param.15) | copy-start | bytes 28
  20.3 9.3 %copy-start.8 = (f32[2,512]{1,0:T(2,128)S(1)}, f32[2,512]{1,0:T(2,128)}, u32[]{:S(2)}) copy-start(f32[2,512]{1,0:T(2,128)} %param.14) | copy-start | bytes 12292
  22.6 4.0 %collective-permute-start = (bf16[2,16,512]{2,1,0:T(8,128)(2,1)S(1)}, bf16[2,16,512]{2,1,0:T(8,128)(2,1)S(1)}, u32[]{:S(2)}, u32[]{:S(2)}) collective-permute-start(bf16[2,16,512]{2,1,0:T(8,128)(2,1)S(1)} %get-tuple-element.85.refs_7_), channel_id=1, source_target_pairs={{0,2},{1,3},{2,0},{3,1},{4,6},{5,7},{6,4},{7,5},{8,10},{9,11},{10,... | collective-permute-start | bytes 98312 | tf_op jit(solution)/shard_map/ppermute | solution.py:40
  24.2 3.9 %collective-permute-start.1 = (bf16[2,16,512]{2,1,0:T(8,128)(2,1)S(1)}, bf16[2,16,512]{2,1,0:T(8,128)(2,1)S(1)}, u32[]{:S(2)}, u32[]{:S(2)}) collective-permute-start(bf16[2,16,512]{2,1,0:T(8,128)(2,1)S(1)} %get-tuple-element.85.refs_7_), channel_id=1, source_target_pairs={{0,4},{1,5},{2,6},{3,7},{4,0},{5,1},{6,2},{7,3},{8,12},{9,13},{10,... | collective-permute-start | bytes 98312 | tf_op jit(solution)/shard_map/ppermute | solution.py:40
  24.7 4.8 %collective-permute-start.2 = (bf16[2,16,512]{2,1,0:T(8,128)(2,1)S(1)}, bf16[2,16,512]{2,1,0:T(8,128)(2,1)S(1)}, u32[]{:S(2)}, u32[]{:S(2)}) collective-permute-start(bf16[2,16,512]{2,1,0:T(8,128)(2,1)S(1)} %get-tuple-element.85.refs_7_), channel_id=1, source_target_pairs={{0,6},{1,7},{2,4},{3,5},{4,2},{5,3},{6,0},{7,1},{8,14},{9,15},{10,... | collective-permute-start | bytes 98312 | tf_op jit(solution)/shard_map/ppermute | solution.py:40
  29.6 2.1 collective-permute-start.3
  39.0 4.0 %collective-permute-start.4 = (bf16[2,16,512]{2,1,0:T(8,128)(2,1)S(1)}, bf16[2,16,512]{2,1,0:T(8,128)(2,1)S(1)}, u32[]{:S(2)}, u32[]{:S(2)}) collective-permute-start(bf16[2,16,512]{2,1,0:T(8,128)(2,1)S(1)} %get-tuple-element.31.refs_7_), channel_id=1, source_target_pairs={{0,2},{1,3},{2,0},{3,1},{4,6},{5,7},{6,4},{7,5},{8,10},{9,11},{10,... | collective-permute-start | bytes 98312 | tf_op jit(solution)/shard_map/ppermute | solution.py:40
  40.5 3.9 %collective-permute-start.5 = (bf16[2,16,512]{2,1,0:T(8,128)(2,1)S(1)}, bf16[2,16,512]{2,1,0:T(8,128)(2,1)S(1)}, u32[]{:S(2)}, u32[]{:S(2)}) collective-permute-start(bf16[2,16,512]{2,1,0:T(8,128)(2,1)S(1)} %get-tuple-element.31.refs_7_), channel_id=1, source_target_pairs={{0,4},{1,5},{2,6},{3,7},{4,0},{5,1},{6,2},{7,3},{8,12},{9,13},{10,... | collective-permute-start | bytes 98312 | tf_op jit(solution)/shard_map/ppermute | solution.py:40
  41.0 4.8 %collective-permute-start.6 = (bf16[2,16,512]{2,1,0:T(8,128)(2,1)S(1)}, bf16[2,16,512]{2,1,0:T(8,128)(2,1)S(1)}, u32[]{:S(2)}, u32[]{:S(2)}) collective-permute-start(bf16[2,16,512]{2,1,0:T(8,128)(2,1)S(1)} %get-tuple-element.31.refs_7_), channel_id=1, source_target_pairs={{0,6},{1,7},{2,4},{3,5},{4,2},{5,3},{6,0},{7,1},{8,14},{9,15},{10,... | collective-permute-start | bytes 98312 | tf_op jit(solution)/shard_map/ppermute | solution.py:40
  45.9 5.0 %collective-permute-start.7 = (bf16[4,2,16,512]{3,2,1,0:T(8,128)(2,1)S(1)}, bf16[4,2,16,512]{3,2,1,0:T(8,128)(2,1)S(1)}, u32[]{:S(2)}, u32[]{:S(2)}) collective-permute-start(bf16[4,2,16,512]{3,2,1,0:T(8,128)(2,1)S(1)} %pad_maximum_fusion.1.refs_0_), channel_id=1, source_target_pairs={{0,1},{1,0},{2,3},{3,2},{4,5},{5,4},{6,7},{7,6},{8,9},{9,8},{10,11... | collective-permute-start | bytes 393224 | tf_op jit(solution)/shard_map/ppermute | solution.py:40
  46.0 4.9 %collective-permute-start.8 = (f32[40,512]{1,0:T(8,128)S(1)}, f32[40,512]{1,0:T(8,128)S(1)}, u32[]{:S(2)}, u32[]{:S(2)}) collective-permute-start(f32[40,512]{1,0:T(8,128)S(1)} %pad_maximum_fusion.11), channel_id=1, source_target_pairs={{0,24},{8,0},{16,8},{24,16},{1,25},{9,1},{17,9},{25,17},{2,26},{10... | collective-permute-start | bytes 245768 | tf_op jit(solution)/shard_map/ppermute | solution.py:188
  58.2 1.3 collective-permute-start.9
  59.5 6.7 %collective-permute-start.10 = (bf16[2,2,16,512]{3,2,1,0:T(8,128)(2,1)S(1)}, bf16[2,2,16,512]{3,2,1,0:T(8,128)(2,1)S(1)}, u32[]{:S(2)}, u32[]{:S(2)}) collective-permute-start(bf16[2,2,16,512]{3,2,1,0:T(8,128)(2,1)S(1)} %pad_maximum_fusion.12), channel_id=1, source_target_pairs={{0,8},{1,13},{2,10},{3,15},{4,12},{5,9},{6,14},{7,11},{8,16},{9,21... | collective-permute-start | bytes 196616 | tf_op jit(solution)/shard_map/ppermute | solution.py:68
  59.6 8.4 %collective-permute-start.11 = (bf16[2,2,16,512]{3,2,1,0:T(8,128)(2,1)S(1)}, bf16[2,2,16,512]{3,2,1,0:T(8,128)(2,1)S(1)}, u32[]{:S(2)}, u32[]{:S(2)}) collective-permute-start(bf16[2,2,16,512]{3,2,1,0:T(8,128)(2,1)S(1)} %pad_maximum_fusion.12), channel_id=1, source_target_pairs={{0,10},{1,15},{2,8},{3,13},{4,14},{5,11},{6,12},{7,9},{8,18},{9,23... | collective-permute-start | bytes 196616 | tf_op jit(solution)/shard_map/ppermute | solution.py:68
  68.0 1.5 collective-permute-start.12
  69.5 3.9 %collective-permute-start.13 = (bf16[2,16,512]{2,1,0:T(8,128)(2,1)S(1)}, bf16[2,16,512]{2,1,0:T(8,128)(2,1)S(1)}, u32[]{:S(2)}, u32[]{:S(2)}) collective-permute-start(bf16[2,16,512]{2,1,0:T(8,128)(2,1)S(1)} %get-tuple-element.34.refs_7_), channel_id=1, source_target_pairs={{0,2},{1,3},{2,0},{3,1},{4,6},{5,7},{6,4},{7,5},{8,10},{9,11},{10,... | collective-permute-start | bytes 98312 | tf_op jit(solution)/shard_map/ppermute | solution.py:40
  70.5 3.9 %collective-permute-start.14 = (bf16[2,16,512]{2,1,0:T(8,128)(2,1)S(1)}, bf16[2,16,512]{2,1,0:T(8,128)(2,1)S(1)}, u32[]{:S(2)}, u32[]{:S(2)}) collective-permute-start(bf16[2,16,512]{2,1,0:T(8,128)(2,1)S(1)} %get-tuple-element.34.refs_7_), channel_id=1, source_target_pairs={{0,4},{1,5},{2,6},{3,7},{4,0},{5,1},{6,2},{7,3},{8,12},{9,13},{10,... | collective-permute-start | bytes 98312 | tf_op jit(solution)/shard_map/ppermute | solution.py:40
  71.5 4.8 %collective-permute-start.15 = (bf16[2,16,512]{2,1,0:T(8,128)(2,1)S(1)}, bf16[2,16,512]{2,1,0:T(8,128)(2,1)S(1)}, u32[]{:S(2)}, u32[]{:S(2)}) collective-permute-start(bf16[2,16,512]{2,1,0:T(8,128)(2,1)S(1)} %get-tuple-element.34.refs_7_), channel_id=1, source_target_pairs={{0,6},{1,7},{2,4},{3,5},{4,2},{5,3},{6,0},{7,1},{8,14},{9,15},{10,... | collective-permute-start | bytes 98312 | tf_op jit(solution)/shard_map/ppermute | solution.py:40
  76.3 1.4 collective-permute-start.16
  77.7 1.2 collective-permute-start.17
  79.0 6.5 %collective-permute-start.18 = (bf16[2,2,16,512]{3,2,1,0:T(8,128)(2,1)S(1)}, bf16[2,2,16,512]{3,2,1,0:T(8,128)(2,1)S(1)}, u32[]{:S(2)}, u32[]{:S(2)}) collective-permute-start(bf16[2,2,16,512]{3,2,1,0:T(8,128)(2,1)S(1)} %pad_maximum_fusion.13), channel_id=1, source_target_pairs={{0,8},{1,13},{2,10},{3,15},{4,12},{5,9},{6,14},{7,11},{8,16},{9,21... | collective-permute-start | bytes 196616 | tf_op jit(solution)/shard_map/ppermute | solution.py:68
  80.4 7.5 %collective-permute-start.19 = (bf16[2,2,16,512]{3,2,1,0:T(8,128)(2,1)S(1)}, bf16[2,2,16,512]{3,2,1,0:T(8,128)(2,1)S(1)}, u32[]{:S(2)}, u32[]{:S(2)}) collective-permute-start(bf16[2,2,16,512]{3,2,1,0:T(8,128)(2,1)S(1)} %pad_maximum_fusion.13), channel_id=1, source_target_pairs={{0,10},{1,15},{2,8},{3,13},{4,14},{5,11},{6,12},{7,9},{8,18},{9,23... | collective-permute-start | bytes 196616 | tf_op jit(solution)/shard_map/ppermute | solution.py:68
  87.9 1.3 collective-permute-start.20
  89.2 3.9 %collective-permute-start.21 = (bf16[2,16,512]{2,1,0:T(8,128)(2,1)S(1)}, bf16[2,16,512]{2,1,0:T(8,128)(2,1)S(1)}, u32[]{:S(2)}, u32[]{:S(2)}) collective-permute-start(bf16[2,16,512]{2,1,0:T(8,128)(2,1)S(1)} %get-tuple-element.38.refs_7_), channel_id=1, source_target_pairs={{0,2},{1,3},{2,0},{3,1},{4,6},{5,7},{6,4},{7,5},{8,10},{9,11},{10,... | collective-permute-start | bytes 98312 | tf_op jit(solution)/shard_map/ppermute | solution.py:40
  90.0 3.9 %collective-permute-start.22 = (bf16[2,16,512]{2,1,0:T(8,128)(2,1)S(1)}, bf16[2,16,512]{2,1,0:T(8,128)(2,1)S(1)}, u32[]{:S(2)}, u32[]{:S(2)}) collective-permute-start(bf16[2,16,512]{2,1,0:T(8,128)(2,1)S(1)} %get-tuple-element.38.refs_7_), channel_id=1, source_target_pairs={{0,4},{1,5},{2,6},{3,7},{4,0},{5,1},{6,2},{7,3},{8,12},{9,13},{10,... | collective-permute-start | bytes 98312 | tf_op jit(solution)/shard_map/ppermute | solution.py:40
  91.3 4.8 %collective-permute-start.23 = (bf16[2,16,512]{2,1,0:T(8,128)(2,1)S(1)}, bf16[2,16,512]{2,1,0:T(8,128)(2,1)S(1)}, u32[]{:S(2)}, u32[]{:S(2)}) collective-permute-start(bf16[2,16,512]{2,1,0:T(8,128)(2,1)S(1)} %get-tuple-element.38.refs_7_), channel_id=1, source_target_pairs={{0,6},{1,7},{2,4},{3,5},{4,2},{5,3},{6,0},{7,1},{8,14},{9,15},{10,... | collective-permute-start | bytes 98312 | tf_op jit(solution)/shard_map/ppermute | solution.py:40
  96.1 1.4 collective-permute-start.24
  97.5 1.2 collective-permute-start.25
  98.7 6.8 %collective-permute-start.26 = (bf16[2,2,16,512]{3,2,1,0:T(8,128)(2,1)S(1)}, bf16[2,2,16,512]{3,2,1,0:T(8,128)(2,1)S(1)}, u32[]{:S(2)}, u32[]{:S(2)}) collective-permute-start(bf16[2,2,16,512]{3,2,1,0:T(8,128)(2,1)S(1)} %pad_maximum_fusion.14), channel_id=1, source_target_pairs={{0,8},{1,13},{2,10},{3,15},{4,12},{5,9},{6,14},{7,11},{8,16},{9,21... | collective-permute-start | bytes 196616 | tf_op jit(solution)/shard_map/ppermute | solution.py:68
  98.8 8.2 %collective-permute-start.27 = (bf16[2,2,16,512]{3,2,1,0:T(8,128)(2,1)S(1)}, bf16[2,2,16,512]{3,2,1,0:T(8,128)(2,1)S(1)}, u32[]{:S(2)}, u32[]{:S(2)}) collective-permute-start(bf16[2,2,16,512]{3,2,1,0:T(8,128)(2,1)S(1)} %pad_maximum_fusion.14), channel_id=1, source_target_pairs={{0,10},{1,15},{2,8},{3,13},{4,14},{5,11},{6,12},{7,9},{8,18},{9,23... | collective-permute-start | bytes 196616 | tf_op jit(solution)/shard_map/ppermute | solution.py:68
  107.1 1.3 collective-permute-start.28
  108.4 3.9 %collective-permute-start.29 = (bf16[2,16,512]{2,1,0:T(8,128)(2,1)S(1)}, bf16[2,16,512]{2,1,0:T(8,128)(2,1)S(1)}, u32[]{:S(2)}, u32[]{:S(2)}) collective-permute-start(bf16[2,16,512]{2,1,0:T(8,128)(2,1)S(1)} %get-tuple-element.42.refs_6_), channel_id=1, source_target_pairs={{0,2},{1,3},{2,0},{3,1},{4,6},{5,7},{6,4},{7,5},{8,10},{9,11},{10,... | collective-permute-start | bytes 98312 | tf_op jit(solution)/shard_map/ppermute | solution.py:40
  109.2 3.9 %collective-permute-start.30 = (bf16[2,16,512]{2,1,0:T(8,128)(2,1)S(1)}, bf16[2,16,512]{2,1,0:T(8,128)(2,1)S(1)}, u32[]{:S(2)}, u32[]{:S(2)}) collective-permute-start(bf16[2,16,512]{2,1,0:T(8,128)(2,1)S(1)} %get-tuple-element.42.refs_6_), channel_id=1, source_target_pairs={{0,4},{1,5},{2,6},{3,7},{4,0},{5,1},{6,2},{7,3},{8,12},{9,13},{10,... | collective-permute-start | bytes 98312 | tf_op jit(solution)/shard_map/ppermute | solution.py:40
  110.4 4.8 %collective-permute-start.31 = (bf16[2,16,512]{2,1,0:T(8,128)(2,1)S(1)}, bf16[2,16,512]{2,1,0:T(8,128)(2,1)S(1)}, u32[]{:S(2)}, u32[]{:S(2)}) collective-permute-start(bf16[2,16,512]{2,1,0:T(8,128)(2,1)S(1)} %get-tuple-element.42.refs_6_), channel_id=1, source_target_pairs={{0,6},{1,7},{2,4},{3,5},{4,2},{5,3},{6,0},{7,1},{8,14},{9,15},{10,... | collective-permute-start | bytes 98312 | tf_op jit(solution)/shard_map/ppermute | solution.py:40
  115.3 1.4 collective-permute-start.32
  116.7 3.9 %collective-permute-start.33 = (bf16[2,16,512]{2,1,0:T(8,128)(2,1)S(1)}, bf16[2,16,512]{2,1,0:T(8,128)(2,1)S(1)}, u32[]{:S(2)}, u32[]{:S(2)}) collective-permute-start(bf16[2,16,512]{2,1,0:T(8,128)(2,1)S(1)} %get-tuple-element.44.refs_6_), channel_id=1, source_target_pairs={{0,2},{1,3},{2,0},{3,1},{4,6},{5,7},{6,4},{7,5},{8,10},{9,11},{10,... | collective-permute-start | bytes 98312 | tf_op jit(solution)/shard_map/ppermute | solution.py:40
  117.5 3.9 %collective-permute-start.34 = (bf16[2,16,512]{2,1,0:T(8,128)(2,1)S(1)}, bf16[2,16,512]{2,1,0:T(8,128)(2,1)S(1)}, u32[]{:S(2)}, u32[]{:S(2)}) collective-permute-start(bf16[2,16,512]{2,1,0:T(8,128)(2,1)S(1)} %get-tuple-element.44.refs_6_), channel_id=1, source_target_pairs={{0,4},{1,5},{2,6},{3,7},{4,0},{5,1},{6,2},{7,3},{8,12},{9,13},{10,... | collective-permute-start | bytes 98312 | tf_op jit(solution)/shard_map/ppermute | solution.py:40
  118.7 4.8 %collective-permute-start.35 = (bf16[2,16,512]{2,1,0:T(8,128)(2,1)S(1)}, bf16[2,16,512]{2,1,0:T(8,128)(2,1)S(1)}, u32[]{:S(2)}, u32[]{:S(2)}) collective-permute-start(bf16[2,16,512]{2,1,0:T(8,128)(2,1)S(1)} %get-tuple-element.44.refs_6_), channel_id=1, source_target_pairs={{0,6},{1,7},{2,4},{3,5},{4,2},{5,3},{6,0},{7,1},{8,14},{9,15},{10,... | collective-permute-start | bytes 98312 | tf_op jit(solution)/shard_map/ppermute | solution.py:40
  123.5 1.4 collective-permute-start.36
  130.7 1.2 collective-permute-start.37
  132.0 8.7 %collective-permute-start.38 = (bf16[2,2,16,512]{3,2,1,0:T(8,128)(2,1)S(1)}, bf16[2,2,16,512]{3,2,1,0:T(8,128)(2,1)S(1)}, u32[]{:S(2)}, u32[]{:S(2)}) collective-permute-start(bf16[2,2,16,512]{3,2,1,0:T(8,128)(2,1)S(1)} %pad_maximum_fusion.15), channel_id=1, source_target_pairs={{0,24},{1,29},{2,26},{3,31},{4,28},{5,25},{6,30},{7,27},{8,0},{9,5... | collective-permute-start | bytes 196616 | tf_op jit(solution)/shard_map/ppermute | solution.py:68
  138.2 5.7 %collective-permute-start.39 = (bf16[2,2,16,512]{3,2,1,0:T(8,128)(2,1)S(1)}, bf16[2,2,16,512]{3,2,1,0:T(8,128)(2,1)S(1)}, u32[]{:S(2)}, u32[]{:S(2)}) collective-permute-start(bf16[2,2,16,512]{3,2,1,0:T(8,128)(2,1)S(1)} %pad_maximum_fusion.15), channel_id=1, source_target_pairs={{0,26},{1,31},{2,24},{3,29},{4,30},{5,27},{6,28},{7,25},{8,2},{9,7... | collective-permute-start | bytes 196616 | tf_op jit(solution)/shard_map/ppermute | solution.py:68
  143.9 1.4 collective-permute-start.40
  145.4 3.9 %collective-permute-start.41 = (bf16[2,16,512]{2,1,0:T(8,128)(2,1)S(1)}, bf16[2,16,512]{2,1,0:T(8,128)(2,1)S(1)}, u32[]{:S(2)}, u32[]{:S(2)}) collective-permute-start(bf16[2,16,512]{2,1,0:T(8,128)(2,1)S(1)} %get-tuple-element.48.refs_6_), channel_id=1, source_target_pairs={{0,2},{1,3},{2,0},{3,1},{4,6},{5,7},{6,4},{7,5},{8,10},{9,11},{10,... | collective-permute-start | bytes 98312 | tf_op jit(solution)/shard_map/ppermute | solution.py:40
  146.1 3.9 %collective-permute-start.42 = (bf16[2,16,512]{2,1,0:T(8,128)(2,1)S(1)}, bf16[2,16,512]{2,1,0:T(8,128)(2,1)S(1)}, u32[]{:S(2)}, u32[]{:S(2)}) collective-permute-start(bf16[2,16,512]{2,1,0:T(8,128)(2,1)S(1)} %get-tuple-element.48.refs_6_), channel_id=1, source_target_pairs={{0,4},{1,5},{2,6},{3,7},{4,0},{5,1},{6,2},{7,3},{8,12},{9,13},{10,... | collective-permute-start | bytes 98312 | tf_op jit(solution)/shard_map/ppermute | solution.py:40
  147.4 4.8 %collective-permute-start.43 = (bf16[2,16,512]{2,1,0:T(8,128)(2,1)S(1)}, bf16[2,16,512]{2,1,0:T(8,128)(2,1)S(1)}, u32[]{:S(2)}, u32[]{:S(2)}) collective-permute-start(bf16[2,16,512]{2,1,0:T(8,128)(2,1)S(1)} %get-tuple-element.48.refs_6_), channel_id=1, source_target_pairs={{0,6},{1,7},{2,4},{3,5},{4,2},{5,3},{6,0},{7,1},{8,14},{9,15},{10,... | collective-permute-start | bytes 98312 | tf_op jit(solution)/shard_map/ppermute | solution.py:40
  152.2 1.4 collective-permute-start.44
  153.6 1.2 collective-permute-start.45
  154.9 4.6 %collective-permute-start.46 = (bf16[2,2,16,512]{3,2,1,0:T(8,128)(2,1)S(1)}, bf16[2,2,16,512]{3,2,1,0:T(8,128)(2,1)S(1)}, u32[]{:S(2)}, u32[]{:S(2)}) collective-permute-start(bf16[2,2,16,512]{3,2,1,0:T(8,128)(2,1)S(1)} %pad_maximum_fusion.16), channel_id=1, source_target_pairs={{0,24},{1,29},{2,26},{3,31},{4,28},{5,25},{6,30},{7,27},{8,0},{9,5... | collective-permute-start | bytes 196616 | tf_op jit(solution)/shard_map/ppermute | solution.py:68
  157.5 5.7 %collective-permute-start.47 = (bf16[2,2,16,512]{3,2,1,0:T(8,128)(2,1)S(1)}, bf16[2,2,16,512]{3,2,1,0:T(8,128)(2,1)S(1)}, u32[]{:S(2)}, u32[]{:S(2)}) collective-permute-start(bf16[2,2,16,512]{3,2,1,0:T(8,128)(2,1)S(1)} %pad_maximum_fusion.16), channel_id=1, source_target_pairs={{0,26},{1,31},{2,24},{3,29},{4,30},{5,27},{6,28},{7,25},{8,2},{9,7... | collective-permute-start | bytes 196616 | tf_op jit(solution)/shard_map/ppermute | solution.py:68
  163.2 1.4 collective-permute-start.48
  164.6 3.9 %collective-permute-start.49 = (bf16[2,16,512]{2,1,0:T(8,128)(2,1)S(1)}, bf16[2,16,512]{2,1,0:T(8,128)(2,1)S(1)}, u32[]{:S(2)}, u32[]{:S(2)}) collective-permute-start(bf16[2,16,512]{2,1,0:T(8,128)(2,1)S(1)} %get-tuple-element.52.refs_6_), channel_id=1, source_target_pairs={{0,2},{1,3},{2,0},{3,1},{4,6},{5,7},{6,4},{7,5},{8,10},{9,11},{10,... | collective-permute-start | bytes 98312 | tf_op jit(solution)/shard_map/ppermute | solution.py:40
  165.4 3.9 %collective-permute-start.50 = (bf16[2,16,512]{2,1,0:T(8,128)(2,1)S(1)}, bf16[2,16,512]{2,1,0:T(8,128)(2,1)S(1)}, u32[]{:S(2)}, u32[]{:S(2)}) collective-permute-start(bf16[2,16,512]{2,1,0:T(8,128)(2,1)S(1)} %get-tuple-element.52.refs_6_), channel_id=1, source_target_pairs={{0,4},{1,5},{2,6},{3,7},{4,0},{5,1},{6,2},{7,3},{8,12},{9,13},{10,... | collective-permute-start | bytes 98312 | tf_op jit(solution)/shard_map/ppermute | solution.py:40
  166.6 4.8 %collective-permute-start.51 = (bf16[2,16,512]{2,1,0:T(8,128)(2,1)S(1)}, bf16[2,16,512]{2,1,0:T(8,128)(2,1)S(1)}, u32[]{:S(2)}, u32[]{:S(2)}) collective-permute-start(bf16[2,16,512]{2,1,0:T(8,128)(2,1)S(1)} %get-tuple-element.52.refs_6_), channel_id=1, source_target_pairs={{0,6},{1,7},{2,4},{3,5},{4,2},{5,3},{6,0},{7,1},{8,14},{9,15},{10,... | collective-permute-start | bytes 98312 | tf_op jit(solution)/shard_map/ppermute | solution.py:40
  171.5 1.4 collective-permute-start.52
  172.9 1.2 collective-permute-start.53
  174.1 5.3 %collective-permute-start.54 = (bf16[2,2,16,512]{3,2,1,0:T(8,128)(2,1)S(1)}, bf16[2,2,16,512]{3,2,1,0:T(8,128)(2,1)S(1)}, u32[]{:S(2)}, u32[]{:S(2)}) collective-permute-start(bf16[2,2,16,512]{3,2,1,0:T(8,128)(2,1)S(1)} %pad_maximum_fusion.17), channel_id=1, source_target_pairs={{0,24},{1,29},{2,26},{3,31},{4,28},{5,25},{6,30},{7,27},{8,0},{9,5... | collective-permute-start | bytes 196616 | tf_op jit(solution)/shard_map/ppermute | solution.py:68
  176.9 5.7 %collective-permute-start.55 = (bf16[2,2,16,512]{3,2,1,0:T(8,128)(2,1)S(1)}, bf16[2,2,16,512]{3,2,1,0:T(8,128)(2,1)S(1)}, u32[]{:S(2)}, u32[]{:S(2)}) collective-permute-start(bf16[2,2,16,512]{3,2,1,0:T(8,128)(2,1)S(1)} %pad_maximum_fusion.17), channel_id=1, source_target_pairs={{0,26},{1,31},{2,24},{3,29},{4,30},{5,27},{6,28},{7,25},{8,2},{9,7... | collective-permute-start | bytes 196616 | tf_op jit(solution)/shard_map/ppermute | solution.py:68
  182.6 1.4 collective-permute-start.56
  185.6 4.0 %collective-permute-start.57 = (bf16[2,16,512]{2,1,0:T(8,128)(2,1)S(1)}, bf16[2,16,512]{2,1,0:T(8,128)(2,1)S(1)}, u32[]{:S(2)}, u32[]{:S(2)}) collective-permute-start(bf16[2,16,512]{2,1,0:T(8,128)(2,1)S(1)} %get-tuple-element.56.refs_6_), channel_id=1, source_target_pairs={{0,2},{1,3},{2,0},{3,1},{4,6},{5,7},{6,4},{7,5},{8,10},{9,11},{10,... | collective-permute-start | bytes 98312 | tf_op jit(solution)/shard_map/ppermute | solution.py:40
  186.9 3.9 %collective-permute-start.58 = (bf16[2,16,512]{2,1,0:T(8,128)(2,1)S(1)}, bf16[2,16,512]{2,1,0:T(8,128)(2,1)S(1)}, u32[]{:S(2)}, u32[]{:S(2)}) collective-permute-start(bf16[2,16,512]{2,1,0:T(8,128)(2,1)S(1)} %get-tuple-element.56.refs_6_), channel_id=1, source_target_pairs={{0,4},{1,5},{2,6},{3,7},{4,0},{5,1},{6,2},{7,3},{8,12},{9,13},{10,... | collective-permute-start | bytes 98312 | tf_op jit(solution)/shard_map/ppermute | solution.py:40
  187.7 4.8 %collective-permute-start.59 = (bf16[2,16,512]{2,1,0:T(8,128)(2,1)S(1)}, bf16[2,16,512]{2,1,0:T(8,128)(2,1)S(1)}, u32[]{:S(2)}, u32[]{:S(2)}) collective-permute-start(bf16[2,16,512]{2,1,0:T(8,128)(2,1)S(1)} %get-tuple-element.56.refs_6_), channel_id=1, source_target_pairs={{0,6},{1,7},{2,4},{3,5},{4,2},{5,3},{6,0},{7,1},{8,14},{9,15},{10,... | collective-permute-start | bytes 98312 | tf_op jit(solution)/shard_map/ppermute | solution.py:40
  192.5 1.4 collective-permute-start.60
  195.5 11.1 %copy-start.5 = (bf16[2,1,2,512,256]{4,3,2,1,0:T(8,128)(2,1)S(1)}, bf16[2,1,2,512,256]{4,3,2,1,0:T(8,128)(2,1)}, u32[]{:S(2)}) copy-start(bf16[2,1,2,512,256]{4,3,2,1,0:T(8,128)(2,1)} %param.11) | copy-start | bytes 3145732
  (8 other events, 41.1 us)

commit v2 on v1

v2 whole, which is shorter than its diff:
```python
import functools

import jax
import jax.numpy as jnp
from jax import lax
from jax.experimental import pallas as pl
from jax.experimental.pallas import tpu as pltpu
from jax.sharding import PartitionSpec as P

IN_VMEM = pl.BlockSpec(memory_space=pltpu.VMEM)


IN_HBM = pl.BlockSpec(memory_space=pltpu.HBM)
IN_SMEM = pl.BlockSpec(memory_space=pltpu.SMEM)


def resident(array):
    return pltpu.with_memory_space_constraint(array, pltpu.VMEM)


def in_hbm(array):
    return pltpu.with_memory_space_constraint(array, pltpu.HBM)


def swapped(shard, mask):
    peers = lax.axis_size("xy")
    return lax.ppermute(shard, "xy", [(i, i ^ mask) for i in range(peers)])


def gathered_within(message, beside=None):
    peers = lax.axis_size("xy")
    fetched = [swapped(message, mask) for mask in reversed(range(2, peers, 2))]
    if beside is not None:
        fetched, beside = lax.optimization_barrier((fetched, beside))
    mine = jnp.stack([message] + fetched[::-1])
    pieces = mine, swapped(mine, 1)
    return pieces if beside is None else (pieces, beside)


def sources_within(peers):
    def sources(me):
        mine = [me ^ mask for mask in range(0, peers, 2)]
        return mine, [peer ^ 1 for peer in mine]

    return sources


def crossed(message, by, arrive):
    peers, groups = lax.axis_size("xy"), lax.axis_size("gz")
    half = peers // 4
    pair = jnp.stack([message, swapped(message, 1)])
    parts = []
    for turn in range(half):
        pairs = []
        for group in range(groups):
            for peer in range(peers):
                target = peer ^ (2 * (turn + (peer % 2) * half))
                pairs.append((group * peers + peer, (group + by) % groups * peers + target))
        parts.append(lax.ppermute(pair, ("gz", "xy"), pairs))
    mine = arrive(jnp.concatenate(parts))
    return mine, swapped(mine, 1)


def sources_crossed(peers):
    half = peers // 4

    def half_of(me):
        return [
            (me ^ (2 * turn) ^ (me % 2 * (2 * half))) ^ core
            for turn in range(half)
            for core in range(2)
        ]

    def sources(me):
        return half_of(me), half_of(me ^ 1)

    return sources


def gated(turn):
    def wrap(body):
        if turn is None:
            body()
        else:
            pl.when(lax.axis_index("gz") == turn)(body)

    return wrap


def in_kernel(body, outs, operands, aliases=None, specs=None, scratch=(), flops=0, moved=0):
    return pl.pallas_call(
        body,
        out_shape=tuple(pltpu.VMEM(shape, dtype) for shape, dtype in outs),
        in_specs=specs or [IN_VMEM] * len(operands),
        out_specs=(IN_VMEM,) * len(outs),
        scratch_shapes=scratch,
        input_output_aliases=aliases or {},
        compiler_params=pltpu.CompilerParams(vmem_limit_bytes=16 * 2**20),
        cost_estimate=pl.CostEstimate(flops=flops, bytes_accessed=moved, transcendentals=0),
    )(*operands)


def real_products(field, matrix):
    return [
        jnp.dot(field, matrix[part], preferred_element_type=jnp.float32) for part in range(2)
    ]


def combined(products):
    first, second = products
    count = first.shape[0] // 2
    return first[:count] - second[count:], second[:count] + first[count:]


def load_kernel(panel, chunks, schur_ref, after_ref, out_ref, sems):
    del after_ref
    rows = schur_ref.shape[2] // chunks
    copies = []
    for part in range(2):
        for chunk in range(chunks):
            span = pl.ds(chunk * rows, rows)
            copies.append(
                pltpu.make_async_copy(
                    schur_ref.at[panel, part, span, :],
                    out_ref.at[part, span, :],
                    sems.at[part * chunks + chunk],
                )
            )
    for copy in copies:
        copy.start()
    for copy in copies:
        copy.wait()


def loaded(panel, schur, after):
    chunks = 4
    shape = schur.shape[1:]
    return in_kernel(
        functools.partial(load_kernel, panel, chunks),
        [(shape, schur.dtype)],
        [in_hbm(schur), after],
        specs=[IN_HBM, pl.BlockSpec(memory_space=pl.ANY)],
        scratch=[pltpu.SemaphoreType.DMA((2 * chunks,))],
        moved=2 * schur.dtype.itemsize * shape[0] * shape[1] * shape[2],
    )[0]


def local_kernel(*refs):
    operands, (solved_ref, sent_ref), held, sems = refs[:6], refs[6:8], refs[8:14], refs[14]
    source_ref, inverse_ref, coupling_ref, rows_ref, link_ref, _ = held
    panel_count, _, side_count, _ = source_ref.shape
    copies = [
        pltpu.make_async_copy(operand, place, sems.at[index])
        for index, (operand, place) in enumerate(zip(operands, held))
    ]
    for copy in copies:
        copy.start()
    copies[0].wait()
    copies[1].wait()
    fields = []
    for panel in range(panel_count):
        field = source_ref[panel].astype(jnp.bfloat16).reshape(2 * side_count, -1)
        solved = combined(real_products(field, inverse_ref.at[panel, 0]))
        for part in range(2):
            solved_ref[panel, part] = solved[part]
        fields.append(jnp.concatenate(solved).astype(jnp.bfloat16))
    copies[2].wait()
    row = 0
    for panel in range(panel_count):
        pushed = combined(real_products(fields[panel], coupling_ref.at[panel, 0]))
        for part in range(2):
            sent_ref[pl.ds(row, side_count), :] = pushed[part]
            row += side_count
    for copy in copies[3:]:
        copy.wait()
    bound = sent_ref.shape[1]
    sent_ref[pl.ds(row, sent_ref.shape[0] - row), :] = jnp.zeros(
        (sent_ref.shape[0] - row, bound), jnp.float32
    )
    sent_ref[pl.ds(row, panel_count), :] = rows_ref[...].astype(jnp.float32)
    row += panel_count
    share = link_ref.shape[1]
    for start in range(0, share, bound):
        width = min(bound, share - start)
        sent_ref[pl.ds(row, 1), pl.ds(0, width)] = link_ref[pl.ds(0, 1), pl.ds(start, width)]
        row += 1


def live(size_ref, panel, start, share):
    rows = start + lax.broadcasted_iota(jnp.int32, (1, share), 1)
    return jnp.where(rows < size_ref[panel], 1.0, 0.0)


def base_kernel(panel, panel_count, size_ref, mine_ref, other_ref, source_ref, base_ref, message_ref):
    _, side_count, share = base_ref.shape
    bound = mine_ref.shape[2]
    count = 2 * side_count
    start = lax.axis_index("xy") * share
    own_rows = start + lax.broadcasted_iota(jnp.int32, (share, bound), 0)
    contract = (((1,), (1,)), ((), ()))
    total = jnp.zeros((2 * count, share), jnp.float32)
    for ref in (mine_ref, other_ref):
        for place in range(ref.shape[0]):
            values = ref[place, pl.ds(count * panel, count), :]
            places = ref[place, pl.ds(count * panel_count + panel, 1), :].astype(jnp.int32)
            hits = jnp.where(own_rows == places, 1.0, 0.0).astype(jnp.bfloat16)
            high = values.astype(jnp.bfloat16)
            low = (values - high.astype(jnp.float32)).astype(jnp.bfloat16)
            total += lax.dot_general(
                jnp.concatenate([high, low]), hits, contract, preferred_element_type=jnp.float32
            )
    contrib = total[:count] + total[count:]
    mask = live(size_ref, panel, start, share)
    for part in range(2):
        rows = slice(part * side_count, (part + 1) * side_count)
        base = mask * (source_ref[panel, part] - contrib[rows])
        base_ref[part] = base
        message_ref[part] = base.astype(jnp.bfloat16)


def scales_kernel(panel_count, side_count, size_ref, link_ref, mine_ref, other_ref, *outs):
    share, bound = link_ref.shape[1], mine_ref.shape[2]
    me = lax.axis_index("xy")
    half = mine_ref.shape[0] // 2
    masks = [live(size_ref, panel, me * share, share) for panel in range(panel_count)]
    for panel in range(panel_count):
        link = link_ref[pl.ds(panel, 1), :]
        outs[panel][...] = masks[panel]
        outs[panel_count + panel][...] = masks[panel] * link
        outs[2 * panel_count + panel][...] = link * masks[panel - 1] if panel else link
    forward_ref, backward_ref = outs[3 * panel_count :]
    first = panel_count * (2 * side_count + 1)
    origins = sources_crossed(4 * half)(me)[0]
    for index, origin in enumerate(origins):
        ref = (mine_ref, other_ref)[index % 2]
        place = index // 2 + me % 2 * half
        reached = live(size_ref, 0, origin * share, share)
        backward_ref[index, 0] = live(size_ref, panel_count - 1, origin * share, share)
        for piece, start in enumerate(range(0, share, bound)):
            width = min(bound, share - start)
            link = ref[place, pl.ds(first + piece, 1), pl.ds(0, width)]
            forward_ref[index, 0, :, pl.ds(start, width)] = reached[:, start : start + width] * link


def part_products(ref, origins, schur_ref, products):
    side_count, share = ref.shape[2:]
    for place, origin in enumerate(origins):
        rows = pl.ds(pl.multiple_of(origin * share, share), share)
        field = ref[place].reshape(2 * side_count, share)
        terms = real_products(field, schur_ref.at[:, rows, :])
        products = terms if products is None else [a + b for a, b in zip(products, terms)]
    return products


def early_kernel(turn, sources, mine_ref, schur_ref, products_ref):
    @gated(turn)
    def _():
        origins = sources(lax.axis_index("xy"))[0]
        products = part_products(mine_ref, origins, schur_ref, None)
        for part in range(2):
            products_ref[part] = products[part]


def late_kernel(turn, sources, names, *refs):
    named = dict(zip(names, refs))
    kept_ref, message_ref = refs[-2:]

    @gated(turn)
    def _():
        origins = sources(lax.axis_index("xy"))[1]
        products = [named["products"][part] for part in range(2)]
        products = part_products(named["other"], origins, named["schur"], products)
        for part, value in enumerate(combined(products)):
            value = named["mask"][...] * value
            if "kept" in named:
                value = named["kept"][part] + value
            kept_ref[part] = value
            if "scale" in named:
                value = named["scale"][...] * value
            if "addend" in named:
                value = named["addend"][part] + value
            message_ref[part] = value.astype(jnp.bfloat16)


def sweep_step(turn, sources, pieces, schur, kept, message, **others):
    mine, other = pieces
    shape = kept.shape
    count = 2 * shape[1]
    flops = 4 * count * shape[2] * shape[2] * mine.shape[0]
    moved = 4 * shape[2] * shape[2] * mine.shape[0]
    products = in_kernel(
        functools.partial(early_kernel, turn, sources),
        [((2, count, shape[2]), jnp.float32)],
        [resident(mine), resident(schur)],
        flops=flops,
        moved=moved,
    )[0]
    named = {"products": products, "other": other, "schur": schur}
    named.update({name: value for name, value in others.items() if value is not None})
    named["kept"], named["message"] = kept, message
    names = list(named)
    if others.get("adds", True) is None:
        names[names.index("kept")] = "old"
    operands = [resident(value) for name, value in named.items() if name != "adds"]
    names = [name for name in names if name != "adds"]
    return in_kernel(
        functools.partial(late_kernel, turn, sources, names),
        [(kept.shape, kept.dtype), (message.shape, message.dtype)],
        operands,
        aliases={len(names) - 2: 0, len(names) - 1: 1},
        flops=flops,
        moved=moved,
    )


def pick_kernel(mine_ref, rows_ref, picked_ref):
    picked = picks(mine_ref, rows_ref, sources_within_list(mine_ref.shape[0])[0])
    for panel, value in enumerate(picked):
        picked_ref[panel] = value


def sources_within_list(chips):
    return sources_within(2 * chips)(lax.axis_index("xy"))


def picks(ref, rows_ref, origins):
    _, panel_count, _, side_count, share = ref.shape
    bound = rows_ref.shape[1]
    found = []
    for panel in range(panel_count):
        total = jnp.zeros((2 * side_count, bound), jnp.float32)
        for place, origin in enumerate(origins):
            rows = origin * share + lax.broadcasted_iota(jnp.int32, (share, bound), 0)
            chosen = jnp.where(rows == rows_ref[pl.ds(panel, 1), :], 1.0, 0.0).astype(jnp.bfloat16)
            field = ref[place, panel].reshape(2 * side_count, share)
            total += jnp.dot(field, chosen, preferred_element_type=jnp.float32)
        found.append(total)
    return found


def inner_kernel(picked_ref, other_ref, rows_ref, coupling_ref, inverse_ref, solved_ref, out_ref):
    contract = (((1,), (1,)), ((), ()))
    more = picks(other_ref, rows_ref, sources_within_list(other_ref.shape[0])[1])
    for panel, value in enumerate(more):
        picked = (picked_ref[panel] + value).astype(jnp.bfloat16)
        lifted = combined(
            [
                lax.dot_general(
                    picked, coupling_ref[panel, 0, part], contract, preferred_element_type=jnp.float32
                )
                for part in range(2)
            ]
        )
        field = jnp.concatenate(lifted).astype(jnp.bfloat16)
        back = combined(real_products(field, inverse_ref.at[panel, 0]))
        for part in range(2):
            out_ref[panel, part] = solved_ref[panel, part] - back[part]


def on_device(
    source_inner, source_front, inner_inverse, coupling, schur_inverse, front_rows, link, front_size
):
    peers, groups = lax.axis_size("xy"), lax.axis_size("gz")
    panel_count, _, side_count, share = source_front.shape
    bound = front_rows.shape[1]
    half = peers // 4
    local = source_inner.shape[3]

    link_rows = -(-share // bound)
    sent_rows = panel_count * (2 * side_count + 1) + link_rows
    sent_rows += -sent_rows % 8
    taken = [source_inner, inner_inverse, coupling, front_rows, link, source_front]
    solved, sent, _, inverse_held, coupling_held, rows_held, link_held, source_held = in_kernel(
        local_kernel,
        [
            ((panel_count, 2, side_count, local), jnp.float32),
            ((sent_rows, bound), jnp.float32),
        ]
        + [(value.shape, value.dtype) for value in taken],
        [in_hbm(value) for value in taken],
        specs=[IN_HBM] * len(taken),
        scratch=[pltpu.SemaphoreType.DMA((len(taken),))],
    )
    (mine, other), first_schur = gathered_within(sent, loaded(0, schur_inverse, sent))
    schurs = [first_schur]
    mine, other = resident(mine), resident(other)
    bases, messages = [], []
    for panel in range(panel_count):
        base, message = in_kernel(
            functools.partial(base_kernel, panel, panel_count),
            [((2, side_count, share), jnp.float32), ((2, side_count, share), jnp.bfloat16)],
            [front_size, mine, other, resident(source_held)],
            specs=[IN_SMEM] + [IN_VMEM] * 3,
            moved=2**22,
        )
        bases.append(base)
        messages.append(message)

    row = ((1, share), jnp.float32)
    arriving = ((2 * half, 1, 1, share), jnp.float32)
    scales = in_kernel(
        functools.partial(scales_kernel, panel_count, side_count),
        [row] * (3 * panel_count) + [arriving] * 2,
        [front_size, resident(link_held), mine, other],
        specs=[IN_SMEM] + [IN_VMEM] * 3,
    )
    masks, forward_scales = scales[:panel_count], scales[panel_count : 2 * panel_count]
    backward_scales = scales[2 * panel_count : 3 * panel_count]
    arriving_forward, arriving_backward = scales[3 * panel_count :]

    def arrive_forward(pieces):
        return (arriving_forward * pieces.astype(jnp.float32)).astype(jnp.bfloat16)

    def arrive_backward(pieces):
        return (arriving_backward * pieces.astype(jnp.float32)).astype(jnp.bfloat16)

    kept = [jnp.zeros((2, side_count, share), jnp.float32) for _ in range(panel_count)]
    message = messages[0]
    within, across = sources_within(peers), sources_crossed(peers)
    rest = [loaded(panel, schur_inverse, message) for panel in range(1, panel_count)]
    (pieces, rest), sources = gathered_within(message, rest), within
    schurs += rest
    for turn in range(-1, groups):
        for panel in range(panel_count):
            own = turn == -1 and panel == 0
            if (turn == -1 and panel > 0) or (turn == 0 and panel == 0):
                continue
            ends = panel == panel_count - 1
            last = turn == groups - 1 and ends
            scale = addend = None
            if last:
                scale = backward_scales[panel]
            elif not ends:
                scale, addend = forward_scales[panel + 1], bases[panel + 1]
            kept[panel], message = sweep_step(
                None if own else turn, sources, pieces, schurs[panel], kept[panel], message,
                mask=masks[panel], scale=scale, addend=addend,
                adds=True if panel == 0 and not own else None,
            )
            if not ends or last:
                pieces, sources = gathered_within(message), within
            else:
                pieces, sources = crossed(message, 1, arrive_forward), across
    for turn in reversed(range(groups)):
        for panel in reversed(range(panel_count)):
            if turn == groups - 1 and panel == panel_count - 1:
                continue
            kept[panel], message = sweep_step(
                turn, sources, pieces, schurs[panel], kept[panel], message,
                mask=masks[panel], scale=backward_scales[panel], adds=True,
            )
            if panel > 0:
                pieces, sources = gathered_within(message), within
            elif turn > 0:
                pieces, sources = crossed(message, -1, arrive_backward), across

    fronts = jnp.stack(kept)
    mine, other = gathered_within(fronts.astype(jnp.bfloat16))
    picked = in_kernel(
        pick_kernel,
        [((panel_count, 2 * side_count, bound), jnp.float32)],
        [resident(mine), resident(rows_held)],
        moved=2**22,
    )[0]
    inner = in_kernel(
        inner_kernel,
        [(solved.shape, jnp.float32)],
        [
            resident(value)
            for value in (picked, other, rows_held, coupling_held, inverse_held, solved)
        ],
    )[0]
    return inner, fronts


def solution(mesh):
    placed = (
        P("gz", None, None, "xy"),
        P("gz", None, None, "xy"),
        P("gz", "xy", None, None, None),
        P("gz", "xy", None, None, None),
        P("gz", None, None, "xy"),
        P("gz", "xy"),
        P("gz", "xy"),
        P("gz"),
    )
    return jax.shard_map(
        on_device,
        mesh=mesh,
        in_specs=placed,
        out_specs=(P("gz", None, None, "xy"), P("gz", None, None, "xy")),
        check_vma=False,
    )
```

time: 210 us -> 172 us (0.82)
  blocking collectives: 21.1 us -> 0 us
  Pallas kernels: 6.15 us -> 23.6 us
  local copies, waits for them, and re-layouts: 18 us -> 0.7 us
  matrix products: 10.2 us -> 0 us
  other arithmetic: 7.76 us -> 1.11 us
  waiting for transfers between devices: 89.1 us -> 84.6 us
  starting transfers between devices: 56.1 us -> 60.3 us
    all_gather x2 -> x0, blocking collectives: 21.1 us -> none  [the longest x1 11.5 us: on_device(): received = lax.all_gather(sent, 'xy', axis=1, tiled=True)]
    pallas_call x15 -> x38, Pallas kernels: 6.15 us -> 23.6 us  [in_kernel(): pl.pallas_call(body, out_shape=tuple((pltpu.VMEM(shape, dtype) for shape,...]
    unnamed x23 -> x5, local copies, waits for them, and re-layouts: 17.4 us -> 0.67 us
    dot_general x20 -> x0, matrix products: 10.2 us -> none  [the longest x6 3.1 us: complex_product(): jnp.dot(flattened, matrix[0], preferred_element_type=jnp.float32)]
    ppermute x48 -> x56, starting transfers between devices: 34.1 us -> 42.6 us  [swapped(): return lax.ppermute(shard, 'xy', [(i, i ^ mask) for i in range(peers)])]
    convert_element_type x8 -> x7, other arithmetic: 3.36 us -> 0.83 us  [the longest x1 0.67 us: on_device(): mine, other = gathered_within(fronts.astype(jnp.bfloat16))]
    ppermute x12, starting transfers between devices: 19.9 us -> 17.7 us  [crossed(): parts.append(lax.ppermute(pair, ('gz', 'xy'), pairs))]
    ppermute x1 -> x0, waiting for transfers between devices: 2.18 us -> none  [on_device(): lax.ppermute(packed, 'gz', [(g, (g - 1) % groups) for g in range(groups)])]
  transfers between devices with their start and end apart: 61 -> 68, of which waited for: 59 -> 62; matrix products, arithmetic and copies ran while one was open for 2% -> 0% of each run, Pallas kernels for 0% -> 8%
where the time goes in v2:
time: 172 us; the launch traced here: 171 us
  waiting for transfers between devices  84.6 us (49%)
  starting transfers between devices  60.3 us (35%)
  Pallas kernels  23.6 us (14%)
    ppermute x56, waiting for transfers between devices, swapped(): return lax.ppermute(shard, 'xy', [(i, i ^ mask) for i in range(peers)])  52 us
    ppermute x56, starting transfers between devices, swapped(): return lax.ppermute(shard, 'xy', [(i, i ^ mask) for i in range(peers)])  42.6 us
    ppermute x12, waiting for transfers between devices, crossed(): parts.append(lax.ppermute(pair, ('gz', 'xy'), pairs))  32.6 us
    pallas_call x38, Pallas kernels, in_kernel(): pl.pallas_call(body, out_shape=tuple((pltpu.VMEM(shape, dtype) for shape,...  23.6 us
    ppermute x12, starting transfers between devices, crossed(): parts.append(lax.ppermute(pair, ('gz', 'xy'), pairs))  17.7 us
  transfers between devices with their start and end apart: 68, of which 62 were waited for; matrix products, arithmetic and copies ran while one was open for 0% of the time, Pallas kernels for 8%

profile of v2, /device:TPU:0, one launch (start us, length us, event | category | flops | bytes accessed | tf_op | source)
XLA Modules:
  0.0 171.4 jit_solution(383722068809864138)
XLA Ops:
  0.6 3.1 %shard_map.95 = (f32[2,2,16,512]{3,2,1,0:T(8,128)S(1)}, f32[72,256]{1,0:T(8,128)S(1)}, f32[2,2,16,512]{3,2,1,0:T(8,128)}, bf16[2,1,2,512,512]{4,3,2,1,0:T(8,128)...) custom-call(f32[2,2,16,512]{3,2,1,0:T(8,128)} %refs_0_.1, ...), custom_call_target="tpu_custom_call" | custom-call | tf_op jit(solution)/shard_map/pallas_call | solution.py:91
  3.8 3.0 %collective-permute-start.2 = (f32[72,256]{1,0:T(8,128)S(1)}, f32[72,256]{1,0:T(8,128)S(1)}, u32[]{:S(2)}, u32[]{:S(2)}) collective-permute-start(f32[72,256]{1,0:T(8,128)S(1)} %get-tuple-element.56.after_ref), channel_id=1, source_target_pairs={{0,2},{1,3},{2,0},{3,1},{4,6},{5,7},{6,4},{7,5},{8,10},{9,11},{10,... | collective-permute-start | bytes 221192 | tf_op jit(solution)/shard_map/ppermute | solution.py:27
  6.8 1.5 collective-permute-start.1
  8.3 3.5 %shard_map.96.schur_ref.refs_2_ = bf16[2,4096,512]{2,1,0:T(8,128)(2,1)S(1)} custom-call(bf16[2,2,4096,512]{3,2,1,0:T(8,128)(2,1)} %schur_ref.3, f32[72,256]{1,0:T(8,128)S(1)} %get-tuple-element.56.after_ref), custom_call_target="tpu_custom_call" | custom-call | bytes 16777216 | tf_op jit(solution)/shard_map/pallas_call | solution.py:91
  11.8 1.7 %collective-permute-done = f32[72,256]{1,0:T(8,128)S(1)} collective-permute-done((f32[72,256]{1,0:T(8,128)S(1)}, f32[72,256]{1,0:T(8,128)S(1)}, u32[]{:S(2)}, u32[]{:S(2)}) %collective-permute-start) | collective-permute-done | bytes 73760 | tf_op jit(solution)/shard_map/ppermute | solution.py:27
  13.7 1.6 collective-permute-done.3.other_ref
  15.2 1.9 %shard_map.98 = (f32[2,16,512]{2,1,0:T(8,128)}, bf16[2,16,512]{2,1,0:T(8,128)(2,1)S(1)}) custom-call(s32[2]{0:T(128)S(1)} %copy-done, f32[4,72,256]{2,1,0:T(8,128)S(1)} %pad_maximum_fusion.mine_ref, f32[4,72,256]{2,1,0:T(8,128)S(1)} %collective-permute-done.3.other_ref, f32[2,2,16,512]{3,2,1,0:T(8,128)S(1)} %get-tuple-element.62.source_ref), custom_call_target="tpu_custom_call" | custom-call | bytes 4194304 | tf_op jit(solution)/shard_map/pallas_call | solution.py:91
  17.7 1.2 collective-permute-start.5
  18.9 1.7 %collective-permute-start.4 = (bf16[2,16,512]{2,1,0:T(8,128)(2,1)S(1)}, bf16[2,16,512]{2,1,0:T(8,128)(2,1)S(1)}, u32[]{:S(2)}, u32[]{:S(2)}) collective-permute-start(bf16[2,16,512]{2,1,0:T(8,128)(2,1)S(1)} %get-tuple-element.63.after_ref.refs_7_), channel_id=1, source_target_pairs={{0,6},{1,7},{2,4},{3,5},{4,2},{5,3},{6,0},{7,1},{8,14},{9,15},{10,... | collective-permute-start | bytes 98312 | tf_op jit(solution)/shard_map/ppermute | solution.py:27
  20.7 3.5 %shard_map.99.schur_ref.refs_2_ = bf16[2,4096,512]{2,1,0:T(8,128)(2,1)S(1)} custom-call(bf16[2,2,4096,512]{3,2,1,0:T(8,128)(2,1)} %schur_ref.3, bf16[2,16,512]{2,1,0:T(8,128)(2,1)S(1)} %get-tuple-element.63.after_ref.refs_7_), custom_call_target="tpu_custom_call" | custom-call | bytes 16777216 | tf_op jit(solution)/shard_map/pallas_call | solution.py:91
  24.3 1.9 %shard_map.101 = (f32[2,16,512]{2,1,0:T(8,128)S(1)}, bf16[2,16,512]{2,1,0:T(8,128)(2,1)}) custom-call(s32[2]{0:T(128)S(1)} %copy-done, f32[4,72,256]{2,1,0:T(8,128)S(1)} %pad_maximum_fusion.mine_ref, f32[4,72,256]{2,1,0:T(8,128)S(1)} %collective-permute-done.3.other_ref, f32[2,2,16,512]{3,2,1,0:T(8,128)S(1)} %get-tuple-element.62.source_ref), custom_call_target="tpu_custom_call" | custom-call | bytes 4194304 | tf_op jit(solution)/shard_map/pallas_call | solution.py:91
  26.2 1.1 shard_map.97
  29.0 1.4 collective-permute-start.10
  31.1 1.5 collective-permute-start.8
  32.6 1.4 collective-permute-done.10
  38.6 1.7 collective-permute-start.14
  40.2 1.6 collective-permute-start.13
  41.8 4.5 %collective-permute-done.14 = bf16[2,2,16,512]{3,2,1,0:T(8,128)(2,1)S(1)} collective-permute-done((bf16[2,2,16,512]{3,2,1,0:T(8,128)(2,1)S(1)}, bf16[2,2,16,512]{3,2,1,0:T(8,128)(2,1)S(1)}, u32[]{:S(2)}, u32[]{:S(2)}) %collective-permute-start.14) | collective-permute-done | bytes 65568 | tf_op jit(solution)/shard_map/ppermute | solution.py:59
  48.6 1.4 collective-permute-start.18
  50.0 1.1 collective-permute-start.17
  52.1 1.4 collective-permute-done.18
  53.9 1.1 collective-permute-done.16
  55.2 1.3 collective-permute-done.19.refs_1_
  57.7 1.7 collective-permute-start.22
  59.4 5.9 %collective-permute-done.22 = bf16[2,2,16,512]{3,2,1,0:T(8,128)(2,1)S(1)} collective-permute-done((bf16[2,2,16,512]{3,2,1,0:T(8,128)(2,1)S(1)}, bf16[2,2,16,512]{3,2,1,0:T(8,128)(2,1)S(1)}, u32[]{:S(2)}, u32[]{:S(2)}) %collective-permute-start.22) | collective-permute-done | bytes 65568 | tf_op jit(solution)/shard_map/ppermute | solution.py:59
  66.1 1.3 collective-permute-done.23.refs_1_
  67.4 1.5 collective-permute-start.26
  70.9 1.3 collective-permute-done.26
  73.8 1.3 collective-permute-done.27.refs_1_
  76.4 1.8 %collective-permute-start.29 = (bf16[2,2,16,512]{3,2,1,0:T(8,128)(2,1)S(1)}, bf16[2,2,16,512]{3,2,1,0:T(8,128)(2,1)S(1)}, u32[]{:S(2)}, u32[]{:S(2)}) collective-permute-start(bf16[2,2,16,512]{3,2,1,0:T(8,128)(2,1)S(1)} %pad_maximum_fusion.14), channel_id=1, source_target_pairs={{0,8},{1,13},{2,10},{3,15},{4,12},{5,9},{6,14},{7,11},{8,16},{9,21... | collective-permute-start | bytes 196616 | tf_op jit(solution)/shard_map/ppermute | solution.py:59
  78.2 5.9 %collective-permute-done.30 = bf16[2,2,16,512]{3,2,1,0:T(8,128)(2,1)S(1)} collective-permute-done((bf16[2,2,16,512]{3,2,1,0:T(8,128)(2,1)S(1)}, bf16[2,2,16,512]{3,2,1,0:T(8,128)(2,1)S(1)}, u32[]{:S(2)}, u32[]{:S(2)}) %collective-permute-start.30) | collective-permute-done | bytes 65568 | tf_op jit(solution)/shard_map/ppermute | solution.py:59
  84.9 1.3 collective-permute-done.31.refs_1_
  86.2 1.4 collective-permute-start.34
  87.6 1.1 collective-permute-start.33
  89.7 1.3 collective-permute-done.34
  91.5 1.1 collective-permute-done.32
  92.8 1.3 collective-permute-done.35.refs_1_
  94.1 1.4 collective-permute-start.38
  97.6 1.3 collective-permute-done.38
  100.5 1.3 collective-permute-done.39.refs_1_
  103.1 3.9 %collective-permute-start.42 = (bf16[2,2,16,512]{3,2,1,0:T(8,128)(2,1)S(1)}, bf16[2,2,16,512]{3,2,1,0:T(8,128)(2,1)S(1)}, u32[]{:S(2)}, u32[]{:S(2)}) collective-permute-start(bf16[2,2,16,512]{3,2,1,0:T(8,128)(2,1)S(1)} %pad_maximum_fusion.15), channel_id=1, source_target_pairs={{0,26},{1,31},{2,24},{3,29},{4,30},{5,27},{6,28},{7,25},{8,2},{9,7... | collective-permute-start | bytes 196616 | tf_op jit(solution)/shard_map/ppermute | solution.py:59
  107.0 2.5 %collective-permute-done.42 = bf16[2,2,16,512]{3,2,1,0:T(8,128)(2,1)S(1)} collective-permute-done((bf16[2,2,16,512]{3,2,1,0:T(8,128)(2,1)S(1)}, bf16[2,2,16,512]{3,2,1,0:T(8,128)(2,1)S(1)}, u32[]{:S(2)}, u32[]{:S(2)}) %collective-permute-start.42) | collective-permute-done | bytes 65568 | tf_op jit(solution)/shard_map/ppermute | solution.py:59
  109.5 2.3 %collective-permute-done.41 = bf16[2,2,16,512]{3,2,1,0:T(8,128)(2,1)S(1)} collective-permute-done((bf16[2,2,16,512]{3,2,1,0:T(8,128)(2,1)S(1)}, bf16[2,2,16,512]{3,2,1,0:T(8,128)(2,1)S(1)}, u32[]{:S(2)}, u32[]{:S(2)}) %collective-permute-start.41) | collective-permute-done | bytes 65568 | tf_op jit(solution)/shard_map/ppermute | solution.py:59
  112.0 1.1 collective-permute-done.43.refs_1_
  113.2 1.6 collective-permute-start.46
  116.7 1.3 collective-permute-done.46
  119.8 1.3 collective-permute-done.47.refs_1_
  122.3 3.6 %collective-permute-start.50 = (bf16[2,2,16,512]{3,2,1,0:T(8,128)(2,1)S(1)}, bf16[2,2,16,512]{3,2,1,0:T(8,128)(2,1)S(1)}, u32[]{:S(2)}, u32[]{:S(2)}) collective-permute-start(bf16[2,2,16,512]{3,2,1,0:T(8,128)(2,1)S(1)} %pad_maximum_fusion.16), channel_id=1, source_target_pairs={{0,26},{1,31},{2,24},{3,29},{4,30},{5,27},{6,28},{7,25},{8,2},{9,7... | collective-permute-start | bytes 196616 | tf_op jit(solution)/shard_map/ppermute | solution.py:59
  125.9 2.4 %collective-permute-done.50 = bf16[2,2,16,512]{3,2,1,0:T(8,128)(2,1)S(1)} collective-permute-done((bf16[2,2,16,512]{3,2,1,0:T(8,128)(2,1)S(1)}, bf16[2,2,16,512]{3,2,1,0:T(8,128)(2,1)S(1)}, u32[]{:S(2)}, u32[]{:S(2)}) %collective-permute-start.50) | collective-permute-done | bytes 65568 | tf_op jit(solution)/shard_map/ppermute | solution.py:59
  128.3 2.4 %collective-permute-done.49 = bf16[2,2,16,512]{3,2,1,0:T(8,128)(2,1)S(1)} collective-permute-done((bf16[2,2,16,512]{3,2,1,0:T(8,128)(2,1)S(1)}, bf16[2,2,16,512]{3,2,1,0:T(8,128)(2,1)S(1)}, u32[]{:S(2)}, u32[]{:S(2)}) %collective-permute-start.49) | collective-permute-done | bytes 65568 | tf_op jit(solution)/shard_map/ppermute | solution.py:59
  130.8 1.3 collective-permute-done.51.refs_1_
  132.1 1.4 collective-permute-start.54
  135.6 1.3 collective-permute-done.54
  138.6 1.3 collective-permute-done.55.refs_1_
  141.1 3.4 %collective-permute-start.58 = (bf16[2,2,16,512]{3,2,1,0:T(8,128)(2,1)S(1)}, bf16[2,2,16,512]{3,2,1,0:T(8,128)(2,1)S(1)}, u32[]{:S(2)}, u32[]{:S(2)}) collective-permute-start(bf16[2,2,16,512]{3,2,1,0:T(8,128)(2,1)S(1)} %pad_maximum_fusion.17), channel_id=1, source_target_pairs={{0,26},{1,31},{2,24},{3,29},{4,30},{5,27},{6,28},{7,25},{8,2},{9,7... | collective-permute-start | bytes 196616 | tf_op jit(solution)/shard_map/ppermute | solution.py:59
  144.6 2.5 %collective-permute-done.58 = bf16[2,2,16,512]{3,2,1,0:T(8,128)(2,1)S(1)} collective-permute-done((bf16[2,2,16,512]{3,2,1,0:T(8,128)(2,1)S(1)}, bf16[2,2,16,512]{3,2,1,0:T(8,128)(2,1)S(1)}, u32[]{:S(2)}, u32[]{:S(2)}) %collective-permute-start.58) | collective-permute-done | bytes 65568 | tf_op jit(solution)/shard_map/ppermute | solution.py:59
  147.1 2.3 %collective-permute-done.57 = bf16[2,2,16,512]{3,2,1,0:T(8,128)(2,1)S(1)} collective-permute-done((bf16[2,2,16,512]{3,2,1,0:T(8,128)(2,1)S(1)}, bf16[2,2,16,512]{3,2,1,0:T(8,128)(2,1)S(1)}, u32[]{:S(2)}, u32[]{:S(2)}) %collective-permute-start.57) | collective-permute-done | bytes 65568 | tf_op jit(solution)/shard_map/ppermute | solution.py:59
  151.6 1.6 collective-permute-start.62
  155.2 1.3 collective-permute-done.62
  161.1 1.5 collective-permute-start.66
  163.5 1.1 collective-permute-start.64
  164.6 1.7 %collective-permute-done.66 = bf16[2,2,16,512]{3,2,1,0:T(8,128)(2,1)S(1)} collective-permute-done((bf16[2,2,16,512]{3,2,1,0:T(8,128)(2,1)S(1)}, bf16[2,2,16,512]{3,2,1,0:T(8,128)(2,1)S(1)}, u32[]{:S(2)}, u32[]{:S(2)}) %collective-permute-start.66) | collective-permute-done | bytes 65568 | tf_op jit(solution)/shard_map/ppermute | solution.py:27
  166.3 1.2 collective-permute-done.65
  169.4 1.3 shard_map.132
  (143 shorter events, 48.0 us)
Async XLA Ops:
  3.8 8.0 %collective-permute-start.2 = (f32[72,256]{1,0:T(8,128)S(1)}, f32[72,256]{1,0:T(8,128)S(1)}, u32[]{:S(2)}, u32[]{:S(2)}) collective-permute-start(f32[72,256]{1,0:T(8,128)S(1)} %get-tuple-element.56.after_ref), channel_id=1, source_target_pairs={{0,2},{1,3},{2,0},{3,1},{4,6},{5,7},{6,4},{7,5},{8,10},{9,11},{10,... | collective-permute-start | bytes 221192 | tf_op jit(solution)/shard_map/ppermute | solution.py:27
  6.8 5.0 %collective-permute-start.1 = (f32[72,256]{1,0:T(8,128)S(1)}, f32[72,256]{1,0:T(8,128)S(1)}, u32[]{:S(2)}, u32[]{:S(2)}) collective-permute-start(f32[72,256]{1,0:T(8,128)S(1)} %get-tuple-element.56.after_ref), channel_id=1, source_target_pairs={{0,4},{1,5},{2,6},{3,7},{4,0},{5,1},{6,2},{7,3},{8,12},{9,13},{10,... | collective-permute-start | bytes 221192 | tf_op jit(solution)/shard_map/ppermute | solution.py:27
  8.3 5.3 %collective-permute-start = (f32[72,256]{1,0:T(8,128)S(1)}, f32[72,256]{1,0:T(8,128)S(1)}, u32[]{:S(2)}, u32[]{:S(2)}) collective-permute-start(f32[72,256]{1,0:T(8,128)S(1)} %get-tuple-element.56.after_ref), channel_id=1, source_target_pairs={{0,6},{1,7},{2,4},{3,5},{4,2},{5,3},{6,0},{7,1},{8,14},{9,15},{10,... | collective-permute-start | bytes 221192 | tf_op jit(solution)/shard_map/ppermute | solution.py:27
  13.6 1.6 collective-permute-start.3
  17.2 7.0 %collective-permute-start.6 = (bf16[2,16,512]{2,1,0:T(8,128)(2,1)S(1)}, bf16[2,16,512]{2,1,0:T(8,128)(2,1)S(1)}, u32[]{:S(2)}, u32[]{:S(2)}) collective-permute-start(bf16[2,16,512]{2,1,0:T(8,128)(2,1)S(1)} %get-tuple-element.63.after_ref.refs_7_), channel_id=1, source_target_pairs={{0,2},{1,3},{2,0},{3,1},{4,6},{5,7},{6,4},{7,5},{8,10},{9,11},{10,... | collective-permute-start | bytes 98312 | tf_op jit(solution)/shard_map/ppermute | solution.py:27
  17.7 6.4 %collective-permute-start.5 = (bf16[2,16,512]{2,1,0:T(8,128)(2,1)S(1)}, bf16[2,16,512]{2,1,0:T(8,128)(2,1)S(1)}, u32[]{:S(2)}, u32[]{:S(2)}) collective-permute-start(bf16[2,16,512]{2,1,0:T(8,128)(2,1)S(1)} %get-tuple-element.63.after_ref.refs_7_), channel_id=1, source_target_pairs={{0,4},{1,5},{2,6},{3,7},{4,0},{5,1},{6,2},{7,3},{8,12},{9,13},{10,... | collective-permute-start | bytes 98312 | tf_op jit(solution)/shard_map/ppermute | solution.py:27
  18.9 5.2 %collective-permute-start.4 = (bf16[2,16,512]{2,1,0:T(8,128)(2,1)S(1)}, bf16[2,16,512]{2,1,0:T(8,128)(2,1)S(1)}, u32[]{:S(2)}, u32[]{:S(2)}) collective-permute-start(bf16[2,16,512]{2,1,0:T(8,128)(2,1)S(1)} %get-tuple-element.63.after_ref.refs_7_), channel_id=1, source_target_pairs={{0,6},{1,7},{2,4},{3,5},{4,2},{5,3},{6,0},{7,1},{8,14},{9,15},{10,... | collective-permute-start | bytes 98312 | tf_op jit(solution)/shard_map/ppermute | solution.py:27
  24.2 3.9 %collective-permute-start.7 = (bf16[4,2,16,512]{3,2,1,0:T(8,128)(2,1)S(1)}, bf16[4,2,16,512]{3,2,1,0:T(8,128)(2,1)S(1)}, u32[]{:S(2)}, u32[]{:S(2)}) collective-permute-start(bf16[4,2,16,512]{3,2,1,0:T(8,128)(2,1)S(1)} %pad_maximum_fusion.2.mine_ref), channel_id=1, source_target_pairs={{0,1},{1,0},{2,3},{3,2},{4,5},{5,4},{6,7},{7,6},{8,9},{9,8},{10,11... | collective-permute-start | bytes 393224 | tf_op jit(solution)/shard_map/ppermute | solution.py:27
  29.0 4.9 %collective-permute-start.10 = (bf16[2,16,512]{2,1,0:T(8,128)(2,1)S(1)}, bf16[2,16,512]{2,1,0:T(8,128)(2,1)S(1)}, u32[]{:S(2)}, u32[]{:S(2)}) collective-permute-start(bf16[2,16,512]{2,1,0:T(8,128)(2,1)S(1)} %get-tuple-element.71.refs_5_), channel_id=1, source_target_pairs={{0,6},{1,7},{2,4},{3,5},{4,2},{5,3},{6,0},{7,1},{8,14},{9,15},{10,... | collective-permute-start | bytes 98312 | tf_op jit(solution)/shard_map/ppermute | solution.py:27
  30.4 4.1 %collective-permute-start.9 = (bf16[2,16,512]{2,1,0:T(8,128)(2,1)S(1)}, bf16[2,16,512]{2,1,0:T(8,128)(2,1)S(1)}, u32[]{:S(2)}, u32[]{:S(2)}) collective-permute-start(bf16[2,16,512]{2,1,0:T(8,128)(2,1)S(1)} %get-tuple-element.71.refs_5_), channel_id=1, source_target_pairs={{0,4},{1,5},{2,6},{3,7},{4,0},{5,1},{6,2},{7,3},{8,12},{9,13},{10,... | collective-permute-start | bytes 98312 | tf_op jit(solution)/shard_map/ppermute | solution.py:27
  31.1 3.9 %collective-permute-start.8 = (bf16[2,16,512]{2,1,0:T(8,128)(2,1)S(1)}, bf16[2,16,512]{2,1,0:T(8,128)(2,1)S(1)}, u32[]{:S(2)}, u32[]{:S(2)}) collective-permute-start(bf16[2,16,512]{2,1,0:T(8,128)(2,1)S(1)} %get-tuple-element.71.refs_5_), channel_id=1, source_target_pairs={{0,2},{1,3},{2,0},{3,1},{4,6},{5,7},{6,4},{7,5},{8,10},{9,11},{10,... | collective-permute-start | bytes 98312 | tf_op jit(solution)/shard_map/ppermute | solution.py:27
  35.0 1.4 collective-permute-start.11
  37.3 1.3 collective-permute-start.12
  38.6 7.7 %collective-permute-start.14 = (bf16[2,2,16,512]{3,2,1,0:T(8,128)(2,1)S(1)}, bf16[2,2,16,512]{3,2,1,0:T(8,128)(2,1)S(1)}, u32[]{:S(2)}, u32[]{:S(2)}) collective-permute-start(bf16[2,2,16,512]{3,2,1,0:T(8,128)(2,1)S(1)} %pad_maximum_fusion.12), channel_id=1, source_target_pairs={{0,10},{1,15},{2,8},{3,13},{4,14},{5,11},{6,12},{7,9},{8,18},{9,23... | collective-permute-start | bytes 196616 | tf_op jit(solution)/shard_map/ppermute | solution.py:59
  40.2 6.8 %collective-permute-start.13 = (bf16[2,2,16,512]{3,2,1,0:T(8,128)(2,1)S(1)}, bf16[2,2,16,512]{3,2,1,0:T(8,128)(2,1)S(1)}, u32[]{:S(2)}, u32[]{:S(2)}) collective-permute-start(bf16[2,2,16,512]{3,2,1,0:T(8,128)(2,1)S(1)} %pad_maximum_fusion.12), channel_id=1, source_target_pairs={{0,8},{1,13},{2,10},{3,15},{4,12},{5,9},{6,14},{7,11},{8,16},{9,21... | collective-permute-start | bytes 196616 | tf_op jit(solution)/shard_map/ppermute | solution.py:59
  47.1 1.5 collective-permute-start.15
  48.6 4.9 %collective-permute-start.18 = (bf16[2,16,512]{2,1,0:T(8,128)(2,1)S(1)}, bf16[2,16,512]{2,1,0:T(8,128)(2,1)S(1)}, u32[]{:S(2)}, u32[]{:S(2)}) collective-permute-start(bf16[2,16,512]{2,1,0:T(8,128)(2,1)S(1)} %get-tuple-element.76.refs_5_), channel_id=1, source_target_pairs={{0,6},{1,7},{2,4},{3,5},{4,2},{5,3},{6,0},{7,1},{8,14},{9,15},{10,... | collective-permute-start | bytes 98312 | tf_op jit(solution)/shard_map/ppermute | solution.py:27
  50.0 3.9 %collective-permute-start.17 = (bf16[2,16,512]{2,1,0:T(8,128)(2,1)S(1)}, bf16[2,16,512]{2,1,0:T(8,128)(2,1)S(1)}, u32[]{:S(2)}, u32[]{:S(2)}) collective-permute-start(bf16[2,16,512]{2,1,0:T(8,128)(2,1)S(1)} %get-tuple-element.76.refs_5_), channel_id=1, source_target_pairs={{0,4},{1,5},{2,6},{3,7},{4,0},{5,1},{6,2},{7,3},{8,12},{9,13},{10,... | collective-permute-start | bytes 98312 | tf_op jit(solution)/shard_map/ppermute | solution.py:27
  51.1 3.9 %collective-permute-start.16 = (bf16[2,16,512]{2,1,0:T(8,128)(2,1)S(1)}, bf16[2,16,512]{2,1,0:T(8,128)(2,1)S(1)}, u32[]{:S(2)}, u32[]{:S(2)}) collective-permute-start(bf16[2,16,512]{2,1,0:T(8,128)(2,1)S(1)} %get-tuple-element.76.refs_5_), channel_id=1, source_target_pairs={{0,2},{1,3},{2,0},{3,1},{4,6},{5,7},{6,4},{7,5},{8,10},{9,11},{10,... | collective-permute-start | bytes 98312 | tf_op jit(solution)/shard_map/ppermute | solution.py:27
  55.0 1.4 collective-permute-start.19
  56.5 1.2 collective-permute-start.20
  57.7 7.6 %collective-permute-start.22 = (bf16[2,2,16,512]{3,2,1,0:T(8,128)(2,1)S(1)}, bf16[2,2,16,512]{3,2,1,0:T(8,128)(2,1)S(1)}, u32[]{:S(2)}, u32[]{:S(2)}) collective-permute-start(bf16[2,2,16,512]{3,2,1,0:T(8,128)(2,1)S(1)} %pad_maximum_fusion.13), channel_id=1, source_target_pairs={{0,10},{1,15},{2,8},{3,13},{4,14},{5,11},{6,12},{7,9},{8,18},{9,23... | collective-permute-start | bytes 196616 | tf_op jit(solution)/shard_map/ppermute | solution.py:59
  59.4 6.6 %collective-permute-start.21 = (bf16[2,2,16,512]{3,2,1,0:T(8,128)(2,1)S(1)}, bf16[2,2,16,512]{3,2,1,0:T(8,128)(2,1)S(1)}, u32[]{:S(2)}, u32[]{:S(2)}) collective-permute-start(bf16[2,2,16,512]{3,2,1,0:T(8,128)(2,1)S(1)} %pad_maximum_fusion.13), channel_id=1, source_target_pairs={{0,8},{1,13},{2,10},{3,15},{4,12},{5,9},{6,14},{7,11},{8,16},{9,21... | collective-permute-start | bytes 196616 | tf_op jit(solution)/shard_map/ppermute | solution.py:59
  66.0 1.4 collective-permute-start.23
  67.4 4.8 %collective-permute-start.26 = (bf16[2,16,512]{2,1,0:T(8,128)(2,1)S(1)}, bf16[2,16,512]{2,1,0:T(8,128)(2,1)S(1)}, u32[]{:S(2)}, u32[]{:S(2)}) collective-permute-start(bf16[2,16,512]{2,1,0:T(8,128)(2,1)S(1)} %get-tuple-element.80.refs_5_), channel_id=1, source_target_pairs={{0,6},{1,7},{2,4},{3,5},{4,2},{5,3},{6,0},{7,1},{8,14},{9,15},{10,... | collective-permute-start | bytes 98312 | tf_op jit(solution)/shard_map/ppermute | solution.py:27
  68.9 3.9 %collective-permute-start.25 = (bf16[2,16,512]{2,1,0:T(8,128)(2,1)S(1)}, bf16[2,16,512]{2,1,0:T(8,128)(2,1)S(1)}, u32[]{:S(2)}, u32[]{:S(2)}) collective-permute-start(bf16[2,16,512]{2,1,0:T(8,128)(2,1)S(1)} %get-tuple-element.80.refs_5_), channel_id=1, source_target_pairs={{0,4},{1,5},{2,6},{3,7},{4,0},{5,1},{6,2},{7,3},{8,12},{9,13},{10,... | collective-permute-start | bytes 98312 | tf_op jit(solution)/shard_map/ppermute | solution.py:27
  69.8 3.9 %collective-permute-start.24 = (bf16[2,16,512]{2,1,0:T(8,128)(2,1)S(1)}, bf16[2,16,512]{2,1,0:T(8,128)(2,1)S(1)}, u32[]{:S(2)}, u32[]{:S(2)}) collective-permute-start(bf16[2,16,512]{2,1,0:T(8,128)(2,1)S(1)} %get-tuple-element.80.refs_5_), channel_id=1, source_target_pairs={{0,2},{1,3},{2,0},{3,1},{4,6},{5,7},{6,4},{7,5},{8,10},{9,11},{10,... | collective-permute-start | bytes 98312 | tf_op jit(solution)/shard_map/ppermute | solution.py:27
  73.7 1.4 collective-permute-start.27
  76.3 7.7 %collective-permute-start.30 = (bf16[2,2,16,512]{3,2,1,0:T(8,128)(2,1)S(1)}, bf16[2,2,16,512]{3,2,1,0:T(8,128)(2,1)S(1)}, u32[]{:S(2)}, u32[]{:S(2)}) collective-permute-start(bf16[2,2,16,512]{3,2,1,0:T(8,128)(2,1)S(1)} %pad_maximum_fusion.14), channel_id=1, source_target_pairs={{0,10},{1,15},{2,8},{3,13},{4,14},{5,11},{6,12},{7,9},{8,18},{9,23... | collective-permute-start | bytes 196616 | tf_op jit(solution)/shard_map/ppermute | solution.py:59
  76.4 8.3 %collective-permute-start.29 = (bf16[2,2,16,512]{3,2,1,0:T(8,128)(2,1)S(1)}, bf16[2,2,16,512]{3,2,1,0:T(8,128)(2,1)S(1)}, u32[]{:S(2)}, u32[]{:S(2)}) collective-permute-start(bf16[2,2,16,512]{3,2,1,0:T(8,128)(2,1)S(1)} %pad_maximum_fusion.14), channel_id=1, source_target_pairs={{0,8},{1,13},{2,10},{3,15},{4,12},{5,9},{6,14},{7,11},{8,16},{9,21... | collective-permute-start | bytes 196616 | tf_op jit(solution)/shard_map/ppermute | solution.py:59
  84.8 1.4 collective-permute-start.31
  86.2 4.8 %collective-permute-start.34 = (bf16[2,16,512]{2,1,0:T(8,128)(2,1)S(1)}, bf16[2,16,512]{2,1,0:T(8,128)(2,1)S(1)}, u32[]{:S(2)}, u32[]{:S(2)}) collective-permute-start(bf16[2,16,512]{2,1,0:T(8,128)(2,1)S(1)} %get-tuple-element.84.refs_6_), channel_id=1, source_target_pairs={{0,6},{1,7},{2,4},{3,5},{4,2},{5,3},{6,0},{7,1},{8,14},{9,15},{10,... | collective-permute-start | bytes 98312 | tf_op jit(solution)/shard_map/ppermute | solution.py:27
  87.6 3.9 %collective-permute-start.33 = (bf16[2,16,512]{2,1,0:T(8,128)(2,1)S(1)}, bf16[2,16,512]{2,1,0:T(8,128)(2,1)S(1)}, u32[]{:S(2)}, u32[]{:S(2)}) collective-permute-start(bf16[2,16,512]{2,1,0:T(8,128)(2,1)S(1)} %get-tuple-element.84.refs_6_), channel_id=1, source_target_pairs={{0,4},{1,5},{2,6},{3,7},{4,0},{5,1},{6,2},{7,3},{8,12},{9,13},{10,... | collective-permute-start | bytes 98312 | tf_op jit(solution)/shard_map/ppermute | solution.py:27
  88.7 3.9 %collective-permute-start.32 = (bf16[2,16,512]{2,1,0:T(8,128)(2,1)S(1)}, bf16[2,16,512]{2,1,0:T(8,128)(2,1)S(1)}, u32[]{:S(2)}, u32[]{:S(2)}) collective-permute-start(bf16[2,16,512]{2,1,0:T(8,128)(2,1)S(1)} %get-tuple-element.84.refs_6_), channel_id=1, source_target_pairs={{0,2},{1,3},{2,0},{3,1},{4,6},{5,7},{6,4},{7,5},{8,10},{9,11},{10,... | collective-permute-start | bytes 98312 | tf_op jit(solution)/shard_map/ppermute | solution.py:27
  92.6 1.4 collective-permute-start.35
  94.1 4.8 %collective-permute-start.38 = (bf16[2,16,512]{2,1,0:T(8,128)(2,1)S(1)}, bf16[2,16,512]{2,1,0:T(8,128)(2,1)S(1)}, u32[]{:S(2)}, u32[]{:S(2)}) collective-permute-start(bf16[2,16,512]{2,1,0:T(8,128)(2,1)S(1)} %get-tuple-element.87.refs_6_), channel_id=1, source_target_pairs={{0,6},{1,7},{2,4},{3,5},{4,2},{5,3},{6,0},{7,1},{8,14},{9,15},{10,... | collective-permute-start | bytes 98312 | tf_op jit(solution)/shard_map/ppermute | solution.py:27
  95.5 3.9 %collective-permute-start.37 = (bf16[2,16,512]{2,1,0:T(8,128)(2,1)S(1)}, bf16[2,16,512]{2,1,0:T(8,128)(2,1)S(1)}, u32[]{:S(2)}, u32[]{:S(2)}) collective-permute-start(bf16[2,16,512]{2,1,0:T(8,128)(2,1)S(1)} %get-tuple-element.87.refs_6_), channel_id=1, source_target_pairs={{0,4},{1,5},{2,6},{3,7},{4,0},{5,1},{6,2},{7,3},{8,12},{9,13},{10,... | collective-permute-start | bytes 98312 | tf_op jit(solution)/shard_map/ppermute | solution.py:27
  96.5 3.9 %collective-permute-start.36 = (bf16[2,16,512]{2,1,0:T(8,128)(2,1)S(1)}, bf16[2,16,512]{2,1,0:T(8,128)(2,1)S(1)}, u32[]{:S(2)}, u32[]{:S(2)}) collective-permute-start(bf16[2,16,512]{2,1,0:T(8,128)(2,1)S(1)} %get-tuple-element.87.refs_6_), channel_id=1, source_target_pairs={{0,2},{1,3},{2,0},{3,1},{4,6},{5,7},{6,4},{7,5},{8,10},{9,11},{10,... | collective-permute-start | bytes 98312 | tf_op jit(solution)/shard_map/ppermute | solution.py:27
  100.4 1.4 collective-permute-start.39
  103.1 6.4 %collective-permute-start.42 = (bf16[2,2,16,512]{3,2,1,0:T(8,128)(2,1)S(1)}, bf16[2,2,16,512]{3,2,1,0:T(8,128)(2,1)S(1)}, u32[]{:S(2)}, u32[]{:S(2)}) collective-permute-start(bf16[2,2,16,512]{3,2,1,0:T(8,128)(2,1)S(1)} %pad_maximum_fusion.15), channel_id=1, source_target_pairs={{0,26},{1,31},{2,24},{3,29},{4,30},{5,27},{6,28},{7,25},{8,2},{9,7... | collective-permute-start | bytes 196616 | tf_op jit(solution)/shard_map/ppermute | solution.py:59
  107.0 4.8 %collective-permute-start.41 = (bf16[2,2,16,512]{3,2,1,0:T(8,128)(2,1)S(1)}, bf16[2,2,16,512]{3,2,1,0:T(8,128)(2,1)S(1)}, u32[]{:S(2)}, u32[]{:S(2)}) collective-permute-start(bf16[2,2,16,512]{3,2,1,0:T(8,128)(2,1)S(1)} %pad_maximum_fusion.15), channel_id=1, source_target_pairs={{0,24},{1,29},{2,26},{3,31},{4,28},{5,25},{6,30},{7,27},{8,0},{9,5... | collective-permute-start | bytes 196616 | tf_op jit(solution)/shard_map/ppermute | solution.py:59
  111.8 1.4 collective-permute-start.43
  113.2 4.8 %collective-permute-start.46 = (bf16[2,16,512]{2,1,0:T(8,128)(2,1)S(1)}, bf16[2,16,512]{2,1,0:T(8,128)(2,1)S(1)}, u32[]{:S(2)}, u32[]{:S(2)}) collective-permute-start(bf16[2,16,512]{2,1,0:T(8,128)(2,1)S(1)} %get-tuple-element.92.refs_6_), channel_id=1, source_target_pairs={{0,6},{1,7},{2,4},{3,5},{4,2},{5,3},{6,0},{7,1},{8,14},{9,15},{10,... | collective-permute-start | bytes 98312 | tf_op jit(solution)/shard_map/ppermute | solution.py:27
  114.7 3.9 %collective-permute-start.45 = (bf16[2,16,512]{2,1,0:T(8,128)(2,1)S(1)}, bf16[2,16,512]{2,1,0:T(8,128)(2,1)S(1)}, u32[]{:S(2)}, u32[]{:S(2)}) collective-permute-start(bf16[2,16,512]{2,1,0:T(8,128)(2,1)S(1)} %get-tuple-element.92.refs_6_), channel_id=1, source_target_pairs={{0,4},{1,5},{2,6},{3,7},{4,0},{5,1},{6,2},{7,3},{8,12},{9,13},{10,... | collective-permute-start | bytes 98312 | tf_op jit(solution)/shard_map/ppermute | solution.py:27
  115.8 3.9 %collective-permute-start.44 = (bf16[2,16,512]{2,1,0:T(8,128)(2,1)S(1)}, bf16[2,16,512]{2,1,0:T(8,128)(2,1)S(1)}, u32[]{:S(2)}, u32[]{:S(2)}) collective-permute-start(bf16[2,16,512]{2,1,0:T(8,128)(2,1)S(1)} %get-tuple-element.92.refs_6_), channel_id=1, source_target_pairs={{0,2},{1,3},{2,0},{3,1},{4,6},{5,7},{6,4},{7,5},{8,10},{9,11},{10,... | collective-permute-start | bytes 98312 | tf_op jit(solution)/shard_map/ppermute | solution.py:27
  119.7 1.4 collective-permute-start.47
  122.3 6.0 %collective-permute-start.50 = (bf16[2,2,16,512]{3,2,1,0:T(8,128)(2,1)S(1)}, bf16[2,2,16,512]{3,2,1,0:T(8,128)(2,1)S(1)}, u32[]{:S(2)}, u32[]{:S(2)}) collective-permute-start(bf16[2,2,16,512]{3,2,1,0:T(8,128)(2,1)S(1)} %pad_maximum_fusion.16), channel_id=1, source_target_pairs={{0,26},{1,31},{2,24},{3,29},{4,30},{5,27},{6,28},{7,25},{8,2},{9,7... | collective-permute-start | bytes 196616 | tf_op jit(solution)/shard_map/ppermute | solution.py:59
  125.9 4.8 %collective-permute-start.49 = (bf16[2,2,16,512]{3,2,1,0:T(8,128)(2,1)S(1)}, bf16[2,2,16,512]{3,2,1,0:T(8,128)(2,1)S(1)}, u32[]{:S(2)}, u32[]{:S(2)}) collective-permute-start(bf16[2,2,16,512]{3,2,1,0:T(8,128)(2,1)S(1)} %pad_maximum_fusion.16), channel_id=1, source_target_pairs={{0,24},{1,29},{2,26},{3,31},{4,28},{5,25},{6,30},{7,27},{8,0},{9,5... | collective-permute-start | bytes 196616 | tf_op jit(solution)/shard_map/ppermute | solution.py:59
  130.7 1.4 collective-permute-start.51
  132.1 4.8 %collective-permute-start.54 = (bf16[2,16,512]{2,1,0:T(8,128)(2,1)S(1)}, bf16[2,16,512]{2,1,0:T(8,128)(2,1)S(1)}, u32[]{:S(2)}, u32[]{:S(2)}) collective-permute-start(bf16[2,16,512]{2,1,0:T(8,128)(2,1)S(1)} %get-tuple-element.96.refs_6_), channel_id=1, source_target_pairs={{0,6},{1,7},{2,4},{3,5},{4,2},{5,3},{6,0},{7,1},{8,14},{9,15},{10,... | collective-permute-start | bytes 98312 | tf_op jit(solution)/shard_map/ppermute | solution.py:27
  133.5 3.9 %collective-permute-start.53 = (bf16[2,16,512]{2,1,0:T(8,128)(2,1)S(1)}, bf16[2,16,512]{2,1,0:T(8,128)(2,1)S(1)}, u32[]{:S(2)}, u32[]{:S(2)}) collective-permute-start(bf16[2,16,512]{2,1,0:T(8,128)(2,1)S(1)} %get-tuple-element.96.refs_6_), channel_id=1, source_target_pairs={{0,4},{1,5},{2,6},{3,7},{4,0},{5,1},{6,2},{7,3},{8,12},{9,13},{10,... | collective-permute-start | bytes 98312 | tf_op jit(solution)/shard_map/ppermute | solution.py:27
  134.5 3.9 %collective-permute-start.52 = (bf16[2,16,512]{2,1,0:T(8,128)(2,1)S(1)}, bf16[2,16,512]{2,1,0:T(8,128)(2,1)S(1)}, u32[]{:S(2)}, u32[]{:S(2)}) collective-permute-start(bf16[2,16,512]{2,1,0:T(8,128)(2,1)S(1)} %get-tuple-element.96.refs_6_), channel_id=1, source_target_pairs={{0,2},{1,3},{2,0},{3,1},{4,6},{5,7},{6,4},{7,5},{8,10},{9,11},{10,... | collective-permute-start | bytes 98312 | tf_op jit(solution)/shard_map/ppermute | solution.py:27
  138.5 1.4 collective-permute-start.55
  141.1 5.9 %collective-permute-start.58 = (bf16[2,2,16,512]{3,2,1,0:T(8,128)(2,1)S(1)}, bf16[2,2,16,512]{3,2,1,0:T(8,128)(2,1)S(1)}, u32[]{:S(2)}, u32[]{:S(2)}) collective-permute-start(bf16[2,2,16,512]{3,2,1,0:T(8,128)(2,1)S(1)} %pad_maximum_fusion.17), channel_id=1, source_target_pairs={{0,26},{1,31},{2,24},{3,29},{4,30},{5,27},{6,28},{7,25},{8,2},{9,7... | collective-permute-start | bytes 196616 | tf_op jit(solution)/shard_map/ppermute | solution.py:59
  144.6 4.8 %collective-permute-start.57 = (bf16[2,2,16,512]{3,2,1,0:T(8,128)(2,1)S(1)}, bf16[2,2,16,512]{3,2,1,0:T(8,128)(2,1)S(1)}, u32[]{:S(2)}, u32[]{:S(2)}) collective-permute-start(bf16[2,2,16,512]{3,2,1,0:T(8,128)(2,1)S(1)} %pad_maximum_fusion.17), channel_id=1, source_target_pairs={{0,24},{1,29},{2,26},{3,31},{4,28},{5,25},{6,30},{7,27},{8,0},{9,5... | collective-permute-start | bytes 196616 | tf_op jit(solution)/shard_map/ppermute | solution.py:59
  149.4 1.4 collective-permute-start.59
  151.6 4.9 %collective-permute-start.62 = (bf16[2,16,512]{2,1,0:T(8,128)(2,1)S(1)}, bf16[2,16,512]{2,1,0:T(8,128)(2,1)S(1)}, u32[]{:S(2)}, u32[]{:S(2)}) collective-permute-start(bf16[2,16,512]{2,1,0:T(8,128)(2,1)S(1)} %get-tuple-element.100.refs_6_), channel_id=1, source_target_pairs={{0,6},{1,7},{2,4},{3,5},{4,2},{5,3},{6,0},{7,1},{8,14},{9,15},{10,... | collective-permute-start | bytes 98312 | tf_op jit(solution)/shard_map/ppermute | solution.py:27
  153.2 3.9 %collective-permute-start.61 = (bf16[2,16,512]{2,1,0:T(8,128)(2,1)S(1)}, bf16[2,16,512]{2,1,0:T(8,128)(2,1)S(1)}, u32[]{:S(2)}, u32[]{:S(2)}) collective-permute-start(bf16[2,16,512]{2,1,0:T(8,128)(2,1)S(1)} %get-tuple-element.100.refs_6_), channel_id=1, source_target_pairs={{0,4},{1,5},{2,6},{3,7},{4,0},{5,1},{6,2},{7,3},{8,12},{9,13},{10,... | collective-permute-start | bytes 98312 | tf_op jit(solution)/shard_map/ppermute | solution.py:27
  154.3 3.9 %collective-permute-start.60 = (bf16[2,16,512]{2,1,0:T(8,128)(2,1)S(1)}, bf16[2,16,512]{2,1,0:T(8,128)(2,1)S(1)}, u32[]{:S(2)}, u32[]{:S(2)}) collective-permute-start(bf16[2,16,512]{2,1,0:T(8,128)(2,1)S(1)} %get-tuple-element.100.refs_6_), channel_id=1, source_target_pairs={{0,2},{1,3},{2,0},{3,1},{4,6},{5,7},{6,4},{7,5},{8,10},{9,11},{10,... | collective-permute-start | bytes 98312 | tf_op jit(solution)/shard_map/ppermute | solution.py:27
  158.2 1.4 collective-permute-start.63
  161.1 5.2 %collective-permute-start.66 = (bf16[2,2,16,512]{3,2,1,0:T(8,128)(2,1)S(1)}, bf16[2,2,16,512]{3,2,1,0:T(8,128)(2,1)S(1)}, u32[]{:S(2)}, u32[]{:S(2)}) collective-permute-start(bf16[2,2,16,512]{3,2,1,0:T(8,128)(2,1)S(1)} %get-tuple-element.108), channel_id=1, source_target_pairs={{0,6},{1,7},{2,4},{3,5},{4,2},{5,3},{6,0},{7,1},{8,14},{9,15},{10,... | collective-permute-start | bytes 196616 | tf_op jit(solution)/shard_map/ppermute | solution.py:27
  162.6 4.9 %collective-permute-start.65 = (bf16[2,2,16,512]{3,2,1,0:T(8,128)(2,1)S(1)}, bf16[2,2,16,512]{3,2,1,0:T(8,128)(2,1)S(1)}, u32[]{:S(2)}, u32[]{:S(2)}) collective-permute-start(bf16[2,2,16,512]{3,2,1,0:T(8,128)(2,1)S(1)} %get-tuple-element.108), channel_id=1, source_target_pairs={{0,4},{1,5},{2,6},{3,7},{4,0},{5,1},{6,2},{7,3},{8,12},{9,13},{10,... | collective-permute-start | bytes 196616 | tf_op jit(solution)/shard_map/ppermute | solution.py:27
  163.5 4.3 %collective-permute-start.64 = (bf16[2,2,16,512]{3,2,1,0:T(8,128)(2,1)S(1)}, bf16[2,2,16,512]{3,2,1,0:T(8,128)(2,1)S(1)}, u32[]{:S(2)}, u32[]{:S(2)}) collective-permute-start(bf16[2,2,16,512]{3,2,1,0:T(8,128)(2,1)S(1)} %get-tuple-element.108), channel_id=1, source_target_pairs={{0,2},{1,3},{2,0},{3,1},{4,6},{5,7},{6,4},{7,5},{8,10},{9,11},{10,... | collective-permute-start | bytes 196616 | tf_op jit(solution)/shard_map/ppermute | solution.py:27
  167.8 1.6 collective-permute-start.67
  (5 other events, 16.3 us)

commit v3 on v2

v3 whole, which is shorter than its diff:
```python
import functools

import jax
import jax.numpy as jnp
from jax import lax
from jax.experimental import pallas as pl
from jax.experimental.pallas import tpu as pltpu
from jax.sharding import PartitionSpec as P

IN_VMEM = pl.BlockSpec(memory_space=pltpu.VMEM)


IN_HBM = pl.BlockSpec(memory_space=pltpu.HBM)
IN_SMEM = pl.BlockSpec(memory_space=pltpu.SMEM)


def resident(array):
    return pltpu.with_memory_space_constraint(array, pltpu.VMEM)


def in_hbm(array):
    return pltpu.with_memory_space_constraint(array, pltpu.HBM)


def swapped(shard, mask):
    peers = lax.axis_size("xy")
    return lax.ppermute(shard, "xy", [(i, i ^ mask) for i in range(peers)])


def masks_within(peers):
    masks = [0] + list(reversed(range(2, peers, 2)))
    return masks[: peers // 4], masks[peers // 4 :]


def in_halves(one, fetched, join, first, beside=()):
    pieces = [(one, swapped(one, 1))]
    made = first(one)
    fetched, made, beside = lax.optimization_barrier((fetched, made, beside))
    two = join(fetched)
    pieces.append((two, swapped(two, 1)))
    return pieces, made, beside


def gathered_within(message, first, beside=()):
    masks = masks_within(lax.axis_size("xy"))
    one, two = [
        [swapped(message, mask) if mask else message for mask in half] for half in masks
    ]
    return in_halves(jnp.stack(one), two, jnp.stack, first, beside)


def sources_within(peers):
    def sources(me):
        found = []
        for masks in masks_within(peers):
            mine = [me ^ mask for mask in masks]
            found.append((mine, [peer ^ 1 for peer in mine]))
        return found

    return sources


def crossed(message, low, arrive, first):
    peers, groups = lax.axis_size("xy"), lax.axis_size("gz")
    half = peers // 4
    pair = jnp.stack([message, swapped(message, 1)])
    parts = []
    for turn in range(half):
        pairs = []
        for group in range(groups):
            for peer in range(peers):
                if group in (low, low + 1):
                    place = (2 * low + 1 - group) * peers + (peer ^ (2 * (turn + peer % 2 * half)))
                else:
                    place = group * peers + (peer ^ 1)
                pairs.append((group * peers + peer, place))
        parts.append(lax.ppermute(pair, ("gz", "xy"), pairs))
    one = arrive(jnp.concatenate(parts[: half // 2]), 0)
    return in_halves(
        one, parts[half // 2 :], lambda rest: arrive(jnp.concatenate(rest), 1), first
    )[:2]


def sources_crossed(peers):
    half = peers // 4

    def half_of(me, turns):
        return [
            (me ^ (2 * turn) ^ (me % 2 * (2 * half))) ^ core for turn in turns for core in range(2)
        ]

    def sources(me):
        return [
            (half_of(me, turns), half_of(me ^ 1, turns))
            for turns in (range(half // 2), range(half // 2, half))
        ]

    return sources


def gated(turn):
    def wrap(body):
        if turn is None:
            body()
        else:
            pl.when(lax.axis_index("gz") == turn)(body)

    return wrap


def in_kernel(body, outs, operands, aliases=None, specs=None, scratch=(), flops=0, moved=0):
    return pl.pallas_call(
        body,
        out_shape=tuple(pltpu.VMEM(shape, dtype) for shape, dtype in outs),
        in_specs=specs or [IN_VMEM] * len(operands),
        out_specs=(IN_VMEM,) * len(outs),
        scratch_shapes=scratch,
        input_output_aliases=aliases or {},
        compiler_params=pltpu.CompilerParams(vmem_limit_bytes=16 * 2**20),
        cost_estimate=pl.CostEstimate(flops=flops, bytes_accessed=moved, transcendentals=0),
    )(*operands)


def real_products(field, matrix):
    return [
        jnp.dot(field, matrix[part], preferred_element_type=jnp.float32) for part in range(2)
    ]


def combined(products):
    first, second = products
    count = first.shape[0] // 2
    return first[:count] - second[count:], second[:count] + first[count:]


def load_kernel(panel, chunks, schur_ref, after_ref, out_ref, sems):
    del after_ref
    rows = schur_ref.shape[2] // chunks
    copies = []
    for part in range(2):
        for chunk in range(chunks):
            span = pl.ds(chunk * rows, rows)
            copies.append(
                pltpu.make_async_copy(
                    schur_ref.at[panel, part, span, :],
                    out_ref.at[part, span, :],
                    sems.at[part * chunks + chunk],
                )
            )
    for copy in copies:
        copy.start()
    for copy in copies:
        copy.wait()


def loaded(panel, schur, after):
    chunks = 4
    shape = schur.shape[1:]
    return in_kernel(
        functools.partial(load_kernel, panel, chunks),
        [(shape, schur.dtype)],
        [in_hbm(schur), after],
        specs=[IN_HBM, pl.BlockSpec(memory_space=pl.ANY)],
        scratch=[pltpu.SemaphoreType.DMA((2 * chunks,))],
        moved=2 * schur.dtype.itemsize * shape[0] * shape[1] * shape[2],
    )[0]


def local_kernel(*refs):
    operands, (solved_ref, sent_ref), held, (tail_ref, sems) = refs[:6], refs[6:8], refs[8:14], refs[14:]
    source_ref, inverse_ref, coupling_ref, rows_ref, link_ref, _ = held
    panel_count, _, side_count, _ = source_ref.shape
    bound, share = sent_ref.shape[1], link_ref.shape[1]
    copies = []
    for index, (operand, place) in enumerate(zip(operands, held)):
        for panel in range(panel_count):
            copies.append(
                pltpu.make_async_copy(
                    operand.at[panel], place.at[panel], sems.at[index * panel_count + panel]
                )
            )
    by_operand = [copies[i * panel_count : (i + 1) * panel_count] for i in range(len(operands))]
    for panel in range(panel_count):
        for index in range(3):
            by_operand[index][panel].start()
    for group in by_operand[3:]:
        for copy in group:
            copy.start()
    for panel in range(panel_count):
        by_operand[0][panel].wait()
        by_operand[1][panel].wait()
        field = source_ref[panel].astype(jnp.bfloat16).reshape(2 * side_count, -1)
        solved = combined(real_products(field, inverse_ref.at[panel, 0]))
        for part in range(2):
            solved_ref[panel, part] = solved[part]
        field = jnp.concatenate(solved).astype(jnp.bfloat16)
        by_operand[2][panel].wait()
        pushed = combined(real_products(field, coupling_ref.at[panel, 0]))
        for part in range(2):
            start = (2 * panel + part) * side_count
            sent_ref[pl.ds(start, side_count), :] = pushed[part].astype(jnp.bfloat16)
    for group in by_operand[3:]:
        for copy in group:
            copy.wait()
    tail_ref[...] = jnp.zeros(tail_ref.shape, jnp.float32)
    for panel in range(panel_count):
        rows = rows_ref[pl.ds(panel, 1), :]
        tail_ref[pl.ds(panel, 1), :] = (rows >> 8).astype(jnp.float32)
        tail_ref[pl.ds(panel_count + panel, 1), :] = (rows & 255).astype(jnp.float32)
    row = 2 * panel_count
    for start in range(0, share, bound):
        width = min(bound, share - start)
        link = link_ref[pl.ds(0, 1), pl.ds(start, width)]
        high = link.astype(jnp.bfloat16).astype(jnp.float32)
        tail_ref[pl.ds(row, 1), pl.ds(0, width)] = high
        tail_ref[pl.ds(row + 1, 1), pl.ds(0, width)] = link - high
        row += 2
    first = 2 * side_count * panel_count
    sent_ref[pl.ds(first, tail_ref.shape[0]), :] = tail_ref[...].astype(jnp.bfloat16)


def tail_of(ref, place, first):
    return ref[place, pl.ds(first, ref.shape[1] - first), :].astype(jnp.float32)


def live(size_ref, panel, start, share):
    rows = start + lax.broadcasted_iota(jnp.int32, (1, share), 1)
    return jnp.where(rows < size_ref[panel], 1.0, 0.0)


def pushed_up(panel, panel_count, count, share, refs, contrib):
    bound = refs[0].shape[2]
    own_rows = lax.axis_index("xy") * share + lax.broadcasted_iota(jnp.int32, (share, bound), 0)
    contract = (((1,), (1,)), ((), ()))
    for ref in refs:
        for place in range(ref.shape[0]):
            values = ref[place, pl.ds(count * panel, count), :]
            tail = tail_of(ref, place, count * panel_count)
            high = tail[panel : panel + 1]
            low = tail[panel_count + panel : panel_count + panel + 1]
            places = (256.0 * high + low).astype(jnp.int32)
            hits = jnp.where(own_rows == places, 1.0, 0.0).astype(jnp.bfloat16)
            contrib += lax.dot_general(values, hits, contract, preferred_element_type=jnp.float32)
    return contrib


def push_kernel(panel, panel_count, *refs):
    refs, contrib_ref = refs[:-1], refs[-1]
    count, share = contrib_ref.shape
    zeros = jnp.zeros((count, share), jnp.float32)
    contrib_ref[...] = pushed_up(panel, panel_count, count, share, refs, zeros)


def base_kernel(panel, panel_count, size_ref, contrib_ref, source_ref, *refs):
    refs, base_ref, message_ref = refs[:-2], refs[-2], refs[-1]
    _, side_count, share = base_ref.shape
    count = 2 * side_count
    contrib = pushed_up(panel, panel_count, count, share, refs, contrib_ref[...])
    mask = live(size_ref, panel, lax.axis_index("xy") * share, share)
    for part in range(2):
        rows = slice(part * side_count, (part + 1) * side_count)
        base = mask * (source_ref[panel, part] - contrib[rows])
        base_ref[part] = base
        message_ref[part] = base.astype(jnp.bfloat16)


def scales_kernel(panel_count, side_count, size_ref, link_ref, *refs):
    shards, outs = refs[:4], refs[4:]
    share, bound = link_ref.shape[1], shards[0].shape[2]
    peers = 2 * (shards[0].shape[0] + shards[2].shape[0])
    me = lax.axis_index("xy")
    masks = [live(size_ref, panel, me * share, share) for panel in range(panel_count)]
    for panel in range(panel_count):
        link = link_ref[pl.ds(panel, 1), :]
        outs[panel][...] = masks[panel]
        outs[panel_count + panel][...] = masks[panel] * link
        outs[2 * panel_count + panel][...] = link * masks[panel - 1] if panel else link
    arriving = outs[3 * panel_count :]
    first = 2 * side_count * panel_count
    links = {}
    for half, masks_half in enumerate(masks_within(peers)):
        for core in range(2):
            for place, mask in enumerate(masks_half):
                tail = tail_of(shards[2 * half + core], place, first)
                found = []
                for piece, start in enumerate(range(0, share, bound)):
                    row = 2 * (panel_count + piece)
                    link = tail[row : row + 1] + tail[row + 1 : row + 2]
                    found.append(link[:, : min(bound, share - start)])
                links[mask ^ core] = found
    for half, (origins, _) in enumerate(sources_crossed(peers)(me)):
        forward_ref, backward_ref = arriving[half], arriving[2 + half]
        for index, origin in enumerate(origins):
            turn = half * (peers // 8) + index // 2
            reached = live(size_ref, 0, origin * share, share)
            backward_ref[index, 0] = live(size_ref, panel_count - 1, origin * share, share)
            masks_of = [2 * (turn + core * (peers // 4)) ^ (index % 2) for core in range(2)]
            for piece, start in enumerate(range(0, share, bound)):
                width = min(bound, share - start)
                one, two = (links[mask][piece] for mask in masks_of)
                link = jnp.where(me % 2 == 0, one, two)
                forward_ref[index, 0, :, pl.ds(start, width)] = (
                    reached[:, start : start + width] * link
                )


def part_products(ref, origins, schur_ref, products):
    side_count, share = ref.shape[2:]
    for place, origin in enumerate(origins):
        rows = pl.ds(pl.multiple_of(origin * share, share), share)
        field = ref[place].reshape(2 * side_count, share)
        terms = real_products(field, schur_ref.at[:, rows, :])
        products = terms if products is None else [a + b for a, b in zip(products, terms)]
    return products


def early_kernel(turn, sources, stage, *refs):
    products_ref = refs[-1]

    @gated(turn)
    def _():
        (mine, other), (more, _) = sources(lax.axis_index("xy"))
        if stage == 0:
            products = part_products(refs[0], mine, refs[1], None)
        else:
            products = [refs[3][part] for part in range(2)]
            products = part_products(refs[0], other, refs[2], products)
            products = part_products(refs[1], more, refs[2], products)
        for part in range(2):
            products_ref[part] = products[part]


def late_kernel(turn, sources, names, *refs):
    named = dict(zip(names, refs))
    kept_ref, message_ref = refs[-2:]

    @gated(turn)
    def _():
        origins = sources(lax.axis_index("xy"))[1][1]
        products = [named["products"][part] for part in range(2)]
        products = part_products(named["other"], origins, named["schur"], products)
        for part, value in enumerate(combined(products)):
            value = named["mask"][...] * value
            if "kept" in named:
                value = named["kept"][part] + value
            kept_ref[part] = value
            if "scale" in named:
                value = named["scale"][...] * value
            if "addend" in named:
                value = named["addend"][part] + value
            message_ref[part] = value.astype(jnp.bfloat16)


def cost_of(mine):
    _, _, side_count, share = mine.shape
    return {
        "flops": 8 * side_count * share * share * mine.shape[0],
        "moved": 4 * share * share * mine.shape[0],
    }


def first_products(turn, sources, schur, mine):
    return in_kernel(
        functools.partial(early_kernel, turn, sources, 0),
        [((2, 2 * mine.shape[2], mine.shape[3]), jnp.float32)],
        [resident(mine), resident(schur)],
        **cost_of(mine),
    )[0]


def more_products(turn, sources, pieces, schur, products):
    (_, other), (more, _) = pieces
    return in_kernel(
        functools.partial(early_kernel, turn, sources, 1),
        [(products.shape, products.dtype)],
        [resident(value) for value in (other, more, schur, products)],
        **cost_of(other),
    )[0]


def sweep_step(turn, sources, pieces, schur, products, kept, message, adds, **others):
    products = more_products(turn, sources, pieces, schur, products)
    named = {"products": products, "other": pieces[1][1], "schur": schur}
    named.update({name: value for name, value in others.items() if value is not None})
    named["kept" if adds else "old"], named["message"] = kept, message
    count = len(named)
    return in_kernel(
        functools.partial(late_kernel, turn, sources, list(named)),
        [(kept.shape, kept.dtype), (message.shape, message.dtype)],
        [resident(value) for value in named.values()],
        aliases={count - 2: 0, count - 1: 1},
        **cost_of(pieces[1][1]),
    )


def last_step(turn, sources, pieces, schur, products, mask, kepts):
    products = more_products(turn, sources, pieces, schur, products)
    operands = [products, pieces[1][1], schur, mask] + kepts
    return in_kernel(
        functools.partial(last_kernel, turn, sources),
        [
            (kepts[0].shape, kepts[0].dtype),
            ((len(kepts),) + kepts[0].shape, jnp.bfloat16),
        ],
        [resident(value) for value in operands],
        aliases={4: 0},
        **cost_of(pieces[1][1]),
    )


def last_kernel(turn, sources, products_ref, other_ref, schur_ref, mask_ref, *refs):
    kepts, kept_ref, message_ref = refs[:-2], refs[-2], refs[-1]
    for panel in range(1, len(kepts)):
        message_ref[panel] = kepts[panel][...].astype(jnp.bfloat16)

    @gated(turn)
    def _():
        origins = sources(lax.axis_index("xy"))[1][1]
        products = [products_ref[part] for part in range(2)]
        products = part_products(other_ref, origins, schur_ref, products)
        for part, value in enumerate(combined(products)):
            value = kepts[0][part] + mask_ref[...] * value
            kept_ref[part] = value
            message_ref[0, part] = value.astype(jnp.bfloat16)

    @pl.when(lax.axis_index("gz") != turn)
    def _():
        message_ref[0] = kepts[0][...].astype(jnp.bfloat16)


def pick_kernel(mine_ref, rows_ref, picked_ref):
    origins = sources_within(4 * mine_ref.shape[0])(lax.axis_index("xy"))[0][0]
    for panel, value in enumerate(picks(mine_ref, rows_ref, origins, None)):
        picked_ref[panel] = value


def picks(ref, rows_ref, origins, picked):
    _, panel_count, _, side_count, share = ref.shape
    bound = rows_ref.shape[1]
    found = []
    for panel in range(panel_count):
        total = picked[panel] if picked else jnp.zeros((2 * side_count, bound), jnp.float32)
        for place, origin in enumerate(origins):
            rows = origin * share + lax.broadcasted_iota(jnp.int32, (share, bound), 0)
            chosen = jnp.where(rows == rows_ref[pl.ds(panel, 1), :], 1.0, 0.0).astype(jnp.bfloat16)
            field = ref[place, panel].reshape(2 * side_count, share)
            total += jnp.dot(field, chosen, preferred_element_type=jnp.float32)
        found.append(total)
    return found


def inner_kernel(
    picked_ref, other_ref, more_ref, rest_ref, rows_ref, coupling_ref, inverse_ref, solved_ref, out_ref, inner_ref, sems
):
    contract = (((1,), (1,)), ((), ()))
    (_, others), (mores, rests) = sources_within(4 * other_ref.shape[0])(lax.axis_index("xy"))
    picked = [picked_ref[panel] for panel in range(picked_ref.shape[0])]
    for ref, origins in ((other_ref, others), (more_ref, mores), (rest_ref, rests)):
        picked = picks(ref, rows_ref, origins, picked)
    copies = []
    for panel, value in enumerate(picked):
        field = value.astype(jnp.bfloat16)
        lifted = combined(
            [
                lax.dot_general(
                    field, coupling_ref[panel, 0, part], contract, preferred_element_type=jnp.float32
                )
                for part in range(2)
            ]
        )
        field = jnp.concatenate(lifted).astype(jnp.bfloat16)
        back = combined(real_products(field, inverse_ref.at[panel, 0]))
        for part in range(2):
            inner_ref[panel, part] = solved_ref[panel, part] - back[part]
        copies.append(
            pltpu.make_async_copy(inner_ref.at[panel], out_ref.at[panel], sems.at[panel])
        )
        copies[-1].start()
    for copy in copies:
        copy.wait()


def on_device(
    source_inner, source_front, inner_inverse, coupling, schur_inverse, front_rows, link, front_size
):
    peers, groups = lax.axis_size("xy"), lax.axis_size("gz")
    panel_count, _, side_count, share = source_front.shape
    bound = front_rows.shape[1]
    half = peers // 4
    local = source_inner.shape[3]

    tail_rows = 2 * panel_count + 2 * -(-share // bound)
    tail_rows += -tail_rows % 16
    sent_rows = 2 * side_count * panel_count + tail_rows
    taken = [source_inner, inner_inverse, coupling, front_rows, link, source_front]
    solved, sent, _, inverse_held, coupling_held, rows_held, link_held, source_held = in_kernel(
        local_kernel,
        [
            ((panel_count, 2, side_count, local), jnp.float32),
            ((sent_rows, bound), jnp.bfloat16),
        ]
        + [(value.shape, value.dtype) for value in taken],
        [in_hbm(value) for value in taken],
        specs=[IN_HBM] * len(taken),
        scratch=[
            pltpu.VMEM((tail_rows, bound), jnp.float32),
            pltpu.SemaphoreType.DMA((len(taken) * panel_count,)),
        ],
    )
    def push(panel, shards):
        return in_kernel(
            functools.partial(push_kernel, panel, panel_count),
            [((2 * side_count, share), jnp.float32)],
            [resident(shard) for shard in shards],
            moved=2**22,
        )[0]

    shards, contrib, schurs = gathered_within(
        sent, lambda mine: push(0, [mine]), [loaded(0, schur_inverse, sent)]
    )
    (mine, other), (more, rest) = [[resident(shard) for shard in half] for half in shards]
    bases, messages = [], []
    for panel in range(panel_count):
        if panel:
            contrib, last_shards = push(panel, [mine, more, other]), [rest]
        else:
            last_shards = [more, other, rest]
        base, message = in_kernel(
            functools.partial(base_kernel, panel, panel_count),
            [((2, side_count, share), jnp.float32), ((2, side_count, share), jnp.bfloat16)],
            [front_size, resident(contrib), resident(source_held)] + last_shards,
            specs=[IN_SMEM] + [IN_VMEM] * (2 + len(last_shards)),
            moved=2**22,
        )
        bases.append(base)
        messages.append(message)

    row = ((1, share), jnp.float32)
    arriving = ((half, 1, 1, share), jnp.float32)
    scales = in_kernel(
        functools.partial(scales_kernel, panel_count, side_count),
        [row] * (3 * panel_count) + [arriving] * 4,
        [front_size, resident(link_held), mine, other, more, rest],
        specs=[IN_SMEM] + [IN_VMEM] * 5,
    )
    masks, forward_scales = scales[:panel_count], scales[panel_count : 2 * panel_count]
    backward_scales = scales[2 * panel_count : 3 * panel_count]
    arriving = scales[3 * panel_count :]

    def arrive_forward(pieces, index):
        return (arriving[index] * pieces.astype(jnp.float32)).astype(jnp.bfloat16)

    def arrive_backward(pieces, index):
        return (arriving[2 + index] * pieces.astype(jnp.float32)).astype(jnp.bfloat16)

    kept = [jnp.zeros((2, side_count, share), jnp.float32) for _ in range(panel_count)]
    within, across = sources_within(peers), sources_crossed(peers)
    order = [(turn, panel) for turn in range(groups) for panel in range(panel_count)]
    steps = [(None, 0, True)] + [step + (True,) for step in order[1:]]
    steps += [step + (False,) for step in reversed(order[:-1])]
    message = messages[0]
    for count, (turn, panel, forward) in enumerate(steps):
        if forward and panel == 0 and turn is not None:
            low, arrive = turn - 1, arrive_forward
        elif not forward and panel == panel_count - 1:
            low, arrive = turn, arrive_backward
        else:
            low = None
        sources = within if low is None else across
        if count == 1 and panel_count > 1:
            rest = [loaded(after, schur_inverse, message) for after in range(1, panel_count)]
            pieces, _, rest = gathered_within(message, lambda mine: (), rest)
            schurs += rest
            products = first_products(turn, sources, schurs[panel], pieces[0][0])
        else:
            first = functools.partial(first_products, turn, sources, schurs[panel])
            if low is not None:
                pieces, products = crossed(message, low, arrive, first)
            elif count == 0:
                beside = (bases[1:], masks, forward_scales, backward_scales, arriving)
                pieces, products, beside = gathered_within(message, first, beside)
                bases[1:], masks, forward_scales, backward_scales, arriving = beside
            else:
                pieces, products, _ = gathered_within(message, first)
        scale = addend = None
        if forward and panel < panel_count - 1:
            scale, addend = forward_scales[panel + 1], bases[panel + 1]
        elif not forward or turn == groups - 1:
            scale = backward_scales[panel]
        if count == len(steps) - 1:
            kept[0], message = last_step(turn, sources, pieces, schurs[0], products, masks[0], kept)
        else:
            kept[panel], message = sweep_step(
                turn, sources, pieces, schurs[panel], products, kept[panel], message,
                not forward or (panel == 0 and turn is not None),
                mask=masks[panel], scale=scale, addend=addend,
            )

    fronts = jnp.stack(kept)
    pick = lambda mine: in_kernel(
        pick_kernel,
        [((panel_count, 2 * side_count, bound), jnp.float32)],
        [resident(mine), resident(rows_held)],
        moved=2**22,
    )[0]
    ((_, other), (more, rest)), picked, fronts = gathered_within(message, pick, fronts)
    operands = [picked, other, more, rest, rows_held, coupling_held, inverse_held, solved]
    inner = pl.pallas_call(
        inner_kernel,
        out_shape=jax.ShapeDtypeStruct(solved.shape, jnp.float32),
        in_specs=[IN_VMEM] * len(operands),
        out_specs=IN_HBM,
        scratch_shapes=[
            pltpu.VMEM(solved.shape, jnp.float32),
            pltpu.SemaphoreType.DMA((panel_count,)),
        ],
        compiler_params=pltpu.CompilerParams(vmem_limit_bytes=16 * 2**20),
    )(*[resident(value) for value in operands])
    return inner, fronts


def solution(mesh):
    placed = (
        P("gz", None, None, "xy"),
        P("gz", None, None, "xy"),
        P("gz", "xy", None, None, None),
        P("gz", "xy", None, None, None),
        P("gz", None, None, "xy"),
        P("gz", "xy"),
        P("gz", "xy"),
        P("gz"),
    )
    return jax.shard_map(
        on_device,
        mesh=mesh,
        in_specs=placed,
        out_specs=(P("gz", None, None, "xy"), P("gz", None, None, "xy")),
        check_vma=False,
    )
```

time: 172 us -> 163 us (0.948)
  waiting for transfers between devices: 84.6 us -> 54.2 us
  starting transfers between devices: 60.3 us -> 81.4 us
    ppermute x12, waiting for transfers between devices: 32.6 us -> 11.2 us  [crossed(): parts.append(lax.ppermute(pair, ('gz', 'xy'), pairs))]
    ppermute x12, starting transfers between devices: 17.7 us -> 34.5 us  [crossed(): parts.append(lax.ppermute(pair, ('gz', 'xy'), pairs))]
    ppermute x56 -> x73, waiting for transfers between devices: 52 us -> 43 us  [swapped(): return lax.ppermute(shard, 'xy', [(i, i ^ mask) for i in range(peers)])]
    ppermute x56 -> x73, starting transfers between devices: 42.6 us -> 46.9 us  [swapped(): return lax.ppermute(shard, 'xy', [(i, i ^ mask) for i in range(peers)])]
    pallas_call x0 -> x1, Pallas kernels: none -> 2.16 us  [on_device(): pl.pallas_call(inner_kernel, out_shape=jax.ShapeDtypeStruct(solved.shape,...]
    pallas_call x38 -> x54, Pallas kernels: 23.6 us -> 22.9 us  [in_kernel(): pl.pallas_call(body, out_shape=tuple((pltpu.VMEM(shape, dtype) for shape,...]
  transfers between devices with their start and end apart: 68 -> 85, of which waited for: 62 -> 63; matrix products, arithmetic and copies ran while one was open for 0% -> 1% of each run, Pallas kernels for 8% -> 10%
where the time goes in v3:
time: 163 us
  starting transfers between devices  81.4 us (50%)
  waiting for transfers between devices  54.2 us (33%)
  Pallas kernels  25.1 us (15%)
    ppermute x73, starting transfers between devices, swapped(): return lax.ppermute(shard, 'xy', [(i, i ^ mask) for i in range(peers)])  46.9 us
    ppermute x73, waiting for transfers between devices, swapped(): return lax.ppermute(shard, 'xy', [(i, i ^ mask) for i in range(peers)])  43 us
    ppermute x12, starting transfers between devices, crossed(): parts.append(lax.ppermute(pair, ('gz', 'xy'), pairs))  34.5 us
    pallas_call x54, Pallas kernels, in_kernel(): pl.pallas_call(body, out_shape=tuple((pltpu.VMEM(shape, dtype) for shape,...  22.9 us
    ppermute x12, waiting for transfers between devices, crossed(): parts.append(lax.ppermute(pair, ('gz', 'xy'), pairs))  11.2 us
  transfers between devices with their start and end apart: 85, of which 63 were waited for; matrix products, arithmetic and copies ran while one was open for 1% of the time, Pallas kernels for 10%

profile of v3, /device:TPU:0, one launch (start us, length us, event | category | flops | bytes accessed | tf_op | source)
XLA Modules:
  0.0 163.3 jit_solution(16558231247854539960)
XLA Ops:
  0.6 3.2 %shard_map.95 = (f32[2,2,16,512]{3,2,1,0:T(8,128)S(1)}, bf16[80,256]{1,0:T(8,128)(2,1)S(1)}, f32[2,2,16,512]{3,2,1,0:T(8,128)}, bf16[2,1,2,512,512]{4,3,2,1,0:T(...) custom-call(f32[2,2,16,512]{3,2,1,0:T(8,128)} %refs_0_.1, ...), custom_call_target="tpu_custom_call" | custom-call | tf_op jit(solution)/shard_map/pallas_call | solution.py:112
  3.9 4.0 %collective-permute-start.2 = (bf16[80,256]{1,0:T(8,128)(2,1)S(1)}, bf16[80,256]{1,0:T(8,128)(2,1)S(1)}, u32[]{:S(2)}, u32[]{:S(2)}) collective-permute-start(bf16[80,256]{1,0:T(8,128)(2,1)S(1)} %get-tuple-element.107.after_ref), channel_id=1, source_target_pairs={{0,6},{1,7},{2,4},{3,5},{4,2},{5,3},{6,0},{7,1},{8,14},{9,15},{10,... | collective-permute-start | bytes 122888 | tf_op jit(solution)/shard_map/ppermute | solution.py:27
  8.5 3.5 %shard_map.97.refs_1_.refs_2_.schur_ref = bf16[2,4096,512]{2,1,0:T(8,128)(2,1)S(1)} custom-call(bf16[2,2,4096,512]{3,2,1,0:T(8,128)(2,1)} %schur_ref.3, bf16[80,256]{1,0:T(8,128)(2,1)S(1)} %get-tuple-element.107.after_ref), custom_call_target="tpu_custom_call" | custom-call | bytes 16777216 | tf_op jit(solution)/shard_map/pallas_call | solution.py:112
  13.8 1.8 %shard_map.98 = (f32[2,16,512]{2,1,0:T(8,128)}, bf16[2,16,512]{2,1,0:T(8,128)(2,1)S(1)}) custom-call(s32[2]{0:T(128)S(1)} %copy-done, f32[32,512]{1,0:T(8,128)S(1)} %shard_map.96.contrib_ref, f32[2,2,16,512]{3,2,1,0:T(8,128)S(1)} %get-tuple-element.109.source_ref, bf16[2,80,256]{2,1,0:T(8,128)(2,1)S(1)} %pad_maximum_fusion.4.refs_0_.refs_1_.refs_2_, ...), custom_call_target="tpu_custom_call" | custom-call | bytes 4194304 | tf_op jit(solution)/shard_map/pallas_call | solution.py:112
  15.6 2.9 %collective-permute-start.7 = (bf16[2,16,512]{2,1,0:T(8,128)(2,1)S(1)}, bf16[2,16,512]{2,1,0:T(8,128)(2,1)S(1)}, u32[]{:S(2)}, u32[]{:S(2)}) collective-permute-start(bf16[2,16,512]{2,1,0:T(8,128)(2,1)S(1)} %get-tuple-element.112.refs_7_), channel_id=1, source_target_pairs={{0,6},{1,7},{2,4},{3,5},{4,2},{5,3},{6,0},{7,1},{8,14},{9,15},{10,... | collective-permute-start | bytes 98312 | tf_op jit(solution)/shard_map/ppermute | solution.py:27
  19.6 1.2 shard_map.102
  20.8 1.4 shard_map.101
  24.9 2.9 %collective-permute-start.10 = (bf16[2,16,512]{2,1,0:T(8,128)(2,1)S(1)}, bf16[2,16,512]{2,1,0:T(8,128)(2,1)S(1)}, u32[]{:S(2)}, u32[]{:S(2)}) collective-permute-start(bf16[2,16,512]{2,1,0:T(8,128)(2,1)S(1)} %get-tuple-element.133.after_ref.refs_5_), channel_id=1, source_target_pairs={{0,6},{1,7},{2,4},{3,5},{4,2},{5,3},{6,0},{7,1},{8,14},{9,15},{10,... | collective-permute-start | bytes 98312 | tf_op jit(solution)/shard_map/ppermute | solution.py:27
  28.4 3.5 %shard_map.105.refs_1_.refs_2_ = bf16[2,4096,512]{2,1,0:T(8,128)(2,1)S(1)} custom-call(bf16[2,2,4096,512]{3,2,1,0:T(8,128)(2,1)} %schur_ref.3, bf16[2,16,512]{2,1,0:T(8,128)(2,1)S(1)} %get-tuple-element.133.after_ref.refs_5_), custom_call_target="tpu_custom_call" | custom-call | bytes 16777216 | tf_op jit(solution)/shard_map/pallas_call | solution.py:112
  34.8 1.1 collective-permute-done.15
  36.8 2.5 %collective-permute-start.18 = (bf16[2,2,16,512]{3,2,1,0:T(8,128)(2,1)S(1)}, bf16[2,2,16,512]{3,2,1,0:T(8,128)(2,1)S(1)}, u32[]{:S(2)}, u32[]{:S(2)}) collective-permute-start(bf16[2,2,16,512]{3,2,1,0:T(8,128)(2,1)S(1)} %pad_maximum_fusion.9), channel_id=1, source_target_pairs={{0,10},{1,15},{2,8},{3,13},{4,14},{5,11},{6,12},{7,9},{8,2},{9,7},... | collective-permute-start | bytes 196616 | tf_op jit(solution)/shard_map/ppermute | solution.py:77
  39.3 1.1 collective-permute-done.16
  40.6 2.9 %collective-permute-done.18 = bf16[2,2,16,512]{3,2,1,0:T(8,128)(2,1)S(1)} collective-permute-done((bf16[2,2,16,512]{3,2,1,0:T(8,128)(2,1)S(1)}, bf16[2,2,16,512]{3,2,1,0:T(8,128)(2,1)S(1)}, u32[]{:S(2)}, u32[]{:S(2)}) %collective-permute-start.18) | collective-permute-done | bytes 65568 | tf_op jit(solution)/shard_map/ppermute | solution.py:77
  43.6 1.2 collective-permute-done.19.refs_1_
  44.9 1.6 collective-permute-start.20
  46.4 1.0 collective-permute-start.23
  47.4 1.0 collective-permute-start.22
  48.3 1.5 collective-permute-done.20
  50.4 1.0 collective-permute-done.22
  51.4 1.2 collective-permute-done.24.refs_1_
  52.8 1.0 collective-permute-done.25
  56.8 1.4 collective-permute-start.30
  58.2 1.0 collective-permute-start.33
  59.2 1.1 collective-permute-start.32
  60.3 1.5 collective-permute-done.30
  62.1 1.0 collective-permute-done.32
  63.2 1.2 collective-permute-done.34.refs_1_
  64.6 1.0 collective-permute-done.35
  68.6 1.6 collective-permute-start.40
  70.1 1.0 collective-permute-start.43
  71.1 1.0 collective-permute-start.42
  72.0 1.5 collective-permute-done.40
  74.1 1.0 collective-permute-done.42
  75.1 1.2 collective-permute-done.44.refs_1_
  76.3 1.4 collective-permute-start.45
  77.8 1.0 collective-permute-start.48
  78.8 1.1 collective-permute-start.47
  79.8 1.7 %collective-permute-done.45 = bf16[2,16,512]{2,1,0:T(8,128)(2,1)S(1)} collective-permute-done((bf16[2,16,512]{2,1,0:T(8,128)(2,1)S(1)}, bf16[2,16,512]{2,1,0:T(8,128)(2,1)S(1)}, u32[]{:S(2)}, u32[]{:S(2)}) %collective-permute-start.45) | collective-permute-done | bytes 32800 | tf_op jit(solution)/shard_map/ppermute | solution.py:27
  81.7 1.0 collective-permute-done.47
  82.9 1.1 collective-permute-done.49.refs_1_
  84.2 1.0 collective-permute-done.50
  88.1 1.6 collective-permute-start.55
  89.7 1.0 collective-permute-start.58
  91.6 1.5 collective-permute-done.55
  93.6 1.0 collective-permute-done.57
  94.7 1.2 collective-permute-done.59.refs_1_
  96.1 1.0 collective-permute-done.60
  100.0 1.4 collective-permute-start.65
  101.5 1.0 collective-permute-start.68
  102.5 1.1 collective-permute-start.67
  103.5 1.5 collective-permute-done.65
  105.4 1.0 collective-permute-done.67
  106.5 1.2 collective-permute-done.69.refs_1_
  107.9 1.0 collective-permute-done.70
  108.9 27.8 %collective-permute-start.71 = (bf16[2,2,16,512]{3,2,1,0:T(8,128)(2,1)S(1)}, bf16[2,2,16,512]{3,2,1,0:T(8,128)(2,1)S(1)}, u32[]{:S(2)}, u32[]{:S(2)}) collective-permute-start(bf16[2,2,16,512]{3,2,1,0:T(8,128)(2,1)S(1)} %pad_maximum_fusion.26), channel_id=1, source_target_pairs={{0,8},{1,13},{2,10},{3,15},{4,12},{5,9},{6,14},{7,11},{8,0},{9,5},... | collective-permute-start | bytes 196616 | tf_op jit(solution)/shard_map/ppermute | solution.py:77
  136.7 1.0 collective-permute-start.73
  137.7 1.5 collective-permute-done.71
  139.8 2.6 %collective-permute-done.73 = bf16[2,2,16,512]{3,2,1,0:T(8,128)(2,1)S(1)} collective-permute-done((bf16[2,2,16,512]{3,2,1,0:T(8,128)(2,1)S(1)}, bf16[2,2,16,512]{3,2,1,0:T(8,128)(2,1)S(1)}, u32[]{:S(2)}, u32[]{:S(2)}) %collective-permute-start.73) | collective-permute-done | bytes 65568 | tf_op jit(solution)/shard_map/ppermute | solution.py:77
  144.2 2.3 %collective-permute-start.75 = (bf16[2,16,512]{2,1,0:T(8,128)(2,1)S(1)}, bf16[2,16,512]{2,1,0:T(8,128)(2,1)S(1)}, u32[]{:S(2)}, u32[]{:S(2)}) collective-permute-start(bf16[2,16,512]{2,1,0:T(8,128)(2,1)S(1)} %get-tuple-element.196), channel_id=1, source_target_pairs={{0,6},{1,7},{2,4},{3,5},{4,2},{5,3},{6,0},{7,1},{8,14},{9,15},{10,... | collective-permute-start | bytes 98312 | tf_op jit(solution)/shard_map/ppermute | solution.py:27
  147.8 1.3 collective-permute-done.75
  152.8 1.7 %collective-permute-start.82 = (bf16[2,2,16,512]{3,2,1,0:T(8,128)(2,1)S(1)}, bf16[2,2,16,512]{3,2,1,0:T(8,128)(2,1)S(1)}, u32[]{:S(2)}, u32[]{:S(2)}) collective-permute-start(bf16[2,2,16,512]{3,2,1,0:T(8,128)(2,1)S(1)} %get-tuple-element.202), channel_id=1, source_target_pairs={{0,6},{1,7},{2,4},{3,5},{4,2},{5,3},{6,0},{7,1},{8,14},{9,15},{10,... | collective-permute-start | bytes 196616 | tf_op jit(solution)/shard_map/ppermute | solution.py:27
  155.0 1.3 collective-permute-start.80
  157.0 1.4 collective-permute-done.82
  160.9 2.2 %shard_map.149 = f32[2,2,16,512]{3,2,1,0:T(8,128)} custom-call(f32[2,32,256]{2,1,0:T(8,128)S(1)} %shard_map.148.picked_ref, bf16[2,2,2,16,512]{4,3,2,1,0:T(8,128)(2,1)S(1)} %collective-permute-done.83.other_ref, bf16[2,2,2,16,512]{4,3,2,1,0:T(8,128)(2,1)S(1)} %pad_maximum_fusion.2.more_ref, bf16[2,2,2,16,512]{4,3,2,1,0:T(8,128)(2,1)S(1)} %collective-permute-done.84.rest_ref, ...), custom_call_target="tpu_custom_call" | custom-call | tf_op jit(solution)/shard_map/pallas_call | solution.py:608
  (210 shorter events, 38.2 us)
Async XLA Ops:
  3.9 8.1 %collective-permute-start.2 = (bf16[80,256]{1,0:T(8,128)(2,1)S(1)}, bf16[80,256]{1,0:T(8,128)(2,1)S(1)}, u32[]{:S(2)}, u32[]{:S(2)}) collective-permute-start(bf16[80,256]{1,0:T(8,128)(2,1)S(1)} %get-tuple-element.107.after_ref), channel_id=1, source_target_pairs={{0,6},{1,7},{2,4},{3,5},{4,2},{5,3},{6,0},{7,1},{8,14},{9,15},{10,... | collective-permute-start | bytes 122888 | tf_op jit(solution)/shard_map/ppermute | solution.py:27
  7.9 4.4 %collective-permute-start.1 = (bf16[80,256]{1,0:T(8,128)(2,1)S(1)}, bf16[80,256]{1,0:T(8,128)(2,1)S(1)}, u32[]{:S(2)}, u32[]{:S(2)}) collective-permute-start(bf16[80,256]{1,0:T(8,128)(2,1)S(1)} %get-tuple-element.107.after_ref), channel_id=1, source_target_pairs={{0,2},{1,3},{2,0},{3,1},{4,6},{5,7},{6,4},{7,5},{8,10},{9,11},{10,... | collective-permute-start | bytes 122888 | tf_op jit(solution)/shard_map/ppermute | solution.py:27
  8.4 4.0 %collective-permute-start = (bf16[80,256]{1,0:T(8,128)(2,1)S(1)}, bf16[80,256]{1,0:T(8,128)(2,1)S(1)}, u32[]{:S(2)}, u32[]{:S(2)}) collective-permute-start(bf16[80,256]{1,0:T(8,128)(2,1)S(1)} %get-tuple-element.107.after_ref), channel_id=1, source_target_pairs={{0,4},{1,5},{2,6},{3,7},{4,0},{5,1},{6,2},{7,3},{8,12},{9,13},{10,... | collective-permute-start | bytes 122888 | tf_op jit(solution)/shard_map/ppermute | solution.py:27
  12.4 1.4 collective-permute-start.4
  15.6 6.7 %collective-permute-start.7 = (bf16[2,16,512]{2,1,0:T(8,128)(2,1)S(1)}, bf16[2,16,512]{2,1,0:T(8,128)(2,1)S(1)}, u32[]{:S(2)}, u32[]{:S(2)}) collective-permute-start(bf16[2,16,512]{2,1,0:T(8,128)(2,1)S(1)} %get-tuple-element.112.refs_7_), channel_id=1, source_target_pairs={{0,6},{1,7},{2,4},{3,5},{4,2},{5,3},{6,0},{7,1},{8,14},{9,15},{10,... | collective-permute-start | bytes 98312 | tf_op jit(solution)/shard_map/ppermute | solution.py:27
  18.4 4.4 %collective-permute-start.6 = (bf16[2,16,512]{2,1,0:T(8,128)(2,1)S(1)}, bf16[2,16,512]{2,1,0:T(8,128)(2,1)S(1)}, u32[]{:S(2)}, u32[]{:S(2)}) collective-permute-start(bf16[2,16,512]{2,1,0:T(8,128)(2,1)S(1)} %get-tuple-element.112.refs_7_), channel_id=1, source_target_pairs={{0,2},{1,3},{2,0},{3,1},{4,6},{5,7},{6,4},{7,5},{8,10},{9,11},{10,... | collective-permute-start | bytes 98312 | tf_op jit(solution)/shard_map/ppermute | solution.py:27
  19.0 3.9 %collective-permute-start.5 = (bf16[2,16,512]{2,1,0:T(8,128)(2,1)S(1)}, bf16[2,16,512]{2,1,0:T(8,128)(2,1)S(1)}, u32[]{:S(2)}, u32[]{:S(2)}) collective-permute-start(bf16[2,16,512]{2,1,0:T(8,128)(2,1)S(1)} %get-tuple-element.112.refs_7_), channel_id=1, source_target_pairs={{0,4},{1,5},{2,6},{3,7},{4,0},{5,1},{6,2},{7,3},{8,12},{9,13},{10,... | collective-permute-start | bytes 98312 | tf_op jit(solution)/shard_map/ppermute | solution.py:27
  22.2 1.3 collective-permute-start.8
  22.9 1.5 collective-permute-start.9
  24.9 7.0 %collective-permute-start.10 = (bf16[2,16,512]{2,1,0:T(8,128)(2,1)S(1)}, bf16[2,16,512]{2,1,0:T(8,128)(2,1)S(1)}, u32[]{:S(2)}, u32[]{:S(2)}) collective-permute-start(bf16[2,16,512]{2,1,0:T(8,128)(2,1)S(1)} %get-tuple-element.133.after_ref.refs_5_), channel_id=1, source_target_pairs={{0,6},{1,7},{2,4},{3,5},{4,2},{5,3},{6,0},{7,1},{8,14},{9,15},{10,... | collective-permute-start | bytes 98312 | tf_op jit(solution)/shard_map/ppermute | solution.py:27
  27.8 4.2 %collective-permute-start.13 = (bf16[2,16,512]{2,1,0:T(8,128)(2,1)S(1)}, bf16[2,16,512]{2,1,0:T(8,128)(2,1)S(1)}, u32[]{:S(2)}, u32[]{:S(2)}) collective-permute-start(bf16[2,16,512]{2,1,0:T(8,128)(2,1)S(1)} %get-tuple-element.133.after_ref.refs_5_), channel_id=1, source_target_pairs={{0,2},{1,3},{2,0},{3,1},{4,6},{5,7},{6,4},{7,5},{8,10},{9,11},{10,... | collective-permute-start | bytes 98312 | tf_op jit(solution)/shard_map/ppermute | solution.py:27
  28.3 3.9 %collective-permute-start.12 = (bf16[2,16,512]{2,1,0:T(8,128)(2,1)S(1)}, bf16[2,16,512]{2,1,0:T(8,128)(2,1)S(1)}, u32[]{:S(2)}, u32[]{:S(2)}) collective-permute-start(bf16[2,16,512]{2,1,0:T(8,128)(2,1)S(1)} %get-tuple-element.133.after_ref.refs_5_), channel_id=1, source_target_pairs={{0,4},{1,5},{2,6},{3,7},{4,0},{5,1},{6,2},{7,3},{8,12},{9,13},{10,... | collective-permute-start | bytes 98312 | tf_op jit(solution)/shard_map/ppermute | solution.py:27
  32.0 1.3 collective-permute-start.11
  32.3 1.8 %collective-permute-start.14 = (bf16[2,2,16,512]{3,2,1,0:T(8,128)(2,1)S(1)}, bf16[2,2,16,512]{3,2,1,0:T(8,128)(2,1)S(1)}, u32[]{:S(2)}, u32[]{:S(2)}) collective-permute-start(bf16[2,2,16,512]{3,2,1,0:T(8,128)(2,1)S(1)} %pad_maximum_fusion.8.refs_1_), channel_id=1, source_target_pairs={{0,1},{1,0},{2,3},{3,2},{4,5},{5,4},{6,7},{7,6},{8,9},{9,8},{10,11... | collective-permute-start | bytes 196616 | tf_op jit(solution)/shard_map/ppermute | solution.py:27
  35.9 4.6 %collective-permute-start.16 = (bf16[2,2,16,512]{3,2,1,0:T(8,128)(2,1)S(1)}, bf16[2,2,16,512]{3,2,1,0:T(8,128)(2,1)S(1)}, u32[]{:S(2)}, u32[]{:S(2)}) collective-permute-start(bf16[2,2,16,512]{3,2,1,0:T(8,128)(2,1)S(1)} %pad_maximum_fusion.9), channel_id=1, source_target_pairs={{0,8},{1,13},{2,10},{3,15},{4,12},{5,9},{6,14},{7,11},{8,0},{9,5},... | collective-permute-start | bytes 196616 | tf_op jit(solution)/shard_map/ppermute | solution.py:77
  36.8 6.7 %collective-permute-start.18 = (bf16[2,2,16,512]{3,2,1,0:T(8,128)(2,1)S(1)}, bf16[2,2,16,512]{3,2,1,0:T(8,128)(2,1)S(1)}, u32[]{:S(2)}, u32[]{:S(2)}) collective-permute-start(bf16[2,2,16,512]{3,2,1,0:T(8,128)(2,1)S(1)} %pad_maximum_fusion.9), channel_id=1, source_target_pairs={{0,10},{1,15},{2,8},{3,13},{4,14},{5,11},{6,12},{7,9},{8,2},{9,7},... | collective-permute-start | bytes 196616 | tf_op jit(solution)/shard_map/ppermute | solution.py:77
  40.5 3.2 %collective-permute-start.17 = (bf16[2,2,16,512]{3,2,1,0:T(8,128)(2,1)S(1)}, bf16[2,2,16,512]{3,2,1,0:T(8,128)(2,1)S(1)}, u32[]{:S(2)}, u32[]{:S(2)}) collective-permute-start(bf16[2,2,16,512]{3,2,1,0:T(8,128)(2,1)S(1)} %multiply_convert_fusion.11.refs_0_), channel_id=1, source_target_pairs={{0,1},{1,0},{2,3},{3,2},{4,5},{5,4},{6,7},{7,6},{8,9},{9,8},{10,11... | collective-permute-start | bytes 196616 | tf_op jit(solution)/shard_map/ppermute | solution.py:27
  43.5 1.3 collective-permute-start.19
  44.9 5.0 %collective-permute-start.20 = (bf16[2,16,512]{2,1,0:T(8,128)(2,1)S(1)}, bf16[2,16,512]{2,1,0:T(8,128)(2,1)S(1)}, u32[]{:S(2)}, u32[]{:S(2)}) collective-permute-start(bf16[2,16,512]{2,1,0:T(8,128)(2,1)S(1)} %get-tuple-element.143.refs_5_), channel_id=1, source_target_pairs={{0,6},{1,7},{2,4},{3,5},{4,2},{5,3},{6,0},{7,1},{8,14},{9,15},{10,... | collective-permute-start | bytes 98312 | tf_op jit(solution)/shard_map/ppermute | solution.py:27
  46.4 3.9 %collective-permute-start.23 = (bf16[2,16,512]{2,1,0:T(8,128)(2,1)S(1)}, bf16[2,16,512]{2,1,0:T(8,128)(2,1)S(1)}, u32[]{:S(2)}, u32[]{:S(2)}) collective-permute-start(bf16[2,16,512]{2,1,0:T(8,128)(2,1)S(1)} %get-tuple-element.143.refs_5_), channel_id=1, source_target_pairs={{0,2},{1,3},{2,0},{3,1},{4,6},{5,7},{6,4},{7,5},{8,10},{9,11},{10,... | collective-permute-start | bytes 98312 | tf_op jit(solution)/shard_map/ppermute | solution.py:27
  47.4 3.9 %collective-permute-start.22 = (bf16[2,16,512]{2,1,0:T(8,128)(2,1)S(1)}, bf16[2,16,512]{2,1,0:T(8,128)(2,1)S(1)}, u32[]{:S(2)}, u32[]{:S(2)}) collective-permute-start(bf16[2,16,512]{2,1,0:T(8,128)(2,1)S(1)} %get-tuple-element.143.refs_5_), channel_id=1, source_target_pairs={{0,4},{1,5},{2,6},{3,7},{4,0},{5,1},{6,2},{7,3},{8,12},{9,13},{10,... | collective-permute-start | bytes 98312 | tf_op jit(solution)/shard_map/ppermute | solution.py:27
  49.9 1.5 collective-permute-start.21
  51.3 1.3 collective-permute-start.24
  53.9 1.3 collective-permute-start.26
  54.1 1.3 collective-permute-start.28
  55.2 1.3 collective-permute-start.27
  55.4 1.3 collective-permute-start.29
  56.8 5.0 %collective-permute-start.30 = (bf16[2,16,512]{2,1,0:T(8,128)(2,1)S(1)}, bf16[2,16,512]{2,1,0:T(8,128)(2,1)S(1)}, u32[]{:S(2)}, u32[]{:S(2)}) collective-permute-start(bf16[2,16,512]{2,1,0:T(8,128)(2,1)S(1)} %get-tuple-element.152.refs_5_), channel_id=1, source_target_pairs={{0,6},{1,7},{2,4},{3,5},{4,2},{5,3},{6,0},{7,1},{8,14},{9,15},{10,... | collective-permute-start | bytes 98312 | tf_op jit(solution)/shard_map/ppermute | solution.py:27
  58.2 3.9 %collective-permute-start.33 = (bf16[2,16,512]{2,1,0:T(8,128)(2,1)S(1)}, bf16[2,16,512]{2,1,0:T(8,128)(2,1)S(1)}, u32[]{:S(2)}, u32[]{:S(2)}) collective-permute-start(bf16[2,16,512]{2,1,0:T(8,128)(2,1)S(1)} %get-tuple-element.152.refs_5_), channel_id=1, source_target_pairs={{0,2},{1,3},{2,0},{3,1},{4,6},{5,7},{6,4},{7,5},{8,10},{9,11},{10,... | collective-permute-start | bytes 98312 | tf_op jit(solution)/shard_map/ppermute | solution.py:27
  59.2 3.9 %collective-permute-start.32 = (bf16[2,16,512]{2,1,0:T(8,128)(2,1)S(1)}, bf16[2,16,512]{2,1,0:T(8,128)(2,1)S(1)}, u32[]{:S(2)}, u32[]{:S(2)}) collective-permute-start(bf16[2,16,512]{2,1,0:T(8,128)(2,1)S(1)} %get-tuple-element.152.refs_5_), channel_id=1, source_target_pairs={{0,4},{1,5},{2,6},{3,7},{4,0},{5,1},{6,2},{7,3},{8,12},{9,13},{10,... | collective-permute-start | bytes 98312 | tf_op jit(solution)/shard_map/ppermute | solution.py:27
  61.8 1.4 collective-permute-start.31
  63.1 1.3 collective-permute-start.34
  65.6 1.3 collective-permute-start.36
  65.9 1.3 collective-permute-start.38
  68.6 5.0 %collective-permute-start.40 = (bf16[2,16,512]{2,1,0:T(8,128)(2,1)S(1)}, bf16[2,16,512]{2,1,0:T(8,128)(2,1)S(1)}, u32[]{:S(2)}, u32[]{:S(2)}) collective-permute-start(bf16[2,16,512]{2,1,0:T(8,128)(2,1)S(1)} %get-tuple-element.161.refs_6_), channel_id=1, source_target_pairs={{0,6},{1,7},{2,4},{3,5},{4,2},{5,3},{6,0},{7,1},{8,14},{9,15},{10,... | collective-permute-start | bytes 98312 | tf_op jit(solution)/shard_map/ppermute | solution.py:27
  70.1 3.9 %collective-permute-start.43 = (bf16[2,16,512]{2,1,0:T(8,128)(2,1)S(1)}, bf16[2,16,512]{2,1,0:T(8,128)(2,1)S(1)}, u32[]{:S(2)}, u32[]{:S(2)}) collective-permute-start(bf16[2,16,512]{2,1,0:T(8,128)(2,1)S(1)} %get-tuple-element.161.refs_6_), channel_id=1, source_target_pairs={{0,2},{1,3},{2,0},{3,1},{4,6},{5,7},{6,4},{7,5},{8,10},{9,11},{10,... | collective-permute-start | bytes 98312 | tf_op jit(solution)/shard_map/ppermute | solution.py:27
  71.1 3.9 %collective-permute-start.42 = (bf16[2,16,512]{2,1,0:T(8,128)(2,1)S(1)}, bf16[2,16,512]{2,1,0:T(8,128)(2,1)S(1)}, u32[]{:S(2)}, u32[]{:S(2)}) collective-permute-start(bf16[2,16,512]{2,1,0:T(8,128)(2,1)S(1)} %get-tuple-element.161.refs_6_), channel_id=1, source_target_pairs={{0,4},{1,5},{2,6},{3,7},{4,0},{5,1},{6,2},{7,3},{8,12},{9,13},{10,... | collective-permute-start | bytes 98312 | tf_op jit(solution)/shard_map/ppermute | solution.py:27
  73.6 1.5 collective-permute-start.41
  76.3 5.2 %collective-permute-start.45 = (bf16[2,16,512]{2,1,0:T(8,128)(2,1)S(1)}, bf16[2,16,512]{2,1,0:T(8,128)(2,1)S(1)}, u32[]{:S(2)}, u32[]{:S(2)}) collective-permute-start(bf16[2,16,512]{2,1,0:T(8,128)(2,1)S(1)} %get-tuple-element.167.refs_6_), channel_id=1, source_target_pairs={{0,6},{1,7},{2,4},{3,5},{4,2},{5,3},{6,0},{7,1},{8,14},{9,15},{10,... | collective-permute-start | bytes 98312 | tf_op jit(solution)/shard_map/ppermute | solution.py:27
  77.8 3.9 %collective-permute-start.48 = (bf16[2,16,512]{2,1,0:T(8,128)(2,1)S(1)}, bf16[2,16,512]{2,1,0:T(8,128)(2,1)S(1)}, u32[]{:S(2)}, u32[]{:S(2)}) collective-permute-start(bf16[2,16,512]{2,1,0:T(8,128)(2,1)S(1)} %get-tuple-element.167.refs_6_), channel_id=1, source_target_pairs={{0,2},{1,3},{2,0},{3,1},{4,6},{5,7},{6,4},{7,5},{8,10},{9,11},{10,... | collective-permute-start | bytes 98312 | tf_op jit(solution)/shard_map/ppermute | solution.py:27
  78.8 3.9 %collective-permute-start.47 = (bf16[2,16,512]{2,1,0:T(8,128)(2,1)S(1)}, bf16[2,16,512]{2,1,0:T(8,128)(2,1)S(1)}, u32[]{:S(2)}, u32[]{:S(2)}) collective-permute-start(bf16[2,16,512]{2,1,0:T(8,128)(2,1)S(1)} %get-tuple-element.167.refs_6_), channel_id=1, source_target_pairs={{0,4},{1,5},{2,6},{3,7},{4,0},{5,1},{6,2},{7,3},{8,12},{9,13},{10,... | collective-permute-start | bytes 98312 | tf_op jit(solution)/shard_map/ppermute | solution.py:27
  85.5 1.3 collective-permute-start.53
  88.1 5.0 %collective-permute-start.55 = (bf16[2,16,512]{2,1,0:T(8,128)(2,1)S(1)}, bf16[2,16,512]{2,1,0:T(8,128)(2,1)S(1)}, u32[]{:S(2)}, u32[]{:S(2)}) collective-permute-start(bf16[2,16,512]{2,1,0:T(8,128)(2,1)S(1)} %get-tuple-element.178.refs_6_), channel_id=1, source_target_pairs={{0,6},{1,7},{2,4},{3,5},{4,2},{5,3},{6,0},{7,1},{8,14},{9,15},{10,... | collective-permute-start | bytes 98312 | tf_op jit(solution)/shard_map/ppermute | solution.py:27
  89.7 3.9 %collective-permute-start.58 = (bf16[2,16,512]{2,1,0:T(8,128)(2,1)S(1)}, bf16[2,16,512]{2,1,0:T(8,128)(2,1)S(1)}, u32[]{:S(2)}, u32[]{:S(2)}) collective-permute-start(bf16[2,16,512]{2,1,0:T(8,128)(2,1)S(1)} %get-tuple-element.178.refs_6_), channel_id=1, source_target_pairs={{0,2},{1,3},{2,0},{3,1},{4,6},{5,7},{6,4},{7,5},{8,10},{9,11},{10,... | collective-permute-start | bytes 98312 | tf_op jit(solution)/shard_map/ppermute | solution.py:27
  90.7 3.9 %collective-permute-start.57 = (bf16[2,16,512]{2,1,0:T(8,128)(2,1)S(1)}, bf16[2,16,512]{2,1,0:T(8,128)(2,1)S(1)}, u32[]{:S(2)}, u32[]{:S(2)}) collective-permute-start(bf16[2,16,512]{2,1,0:T(8,128)(2,1)S(1)} %get-tuple-element.178.refs_6_), channel_id=1, source_target_pairs={{0,4},{1,5},{2,6},{3,7},{4,0},{5,1},{6,2},{7,3},{8,12},{9,13},{10,... | collective-permute-start | bytes 98312 | tf_op jit(solution)/shard_map/ppermute | solution.py:27
  93.2 1.5 collective-permute-start.56
  97.4 1.3 collective-permute-start.63
  100.0 5.0 %collective-permute-start.65 = (bf16[2,16,512]{2,1,0:T(8,128)(2,1)S(1)}, bf16[2,16,512]{2,1,0:T(8,128)(2,1)S(1)}, u32[]{:S(2)}, u32[]{:S(2)}) collective-permute-start(bf16[2,16,512]{2,1,0:T(8,128)(2,1)S(1)} %get-tuple-element.187.refs_6_), channel_id=1, source_target_pairs={{0,6},{1,7},{2,4},{3,5},{4,2},{5,3},{6,0},{7,1},{8,14},{9,15},{10,... | collective-permute-start | bytes 98312 | tf_op jit(solution)/shard_map/ppermute | solution.py:27
  101.5 3.9 %collective-permute-start.68 = (bf16[2,16,512]{2,1,0:T(8,128)(2,1)S(1)}, bf16[2,16,512]{2,1,0:T(8,128)(2,1)S(1)}, u32[]{:S(2)}, u32[]{:S(2)}) collective-permute-start(bf16[2,16,512]{2,1,0:T(8,128)(2,1)S(1)} %get-tuple-element.187.refs_6_), channel_id=1, source_target_pairs={{0,2},{1,3},{2,0},{3,1},{4,6},{5,7},{6,4},{7,5},{8,10},{9,11},{10,... | collective-permute-start | bytes 98312 | tf_op jit(solution)/shard_map/ppermute | solution.py:27
  102.5 3.9 %collective-permute-start.67 = (bf16[2,16,512]{2,1,0:T(8,128)(2,1)S(1)}, bf16[2,16,512]{2,1,0:T(8,128)(2,1)S(1)}, u32[]{:S(2)}, u32[]{:S(2)}) collective-permute-start(bf16[2,16,512]{2,1,0:T(8,128)(2,1)S(1)} %get-tuple-element.187.refs_6_), channel_id=1, source_target_pairs={{0,4},{1,5},{2,6},{3,7},{4,0},{5,1},{6,2},{7,3},{8,12},{9,13},{10,... | collective-permute-start | bytes 98312 | tf_op jit(solution)/shard_map/ppermute | solution.py:27
  105.0 1.4 collective-permute-start.66
  108.9 30.3 %collective-permute-start.71 = (bf16[2,2,16,512]{3,2,1,0:T(8,128)(2,1)S(1)}, bf16[2,2,16,512]{3,2,1,0:T(8,128)(2,1)S(1)}, u32[]{:S(2)}, u32[]{:S(2)}) collective-permute-start(bf16[2,2,16,512]{3,2,1,0:T(8,128)(2,1)S(1)} %pad_maximum_fusion.26), channel_id=1, source_target_pairs={{0,8},{1,13},{2,10},{3,15},{4,12},{5,9},{6,14},{7,11},{8,0},{9,5},... | collective-permute-start | bytes 196616 | tf_op jit(solution)/shard_map/ppermute | solution.py:77
  136.7 5.7 %collective-permute-start.73 = (bf16[2,2,16,512]{3,2,1,0:T(8,128)(2,1)S(1)}, bf16[2,2,16,512]{3,2,1,0:T(8,128)(2,1)S(1)}, u32[]{:S(2)}, u32[]{:S(2)}) collective-permute-start(bf16[2,2,16,512]{3,2,1,0:T(8,128)(2,1)S(1)} %pad_maximum_fusion.26), channel_id=1, source_target_pairs={{0,10},{1,15},{2,8},{3,13},{4,14},{5,11},{6,12},{7,9},{8,2},{9,7},... | collective-permute-start | bytes 196616 | tf_op jit(solution)/shard_map/ppermute | solution.py:77
  139.2 3.6 %collective-permute-start.72 = (bf16[2,2,16,512]{3,2,1,0:T(8,128)(2,1)S(1)}, bf16[2,2,16,512]{3,2,1,0:T(8,128)(2,1)S(1)}, u32[]{:S(2)}, u32[]{:S(2)}) collective-permute-start(bf16[2,2,16,512]{3,2,1,0:T(8,128)(2,1)S(1)} %multiply_convert_fusion.1.refs_0_), channel_id=1, source_target_pairs={{0,1},{1,0},{2,3},{3,2},{4,5},{5,4},{6,7},{7,6},{8,9},{9,8},{10,11... | collective-permute-start | bytes 196616 | tf_op jit(solution)/shard_map/ppermute | solution.py:27
  142.4 1.3 collective-permute-start.74
  144.2 4.9 %collective-permute-start.75 = (bf16[2,16,512]{2,1,0:T(8,128)(2,1)S(1)}, bf16[2,16,512]{2,1,0:T(8,128)(2,1)S(1)}, u32[]{:S(2)}, u32[]{:S(2)}) collective-permute-start(bf16[2,16,512]{2,1,0:T(8,128)(2,1)S(1)} %get-tuple-element.196), channel_id=1, source_target_pairs={{0,6},{1,7},{2,4},{3,5},{4,2},{5,3},{6,0},{7,1},{8,14},{9,15},{10,... | collective-permute-start | bytes 98312 | tf_op jit(solution)/shard_map/ppermute | solution.py:27
  146.5 3.9 %collective-permute-start.78 = (bf16[2,16,512]{2,1,0:T(8,128)(2,1)S(1)}, bf16[2,16,512]{2,1,0:T(8,128)(2,1)S(1)}, u32[]{:S(2)}, u32[]{:S(2)}) collective-permute-start(bf16[2,16,512]{2,1,0:T(8,128)(2,1)S(1)} %get-tuple-element.196), channel_id=1, source_target_pairs={{0,2},{1,3},{2,0},{3,1},{4,6},{5,7},{6,4},{7,5},{8,10},{9,11},{10,... | collective-permute-start | bytes 98312 | tf_op jit(solution)/shard_map/ppermute | solution.py:27
  147.0 3.9 %collective-permute-start.77 = (bf16[2,16,512]{2,1,0:T(8,128)(2,1)S(1)}, bf16[2,16,512]{2,1,0:T(8,128)(2,1)S(1)}, u32[]{:S(2)}, u32[]{:S(2)}) collective-permute-start(bf16[2,16,512]{2,1,0:T(8,128)(2,1)S(1)} %get-tuple-element.196), channel_id=1, source_target_pairs={{0,4},{1,5},{2,6},{3,7},{4,0},{5,1},{6,2},{7,3},{8,12},{9,13},{10,... | collective-permute-start | bytes 98312 | tf_op jit(solution)/shard_map/ppermute | solution.py:27
  149.1 1.9 %collective-permute-start.76 = (bf16[2,2,16,512]{3,2,1,0:T(8,128)(2,1)S(1)}, bf16[2,2,16,512]{3,2,1,0:T(8,128)(2,1)S(1)}, u32[]{:S(2)}, u32[]{:S(2)}) collective-permute-start(bf16[2,2,16,512]{3,2,1,0:T(8,128)(2,1)S(1)} %pad_maximum_fusion.27.refs_0_), channel_id=1, source_target_pairs={{0,1},{1,0},{2,3},{3,2},{4,5},{5,4},{6,7},{7,6},{8,9},{9,8},{10,11... | collective-permute-start | bytes 196616 | tf_op jit(solution)/shard_map/ppermute | solution.py:27
  152.8 5.6 %collective-permute-start.82 = (bf16[2,2,16,512]{3,2,1,0:T(8,128)(2,1)S(1)}, bf16[2,2,16,512]{3,2,1,0:T(8,128)(2,1)S(1)}, u32[]{:S(2)}, u32[]{:S(2)}) collective-permute-start(bf16[2,2,16,512]{3,2,1,0:T(8,128)(2,1)S(1)} %get-tuple-element.202), channel_id=1, source_target_pairs={{0,6},{1,7},{2,4},{3,5},{4,2},{5,3},{6,0},{7,1},{8,14},{9,15},{10,... | collective-permute-start | bytes 196616 | tf_op jit(solution)/shard_map/ppermute | solution.py:27
  154.5 4.3 %collective-permute-start.81 = (bf16[2,2,16,512]{3,2,1,0:T(8,128)(2,1)S(1)}, bf16[2,2,16,512]{3,2,1,0:T(8,128)(2,1)S(1)}, u32[]{:S(2)}, u32[]{:S(2)}) collective-permute-start(bf16[2,2,16,512]{3,2,1,0:T(8,128)(2,1)S(1)} %get-tuple-element.202), channel_id=1, source_target_pairs={{0,2},{1,3},{2,0},{3,1},{4,6},{5,7},{6,4},{7,5},{8,10},{9,11},{10,... | collective-permute-start | bytes 196616 | tf_op jit(solution)/shard_map/ppermute | solution.py:27
  155.0 4.3 %collective-permute-start.80 = (bf16[2,2,16,512]{3,2,1,0:T(8,128)(2,1)S(1)}, bf16[2,2,16,512]{3,2,1,0:T(8,128)(2,1)S(1)}, u32[]{:S(2)}, u32[]{:S(2)}) collective-permute-start(bf16[2,2,16,512]{3,2,1,0:T(8,128)(2,1)S(1)} %get-tuple-element.202), channel_id=1, source_target_pairs={{0,4},{1,5},{2,6},{3,7},{4,0},{5,1},{6,2},{7,3},{8,12},{9,13},{10,... | collective-permute-start | bytes 196616 | tf_op jit(solution)/shard_map/ppermute | solution.py:27
  159.3 1.4 collective-permute-start.84
  159.4 1.5 collective-permute-start.83
  (22 other events, 37.0 us)

commit v4 on v3

v4 whole, which is shorter than its diff:
```python
import functools

import jax
import jax.numpy as jnp
from jax import lax
from jax.experimental import pallas as pl
from jax.experimental.pallas import tpu as pltpu
from jax.sharding import PartitionSpec as P

IN_VMEM = pl.BlockSpec(memory_space=pltpu.VMEM)


IN_HBM = pl.BlockSpec(memory_space=pltpu.HBM)
IN_SMEM = pl.BlockSpec(memory_space=pltpu.SMEM)


def resident(array):
    return pltpu.with_memory_space_constraint(array, pltpu.VMEM)


def in_hbm(array):
    return pltpu.with_memory_space_constraint(array, pltpu.HBM)


def swapped(shard, mask, turn=None):
    peers, groups = lax.axis_size("xy"), lax.axis_size("gz")
    pairs = []
    for group in range(groups):
        used = mask if turn is None or (group - turn) % 2 == 0 else 1
        pairs += [(group * peers + peer, group * peers + (peer ^ used)) for peer in range(peers)]
    return lax.ppermute(shard, ("gz", "xy"), pairs)


def masks_within(peers):
    masks = [0] + list(reversed(range(2, peers, 2)))
    return masks[: peers // 4], masks[peers // 4 :]


def in_parts(one, fetched, first, beside=()):
    pieces = [(one, swapped(one, 1))]
    made = first(one)
    fetched, made, beside = lax.optimization_barrier((fetched, made, beside))
    two = jnp.stack(fetched)
    pieces.append((two, swapped(two, 1)))
    return pieces, made, beside


def gathered_within(message, turn, first, beside=()):
    one, two = [
        [swapped(message, mask, turn) if mask else message for mask in part]
        for part in masks_within(lax.axis_size("xy"))
    ]
    return in_parts(jnp.stack(one), two, first, beside)


def sources_within(peers):
    def sources(me):
        found = []
        for masks in masks_within(peers):
            mine = [me ^ mask for mask in masks]
            found.append((mine, [peer ^ 1 for peer in mine]))
        return found

    return sources


def crossed(message, low, own_scale, far_scale, first):
    peers, groups = lax.axis_size("xy"), lax.axis_size("gz")

    def across(mask):
        pairs = []
        for group in range(groups):
            for peer in range(peers):
                if group in (low, low + 1):
                    place = (2 * low + 1 - group) * peers + (peer ^ mask)
                else:
                    place = group * peers + (peer ^ 1)
                pairs.append((group * peers + peer, place))
        return lax.ppermute(message, ("gz", "xy"), pairs)

    far, near = masks_within(peers)
    own = (own_scale * across(0).astype(jnp.float32)).astype(jnp.bfloat16)
    fetched = jnp.stack([across(mask) for mask in far[1:]])
    fetched = (far_scale * fetched.astype(jnp.float32)).astype(jnp.bfloat16)
    one = jnp.concatenate([own[None], fetched])
    return in_parts(one, [swapped(own, mask) for mask in near], first)[:2]


def gated(turn):
    def wrap(body):
        if turn is None:
            body()
        else:
            pl.when(lax.axis_index("gz") == turn)(body)

    return wrap


def in_kernel(body, outs, operands, aliases=None, specs=None, scratch=(), flops=0, moved=0):
    return pl.pallas_call(
        body,
        out_shape=tuple(pltpu.VMEM(shape, dtype) for shape, dtype in outs),
        in_specs=specs or [IN_VMEM] * len(operands),
        out_specs=(IN_VMEM,) * len(outs),
        scratch_shapes=scratch,
        input_output_aliases=aliases or {},
        compiler_params=pltpu.CompilerParams(vmem_limit_bytes=16 * 2**20),
        cost_estimate=pl.CostEstimate(flops=flops, bytes_accessed=moved, transcendentals=0),
    )(*operands)


def real_products(field, matrix):
    return [
        jnp.dot(field, matrix[part], preferred_element_type=jnp.float32) for part in range(2)
    ]


def combined(products):
    first, second = products
    count = first.shape[0] // 2
    return first[:count] - second[count:], second[:count] + first[count:]


def panel_copies(panel, schur_ref, out_ref, sems):
    chunks = sems.shape[0] // 2
    rows = schur_ref.shape[2] // chunks
    copies = []
    for part in range(2):
        for chunk in range(chunks):
            span = pl.ds(chunk * rows, rows)
            copies.append(
                pltpu.make_async_copy(
                    schur_ref.at[panel, part, span, :],
                    out_ref.at[part, span, :],
                    sems.at[part * chunks + chunk],
                )
            )
    for copy in copies:
        copy.start()
    return copies


def load_kernel(schur_ref, after_ref, out_ref, sems):
    del after_ref
    for copy in panel_copies(0, schur_ref, out_ref, sems):
        copy.wait()


def loaded(schur, after):
    return in_kernel(
        load_kernel,
        [(schur.shape[1:], schur.dtype)],
        [in_hbm(schur), after],
        specs=[IN_HBM, pl.BlockSpec(memory_space=pl.ANY)],
        scratch=[pltpu.SemaphoreType.DMA((8,))],
        moved=schur.dtype.itemsize * schur[0].size,
    )[0]


def local_kernel(*refs):
    operands, size_in, (solved_ref, sent_ref), held = refs[:6], refs[6], refs[7:9], refs[9:15]
    rows_out, (far_first, far_last), (sizes, tail_ref, sems) = refs[15:-5], refs[-5:-3], refs[-3:]
    source_ref, inverse_ref, coupling_ref, rows_ref, link_ref, _ = held
    panel_count, _, side_count, _ = source_ref.shape
    bound, share = sent_ref.shape[1], link_ref.shape[1]
    copies = []
    for index, (operand, place) in enumerate(zip(operands, held)):
        for panel in range(panel_count):
            copies.append(
                pltpu.make_async_copy(
                    operand.at[panel], place.at[panel], sems.at[index * panel_count + panel]
                )
            )
    by_operand = [copies[i * panel_count : (i + 1) * panel_count] for i in range(len(operands))]
    size_copy = pltpu.make_async_copy(size_in, sizes, sems.at[len(copies)])
    size_copy.start()
    for panel in range(panel_count):
        for index in range(3):
            by_operand[index][panel].start()
    for group in by_operand[3:]:
        for copy in group:
            copy.start()
    for panel in range(panel_count):
        by_operand[0][panel].wait()
        by_operand[1][panel].wait()
        field = source_ref[panel].astype(jnp.bfloat16).reshape(2 * side_count, -1)
        solved = combined(real_products(field, inverse_ref.at[panel, 0]))
        for part in range(2):
            solved_ref[panel, part] = solved[part]
        field = jnp.concatenate(solved).astype(jnp.bfloat16)
        by_operand[2][panel].wait()
        pushed = combined(real_products(field, coupling_ref.at[panel, 0]))
        for part in range(2):
            start = (2 * panel + part) * side_count
            sent_ref[pl.ds(start, side_count), :] = pushed[part].astype(jnp.bfloat16)
    for group in by_operand[3:]:
        for copy in group:
            copy.wait()
    tail_ref[...] = jnp.zeros(tail_ref.shape, jnp.float32)
    for panel in range(panel_count):
        rows = rows_ref[pl.ds(panel, 1), :]
        tail_ref[pl.ds(panel, 1), :] = (rows >> 8).astype(jnp.float32)
        tail_ref[pl.ds(panel_count + panel, 1), :] = (rows & 255).astype(jnp.float32)
    row = 2 * panel_count
    for start in range(0, share, bound):
        width = min(bound, share - start)
        link = link_ref[pl.ds(0, 1), pl.ds(start, width)]
        high = link.astype(jnp.bfloat16).astype(jnp.float32)
        tail_ref[pl.ds(row, 1), pl.ds(0, width)] = high
        tail_ref[pl.ds(row + 1, 1), pl.ds(0, width)] = link - high
        row += 2
    first = 2 * side_count * panel_count
    sent_ref[pl.ds(first, tail_ref.shape[0]), :] = tail_ref[...].astype(jnp.bfloat16)
    size_copy.wait()
    me = lax.axis_index("xy")
    masks = [live(sizes, panel, me * share, share) for panel in range(panel_count)]
    for panel in range(panel_count):
        link = link_ref[pl.ds(panel, 1), :]
        rows_out[panel][...] = masks[panel]
        rows_out[panel_count + panel][...] = masks[panel] * link
        rows_out[2 * panel_count + panel][...] = link * masks[panel - 1] if panel else link
    for index, mask in enumerate(masks_within(4 * (1 + far_first.shape[0]))[0][1:]):
        start = (me ^ mask) * share
        far_first[index, 0] = live(sizes, 0, start, share)
        far_last[index, 0] = live(sizes, panel_count - 1, start, share)


def tail_of(ref, place, first):
    return ref[place, pl.ds(first, ref.shape[1] - first), :].astype(jnp.float32)


def live(size_ref, panel, start, share):
    rows = start + lax.broadcasted_iota(jnp.int32, (1, share), 1)
    return jnp.where(rows < size_ref[panel], 1.0, 0.0)


def pushed_up(panel, panel_count, count, share, refs, contrib):
    bound = refs[0].shape[2]
    own_rows = lax.axis_index("xy") * share + lax.broadcasted_iota(jnp.int32, (share, bound), 0)
    contract = (((1,), (1,)), ((), ()))
    for ref in refs:
        for place in range(ref.shape[0]):
            values = ref[place, pl.ds(count * panel, count), :]
            tail = tail_of(ref, place, count * panel_count)
            high = tail[panel : panel + 1]
            low = tail[panel_count + panel : panel_count + panel + 1]
            places = (256.0 * high + low).astype(jnp.int32)
            hits = jnp.where(own_rows == places, 1.0, 0.0).astype(jnp.bfloat16)
            contrib += lax.dot_general(values, hits, contract, preferred_element_type=jnp.float32)
    return contrib


def push_kernel(panel, panel_count, parts, *refs):
    contrib_ref = refs[-1]
    count, share = contrib_ref.shape
    contrib = refs[parts][...] if len(refs) > parts + 1 else jnp.zeros((count, share), jnp.float32)
    contrib_ref[...] = pushed_up(panel, panel_count, count, share, refs[:parts], contrib)


def base_kernel(panel, panel_count, mask_ref, contrib_ref, source_ref, *refs):
    refs, base_ref, message_ref = refs[:-2], refs[-2], refs[-1]
    _, side_count, share = base_ref.shape
    count = 2 * side_count
    contrib = pushed_up(panel, panel_count, count, share, refs, contrib_ref[...])
    for part in range(2):
        rows = slice(part * side_count, (part + 1) * side_count)
        base = mask_ref[...] * (source_ref[panel, part] - contrib[rows])
        base_ref[part] = base
        message_ref[part] = base.astype(jnp.bfloat16)


def later_kernel(panel, panel_count, mask_ref, source_ref, *refs):
    shards, schur_ref, base_ref, out_ref, sems = refs[:4], refs[4], refs[6], refs[7], refs[8]
    copies = panel_copies(panel, schur_ref, out_ref, sems)
    _, side_count, share = base_ref.shape
    count = 2 * side_count
    zeros = jnp.zeros((count, share), jnp.float32)
    contrib = pushed_up(panel, panel_count, count, share, shards, zeros)
    for part in range(2):
        rows = slice(part * side_count, (part + 1) * side_count)
        base_ref[part] = mask_ref[...] * (source_ref[panel, part] - contrib[rows])
    for copy in copies:
        copy.wait()


def far_kernel(panel_count, side_count, mask_ref, far_ref, scale_ref):
    share, bound = scale_ref.shape[3], far_ref.shape[2]
    for index in range(scale_ref.shape[0]):
        tail = tail_of(far_ref, 1 + index, 2 * side_count * panel_count)
        for piece, place in enumerate(range(0, share, bound)):
            columns = pl.ds(place, min(bound, share - place))
            row = 2 * (panel_count + piece)
            link = (tail[row : row + 1] + tail[row + 1 : row + 2])[:, : columns.size]
            scale_ref[index, 0, :, columns] = mask_ref[index, 0, :, columns] * link


def part_products(ref, origins, schur_ref, products):
    side_count, share = ref.shape[2:]
    for place, origin in enumerate(origins):
        rows = pl.ds(pl.multiple_of(origin * share, share), share)
        field = ref[place].reshape(2 * side_count, share)
        terms = real_products(field, schur_ref.at[:, rows, :])
        products = terms if products is None else [a + b for a, b in zip(products, terms)]
    return products


def products_kernel(turn, sources, which, *refs):
    schur_ref, products_ref = refs[len(which)], refs[-1]

    @gated(turn)
    def _():
        origins = sources(lax.axis_index("xy"))
        products = None
        if len(refs) > len(which) + 2:
            products = [refs[len(which) + 1][part] for part in range(2)]
        for ref, (part, core) in zip(refs, which):
            products = part_products(ref, origins[part][core], schur_ref, products)
        for part in range(2):
            products_ref[part] = products[part]


def late_kernel(turn, sources, names, *refs):
    named = dict(zip(names, refs))
    kept_ref, message_ref = refs[-2:]

    @gated(turn)
    def _():
        origins = sources(lax.axis_index("xy"))[-1][1]
        products = [named["products"][part] for part in range(2)]
        products = part_products(named["other"], origins, named["schur"], products)
        for part, value in enumerate(combined(products)):
            value = named["mask"][...] * value
            if "kept" in named:
                value = named["kept"][part] + value
            kept_ref[part] = value
            if "scale" in named:
                value = named["scale"][...] * value
            if "addend" in named:
                value = named["addend"][part] + value
            message_ref[part] = value.astype(jnp.bfloat16)


def cost_of(mine):
    _, _, side_count, share = mine.shape
    return {
        "flops": 8 * side_count * share * share * mine.shape[0],
        "moved": 4 * share * share * mine.shape[0],
    }


def products_of(turn, sources, which, parts, schur, products=None):
    side_count, share = parts[0].shape[2:]
    operands = [*parts, schur] + ([] if products is None else [products])
    return in_kernel(
        functools.partial(products_kernel, turn, sources, which),
        [((2, 2 * side_count, share), jnp.float32)],
        [resident(value) for value in operands],
        **cost_of(parts[0]),
    )[0]


def first_products(turn, sources, schur, mine):
    return products_of(turn, sources, [(0, 0)], [mine], schur)


def more_products(turn, sources, pieces, schur, products):
    (_, other), (more, _) = pieces
    return products_of(turn, sources, [(0, 1), (1, 0)], [other, more], schur, products)


def sweep_step(turn, sources, pieces, schur, products, kept, message, adds, **others):
    products = more_products(turn, sources, pieces, schur, products)
    named = {"products": products, "other": pieces[-1][1], "schur": schur}
    named.update({name: value for name, value in others.items() if value is not None})
    named["kept" if adds else "old"], named["message"] = kept, message
    count = len(named)
    return in_kernel(
        functools.partial(late_kernel, turn, sources, list(named)),
        [(kept.shape, kept.dtype), (message.shape, message.dtype)],
        [resident(value) for value in named.values()],
        aliases={count - 2: 0, count - 1: 1},
        **cost_of(pieces[-1][1]),
    )


def last_step(turn, sources, pieces, schur, products, mask, kepts):
    products = more_products(turn, sources, pieces, schur, products)
    operands = [products, pieces[-1][1], schur, mask] + kepts
    return in_kernel(
        functools.partial(last_kernel, turn, sources),
        [
            (kepts[0].shape, kepts[0].dtype),
            ((len(kepts),) + kepts[0].shape, jnp.bfloat16),
        ],
        [resident(value) for value in operands],
        aliases={4: 0},
        **cost_of(pieces[-1][1]),
    )


def last_kernel(turn, sources, products_ref, other_ref, schur_ref, mask_ref, *refs):
    kepts, kept_ref, message_ref = refs[:-2], refs[-2], refs[-1]
    for panel in range(1, len(kepts)):
        message_ref[panel] = kepts[panel][...].astype(jnp.bfloat16)

    @gated(turn)
    def _():
        origins = sources(lax.axis_index("xy"))[-1][1]
        products = [products_ref[part] for part in range(2)]
        products = part_products(other_ref, origins, schur_ref, products)
        for part, value in enumerate(combined(products)):
            value = kepts[0][part] + mask_ref[...] * value
            kept_ref[part] = value
            message_ref[0, part] = value.astype(jnp.bfloat16)

    @pl.when(lax.axis_index("gz") != turn)
    def _():
        message_ref[0] = kepts[0][...].astype(jnp.bfloat16)


def pick_kernel(sources, which, *refs):
    rows_ref, picked_ref = refs[len(which)], refs[-1]
    origins = sources(lax.axis_index("xy"))
    picked = None
    if len(refs) > len(which) + 2:
        picked = [refs[len(which) + 1][panel] for panel in range(picked_ref.shape[0])]
    for ref, (part, core) in zip(refs, which):
        picked = picks(ref, rows_ref, origins[part][core], picked)
    for panel, value in enumerate(picked):
        picked_ref[panel] = value


def picks(ref, rows_ref, origins, picked):
    _, panel_count, _, side_count, share = ref.shape
    bound = rows_ref.shape[1]
    found = []
    for panel in range(panel_count):
        total = picked[panel] if picked else jnp.zeros((2 * side_count, bound), jnp.float32)
        for place, origin in enumerate(origins):
            rows = origin * share + lax.broadcasted_iota(jnp.int32, (share, bound), 0)
            chosen = jnp.where(rows == rows_ref[pl.ds(panel, 1), :], 1.0, 0.0).astype(jnp.bfloat16)
            field = ref[place, panel].reshape(2 * side_count, share)
            total += jnp.dot(field, chosen, preferred_element_type=jnp.float32)
        found.append(total)
    return found


def inner_kernel(
    sources, picked_ref, last_ref, rows_ref, coupling_ref, inverse_ref, solved_ref, out_ref, inner_ref, sems
):
    contract = (((1,), (1,)), ((), ()))
    origins = sources(lax.axis_index("xy"))[-1][1]
    picked = picks(last_ref, rows_ref, origins, [picked_ref[p] for p in range(picked_ref.shape[0])])
    lifted = [
        combined(
            [
                lax.dot_general(
                    value.astype(jnp.bfloat16),
                    coupling_ref[panel, 0, part],
                    contract,
                    preferred_element_type=jnp.float32,
                )
                for part in range(2)
            ]
        )
        for panel, value in enumerate(picked)
    ]
    copies = []
    for panel, value in enumerate(lifted):
        field = jnp.concatenate(value).astype(jnp.bfloat16)
        back = combined(real_products(field, inverse_ref.at[panel, 0]))
        for part in range(2):
            inner_ref[panel, part] = solved_ref[panel, part] - back[part]
        copies.append(
            pltpu.make_async_copy(inner_ref.at[panel], out_ref.at[panel], sems.at[panel])
        )
        copies[-1].start()
    for copy in copies:
        copy.wait()


def on_device(
    source_inner, source_front, inner_inverse, coupling, schur_inverse, front_rows, link, front_size
):
    peers, groups = lax.axis_size("xy"), lax.axis_size("gz")
    panel_count, _, side_count, share = source_front.shape
    bound = front_rows.shape[1]
    local = source_inner.shape[3]

    tail_rows = 2 * panel_count + 2 * -(-share // bound)
    tail_rows += -tail_rows % 16
    sent_rows = 2 * side_count * panel_count + tail_rows
    taken = [source_inner, inner_inverse, coupling, front_rows, link, source_front]
    row = ((1, share), jnp.float32)
    arriving = ((peers // 4 - 1, 1, 1, share), jnp.float32)
    solved, sent, _, inverse_held, coupling_held, rows_held, _, source_held, *scales = in_kernel(
        local_kernel,
        [
            ((panel_count, 2, side_count, local), jnp.float32),
            ((sent_rows, bound), jnp.bfloat16),
        ]
        + [(value.shape, value.dtype) for value in taken]
        + [row] * (3 * panel_count)
        + [arriving] * 2,
        [in_hbm(value) for value in taken + [front_size]],
        specs=[IN_HBM] * (len(taken) + 1),
        scratch=[
            pltpu.SMEM(front_size.shape, jnp.int32),
            pltpu.VMEM((tail_rows, bound), jnp.float32),
            pltpu.SemaphoreType.DMA((len(taken) * panel_count + 1,)),
        ],
    )
    masks, forward_scales = scales[:panel_count], scales[panel_count : 2 * panel_count]
    backward_scales, far_scales = scales[2 * panel_count : 3 * panel_count], scales[3 * panel_count :]

    def push(panel, shards, contrib=None):
        operands = shards + ([] if contrib is None else [contrib])
        return in_kernel(
            functools.partial(push_kernel, panel, panel_count, len(shards)),
            [((2 * side_count, share), jnp.float32)],
            [resident(value) for value in operands],
            moved=2**22,
        )[0]

    shards, contrib, schurs = gathered_within(
        sent, None, lambda mine: push(0, [mine]), [loaded(schur_inverse, sent)]
    )
    shards = [shard for part in shards for shard in part]
    contrib = push(0, shards[1:3], contrib)
    operands = [masks[0], contrib, source_held, shards[3]]
    base, message = in_kernel(
        functools.partial(base_kernel, 0, panel_count),
        [((2, side_count, share), jnp.float32), ((2, side_count, share), jnp.bfloat16)],
        [resident(value) for value in operands],
        moved=2**22,
    )
    bases = [base]
    for panel in range(1, panel_count):
        operands = [resident(value) for value in (masks[panel], source_held, *shards)]
        base, schur = in_kernel(
            functools.partial(later_kernel, panel, panel_count),
            [((2, side_count, share), jnp.float32), (schur_inverse.shape[1:], schur_inverse.dtype)],
            operands + [in_hbm(schur_inverse), message],
            specs=[IN_VMEM] * len(operands) + [IN_HBM, pl.BlockSpec(memory_space=pl.ANY)],
            scratch=[pltpu.SemaphoreType.DMA((8,))],
            moved=2**23,
        )
        bases.append(base)
        schurs.append(schur)
    far_scales[0] = in_kernel(
        functools.partial(far_kernel, panel_count, side_count),
        [arriving],
        [resident(far_scales[0]), resident(shards[0])],
    )[0]

    kept = [jnp.zeros((2, side_count, share), jnp.float32) for _ in range(panel_count)]
    sources = sources_within(peers)
    order = [(turn, panel) for turn in range(groups) for panel in range(panel_count)]
    steps = [(None, 0, True)] + [step + (True,) for step in order[1:]]
    steps += [step + (False,) for step in reversed(order[:-1])]
    for count, (turn, panel, forward) in enumerate(steps):
        if forward and panel == 0 and turn is not None:
            low, own_scale, far_scale = turn - 1, forward_scales[0], far_scales[0]
        elif not forward and panel == panel_count - 1:
            low, own_scale, far_scale = turn, masks[panel], far_scales[1]
        else:
            low = None
        first = functools.partial(first_products, turn, sources, schurs[panel])
        if low is not None:
            pieces, products = crossed(message, low, own_scale, far_scale, first)
        elif count == 0:
            beside = (bases[1:], schurs[1:], far_scales)
            pieces, products, beside = gathered_within(message, None, first, beside)
            bases[1:], schurs[1:], far_scales = beside
        else:
            pieces, products, _ = gathered_within(message, turn, first)
        scale = addend = None
        if forward and panel < panel_count - 1:
            scale, addend = forward_scales[panel + 1], bases[panel + 1]
        elif not forward or turn == groups - 1:
            scale = backward_scales[panel]
        if count == len(steps) - 1:
            kept[0], message = last_step(turn, sources, pieces, schurs[0], products, masks[0], kept)
        else:
            kept[panel], message = sweep_step(
                turn, sources, pieces, schurs[panel], products, kept[panel], message,
                not forward or (panel == 0 and turn is not None),
                mask=masks[panel], scale=scale, addend=addend,
            )

    fronts = jnp.stack(kept)

    def pick(which, parts, *picked):
        return in_kernel(
            functools.partial(pick_kernel, sources, which),
            [((panel_count, 2 * side_count, bound), jnp.float32)],
            [resident(value) for value in (*parts, rows_held, *picked)],
            moved=2**22,
        )[0]

    pieces, picked, _ = gathered_within(message, None, lambda mine: pick([(0, 0)], [mine]))
    (_, other), (more, last) = pieces
    picked = pick([(0, 1), (1, 0)], [other, more], picked)
    operands = [picked, last, rows_held, coupling_held, inverse_held, solved]
    inner = pl.pallas_call(
        functools.partial(inner_kernel, sources),
        out_shape=jax.ShapeDtypeStruct(solved.shape, jnp.float32),
        in_specs=[IN_VMEM] * len(operands),
        out_specs=IN_HBM,
        scratch_shapes=[
            pltpu.VMEM(solved.shape, jnp.float32),
            pltpu.SemaphoreType.DMA((panel_count,)),
        ],
        compiler_params=pltpu.CompilerParams(vmem_limit_bytes=16 * 2**20),
    )(*[resident(value) for value in operands])
    return inner, fronts


def solution(mesh):
    placed = (
        P("gz", None, None, "xy"),
        P("gz", None, None, "xy"),
        P("gz", "xy", None, None, None),
        P("gz", "xy", None, None, None),
        P("gz", None, None, "xy"),
        P("gz", "xy"),
        P("gz", "xy"),
        P("gz"),
    )
    return jax.shard_map(
        on_device,
        mesh=mesh,
        in_specs=placed,
        out_specs=(P("gz", None, None, "xy"), P("gz", None, None, "xy")),
        check_vma=False,
    )
```

time: 163 us -> 161 us (0.988)
  Pallas kernels: 25.1 us -> 21.8 us
    pallas_call x54, Pallas kernels: 22.9 us -> 20.2 us  [in_kernel(): pl.pallas_call(body, out_shape=tuple((pltpu.VMEM(shape, dtype) for shape,...]
    ppermute x85 -> x91, starting transfers between devices: 81.4 us -> 82.3 us  [the longest x79 45.2 us: swapped(): return lax.ppermute(shard, ('gz', 'xy'), pairs)]
    ppermute x85 -> x91, waiting for transfers between devices: 54.2 us -> 54.4 us  [the longest x79 46.6 us: swapped(): return lax.ppermute(shard, ('gz', 'xy'), pairs)]
  transfers between devices with their start and end apart: 85 -> 91, of which waited for: 63 -> 63; matrix products, arithmetic and copies ran while one was open for 1% -> 1% of each run, Pallas kernels for 10% -> 9%
where the time goes in v4:
time: 161 us
  starting transfers between devices  82.3 us (51%)
  waiting for transfers between devices  54.4 us (34%)
  Pallas kernels  21.8 us (14%)
  between operations  1.62 us (1%)
    ppermute x79, waiting for transfers between devices, swapped(): return lax.ppermute(shard, ('gz', 'xy'), pairs)  46.6 us
    ppermute x79, starting transfers between devices, swapped(): return lax.ppermute(shard, ('gz', 'xy'), pairs)  45.2 us
    ppermute x12, starting transfers between devices, across(): return lax.ppermute(message, ('gz', 'xy'), pairs)  37.1 us
    pallas_call x54, Pallas kernels, in_kernel(): pl.pallas_call(body, out_shape=tuple((pltpu.VMEM(shape, dtype) for shape,...  20.2 us
    ppermute x12, waiting for transfers between devices, across(): return lax.ppermute(message, ('gz', 'xy'), pairs)  7.81 us
  transfers between devices with their start and end apart: 91, of which 63 were waited for; matrix products, arithmetic and copies ran while one was open for 1% of the time, Pallas kernels for 9%

profile of v4, /device:TPU:0, one launch (start us, length us, event | category | flops | bytes accessed | tf_op | source)
XLA Modules:
  0.0 161.2 jit_solution(4856198614538977453)
XLA Ops:
  0.6 3.3 %shard_map.95 = (f32[2,2,16,512]{3,2,1,0:T(8,128)S(1)}, bf16[80,256]{1,0:T(8,128)(2,1)S(1)}, f32[2,2,16,512]{3,2,1,0:T(8,128)}, bf16[2,1,2,512,512]{4,3,2,1,0:T(...) custom-call(f32[2,2,16,512]{3,2,1,0:T(8,128)} %refs_0_.1, ...), custom_call_target="tpu_custom_call" | custom-call | tf_op jit(solution)/shard_map/pallas_call | solution.py:100
  3.9 4.0 %collective-permute-start = (bf16[80,256]{1,0:T(8,128)(2,1)S(1)}, bf16[80,256]{1,0:T(8,128)(2,1)S(1)}, u32[]{:S(2)}, u32[]{:S(2)}) collective-permute-start(bf16[80,256]{1,0:T(8,128)(2,1)S(1)} %get-tuple-element.108.after_ref), channel_id=1, source_target_pairs={{0,6},{1,7},{2,4},{3,5},{4,2},{5,3},{6,0},{7,1},{8,14},{9,15},{10,... | collective-permute-start | bytes 122888 | tf_op jit(solution)/shard_map/ppermute | solution.py:31
  8.5 3.5 %shard_map.97.refs_1_.refs_2_.schur_ref = bf16[2,4096,512]{2,1,0:T(8,128)(2,1)S(1)} custom-call(bf16[2,2,4096,512]{3,2,1,0:T(8,128)(2,1)} %refs_4_.3, bf16[80,256]{1,0:T(8,128)(2,1)S(1)} %get-tuple-element.108.after_ref), custom_call_target="tpu_custom_call" | custom-call | bytes 8388608 | tf_op jit(solution)/shard_map/pallas_call | solution.py:100
  12.9 0.7 collective-permute-done.1.refs_0_.refs_1_
  14.0 0.9 shard_map.99
  15.0 2.8 %collective-permute-start.5 = (bf16[2,16,512]{2,1,0:T(8,128)(2,1)S(1)}, bf16[2,16,512]{2,1,0:T(8,128)(2,1)S(1)}, u32[]{:S(2)}, u32[]{:S(2)}) collective-permute-start(bf16[2,16,512]{2,1,0:T(8,128)(2,1)S(1)} %get-tuple-element.113.refs_5_.refs_7_), channel_id=1, source_target_pairs={{0,6},{1,7},{2,4},{3,5},{4,2},{5,3},{6,0},{7,1},{8,14},{9,15},{10,... | collective-permute-start | bytes 98312 | tf_op jit(solution)/shard_map/ppermute | solution.py:31
  18.5 3.8 %shard_map.101 = (f32[2,16,512]{2,1,0:T(8,128)S(1)}, bf16[2,4096,512]{2,1,0:T(8,128)(2,1)S(1)}) custom-call(f32[1,512]{1,0:T(1,128)S(1)} %get-tuple-element.105.mask_ref.refs_3_, f32[2,2,16,512]{3,2,1,0:T(8,128)S(1)} %get-tuple-element.112.source_ref, bf16[2,80,256]{2,1,0:T(8,128)(2,1)S(1)} %pad_maximum_fusion.3.refs_0_.far_ref, ...), custom_call_target="tpu_custom_call" | custom-call | bytes 8388608 | tf_op jit(solution)/shard_map/pallas_call | solution.py:100
  23.6 0.8 shard_map.103.refs_0_
  25.0 2.9 %collective-permute-start.10 = (bf16[2,16,512]{2,1,0:T(8,128)(2,1)S(1)}, bf16[2,16,512]{2,1,0:T(8,128)(2,1)S(1)}, u32[]{:S(2)}, u32[]{:S(2)}) collective-permute-start(bf16[2,16,512]{2,1,0:T(8,128)(2,1)S(1)} %get-tuple-element.124.refs_5_), channel_id=1, source_target_pairs={{0,6},{1,7},{2,4},{3,5},{4,2},{5,3},{6,0},{7,1},{8,9},{9,8},{10,11... | collective-permute-start | bytes 98312 | tf_op jit(solution)/shard_map/ppermute | solution.py:31
  28.5 1.3 collective-permute-done.10
  30.4 1.4 collective-permute-done.12
  32.4 0.8 shard_map.106.refs_0_
  34.2 2.9 %collective-permute-start.16 = (bf16[2,16,512]{2,1,0:T(8,128)(2,1)S(1)}, bf16[2,16,512]{2,1,0:T(8,128)(2,1)S(1)}, u32[]{:S(2)}, u32[]{:S(2)}) collective-permute-start(bf16[2,16,512]{2,1,0:T(8,128)(2,1)S(1)} %get-tuple-element.129.refs_7_), channel_id=1, source_target_pairs={{0,14},{1,15},{2,12},{3,13},{4,10},{5,11},{6,8},{7,9},{8,6},{9,7},... | collective-permute-start | bytes 98312 | tf_op jit(solution)/shard_map/ppermute | solution.py:79
  37.1 1.1 collective-permute-done.15
  38.3 1.4 collective-permute-start.18
  39.7 0.8 collective-permute-start.19
  40.6 1.6 %collective-permute-done.18 = bf16[2,16,512]{2,1,0:T(8,128)(2,1)S(1)} collective-permute-done((bf16[2,16,512]{2,1,0:T(8,128)(2,1)S(1)}, bf16[2,16,512]{2,1,0:T(8,128)(2,1)S(1)}, u32[]{:S(2)}, u32[]{:S(2)}) %collective-permute-start.18) | collective-permute-done | bytes 32800 | tf_op jit(solution)/shard_map/ppermute | solution.py:31
  42.2 1.4 collective-permute-done.19
  43.7 1.2 collective-permute-done.20.refs_1_
  48.5 0.7 collective-permute-done.26
  49.2 0.7 collective-permute-start.29
  50.5 2.7 %collective-permute-done.29 = bf16[2,16,512]{2,1,0:T(8,128)(2,1)S(1)} collective-permute-done((bf16[2,16,512]{2,1,0:T(8,128)(2,1)S(1)}, bf16[2,16,512]{2,1,0:T(8,128)(2,1)S(1)}, u32[]{:S(2)}, u32[]{:S(2)}) %collective-permute-start.29) | collective-permute-done | bytes 32800 | tf_op jit(solution)/shard_map/ppermute | solution.py:31
  54.0 1.2 collective-permute-done.31.refs_1_
  55.2 1.6 collective-permute-start.32
  57.0 1.6 %collective-permute-start.35 = (bf16[2,16,512]{2,1,0:T(8,128)(2,1)S(1)}, bf16[2,16,512]{2,1,0:T(8,128)(2,1)S(1)}, u32[]{:S(2)}, u32[]{:S(2)}) collective-permute-start(bf16[2,16,512]{2,1,0:T(8,128)(2,1)S(1)} %get-tuple-element.145.refs_5_), channel_id=1, source_target_pairs={{0,2},{1,3},{2,0},{3,1},{4,6},{5,7},{6,4},{7,5},{8,9},{9,8},{10,11... | collective-permute-start | bytes 98312 | tf_op jit(solution)/shard_map/ppermute | solution.py:31
  58.7 1.3 collective-permute-done.32
  61.3 0.9 collective-permute-done.36.refs_1_
  62.8 0.7 collective-permute-done.37
  63.5 1.8 %collective-permute-start.40 = (bf16[2,16,512]{2,1,0:T(8,128)(2,1)S(1)}, bf16[2,16,512]{2,1,0:T(8,128)(2,1)S(1)}, u32[]{:S(2)}, u32[]{:S(2)}) collective-permute-start(bf16[2,16,512]{2,1,0:T(8,128)(2,1)S(1)} %multiply_convert_fusion.7), channel_id=1, source_target_pairs={{0,4},{1,5},{2,6},{3,7},{4,0},{5,1},{6,2},{7,3},{8,12},{9,13},{10,... | collective-permute-start | bytes 98312 | tf_op jit(solution)/shard_map/ppermute | solution.py:31
  65.3 1.3 collective-permute-start.41
  66.7 0.7 collective-permute-done.40
  67.5 1.7 %collective-permute-done.41 = bf16[2,16,512]{2,1,0:T(8,128)(2,1)S(1)} collective-permute-done((bf16[2,16,512]{2,1,0:T(8,128)(2,1)S(1)}, bf16[2,16,512]{2,1,0:T(8,128)(2,1)S(1)}, u32[]{:S(2)}, u32[]{:S(2)}) %collective-permute-start.41) | collective-permute-done | bytes 32800 | tf_op jit(solution)/shard_map/ppermute | solution.py:31
  69.3 1.2 collective-permute-done.42.refs_1_
  77.2 0.7 collective-permute-done.53
  78.2 1.6 %collective-permute-start.57 = (bf16[2,16,512]{2,1,0:T(8,128)(2,1)S(1)}, bf16[2,16,512]{2,1,0:T(8,128)(2,1)S(1)}, u32[]{:S(2)}, u32[]{:S(2)}) collective-permute-start(bf16[2,16,512]{2,1,0:T(8,128)(2,1)S(1)} %multiply_convert_fusion.5), channel_id=1, source_target_pairs={{0,2},{1,3},{2,0},{3,1},{4,6},{5,7},{6,4},{7,5},{8,10},{9,11},{10,... | collective-permute-start | bytes 98312 | tf_op jit(solution)/shard_map/ppermute | solution.py:31
  80.0 1.8 %collective-permute-done.56 = bf16[2,16,512]{2,1,0:T(8,128)(2,1)S(1)} collective-permute-done((bf16[2,16,512]{2,1,0:T(8,128)(2,1)S(1)}, bf16[2,16,512]{2,1,0:T(8,128)(2,1)S(1)}, u32[]{:S(2)}, u32[]{:S(2)}) %collective-permute-start.56) | collective-permute-done | bytes 32800 | tf_op jit(solution)/shard_map/ppermute | solution.py:31
  82.3 1.2 collective-permute-done.58.refs_1_
  83.5 2.4 %collective-permute-start.59 = (bf16[2,16,512]{2,1,0:T(8,128)(2,1)S(1)}, bf16[2,16,512]{2,1,0:T(8,128)(2,1)S(1)}, u32[]{:S(2)}, u32[]{:S(2)}) collective-permute-start(bf16[2,16,512]{2,1,0:T(8,128)(2,1)S(1)} %get-tuple-element.173.refs_6_), channel_id=1, source_target_pairs={{0,6},{1,7},{2,4},{3,5},{4,2},{5,3},{6,0},{7,1},{8,9},{9,8},{10,11... | collective-permute-start | bytes 98312 | tf_op jit(solution)/shard_map/ppermute | solution.py:31
  87.0 1.3 collective-permute-done.59
  88.4 1.4 collective-permute-done.61
  90.6 1.2 collective-permute-done.63.refs_1_
  92.3 0.7 collective-permute-done.64
  93.1 1.4 collective-permute-start.67
  94.5 0.8 collective-permute-start.68
  95.4 1.6 %collective-permute-done.67 = bf16[2,16,512]{2,1,0:T(8,128)(2,1)S(1)} collective-permute-done((bf16[2,16,512]{2,1,0:T(8,128)(2,1)S(1)}, bf16[2,16,512]{2,1,0:T(8,128)(2,1)S(1)}, u32[]{:S(2)}, u32[]{:S(2)}) %collective-permute-start.67) | collective-permute-done | bytes 32800 | tf_op jit(solution)/shard_map/ppermute | solution.py:31
  97.0 1.4 collective-permute-done.68
  98.5 1.2 collective-permute-done.69.refs_1_
  102.8 31.7 %collective-permute-start.75 = (bf16[2,16,512]{2,1,0:T(8,128)(2,1)S(1)}, bf16[2,16,512]{2,1,0:T(8,128)(2,1)S(1)}, u32[]{:S(2)}, u32[]{:S(2)}) collective-permute-start(bf16[2,16,512]{2,1,0:T(8,128)(2,1)S(1)} %get-tuple-element.188.refs_6_), channel_id=1, source_target_pairs={{0,8},{1,9},{2,10},{3,11},{4,12},{5,13},{6,14},{7,15},{8,0},{9,1},... | collective-permute-start | bytes 98312 | tf_op jit(solution)/shard_map/ppermute | solution.py:79
  134.8 1.5 collective-permute-done.75
  136.4 0.8 collective-permute-start.78
  137.9 2.4 %collective-permute-done.76 = bf16[2,16,512]{2,1,0:T(8,128)(2,1)S(1)} collective-permute-done((bf16[2,16,512]{2,1,0:T(8,128)(2,1)S(1)}, bf16[2,16,512]{2,1,0:T(8,128)(2,1)S(1)}, u32[]{:S(2)}, u32[]{:S(2)}) %collective-permute-start.76) | collective-permute-done | bytes 32800 | tf_op jit(solution)/shard_map/ppermute | solution.py:79
  141.6 0.8 shard_map.142.refs_0_
  142.9 1.4 collective-permute-start.81
  144.3 0.8 collective-permute-start.83
  145.1 1.4 collective-permute-start.84
  146.5 1.3 collective-permute-done.81
  148.4 0.7 collective-permute-done.84
  149.1 0.8 shard_map.145.products_ref
  150.8 2.1 %collective-permute-start.86 = (bf16[2,2,16,512]{3,2,1,0:T(8,128)(2,1)S(1)}, bf16[2,2,16,512]{3,2,1,0:T(8,128)(2,1)S(1)}, u32[]{:S(2)}, u32[]{:S(2)}) collective-permute-start(bf16[2,2,16,512]{3,2,1,0:T(8,128)(2,1)S(1)} %get-tuple-element.199), channel_id=1, source_target_pairs={{0,6},{1,7},{2,4},{3,5},{4,2},{5,3},{6,0},{7,1},{8,14},{9,15},{10,... | collective-permute-start | bytes 196616 | tf_op jit(solution)/shard_map/ppermute | solution.py:31
  153.0 0.7 collective-permute-start.88
  153.7 0.7 collective-permute-start.89
  154.4 1.7 %collective-permute-done.86 = bf16[2,2,16,512]{3,2,1,0:T(8,128)(2,1)S(1)} collective-permute-done((bf16[2,2,16,512]{3,2,1,0:T(8,128)(2,1)S(1)}, bf16[2,2,16,512]{3,2,1,0:T(8,128)(2,1)S(1)}, u32[]{:S(2)}, u32[]{:S(2)}) %collective-permute-start.86) | collective-permute-done | bytes 65568 | tf_op jit(solution)/shard_map/ppermute | solution.py:31
  156.5 0.9 collective-permute-done.88
  159.4 1.7 %shard_map.149 = f32[2,2,16,512]{3,2,1,0:T(8,128)} custom-call(f32[2,32,256]{2,1,0:T(8,128)S(1)} %shard_map.148.picked_ref, bf16[2,2,2,16,512]{4,3,2,1,0:T(8,128)(2,1)S(1)} %collective-permute-done.90.last_ref, s32[2,256]{1,0:T(2,128)S(1)} %get-tuple-element.200.refs_1_.refs_2_.rows_ref, bf16[2,1,2,512,256]{4,3,2,1,0:T(8,128)(2,1)S(1)} %get-tuple-element.204.coupling_ref, ...), custom_call_target="tpu_custom_call" | custom-call | tf_op jit(solution)/shard_map/pallas_call | solution.py:605
  (228 shorter events, 34.4 us)
Async XLA Ops:
  3.9 8.1 %collective-permute-start = (bf16[80,256]{1,0:T(8,128)(2,1)S(1)}, bf16[80,256]{1,0:T(8,128)(2,1)S(1)}, u32[]{:S(2)}, u32[]{:S(2)}) collective-permute-start(bf16[80,256]{1,0:T(8,128)(2,1)S(1)} %get-tuple-element.108.after_ref), channel_id=1, source_target_pairs={{0,6},{1,7},{2,4},{3,5},{4,2},{5,3},{6,0},{7,1},{8,14},{9,15},{10,... | collective-permute-start | bytes 122888 | tf_op jit(solution)/shard_map/ppermute | solution.py:31
  7.9 4.4 %collective-permute-start.2 = (bf16[80,256]{1,0:T(8,128)(2,1)S(1)}, bf16[80,256]{1,0:T(8,128)(2,1)S(1)}, u32[]{:S(2)}, u32[]{:S(2)}) collective-permute-start(bf16[80,256]{1,0:T(8,128)(2,1)S(1)} %get-tuple-element.108.after_ref), channel_id=1, source_target_pairs={{0,4},{1,5},{2,6},{3,7},{4,0},{5,1},{6,2},{7,3},{8,12},{9,13},{10,... | collective-permute-start | bytes 122888 | tf_op jit(solution)/shard_map/ppermute | solution.py:31
  8.4 4.0 %collective-permute-start.3 = (bf16[80,256]{1,0:T(8,128)(2,1)S(1)}, bf16[80,256]{1,0:T(8,128)(2,1)S(1)}, u32[]{:S(2)}, u32[]{:S(2)}) collective-permute-start(bf16[80,256]{1,0:T(8,128)(2,1)S(1)} %get-tuple-element.108.after_ref), channel_id=1, source_target_pairs={{0,2},{1,3},{2,0},{3,1},{4,6},{5,7},{6,4},{7,5},{8,10},{9,11},{10,... | collective-permute-start | bytes 122888 | tf_op jit(solution)/shard_map/ppermute | solution.py:31
  12.4 1.6 %collective-permute-start.4 = (bf16[2,80,256]{2,1,0:T(8,128)(2,1)S(1)}, bf16[2,80,256]{2,1,0:T(8,128)(2,1)S(1)}, u32[]{:S(2)}, u32[]{:S(2)}) collective-permute-start(bf16[2,80,256]{2,1,0:T(8,128)(2,1)S(1)} %pad_maximum_fusion.4.refs_1_.refs_2_), channel_id=1, source_target_pairs={{0,1},{1,0},{2,3},{3,2},{4,5},{5,4},{6,7},{7,6},{8,9},{9,8},{10,11... | collective-permute-start | bytes 245768 | tf_op jit(solution)/shard_map/ppermute | solution.py:31
  15.0 7.3 %collective-permute-start.5 = (bf16[2,16,512]{2,1,0:T(8,128)(2,1)S(1)}, bf16[2,16,512]{2,1,0:T(8,128)(2,1)S(1)}, u32[]{:S(2)}, u32[]{:S(2)}) collective-permute-start(bf16[2,16,512]{2,1,0:T(8,128)(2,1)S(1)} %get-tuple-element.113.refs_5_.refs_7_), channel_id=1, source_target_pairs={{0,6},{1,7},{2,4},{3,5},{4,2},{5,3},{6,0},{7,1},{8,14},{9,15},{10,... | collective-permute-start | bytes 98312 | tf_op jit(solution)/shard_map/ppermute | solution.py:31
  17.8 5.1 %collective-permute-start.7 = (bf16[2,16,512]{2,1,0:T(8,128)(2,1)S(1)}, bf16[2,16,512]{2,1,0:T(8,128)(2,1)S(1)}, u32[]{:S(2)}, u32[]{:S(2)}) collective-permute-start(bf16[2,16,512]{2,1,0:T(8,128)(2,1)S(1)} %get-tuple-element.113.refs_5_.refs_7_), channel_id=1, source_target_pairs={{0,4},{1,5},{2,6},{3,7},{4,0},{5,1},{6,2},{7,3},{8,12},{9,13},{10,... | collective-permute-start | bytes 98312 | tf_op jit(solution)/shard_map/ppermute | solution.py:31
  18.4 4.5 %collective-permute-start.8 = (bf16[2,16,512]{2,1,0:T(8,128)(2,1)S(1)}, bf16[2,16,512]{2,1,0:T(8,128)(2,1)S(1)}, u32[]{:S(2)}, u32[]{:S(2)}) collective-permute-start(bf16[2,16,512]{2,1,0:T(8,128)(2,1)S(1)} %get-tuple-element.113.refs_5_.refs_7_), channel_id=1, source_target_pairs={{0,2},{1,3},{2,0},{3,1},{4,6},{5,7},{6,4},{7,5},{8,10},{9,11},{10,... | collective-permute-start | bytes 98312 | tf_op jit(solution)/shard_map/ppermute | solution.py:31
  22.3 1.3 collective-permute-start.6
  22.9 1.6 collective-permute-start.9
  25.0 4.9 %collective-permute-start.10 = (bf16[2,16,512]{2,1,0:T(8,128)(2,1)S(1)}, bf16[2,16,512]{2,1,0:T(8,128)(2,1)S(1)}, u32[]{:S(2)}, u32[]{:S(2)}) collective-permute-start(bf16[2,16,512]{2,1,0:T(8,128)(2,1)S(1)} %get-tuple-element.124.refs_5_), channel_id=1, source_target_pairs={{0,6},{1,7},{2,4},{3,5},{4,2},{5,3},{6,0},{7,1},{8,9},{9,8},{10,11... | collective-permute-start | bytes 98312 | tf_op jit(solution)/shard_map/ppermute | solution.py:31
  27.9 3.9 %collective-permute-start.12 = (bf16[2,16,512]{2,1,0:T(8,128)(2,1)S(1)}, bf16[2,16,512]{2,1,0:T(8,128)(2,1)S(1)}, u32[]{:S(2)}, u32[]{:S(2)}) collective-permute-start(bf16[2,16,512]{2,1,0:T(8,128)(2,1)S(1)} %get-tuple-element.124.refs_5_), channel_id=1, source_target_pairs={{0,4},{1,5},{2,6},{3,7},{4,0},{5,1},{6,2},{7,3},{8,9},{9,8},{10,11... | collective-permute-start | bytes 98312 | tf_op jit(solution)/shard_map/ppermute | solution.py:31
  28.4 3.9 %collective-permute-start.13 = (bf16[2,16,512]{2,1,0:T(8,128)(2,1)S(1)}, bf16[2,16,512]{2,1,0:T(8,128)(2,1)S(1)}, u32[]{:S(2)}, u32[]{:S(2)}) collective-permute-start(bf16[2,16,512]{2,1,0:T(8,128)(2,1)S(1)} %get-tuple-element.124.refs_5_), channel_id=1, source_target_pairs={{0,2},{1,3},{2,0},{3,1},{4,6},{5,7},{6,4},{7,5},{8,9},{9,8},{10,11... | collective-permute-start | bytes 98312 | tf_op jit(solution)/shard_map/ppermute | solution.py:31
  29.9 2.5 %collective-permute-start.11 = (bf16[2,2,16,512]{3,2,1,0:T(8,128)(2,1)S(1)}, bf16[2,2,16,512]{3,2,1,0:T(8,128)(2,1)S(1)}, u32[]{:S(2)}, u32[]{:S(2)}) collective-permute-start(bf16[2,2,16,512]{3,2,1,0:T(8,128)(2,1)S(1)} %pad_maximum_fusion.7.refs_0_), channel_id=1, source_target_pairs={{0,1},{1,0},{2,3},{3,2},{4,5},{5,4},{6,7},{7,6},{8,9},{9,8},{10,11... | collective-permute-start | bytes 196616 | tf_op jit(solution)/shard_map/ppermute | solution.py:31
  32.3 1.3 collective-permute-start.14
  34.1 4.1 %collective-permute-start.15 = (bf16[2,16,512]{2,1,0:T(8,128)(2,1)S(1)}, bf16[2,16,512]{2,1,0:T(8,128)(2,1)S(1)}, u32[]{:S(2)}, u32[]{:S(2)}) collective-permute-start(bf16[2,16,512]{2,1,0:T(8,128)(2,1)S(1)} %get-tuple-element.129.refs_7_), channel_id=1, source_target_pairs={{0,8},{1,9},{2,10},{3,11},{4,12},{5,13},{6,14},{7,15},{8,0},{9,1},... | collective-permute-start | bytes 98312 | tf_op jit(solution)/shard_map/ppermute | solution.py:79
  34.2 6.3 %collective-permute-start.16 = (bf16[2,16,512]{2,1,0:T(8,128)(2,1)S(1)}, bf16[2,16,512]{2,1,0:T(8,128)(2,1)S(1)}, u32[]{:S(2)}, u32[]{:S(2)}) collective-permute-start(bf16[2,16,512]{2,1,0:T(8,128)(2,1)S(1)} %get-tuple-element.129.refs_7_), channel_id=1, source_target_pairs={{0,14},{1,15},{2,12},{3,13},{4,10},{5,11},{6,8},{7,9},{8,6},{9,7},... | collective-permute-start | bytes 98312 | tf_op jit(solution)/shard_map/ppermute | solution.py:79
  38.3 4.0 %collective-permute-start.18 = (bf16[2,16,512]{2,1,0:T(8,128)(2,1)S(1)}, bf16[2,16,512]{2,1,0:T(8,128)(2,1)S(1)}, u32[]{:S(2)}, u32[]{:S(2)}) collective-permute-start(bf16[2,16,512]{2,1,0:T(8,128)(2,1)S(1)} %multiply_convert_fusion.11), channel_id=1, source_target_pairs={{0,4},{1,5},{2,6},{3,7},{4,0},{5,1},{6,2},{7,3},{8,12},{9,13},{10,... | collective-permute-start | bytes 98312 | tf_op jit(solution)/shard_map/ppermute | solution.py:31
  39.7 3.9 %collective-permute-start.19 = (bf16[2,16,512]{2,1,0:T(8,128)(2,1)S(1)}, bf16[2,16,512]{2,1,0:T(8,128)(2,1)S(1)}, u32[]{:S(2)}, u32[]{:S(2)}) collective-permute-start(bf16[2,16,512]{2,1,0:T(8,128)(2,1)S(1)} %multiply_convert_fusion.11), channel_id=1, source_target_pairs={{0,2},{1,3},{2,0},{3,1},{4,6},{5,7},{6,4},{7,5},{8,10},{9,11},{10,... | collective-permute-start | bytes 98312 | tf_op jit(solution)/shard_map/ppermute | solution.py:31
  40.5 3.2 %collective-permute-start.17 = (bf16[2,2,16,512]{3,2,1,0:T(8,128)(2,1)S(1)}, bf16[2,2,16,512]{3,2,1,0:T(8,128)(2,1)S(1)}, u32[]{:S(2)}, u32[]{:S(2)}) collective-permute-start(bf16[2,2,16,512]{3,2,1,0:T(8,128)(2,1)S(1)} %pad_maximum_fusion.9.refs_0_), channel_id=1, source_target_pairs={{0,1},{1,0},{2,3},{3,2},{4,5},{5,4},{6,7},{7,6},{8,9},{9,8},{10,11... | collective-permute-start | bytes 196616 | tf_op jit(solution)/shard_map/ppermute | solution.py:31
  43.6 1.3 collective-permute-start.20
  46.2 1.3 collective-permute-start.22
  46.7 1.3 collective-permute-start.25
  48.2 2.2 %collective-permute-start.27 = (bf16[2,16,512]{2,1,0:T(8,128)(2,1)S(1)}, bf16[2,16,512]{2,1,0:T(8,128)(2,1)S(1)}, u32[]{:S(2)}, u32[]{:S(2)}) collective-permute-start(bf16[2,16,512]{2,1,0:T(8,128)(2,1)S(1)} %get-tuple-element.140.refs_7_), channel_id=1, source_target_pairs={{0,1},{1,0},{2,3},{3,2},{4,5},{5,4},{6,7},{7,6},{8,22},{9,23},{10,... | collective-permute-start | bytes 98312 | tf_op jit(solution)/shard_map/ppermute | solution.py:79
  49.2 4.0 %collective-permute-start.29 = (bf16[2,16,512]{2,1,0:T(8,128)(2,1)S(1)}, bf16[2,16,512]{2,1,0:T(8,128)(2,1)S(1)}, u32[]{:S(2)}, u32[]{:S(2)}) collective-permute-start(bf16[2,16,512]{2,1,0:T(8,128)(2,1)S(1)} %multiply_convert_fusion.9), channel_id=1, source_target_pairs={{0,4},{1,5},{2,6},{3,7},{4,0},{5,1},{6,2},{7,3},{8,12},{9,13},{10,... | collective-permute-start | bytes 98312 | tf_op jit(solution)/shard_map/ppermute | solution.py:31
  49.9 3.9 %collective-permute-start.30 = (bf16[2,16,512]{2,1,0:T(8,128)(2,1)S(1)}, bf16[2,16,512]{2,1,0:T(8,128)(2,1)S(1)}, u32[]{:S(2)}, u32[]{:S(2)}) collective-permute-start(bf16[2,16,512]{2,1,0:T(8,128)(2,1)S(1)} %multiply_convert_fusion.9), channel_id=1, source_target_pairs={{0,2},{1,3},{2,0},{3,1},{4,6},{5,7},{6,4},{7,5},{8,10},{9,11},{10,... | collective-permute-start | bytes 98312 | tf_op jit(solution)/shard_map/ppermute | solution.py:31
  50.4 3.6 %collective-permute-start.28 = (bf16[2,2,16,512]{3,2,1,0:T(8,128)(2,1)S(1)}, bf16[2,2,16,512]{3,2,1,0:T(8,128)(2,1)S(1)}, u32[]{:S(2)}, u32[]{:S(2)}) collective-permute-start(bf16[2,2,16,512]{3,2,1,0:T(8,128)(2,1)S(1)} %pad_maximum_fusion.13.refs_0_), channel_id=1, source_target_pairs={{0,1},{1,0},{2,3},{3,2},{4,5},{5,4},{6,7},{7,6},{8,9},{9,8},{10,11... | collective-permute-start | bytes 196616 | tf_op jit(solution)/shard_map/ppermute | solution.py:31
  53.9 1.3 collective-permute-start.31
  55.2 4.8 %collective-permute-start.32 = (bf16[2,16,512]{2,1,0:T(8,128)(2,1)S(1)}, bf16[2,16,512]{2,1,0:T(8,128)(2,1)S(1)}, u32[]{:S(2)}, u32[]{:S(2)}) collective-permute-start(bf16[2,16,512]{2,1,0:T(8,128)(2,1)S(1)} %get-tuple-element.145.refs_5_), channel_id=1, source_target_pairs={{0,6},{1,7},{2,4},{3,5},{4,2},{5,3},{6,0},{7,1},{8,9},{9,8},{10,11... | collective-permute-start | bytes 98312 | tf_op jit(solution)/shard_map/ppermute | solution.py:31
  56.7 3.9 %collective-permute-start.34 = (bf16[2,16,512]{2,1,0:T(8,128)(2,1)S(1)}, bf16[2,16,512]{2,1,0:T(8,128)(2,1)S(1)}, u32[]{:S(2)}, u32[]{:S(2)}) collective-permute-start(bf16[2,16,512]{2,1,0:T(8,128)(2,1)S(1)} %get-tuple-element.145.refs_5_), channel_id=1, source_target_pairs={{0,4},{1,5},{2,6},{3,7},{4,0},{5,1},{6,2},{7,3},{8,9},{9,8},{10,11... | collective-permute-start | bytes 98312 | tf_op jit(solution)/shard_map/ppermute | solution.py:31
  57.0 3.9 %collective-permute-start.35 = (bf16[2,16,512]{2,1,0:T(8,128)(2,1)S(1)}, bf16[2,16,512]{2,1,0:T(8,128)(2,1)S(1)}, u32[]{:S(2)}, u32[]{:S(2)}) collective-permute-start(bf16[2,16,512]{2,1,0:T(8,128)(2,1)S(1)} %get-tuple-element.145.refs_5_), channel_id=1, source_target_pairs={{0,2},{1,3},{2,0},{3,1},{4,6},{5,7},{6,4},{7,5},{8,9},{9,8},{10,11... | collective-permute-start | bytes 98312 | tf_op jit(solution)/shard_map/ppermute | solution.py:31
  60.0 1.3 collective-permute-start.33
  61.0 1.3 collective-permute-start.36
  62.4 4.2 %collective-permute-start.38 = (bf16[2,16,512]{2,1,0:T(8,128)(2,1)S(1)}, bf16[2,16,512]{2,1,0:T(8,128)(2,1)S(1)}, u32[]{:S(2)}, u32[]{:S(2)}) collective-permute-start(bf16[2,16,512]{2,1,0:T(8,128)(2,1)S(1)} %get-tuple-element.150.refs_7_), channel_id=1, source_target_pairs={{0,1},{1,0},{2,3},{3,2},{4,5},{5,4},{6,7},{7,6},{8,9},{9,8},{10,11... | collective-permute-start | bytes 98312 | tf_op jit(solution)/shard_map/ppermute | solution.py:79
  63.5 4.0 %collective-permute-start.40 = (bf16[2,16,512]{2,1,0:T(8,128)(2,1)S(1)}, bf16[2,16,512]{2,1,0:T(8,128)(2,1)S(1)}, u32[]{:S(2)}, u32[]{:S(2)}) collective-permute-start(bf16[2,16,512]{2,1,0:T(8,128)(2,1)S(1)} %multiply_convert_fusion.7), channel_id=1, source_target_pairs={{0,4},{1,5},{2,6},{3,7},{4,0},{5,1},{6,2},{7,3},{8,12},{9,13},{10,... | collective-permute-start | bytes 98312 | tf_op jit(solution)/shard_map/ppermute | solution.py:31
  65.3 3.9 %collective-permute-start.41 = (bf16[2,16,512]{2,1,0:T(8,128)(2,1)S(1)}, bf16[2,16,512]{2,1,0:T(8,128)(2,1)S(1)}, u32[]{:S(2)}, u32[]{:S(2)}) collective-permute-start(bf16[2,16,512]{2,1,0:T(8,128)(2,1)S(1)} %multiply_convert_fusion.7), channel_id=1, source_target_pairs={{0,2},{1,3},{2,0},{3,1},{4,6},{5,7},{6,4},{7,5},{8,10},{9,11},{10,... | collective-permute-start | bytes 98312 | tf_op jit(solution)/shard_map/ppermute | solution.py:31
  66.6 2.7 %collective-permute-start.39 = (bf16[2,2,16,512]{3,2,1,0:T(8,128)(2,1)S(1)}, bf16[2,2,16,512]{3,2,1,0:T(8,128)(2,1)S(1)}, u32[]{:S(2)}, u32[]{:S(2)}) collective-permute-start(bf16[2,2,16,512]{3,2,1,0:T(8,128)(2,1)S(1)} %pad_maximum_fusion.17.refs_0_), channel_id=1, source_target_pairs={{0,1},{1,0},{2,3},{3,2},{4,5},{5,4},{6,7},{7,6},{8,9},{9,8},{10,11... | collective-permute-start | bytes 196616 | tf_op jit(solution)/shard_map/ppermute | solution.py:31
  69.2 1.3 collective-permute-start.42
  71.8 1.3 collective-permute-start.44
  72.3 1.3 collective-permute-start.47
  74.8 1.3 collective-permute-start.49
  76.8 3.1 %collective-permute-start.54 = (bf16[2,16,512]{2,1,0:T(8,128)(2,1)S(1)}, bf16[2,16,512]{2,1,0:T(8,128)(2,1)S(1)}, u32[]{:S(2)}, u32[]{:S(2)}) collective-permute-start(bf16[2,16,512]{2,1,0:T(8,128)(2,1)S(1)} %get-tuple-element.167.refs_6_), channel_id=1, source_target_pairs={{0,1},{1,0},{2,3},{3,2},{4,5},{5,4},{6,7},{7,6},{8,9},{9,8},{10,11... | collective-permute-start | bytes 98312 | tf_op jit(solution)/shard_map/ppermute | solution.py:79
  77.9 4.0 %collective-permute-start.56 = (bf16[2,16,512]{2,1,0:T(8,128)(2,1)S(1)}, bf16[2,16,512]{2,1,0:T(8,128)(2,1)S(1)}, u32[]{:S(2)}, u32[]{:S(2)}) collective-permute-start(bf16[2,16,512]{2,1,0:T(8,128)(2,1)S(1)} %multiply_convert_fusion.5), channel_id=1, source_target_pairs={{0,4},{1,5},{2,6},{3,7},{4,0},{5,1},{6,2},{7,3},{8,12},{9,13},{10,... | collective-permute-start | bytes 98312 | tf_op jit(solution)/shard_map/ppermute | solution.py:31
  78.2 3.9 %collective-permute-start.57 = (bf16[2,16,512]{2,1,0:T(8,128)(2,1)S(1)}, bf16[2,16,512]{2,1,0:T(8,128)(2,1)S(1)}, u32[]{:S(2)}, u32[]{:S(2)}) collective-permute-start(bf16[2,16,512]{2,1,0:T(8,128)(2,1)S(1)} %multiply_convert_fusion.5), channel_id=1, source_target_pairs={{0,2},{1,3},{2,0},{3,1},{4,6},{5,7},{6,4},{7,5},{8,10},{9,11},{10,... | collective-permute-start | bytes 98312 | tf_op jit(solution)/shard_map/ppermute | solution.py:31
  79.9 2.3 %collective-permute-start.55 = (bf16[2,2,16,512]{3,2,1,0:T(8,128)(2,1)S(1)}, bf16[2,2,16,512]{3,2,1,0:T(8,128)(2,1)S(1)}, u32[]{:S(2)}, u32[]{:S(2)}) collective-permute-start(bf16[2,2,16,512]{3,2,1,0:T(8,128)(2,1)S(1)} %pad_maximum_fusion.23.refs_0_), channel_id=1, source_target_pairs={{0,1},{1,0},{2,3},{3,2},{4,5},{5,4},{6,7},{7,6},{8,9},{9,8},{10,11... | collective-permute-start | bytes 196616 | tf_op jit(solution)/shard_map/ppermute | solution.py:31
  83.5 4.8 %collective-permute-start.59 = (bf16[2,16,512]{2,1,0:T(8,128)(2,1)S(1)}, bf16[2,16,512]{2,1,0:T(8,128)(2,1)S(1)}, u32[]{:S(2)}, u32[]{:S(2)}) collective-permute-start(bf16[2,16,512]{2,1,0:T(8,128)(2,1)S(1)} %get-tuple-element.173.refs_6_), channel_id=1, source_target_pairs={{0,6},{1,7},{2,4},{3,5},{4,2},{5,3},{6,0},{7,1},{8,9},{9,8},{10,11... | collective-permute-start | bytes 98312 | tf_op jit(solution)/shard_map/ppermute | solution.py:31
  85.9 3.9 %collective-permute-start.61 = (bf16[2,16,512]{2,1,0:T(8,128)(2,1)S(1)}, bf16[2,16,512]{2,1,0:T(8,128)(2,1)S(1)}, u32[]{:S(2)}, u32[]{:S(2)}) collective-permute-start(bf16[2,16,512]{2,1,0:T(8,128)(2,1)S(1)} %get-tuple-element.173.refs_6_), channel_id=1, source_target_pairs={{0,4},{1,5},{2,6},{3,7},{4,0},{5,1},{6,2},{7,3},{8,9},{9,8},{10,11... | collective-permute-start | bytes 98312 | tf_op jit(solution)/shard_map/ppermute | solution.py:31
  86.6 3.9 %collective-permute-start.62 = (bf16[2,16,512]{2,1,0:T(8,128)(2,1)S(1)}, bf16[2,16,512]{2,1,0:T(8,128)(2,1)S(1)}, u32[]{:S(2)}, u32[]{:S(2)}) collective-permute-start(bf16[2,16,512]{2,1,0:T(8,128)(2,1)S(1)} %get-tuple-element.173.refs_6_), channel_id=1, source_target_pairs={{0,2},{1,3},{2,0},{3,1},{4,6},{5,7},{6,4},{7,5},{8,9},{9,8},{10,11... | collective-permute-start | bytes 98312 | tf_op jit(solution)/shard_map/ppermute | solution.py:31
  88.3 2.3 %collective-permute-start.60 = (bf16[2,2,16,512]{3,2,1,0:T(8,128)(2,1)S(1)}, bf16[2,2,16,512]{3,2,1,0:T(8,128)(2,1)S(1)}, u32[]{:S(2)}, u32[]{:S(2)}) collective-permute-start(bf16[2,2,16,512]{3,2,1,0:T(8,128)(2,1)S(1)} %pad_maximum_fusion.25.refs_0_), channel_id=1, source_target_pairs={{0,1},{1,0},{2,3},{3,2},{4,5},{5,4},{6,7},{7,6},{8,9},{9,8},{10,11... | collective-permute-start | bytes 196616 | tf_op jit(solution)/shard_map/ppermute | solution.py:31
  92.0 3.3 %collective-permute-start.65 = (bf16[2,16,512]{2,1,0:T(8,128)(2,1)S(1)}, bf16[2,16,512]{2,1,0:T(8,128)(2,1)S(1)}, u32[]{:S(2)}, u32[]{:S(2)}) collective-permute-start(bf16[2,16,512]{2,1,0:T(8,128)(2,1)S(1)} %get-tuple-element.178.refs_6_), channel_id=1, source_target_pairs={{0,1},{1,0},{2,3},{3,2},{4,5},{5,4},{6,7},{7,6},{8,22},{9,23},{10,... | collective-permute-start | bytes 98312 | tf_op jit(solution)/shard_map/ppermute | solution.py:79
  93.1 4.0 %collective-permute-start.67 = (bf16[2,16,512]{2,1,0:T(8,128)(2,1)S(1)}, bf16[2,16,512]{2,1,0:T(8,128)(2,1)S(1)}, u32[]{:S(2)}, u32[]{:S(2)}) collective-permute-start(bf16[2,16,512]{2,1,0:T(8,128)(2,1)S(1)} %multiply_convert_fusion.3), channel_id=1, source_target_pairs={{0,4},{1,5},{2,6},{3,7},{4,0},{5,1},{6,2},{7,3},{8,12},{9,13},{10,... | collective-permute-start | bytes 98312 | tf_op jit(solution)/shard_map/ppermute | solution.py:31
  94.5 3.9 %collective-permute-start.68 = (bf16[2,16,512]{2,1,0:T(8,128)(2,1)S(1)}, bf16[2,16,512]{2,1,0:T(8,128)(2,1)S(1)}, u32[]{:S(2)}, u32[]{:S(2)}) collective-permute-start(bf16[2,16,512]{2,1,0:T(8,128)(2,1)S(1)} %multiply_convert_fusion.3), channel_id=1, source_target_pairs={{0,2},{1,3},{2,0},{3,1},{4,6},{5,7},{6,4},{7,5},{8,10},{9,11},{10,... | collective-permute-start | bytes 98312 | tf_op jit(solution)/shard_map/ppermute | solution.py:31
  95.3 3.2 %collective-permute-start.66 = (bf16[2,2,16,512]{3,2,1,0:T(8,128)(2,1)S(1)}, bf16[2,2,16,512]{3,2,1,0:T(8,128)(2,1)S(1)}, u32[]{:S(2)}, u32[]{:S(2)}) collective-permute-start(bf16[2,2,16,512]{3,2,1,0:T(8,128)(2,1)S(1)} %pad_maximum_fusion.27.refs_0_), channel_id=1, source_target_pairs={{0,1},{1,0},{2,3},{3,2},{4,5},{5,4},{6,7},{7,6},{8,9},{9,8},{10,11... | collective-permute-start | bytes 196616 | tf_op jit(solution)/shard_map/ppermute | solution.py:31
  102.8 33.6 %collective-permute-start.75 = (bf16[2,16,512]{2,1,0:T(8,128)(2,1)S(1)}, bf16[2,16,512]{2,1,0:T(8,128)(2,1)S(1)}, u32[]{:S(2)}, u32[]{:S(2)}) collective-permute-start(bf16[2,16,512]{2,1,0:T(8,128)(2,1)S(1)} %get-tuple-element.188.refs_6_), channel_id=1, source_target_pairs={{0,8},{1,9},{2,10},{3,11},{4,12},{5,13},{6,14},{7,15},{8,0},{9,1},... | collective-permute-start | bytes 98312 | tf_op jit(solution)/shard_map/ppermute | solution.py:79
  134.5 5.8 %collective-permute-start.76 = (bf16[2,16,512]{2,1,0:T(8,128)(2,1)S(1)}, bf16[2,16,512]{2,1,0:T(8,128)(2,1)S(1)}, u32[]{:S(2)}, u32[]{:S(2)}) collective-permute-start(bf16[2,16,512]{2,1,0:T(8,128)(2,1)S(1)} %get-tuple-element.188.refs_6_), channel_id=1, source_target_pairs={{0,14},{1,15},{2,12},{3,13},{4,10},{5,11},{6,8},{7,9},{8,6},{9,7},... | collective-permute-start | bytes 98312 | tf_op jit(solution)/shard_map/ppermute | solution.py:79
  136.4 4.4 %collective-permute-start.78 = (bf16[2,16,512]{2,1,0:T(8,128)(2,1)S(1)}, bf16[2,16,512]{2,1,0:T(8,128)(2,1)S(1)}, u32[]{:S(2)}, u32[]{:S(2)}) collective-permute-start(bf16[2,16,512]{2,1,0:T(8,128)(2,1)S(1)} %multiply_convert_fusion.1), channel_id=1, source_target_pairs={{0,4},{1,5},{2,6},{3,7},{4,0},{5,1},{6,2},{7,3},{8,12},{9,13},{10,... | collective-permute-start | bytes 98312 | tf_op jit(solution)/shard_map/ppermute | solution.py:31
  137.2 3.9 %collective-permute-start.79 = (bf16[2,16,512]{2,1,0:T(8,128)(2,1)S(1)}, bf16[2,16,512]{2,1,0:T(8,128)(2,1)S(1)}, u32[]{:S(2)}, u32[]{:S(2)}) collective-permute-start(bf16[2,16,512]{2,1,0:T(8,128)(2,1)S(1)} %multiply_convert_fusion.1), channel_id=1, source_target_pairs={{0,2},{1,3},{2,0},{3,1},{4,6},{5,7},{6,4},{7,5},{8,10},{9,11},{10,... | collective-permute-start | bytes 98312 | tf_op jit(solution)/shard_map/ppermute | solution.py:31
  142.9 4.9 %collective-permute-start.81 = (bf16[2,16,512]{2,1,0:T(8,128)(2,1)S(1)}, bf16[2,16,512]{2,1,0:T(8,128)(2,1)S(1)}, u32[]{:S(2)}, u32[]{:S(2)}) collective-permute-start(bf16[2,16,512]{2,1,0:T(8,128)(2,1)S(1)} %get-tuple-element.193), channel_id=1, source_target_pairs={{0,6},{1,7},{2,4},{3,5},{4,2},{5,3},{6,0},{7,1},{8,9},{9,8},{10,11... | collective-permute-start | bytes 98312 | tf_op jit(solution)/shard_map/ppermute | solution.py:31
  144.3 4.0 %collective-permute-start.83 = (bf16[2,16,512]{2,1,0:T(8,128)(2,1)S(1)}, bf16[2,16,512]{2,1,0:T(8,128)(2,1)S(1)}, u32[]{:S(2)}, u32[]{:S(2)}) collective-permute-start(bf16[2,16,512]{2,1,0:T(8,128)(2,1)S(1)} %get-tuple-element.193), channel_id=1, source_target_pairs={{0,4},{1,5},{2,6},{3,7},{4,0},{5,1},{6,2},{7,3},{8,9},{9,8},{10,11... | collective-permute-start | bytes 98312 | tf_op jit(solution)/shard_map/ppermute | solution.py:31
  145.1 3.9 %collective-permute-start.84 = (bf16[2,16,512]{2,1,0:T(8,128)(2,1)S(1)}, bf16[2,16,512]{2,1,0:T(8,128)(2,1)S(1)}, u32[]{:S(2)}, u32[]{:S(2)}) collective-permute-start(bf16[2,16,512]{2,1,0:T(8,128)(2,1)S(1)} %get-tuple-element.193), channel_id=1, source_target_pairs={{0,2},{1,3},{2,0},{3,1},{4,6},{5,7},{6,4},{7,5},{8,9},{9,8},{10,11... | collective-permute-start | bytes 98312 | tf_op jit(solution)/shard_map/ppermute | solution.py:31
  150.8 5.3 %collective-permute-start.86 = (bf16[2,2,16,512]{3,2,1,0:T(8,128)(2,1)S(1)}, bf16[2,2,16,512]{3,2,1,0:T(8,128)(2,1)S(1)}, u32[]{:S(2)}, u32[]{:S(2)}) collective-permute-start(bf16[2,2,16,512]{3,2,1,0:T(8,128)(2,1)S(1)} %get-tuple-element.199), channel_id=1, source_target_pairs={{0,6},{1,7},{2,4},{3,5},{4,2},{5,3},{6,0},{7,1},{8,14},{9,15},{10,... | collective-permute-start | bytes 196616 | tf_op jit(solution)/shard_map/ppermute | solution.py:31
  153.0 4.5 %collective-permute-start.88 = (bf16[2,2,16,512]{3,2,1,0:T(8,128)(2,1)S(1)}, bf16[2,2,16,512]{3,2,1,0:T(8,128)(2,1)S(1)}, u32[]{:S(2)}, u32[]{:S(2)}) collective-permute-start(bf16[2,2,16,512]{3,2,1,0:T(8,128)(2,1)S(1)} %get-tuple-element.199), channel_id=1, source_target_pairs={{0,4},{1,5},{2,6},{3,7},{4,0},{5,1},{6,2},{7,3},{8,12},{9,13},{10,... | collective-permute-start | bytes 196616 | tf_op jit(solution)/shard_map/ppermute | solution.py:31
  153.7 4.3 %collective-permute-start.89 = (bf16[2,2,16,512]{3,2,1,0:T(8,128)(2,1)S(1)}, bf16[2,2,16,512]{3,2,1,0:T(8,128)(2,1)S(1)}, u32[]{:S(2)}, u32[]{:S(2)}) collective-permute-start(bf16[2,2,16,512]{3,2,1,0:T(8,128)(2,1)S(1)} %get-tuple-element.199), channel_id=1, source_target_pairs={{0,2},{1,3},{2,0},{3,1},{4,6},{5,7},{6,4},{7,5},{8,10},{9,11},{10,... | collective-permute-start | bytes 196616 | tf_op jit(solution)/shard_map/ppermute | solution.py:31
  156.2 2.6 %collective-permute-start.87 = (bf16[2,2,2,16,512]{4,3,2,1,0:T(8,128)(2,1)S(1)}, bf16[2,2,2,16,512]{4,3,2,1,0:T(8,128)(2,1)S(1)}, u32[]{:S(2)}, u32[]{:S(2)}) collective-permute-start(bf16[2,2,2,16,512]{4,3,2,1,0:T(8,128)(2,1)S(1)} %pad_maximum_fusion.refs_0_), channel_id=1, source_target_pairs={{0,1},{1,0},{2,3},{3,2},{4,5},{5,4},{6,7},{7,6},{8,9},{9,8},{10,11... | collective-permute-start | bytes 393224 | tf_op jit(solution)/shard_map/ppermute | solution.py:31
  158.0 1.4 collective-permute-start.90
  (27 other events, 34.1 us)

commit v5 on v4

--- a/solution.py
+++ b/solution.py
@@ -36,11 +36,11 @@
     return masks[: peers // 4], masks[peers // 4 :]
 
 
-def in_parts(one, fetched, first, beside=()):
+def in_parts(one, fetched, first, beside=(), join=jnp.stack):
     pieces = [(one, swapped(one, 1))]
     made = first(one)
     fetched, made, beside = lax.optimization_barrier((fetched, made, beside))
-    two = jnp.stack(fetched)
+    two = join(fetched)
     pieces.append((two, swapped(two, 1)))
     return pieces, made, beside
 
@@ -53,10 +53,10 @@
     return in_parts(jnp.stack(one), two, first, beside)
 
 
-def sources_within(peers):
+def sources_by(parts):
     def sources(me):
         found = []
-        for masks in masks_within(peers):
+        for masks in parts:
             mine = [me ^ mask for mask in masks]
             found.append((mine, [peer ^ 1 for peer in mine]))
         return found
@@ -64,26 +64,35 @@
     return sources
 
 
-def crossed(message, low, own_scale, far_scale, first):
+def masks_across(peers):
+    masks = list(reversed(range(0, peers, 2)))
+    return masks[: peers // 4], masks[peers // 4 :]
+
+
+def crossed(message, low, by, scales, first):
     peers, groups = lax.axis_size("xy"), lax.axis_size("gz")
 
     def across(mask):
         pairs = []
         for group in range(groups):
+            lower = group if (group - low) % 2 == 0 else group - 1
+            joined = 0 <= lower and lower + 1 < groups
             for peer in range(peers):
-                if group in (low, low + 1):
-                    place = (2 * low + 1 - group) * peers + (peer ^ mask)
+                if mask == 0:
+                    place = (2 * lower + 1 - group) * peers + peer if joined else group * peers + (peer ^ 1)
+                elif joined and group == (lower if by > 0 else lower + 1):
+                    place = (group + by) * peers + (peer ^ mask)
                 else:
-                    place = group * peers + (peer ^ 1)
+                    continue
                 pairs.append((group * peers + peer, place))
         return lax.ppermute(message, ("gz", "xy"), pairs)
 
-    far, near = masks_within(peers)
-    own = (own_scale * across(0).astype(jnp.float32)).astype(jnp.bfloat16)
-    fetched = jnp.stack([across(mask) for mask in far[1:]])
-    fetched = (far_scale * fetched.astype(jnp.float32)).astype(jnp.bfloat16)
-    one = jnp.concatenate([own[None], fetched])
-    return in_parts(one, [swapped(own, mask) for mask in near], first)[:2]
+    def scaled(part, scale):
+        return (scale * jnp.stack(part).astype(jnp.float32)).astype(jnp.bfloat16)
+
+    one, two = [[across(mask) for mask in part] for part in masks_across(peers)]
+    join = functools.partial(scaled, scale=scales[1])
+    return in_parts(scaled(one, scales[0]), two, first, join=join)[:2]
 
 
 def gated(turn):
@@ -159,7 +168,7 @@
 
 def local_kernel(*refs):
     operands, size_in, (solved_ref, sent_ref), held = refs[:6], refs[6], refs[7:9], refs[9:15]
-    rows_out, (far_first, far_last), (sizes, tail_ref, sems) = refs[15:-5], refs[-5:-3], refs[-3:]
+    rows_out, met, (sizes, tail_ref, sems) = refs[15:-7], refs[-7:-3], refs[-3:]
     source_ref, inverse_ref, coupling_ref, rows_ref, link_ref, _ = held
     panel_count, _, side_count, _ = source_ref.shape
     bound, share = sent_ref.shape[1], link_ref.shape[1]
@@ -219,10 +228,11 @@
         rows_out[panel][...] = masks[panel]
         rows_out[panel_count + panel][...] = masks[panel] * link
         rows_out[2 * panel_count + panel][...] = link * masks[panel - 1] if panel else link
-    for index, mask in enumerate(masks_within(4 * (1 + far_first.shape[0]))[0][1:]):
-        start = (me ^ mask) * share
-        far_first[index, 0] = live(sizes, 0, start, share)
-        far_last[index, 0] = live(sizes, panel_count - 1, start, share)
+    for half, part in enumerate(masks_across(4 * met[0].shape[0])):
+        for index, mask in enumerate(part):
+            start = (me ^ mask) * share
+            met[half][index, 0] = live(sizes, 0, start, share)
+            met[2 + half][index, 0] = live(sizes, panel_count - 1, start, share)
 
 
 def tail_of(ref, place, first):
@@ -283,15 +293,20 @@
         copy.wait()
 
 
-def far_kernel(panel_count, side_count, mask_ref, far_ref, scale_ref):
-    share, bound = scale_ref.shape[3], far_ref.shape[2]
-    for index in range(scale_ref.shape[0]):
-        tail = tail_of(far_ref, 1 + index, 2 * side_count * panel_count)
-        for piece, place in enumerate(range(0, share, bound)):
-            columns = pl.ds(place, min(bound, share - place))
-            row = 2 * (panel_count + piece)
-            link = (tail[row : row + 1] + tail[row + 1 : row + 2])[:, : columns.size]
-            scale_ref[index, 0, :, columns] = mask_ref[index, 0, :, columns] * link
+def link_kernel(panel_count, side_count, one_mask, two_mask, one_ref, two_ref, one_out, two_out):
+    share, bound = one_out.shape[3], one_ref.shape[2]
+    peers = 4 * one_out.shape[0]
+    tails = {}
+    for ref, part in zip((one_ref, two_ref), masks_within(peers)):
+        for index, mask in enumerate(part):
+            tails[mask] = tail_of(ref, index, 2 * side_count * panel_count)
+    for mask_ref, out, part in zip((one_mask, two_mask), (one_out, two_out), masks_across(peers)):
+        for index, mask in enumerate(part):
+            for piece, place in enumerate(range(0, share, bound)):
+                columns = pl.ds(place, min(bound, share - place))
+                row = 2 * (panel_count + piece)
+                link = tails[mask][row : row + 1] + tails[mask][row + 1 : row + 2]
+                out[index, 0, :, columns] = mask_ref[index, 0, :, columns] * link[:, : columns.size]
 
 
 def part_products(ref, origins, schur_ref, products):
@@ -492,7 +507,7 @@
     sent_rows = 2 * side_count * panel_count + tail_rows
     taken = [source_inner, inner_inverse, coupling, front_rows, link, source_front]
     row = ((1, share), jnp.float32)
-    arriving = ((peers // 4 - 1, 1, 1, share), jnp.float32)
+    arriving = ((peers // 4, 1, 1, share), jnp.float32)
     solved, sent, _, inverse_held, coupling_held, rows_held, _, source_held, *scales = in_kernel(
         local_kernel,
         [
@@ -501,7 +516,7 @@
         ]
         + [(value.shape, value.dtype) for value in taken]
         + [row] * (3 * panel_count)
-        + [arriving] * 2,
+        + [arriving] * 4,
         [in_hbm(value) for value in taken + [front_size]],
         specs=[IN_HBM] * (len(taken) + 1),
         scratch=[
@@ -511,7 +526,7 @@
         ],
     )
     masks, forward_scales = scales[:panel_count], scales[panel_count : 2 * panel_count]
-    backward_scales, far_scales = scales[2 * panel_count : 3 * panel_count], scales[3 * panel_count :]
+    backward_scales, met = scales[2 * panel_count : 3 * panel_count], scales[3 * panel_count :]
 
     def push(panel, shards, contrib=None):
         operands = shards + ([] if contrib is None else [contrib])
@@ -547,31 +562,32 @@
         )
         bases.append(base)
         schurs.append(schur)
-    far_scales[0] = in_kernel(
-        functools.partial(far_kernel, panel_count, side_count),
-        [arriving],
-        [resident(far_scales[0]), resident(shards[0])],
-    )[0]
+    met[:2] = in_kernel(
+        functools.partial(link_kernel, panel_count, side_count),
+        [arriving] * 2,
+        [resident(value) for value in (met[0], met[1], shards[0], shards[2])],
+    )
 
     kept = [jnp.zeros((2, side_count, share), jnp.float32) for _ in range(panel_count)]
-    sources = sources_within(peers)
+    within, across = sources_by(masks_within(peers)), sources_by(masks_across(peers))
     order = [(turn, panel) for turn in range(groups) for panel in range(panel_count)]
     steps = [(None, 0, True)] + [step + (True,) for step in order[1:]]
     steps += [step + (False,) for step in reversed(order[:-1])]
     for count, (turn, panel, forward) in enumerate(steps):
         if forward and panel == 0 and turn is not None:
-            low, own_scale, far_scale = turn - 1, forward_scales[0], far_scales[0]
+            low, by, scales = turn - 1, 1, met[:2]
         elif not forward and panel == panel_count - 1:
-            low, own_scale, far_scale = turn, masks[panel], far_scales[1]
+            low, by, scales = turn, -1, met[2:]
         else:
             low = None
+        sources = within if low is None else across
         first = functools.partial(first_products, turn, sources, schurs[panel])
         if low is not None:
-            pieces, products = crossed(message, low, own_scale, far_scale, first)
+            pieces, products = crossed(message, low, by, scales, first)
         elif count == 0:
-            beside = (bases[1:], schurs[1:], far_scales)
+            beside = (bases[1:], schurs[1:], met)
             pieces, products, beside = gathered_within(message, None, first, beside)
-            bases[1:], schurs[1:], far_scales = beside
+            bases[1:], schurs[1:], met = beside
         else:
             pieces, products, _ = gathered_within(message, turn, first)
         scale = addend = None
@@ -592,7 +608,7 @@
 
     def pick(which, parts, *picked):
         return in_kernel(
-            functools.partial(pick_kernel, sources, which),
+            functools.partial(pick_kernel, within, which),
             [((panel_count, 2 * side_count, bound), jnp.float32)],
             [resident(value) for value in (*parts, rows_held, *picked)],
             moved=2**22,
@@ -603,7 +619,7 @@
     picked = pick([(0, 1), (1, 0)], [other, more], picked)
     operands = [picked, last, rows_held, coupling_held, inverse_held, solved]
     inner = pl.pallas_call(
-        functools.partial(inner_kernel, sources),
+        functools.partial(inner_kernel, within),
         out_shape=jax.ShapeDtypeStruct(solved.shape, jnp.float32),
         in_specs=[IN_VMEM] * len(operands),
         out_specs=IN_HBM,

time: 161 us -> 158 us (0.981)
  waiting for transfers between devices: 54.4 us -> 44.6 us
  starting transfers between devices: 82.3 us -> 88.6 us
    ppermute x12 -> x24, starting transfers between devices: 37.1 us -> 54.7 us  [across(): return lax.ppermute(message, ('gz', 'xy'), pairs)]
    ppermute x79 -> x67, waiting for transfers between devices: 46.6 us -> 31.7 us  [swapped(): return lax.ppermute(shard, ('gz', 'xy'), pairs)]
    ppermute x79 -> x67, starting transfers between devices: 45.2 us -> 34 us  [swapped(): return lax.ppermute(shard, ('gz', 'xy'), pairs)]
    ppermute x12 -> x24, waiting for transfers between devices: 7.81 us -> 12.9 us  [across(): return lax.ppermute(message, ('gz', 'xy'), pairs)]
  transfers between devices with their start and end apart: 91 -> 91, of which waited for: 63 -> 60; matrix products, arithmetic and copies ran while one was open for 1% -> 1% of each run, Pallas kernels for 9% -> 9%
where the time goes in v5:
time: 158 us
  starting transfers between devices  88.6 us (56%)
  waiting for transfers between devices  44.6 us (28%)
  Pallas kernels  21.8 us (14%)
  between operations  1.61 us (1%)
    ppermute x24, starting transfers between devices, across(): return lax.ppermute(message, ('gz', 'xy'), pairs)  54.7 us
    ppermute x67, starting transfers between devices, swapped(): return lax.ppermute(shard, ('gz', 'xy'), pairs)  34 us
    ppermute x67, waiting for transfers between devices, swapped(): return lax.ppermute(shard, ('gz', 'xy'), pairs)  31.7 us
    pallas_call x54, Pallas kernels, in_kernel(): pl.pallas_call(body, out_shape=tuple((pltpu.VMEM(shape, dtype) for shape,...  20.1 us
    ppermute x24, waiting for transfers between devices, across(): return lax.ppermute(message, ('gz', 'xy'), pairs)  12.9 us
  transfers between devices with their start and end apart: 91, of which 60 were waited for; matrix products, arithmetic and copies ran while one was open for 1% of the time, Pallas kernels for 9%

profile of v5, /device:TPU:0, one launch (start us, length us, event | category | flops | bytes accessed | tf_op | source)
XLA Modules:
  0.0 157.7 jit_solution(6558928273852669222)
XLA Ops:
  0.6 3.3 %shard_map.95 = (f32[2,2,16,512]{3,2,1,0:T(8,128)S(1)}, bf16[80,256]{1,0:T(8,128)(2,1)S(1)}, f32[2,2,16,512]{3,2,1,0:T(8,128)}, bf16[2,1,2,512,512]{4,3,2,1,0:T(...) custom-call(f32[2,2,16,512]{3,2,1,0:T(8,128)} %refs_0_.1, ...), custom_call_target="tpu_custom_call" | custom-call | tf_op jit(solution)/shard_map/pallas_call | solution.py:109
  3.9 4.0 %collective-permute-start = (bf16[80,256]{1,0:T(8,128)(2,1)S(1)}, bf16[80,256]{1,0:T(8,128)(2,1)S(1)}, u32[]{:S(2)}, u32[]{:S(2)}) collective-permute-start(bf16[80,256]{1,0:T(8,128)(2,1)S(1)} %get-tuple-element.111.after_ref), channel_id=1, source_target_pairs={{0,6},{1,7},{2,4},{3,5},{4,2},{5,3},{6,0},{7,1},{8,14},{9,15},{10,... | collective-permute-start | bytes 122888 | tf_op jit(solution)/shard_map/ppermute | solution.py:31
  8.5 3.5 %shard_map.97.refs_1_.refs_2_.schur_ref = bf16[2,4096,512]{2,1,0:T(8,128)(2,1)S(1)} custom-call(bf16[2,2,4096,512]{3,2,1,0:T(8,128)(2,1)} %refs_4_.3, bf16[80,256]{1,0:T(8,128)(2,1)S(1)} %get-tuple-element.111.after_ref), custom_call_target="tpu_custom_call" | custom-call | bytes 8388608 | tf_op jit(solution)/shard_map/pallas_call | solution.py:109
  12.9 0.7 collective-permute-done.1.refs_0_.refs_1_
  14.0 0.9 shard_map.99
  15.0 2.8 %collective-permute-start.7 = (bf16[2,16,512]{2,1,0:T(8,128)(2,1)S(1)}, bf16[2,16,512]{2,1,0:T(8,128)(2,1)S(1)}, u32[]{:S(2)}, u32[]{:S(2)}) collective-permute-start(bf16[2,16,512]{2,1,0:T(8,128)(2,1)S(1)} %get-tuple-element.116.refs_5_.refs_7_), channel_id=1, source_target_pairs={{0,6},{1,7},{2,4},{3,5},{4,2},{5,3},{6,0},{7,1},{8,14},{9,15},{10,... | collective-permute-start | bytes 98312 | tf_op jit(solution)/shard_map/ppermute | solution.py:31
  18.5 3.8 %shard_map.101 = (f32[2,16,512]{2,1,0:T(8,128)S(1)}, bf16[2,4096,512]{2,1,0:T(8,128)(2,1)S(1)}) custom-call(f32[1,512]{1,0:T(1,128)S(1)} %get-tuple-element.118.mask_ref.refs_3_, f32[2,2,16,512]{3,2,1,0:T(8,128)S(1)} %get-tuple-element.115.source_ref, bf16[2,80,256]{2,1,0:T(8,128)(2,1)S(1)} %pad_maximum_fusion.3.refs_0_.one_ref, ...), custom_call_target="tpu_custom_call" | custom-call | bytes 8388608 | tf_op jit(solution)/shard_map/pallas_call | solution.py:109
  23.7 0.8 shard_map.103.refs_0_
  25.0 2.9 %collective-permute-start.10 = (bf16[2,16,512]{2,1,0:T(8,128)(2,1)S(1)}, bf16[2,16,512]{2,1,0:T(8,128)(2,1)S(1)}, u32[]{:S(2)}, u32[]{:S(2)}) collective-permute-start(bf16[2,16,512]{2,1,0:T(8,128)(2,1)S(1)} %get-tuple-element.134.refs_5_), channel_id=1, source_target_pairs={{0,6},{1,7},{2,4},{3,5},{4,2},{5,3},{6,0},{7,1},{8,9},{9,8},{10,11... | collective-permute-start | bytes 98312 | tf_op jit(solution)/shard_map/ppermute | solution.py:31
  28.6 1.3 collective-permute-done.10
  30.4 1.4 collective-permute-done.12
  32.4 0.8 shard_map.106.refs_0_
  34.1 1.3 collective-permute-start.15
  35.4 1.3 collective-permute-start.16
  36.8 1.3 collective-permute-start.18
  38.4 1.2 collective-permute-done.18
  39.7 2.4 %collective-permute-done.19 = bf16[2,16,512]{2,1,0:T(8,128)(2,1)S(1)} collective-permute-done((bf16[2,16,512]{2,1,0:T(8,128)(2,1)S(1)}, bf16[2,16,512]{2,1,0:T(8,128)(2,1)S(1)}, u32[]{:S(2)}, u32[]{:S(2)}) %collective-permute-start.19) | collective-permute-done | bytes 32800 | tf_op jit(solution)/shard_map/ppermute | solution.py:88
  42.2 1.2 collective-permute-done.20.refs_1_
  46.4 0.7 collective-permute-start.26
  47.1 0.7 collective-permute-start.27
  47.8 0.7 collective-permute-start.29
  50.0 1.0 collective-permute-done.31.refs_1_
  51.1 1.5 collective-permute-start.32
  52.8 1.7 %collective-permute-start.35 = (bf16[2,16,512]{2,1,0:T(8,128)(2,1)S(1)}, bf16[2,16,512]{2,1,0:T(8,128)(2,1)S(1)}, u32[]{:S(2)}, u32[]{:S(2)}) collective-permute-start(bf16[2,16,512]{2,1,0:T(8,128)(2,1)S(1)} %get-tuple-element.155.refs_5_), channel_id=1, source_target_pairs={{0,2},{1,3},{2,0},{3,1},{4,6},{5,7},{6,4},{7,5},{8,9},{9,8},{10,11... | collective-permute-start | bytes 98312 | tf_op jit(solution)/shard_map/ppermute | solution.py:31
  54.5 1.3 collective-permute-done.32
  57.2 0.9 collective-permute-done.36.refs_1_
  58.1 10.1 %collective-permute-start.37 = (bf16[2,16,512]{2,1,0:T(8,128)(2,1)S(1)}, bf16[2,16,512]{2,1,0:T(8,128)(2,1)S(1)}, u32[]{:S(2)}, u32[]{:S(2)}) collective-permute-start(bf16[2,16,512]{2,1,0:T(8,128)(2,1)S(1)} %get-tuple-element.160.refs_7_), channel_id=1, source_target_pairs={{0,14},{1,15},{2,12},{3,13},{4,10},{5,11},{6,8},{7,9},{16,30},{17,... | collective-permute-start | bytes 98312 | tf_op jit(solution)/shard_map/ppermute | solution.py:88
  68.2 1.3 collective-permute-start.38
  69.5 1.3 collective-permute-start.40
  71.2 1.2 collective-permute-done.40
  72.3 2.4 %collective-permute-done.41 = bf16[2,16,512]{2,1,0:T(8,128)(2,1)S(1)} collective-permute-done((bf16[2,16,512]{2,1,0:T(8,128)(2,1)S(1)}, bf16[2,16,512]{2,1,0:T(8,128)(2,1)S(1)}, u32[]{:S(2)}, u32[]{:S(2)}) %collective-permute-start.41) | collective-permute-done | bytes 32800 | tf_op jit(solution)/shard_map/ppermute | solution.py:88
  74.9 1.2 collective-permute-done.42.refs_1_
  82.2 1.3 collective-permute-start.53
  83.5 1.3 collective-permute-start.54
  84.8 1.3 collective-permute-start.56
  86.1 9.9 %collective-permute-start.57 = (bf16[2,16,512]{2,1,0:T(8,128)(2,1)S(1)}, bf16[2,16,512]{2,1,0:T(8,128)(2,1)S(1)}, u32[]{:S(2)}, u32[]{:S(2)}) collective-permute-start(bf16[2,16,512]{2,1,0:T(8,128)(2,1)S(1)} %get-tuple-element.177.refs_6_), channel_id=1, source_target_pairs={{0,8},{1,9},{2,10},{3,11},{4,12},{5,13},{6,14},{7,15},{8,0},{9,1},... | collective-permute-start | bytes 98312 | tf_op jit(solution)/shard_map/ppermute | solution.py:88
  96.6 1.7 %collective-permute-done.56 = bf16[2,16,512]{2,1,0:T(8,128)(2,1)S(1)} collective-permute-done((bf16[2,16,512]{2,1,0:T(8,128)(2,1)S(1)}, bf16[2,16,512]{2,1,0:T(8,128)(2,1)S(1)}, u32[]{:S(2)}, u32[]{:S(2)}) %collective-permute-start.56) | collective-permute-done | bytes 32800 | tf_op jit(solution)/shard_map/ppermute | solution.py:88
  98.4 1.2 collective-permute-done.58.refs_1_
  99.6 1.1 collective-permute-start.59
  100.7 1.5 collective-permute-start.61
  102.2 0.9 collective-permute-start.62
  103.1 1.4 collective-permute-done.59
  104.8 1.3 collective-permute-done.62
  106.3 1.2 collective-permute-done.63.refs_1_
  107.5 0.7 collective-permute-start.64
  108.1 0.7 collective-permute-start.65
  108.8 0.7 collective-permute-start.67
  111.0 1.0 collective-permute-done.69.refs_1_
  115.1 1.3 collective-permute-start.75
  116.4 1.3 collective-permute-start.76
  117.7 1.3 collective-permute-start.78
  119.0 16.0 %collective-permute-start.79 = (bf16[2,16,512]{2,1,0:T(8,128)(2,1)S(1)}, bf16[2,16,512]{2,1,0:T(8,128)(2,1)S(1)}, u32[]{:S(2)}, u32[]{:S(2)}) collective-permute-start(bf16[2,16,512]{2,1,0:T(8,128)(2,1)S(1)} %get-tuple-element.198.refs_6_), channel_id=1, source_target_pairs={{0,8},{1,9},{2,10},{3,11},{4,12},{5,13},{6,14},{7,15},{8,0},{9,1},... | collective-permute-start | bytes 98312 | tf_op jit(solution)/shard_map/ppermute | solution.py:88
  135.0 0.8 collective-permute-done.75
  137.8 0.8 shard_map.142.refs_0_
  139.3 1.9 %collective-permute-start.81 = (bf16[2,16,512]{2,1,0:T(8,128)(2,1)S(1)}, bf16[2,16,512]{2,1,0:T(8,128)(2,1)S(1)}, u32[]{:S(2)}, u32[]{:S(2)}) collective-permute-start(bf16[2,16,512]{2,1,0:T(8,128)(2,1)S(1)} %get-tuple-element.203), channel_id=1, source_target_pairs={{0,6},{1,7},{2,4},{3,5},{4,2},{5,3},{6,0},{7,1},{8,9},{9,8},{10,11... | collective-permute-start | bytes 98312 | tf_op jit(solution)/shard_map/ppermute | solution.py:31
  141.8 1.1 collective-permute-start.84
  142.9 1.4 collective-permute-done.81
  145.8 0.8 shard_map.145.products_ref
  147.5 2.1 %collective-permute-start.86 = (bf16[2,2,16,512]{3,2,1,0:T(8,128)(2,1)S(1)}, bf16[2,2,16,512]{3,2,1,0:T(8,128)(2,1)S(1)}, u32[]{:S(2)}, u32[]{:S(2)}) collective-permute-start(bf16[2,2,16,512]{3,2,1,0:T(8,128)(2,1)S(1)} %get-tuple-element.209), channel_id=1, source_target_pairs={{0,6},{1,7},{2,4},{3,5},{4,2},{5,3},{6,0},{7,1},{8,14},{9,15},{10,... | collective-permute-start | bytes 196616 | tf_op jit(solution)/shard_map/ppermute | solution.py:31
  150.2 0.9 collective-permute-start.89
  151.1 1.7 %collective-permute-done.86 = bf16[2,2,16,512]{3,2,1,0:T(8,128)(2,1)S(1)} collective-permute-done((bf16[2,2,16,512]{3,2,1,0:T(8,128)(2,1)S(1)}, bf16[2,2,16,512]{3,2,1,0:T(8,128)(2,1)S(1)}, u32[]{:S(2)}, u32[]{:S(2)}) %collective-permute-start.86) | collective-permute-done | bytes 65568 | tf_op jit(solution)/shard_map/ppermute | solution.py:31
  153.2 0.9 collective-permute-done.88
  154.5 0.7 pad_maximum_fusion.2
  155.9 1.6 %shard_map.149 = f32[2,2,16,512]{3,2,1,0:T(8,128)} custom-call(f32[2,32,256]{2,1,0:T(8,128)S(1)} %shard_map.148.picked_ref, bf16[2,2,2,16,512]{4,3,2,1,0:T(8,128)(2,1)S(1)} %collective-permute-done.90.last_ref, s32[2,256]{1,0:T(2,128)S(1)} %get-tuple-element.210.refs_1_.refs_2_.rows_ref, bf16[2,1,2,512,256]{4,3,2,1,0:T(8,128)(2,1)S(1)} %get-tuple-element.214.coupling_ref, ...), custom_call_target="tpu_custom_call" | custom-call | tf_op jit(solution)/shard_map/pallas_call | solution.py:621
  (214 shorter events, 33.4 us)
Async XLA Ops:
  3.9 8.1 %collective-permute-start = (bf16[80,256]{1,0:T(8,128)(2,1)S(1)}, bf16[80,256]{1,0:T(8,128)(2,1)S(1)}, u32[]{:S(2)}, u32[]{:S(2)}) collective-permute-start(bf16[80,256]{1,0:T(8,128)(2,1)S(1)} %get-tuple-element.111.after_ref), channel_id=1, source_target_pairs={{0,6},{1,7},{2,4},{3,5},{4,2},{5,3},{6,0},{7,1},{8,14},{9,15},{10,... | collective-permute-start | bytes 122888 | tf_op jit(solution)/shard_map/ppermute | solution.py:31
  7.9 4.4 %collective-permute-start.2 = (bf16[80,256]{1,0:T(8,128)(2,1)S(1)}, bf16[80,256]{1,0:T(8,128)(2,1)S(1)}, u32[]{:S(2)}, u32[]{:S(2)}) collective-permute-start(bf16[80,256]{1,0:T(8,128)(2,1)S(1)} %get-tuple-element.111.after_ref), channel_id=1, source_target_pairs={{0,4},{1,5},{2,6},{3,7},{4,0},{5,1},{6,2},{7,3},{8,12},{9,13},{10,... | collective-permute-start | bytes 122888 | tf_op jit(solution)/shard_map/ppermute | solution.py:31
  8.4 4.0 %collective-permute-start.3 = (bf16[80,256]{1,0:T(8,128)(2,1)S(1)}, bf16[80,256]{1,0:T(8,128)(2,1)S(1)}, u32[]{:S(2)}, u32[]{:S(2)}) collective-permute-start(bf16[80,256]{1,0:T(8,128)(2,1)S(1)} %get-tuple-element.111.after_ref), channel_id=1, source_target_pairs={{0,2},{1,3},{2,0},{3,1},{4,6},{5,7},{6,4},{7,5},{8,10},{9,11},{10,... | collective-permute-start | bytes 122888 | tf_op jit(solution)/shard_map/ppermute | solution.py:31
  12.4 1.6 %collective-permute-start.4 = (bf16[2,80,256]{2,1,0:T(8,128)(2,1)S(1)}, bf16[2,80,256]{2,1,0:T(8,128)(2,1)S(1)}, u32[]{:S(2)}, u32[]{:S(2)}) collective-permute-start(bf16[2,80,256]{2,1,0:T(8,128)(2,1)S(1)} %pad_maximum_fusion.4.refs_1_.refs_2_.two_ref), channel_id=1, source_target_pairs={{0,1},{1,0},{2,3},{3,2},{4,5},{5,4},{6,7},{7,6},{8,9},{9,8},{10,11... | collective-permute-start | bytes 245768 | tf_op jit(solution)/shard_map/ppermute | solution.py:31
  15.0 7.4 %collective-permute-start.7 = (bf16[2,16,512]{2,1,0:T(8,128)(2,1)S(1)}, bf16[2,16,512]{2,1,0:T(8,128)(2,1)S(1)}, u32[]{:S(2)}, u32[]{:S(2)}) collective-permute-start(bf16[2,16,512]{2,1,0:T(8,128)(2,1)S(1)} %get-tuple-element.116.refs_5_.refs_7_), channel_id=1, source_target_pairs={{0,6},{1,7},{2,4},{3,5},{4,2},{5,3},{6,0},{7,1},{8,14},{9,15},{10,... | collective-permute-start | bytes 98312 | tf_op jit(solution)/shard_map/ppermute | solution.py:31
  17.8 5.1 %collective-permute-start.5 = (bf16[2,16,512]{2,1,0:T(8,128)(2,1)S(1)}, bf16[2,16,512]{2,1,0:T(8,128)(2,1)S(1)}, u32[]{:S(2)}, u32[]{:S(2)}) collective-permute-start(bf16[2,16,512]{2,1,0:T(8,128)(2,1)S(1)} %get-tuple-element.116.refs_5_.refs_7_), channel_id=1, source_target_pairs={{0,4},{1,5},{2,6},{3,7},{4,0},{5,1},{6,2},{7,3},{8,12},{9,13},{10,... | collective-permute-start | bytes 98312 | tf_op jit(solution)/shard_map/ppermute | solution.py:31
  18.4 4.5 %collective-permute-start.6 = (bf16[2,16,512]{2,1,0:T(8,128)(2,1)S(1)}, bf16[2,16,512]{2,1,0:T(8,128)(2,1)S(1)}, u32[]{:S(2)}, u32[]{:S(2)}) collective-permute-start(bf16[2,16,512]{2,1,0:T(8,128)(2,1)S(1)} %get-tuple-element.116.refs_5_.refs_7_), channel_id=1, source_target_pairs={{0,2},{1,3},{2,0},{3,1},{4,6},{5,7},{6,4},{7,5},{8,10},{9,11},{10,... | collective-permute-start | bytes 98312 | tf_op jit(solution)/shard_map/ppermute | solution.py:31
  22.3 1.3 collective-permute-start.8
  22.9 1.6 collective-permute-start.9
  25.0 4.9 %collective-permute-start.10 = (bf16[2,16,512]{2,1,0:T(8,128)(2,1)S(1)}, bf16[2,16,512]{2,1,0:T(8,128)(2,1)S(1)}, u32[]{:S(2)}, u32[]{:S(2)}) collective-permute-start(bf16[2,16,512]{2,1,0:T(8,128)(2,1)S(1)} %get-tuple-element.134.refs_5_), channel_id=1, source_target_pairs={{0,6},{1,7},{2,4},{3,5},{4,2},{5,3},{6,0},{7,1},{8,9},{9,8},{10,11... | collective-permute-start | bytes 98312 | tf_op jit(solution)/shard_map/ppermute | solution.py:31
  27.9 3.9 %collective-permute-start.12 = (bf16[2,16,512]{2,1,0:T(8,128)(2,1)S(1)}, bf16[2,16,512]{2,1,0:T(8,128)(2,1)S(1)}, u32[]{:S(2)}, u32[]{:S(2)}) collective-permute-start(bf16[2,16,512]{2,1,0:T(8,128)(2,1)S(1)} %get-tuple-element.134.refs_5_), channel_id=1, source_target_pairs={{0,4},{1,5},{2,6},{3,7},{4,0},{5,1},{6,2},{7,3},{8,9},{9,8},{10,11... | collective-permute-start | bytes 98312 | tf_op jit(solution)/shard_map/ppermute | solution.py:31
  28.4 3.9 %collective-permute-start.13 = (bf16[2,16,512]{2,1,0:T(8,128)(2,1)S(1)}, bf16[2,16,512]{2,1,0:T(8,128)(2,1)S(1)}, u32[]{:S(2)}, u32[]{:S(2)}) collective-permute-start(bf16[2,16,512]{2,1,0:T(8,128)(2,1)S(1)} %get-tuple-element.134.refs_5_), channel_id=1, source_target_pairs={{0,2},{1,3},{2,0},{3,1},{4,6},{5,7},{6,4},{7,5},{8,9},{9,8},{10,11... | collective-permute-start | bytes 98312 | tf_op jit(solution)/shard_map/ppermute | solution.py:31
  29.9 2.5 %collective-permute-start.11 = (bf16[2,2,16,512]{3,2,1,0:T(8,128)(2,1)S(1)}, bf16[2,2,16,512]{3,2,1,0:T(8,128)(2,1)S(1)}, u32[]{:S(2)}, u32[]{:S(2)}) collective-permute-start(bf16[2,2,16,512]{3,2,1,0:T(8,128)(2,1)S(1)} %pad_maximum_fusion.7.refs_0_), channel_id=1, source_target_pairs={{0,1},{1,0},{2,3},{3,2},{4,5},{5,4},{6,7},{7,6},{8,9},{9,8},{10,11... | collective-permute-start | bytes 196616 | tf_op jit(solution)/shard_map/ppermute | solution.py:31
  32.3 1.3 collective-permute-start.14
  34.1 4.0 %collective-permute-start.15 = (bf16[2,16,512]{2,1,0:T(8,128)(2,1)S(1)}, bf16[2,16,512]{2,1,0:T(8,128)(2,1)S(1)}, u32[]{:S(2)}, u32[]{:S(2)}) collective-permute-start(bf16[2,16,512]{2,1,0:T(8,128)(2,1)S(1)} %get-tuple-element.139.refs_7_), channel_id=1, source_target_pairs={{0,14},{1,15},{2,12},{3,13},{4,10},{5,11},{6,8},{7,9},{16,30},{17,... | collective-permute-start | bytes 98312 | tf_op jit(solution)/shard_map/ppermute | solution.py:88
  35.4 2.9 %collective-permute-start.16 = (bf16[2,16,512]{2,1,0:T(8,128)(2,1)S(1)}, bf16[2,16,512]{2,1,0:T(8,128)(2,1)S(1)}, u32[]{:S(2)}, u32[]{:S(2)}) collective-permute-start(bf16[2,16,512]{2,1,0:T(8,128)(2,1)S(1)} %get-tuple-element.139.refs_7_), channel_id=1, source_target_pairs={{0,12},{1,13},{2,14},{3,15},{4,8},{5,9},{6,10},{7,11},{16,28},{17,... | collective-permute-start | bytes 98312 | tf_op jit(solution)/shard_map/ppermute | solution.py:88
  36.8 2.9 %collective-permute-start.18 = (bf16[2,16,512]{2,1,0:T(8,128)(2,1)S(1)}, bf16[2,16,512]{2,1,0:T(8,128)(2,1)S(1)}, u32[]{:S(2)}, u32[]{:S(2)}) collective-permute-start(bf16[2,16,512]{2,1,0:T(8,128)(2,1)S(1)} %get-tuple-element.139.refs_7_), channel_id=1, source_target_pairs={{0,10},{1,11},{2,8},{3,9},{4,14},{5,15},{6,12},{7,13},{16,26},{17,... | collective-permute-start | bytes 98312 | tf_op jit(solution)/shard_map/ppermute | solution.py:88
  38.1 4.0 %collective-permute-start.19 = (bf16[2,16,512]{2,1,0:T(8,128)(2,1)S(1)}, bf16[2,16,512]{2,1,0:T(8,128)(2,1)S(1)}, u32[]{:S(2)}, u32[]{:S(2)}) collective-permute-start(bf16[2,16,512]{2,1,0:T(8,128)(2,1)S(1)} %get-tuple-element.139.refs_7_), channel_id=1, source_target_pairs={{0,8},{1,9},{2,10},{3,11},{4,12},{5,13},{6,14},{7,15},{8,0},{9,1},... | collective-permute-start | bytes 98312 | tf_op jit(solution)/shard_map/ppermute | solution.py:88
  38.3 3.8 %collective-permute-start.17 = (bf16[2,2,16,512]{3,2,1,0:T(8,128)(2,1)S(1)}, bf16[2,2,16,512]{3,2,1,0:T(8,128)(2,1)S(1)}, u32[]{:S(2)}, u32[]{:S(2)}) collective-permute-start(bf16[2,2,16,512]{3,2,1,0:T(8,128)(2,1)S(1)} %multiply_convert_fusion.11.refs_0_), channel_id=1, source_target_pairs={{0,1},{1,0},{2,3},{3,2},{4,5},{5,4},{6,7},{7,6},{8,9},{9,8},{10,11... | collective-permute-start | bytes 196616 | tf_op jit(solution)/shard_map/ppermute | solution.py:31
  42.1 1.3 collective-permute-start.20
  44.6 1.3 collective-permute-start.22
  45.1 1.3 collective-permute-start.25
  46.4 2.2 %collective-permute-start.26 = (bf16[2,16,512]{2,1,0:T(8,128)(2,1)S(1)}, bf16[2,16,512]{2,1,0:T(8,128)(2,1)S(1)}, u32[]{:S(2)}, u32[]{:S(2)}) collective-permute-start(bf16[2,16,512]{2,1,0:T(8,128)(2,1)S(1)} %get-tuple-element.150.refs_7_), channel_id=1, source_target_pairs={{8,22},{9,23},{10,20},{11,21},{12,18},{13,19},{14,16},{15,17}} | collective-permute-start | bytes 98312 | tf_op jit(solution)/shard_map/ppermute | solution.py:88
  47.1 1.6 collective-permute-start.27
  47.8 1.3 collective-permute-start.29
  48.7 1.3 collective-permute-start.28
  49.7 1.3 collective-permute-start.31
  51.1 4.8 %collective-permute-start.32 = (bf16[2,16,512]{2,1,0:T(8,128)(2,1)S(1)}, bf16[2,16,512]{2,1,0:T(8,128)(2,1)S(1)}, u32[]{:S(2)}, u32[]{:S(2)}) collective-permute-start(bf16[2,16,512]{2,1,0:T(8,128)(2,1)S(1)} %get-tuple-element.155.refs_5_), channel_id=1, source_target_pairs={{0,6},{1,7},{2,4},{3,5},{4,2},{5,3},{6,0},{7,1},{8,9},{9,8},{10,11... | collective-permute-start | bytes 98312 | tf_op jit(solution)/shard_map/ppermute | solution.py:31
  52.5 3.9 %collective-permute-start.34 = (bf16[2,16,512]{2,1,0:T(8,128)(2,1)S(1)}, bf16[2,16,512]{2,1,0:T(8,128)(2,1)S(1)}, u32[]{:S(2)}, u32[]{:S(2)}) collective-permute-start(bf16[2,16,512]{2,1,0:T(8,128)(2,1)S(1)} %get-tuple-element.155.refs_5_), channel_id=1, source_target_pairs={{0,4},{1,5},{2,6},{3,7},{4,0},{5,1},{6,2},{7,3},{8,9},{9,8},{10,11... | collective-permute-start | bytes 98312 | tf_op jit(solution)/shard_map/ppermute | solution.py:31
  52.8 3.9 %collective-permute-start.35 = (bf16[2,16,512]{2,1,0:T(8,128)(2,1)S(1)}, bf16[2,16,512]{2,1,0:T(8,128)(2,1)S(1)}, u32[]{:S(2)}, u32[]{:S(2)}) collective-permute-start(bf16[2,16,512]{2,1,0:T(8,128)(2,1)S(1)} %get-tuple-element.155.refs_5_), channel_id=1, source_target_pairs={{0,2},{1,3},{2,0},{3,1},{4,6},{5,7},{6,4},{7,5},{8,9},{9,8},{10,11... | collective-permute-start | bytes 98312 | tf_op jit(solution)/shard_map/ppermute | solution.py:31
  55.9 1.3 collective-permute-start.33
  56.7 1.3 collective-permute-start.36
  58.1 12.8 %collective-permute-start.37 = (bf16[2,16,512]{2,1,0:T(8,128)(2,1)S(1)}, bf16[2,16,512]{2,1,0:T(8,128)(2,1)S(1)}, u32[]{:S(2)}, u32[]{:S(2)}) collective-permute-start(bf16[2,16,512]{2,1,0:T(8,128)(2,1)S(1)} %get-tuple-element.160.refs_7_), channel_id=1, source_target_pairs={{0,14},{1,15},{2,12},{3,13},{4,10},{5,11},{6,8},{7,9},{16,30},{17,... | collective-permute-start | bytes 98312 | tf_op jit(solution)/shard_map/ppermute | solution.py:88
  68.2 2.9 %collective-permute-start.38 = (bf16[2,16,512]{2,1,0:T(8,128)(2,1)S(1)}, bf16[2,16,512]{2,1,0:T(8,128)(2,1)S(1)}, u32[]{:S(2)}, u32[]{:S(2)}) collective-permute-start(bf16[2,16,512]{2,1,0:T(8,128)(2,1)S(1)} %get-tuple-element.160.refs_7_), channel_id=1, source_target_pairs={{0,12},{1,13},{2,14},{3,15},{4,8},{5,9},{6,10},{7,11},{16,28},{17,... | collective-permute-start | bytes 98312 | tf_op jit(solution)/shard_map/ppermute | solution.py:88
  69.5 2.9 %collective-permute-start.40 = (bf16[2,16,512]{2,1,0:T(8,128)(2,1)S(1)}, bf16[2,16,512]{2,1,0:T(8,128)(2,1)S(1)}, u32[]{:S(2)}, u32[]{:S(2)}) collective-permute-start(bf16[2,16,512]{2,1,0:T(8,128)(2,1)S(1)} %get-tuple-element.160.refs_7_), channel_id=1, source_target_pairs={{0,10},{1,11},{2,8},{3,9},{4,14},{5,15},{6,12},{7,13},{16,26},{17,... | collective-permute-start | bytes 98312 | tf_op jit(solution)/shard_map/ppermute | solution.py:88
  70.8 4.0 %collective-permute-start.41 = (bf16[2,16,512]{2,1,0:T(8,128)(2,1)S(1)}, bf16[2,16,512]{2,1,0:T(8,128)(2,1)S(1)}, u32[]{:S(2)}, u32[]{:S(2)}) collective-permute-start(bf16[2,16,512]{2,1,0:T(8,128)(2,1)S(1)} %get-tuple-element.160.refs_7_), channel_id=1, source_target_pairs={{0,8},{1,9},{2,10},{3,11},{4,12},{5,13},{6,14},{7,15},{8,0},{9,1},... | collective-permute-start | bytes 98312 | tf_op jit(solution)/shard_map/ppermute | solution.py:88
  71.0 3.8 %collective-permute-start.39 = (bf16[2,2,16,512]{3,2,1,0:T(8,128)(2,1)S(1)}, bf16[2,2,16,512]{3,2,1,0:T(8,128)(2,1)S(1)}, u32[]{:S(2)}, u32[]{:S(2)}) collective-permute-start(bf16[2,2,16,512]{3,2,1,0:T(8,128)(2,1)S(1)} %multiply_convert_fusion.7.refs_0_), channel_id=1, source_target_pairs={{0,1},{1,0},{2,3},{3,2},{4,5},{5,4},{6,7},{7,6},{8,9},{9,8},{10,11... | collective-permute-start | bytes 196616 | tf_op jit(solution)/shard_map/ppermute | solution.py:31
  74.7 1.3 collective-permute-start.42
  82.2 13.8 %collective-permute-start.53 = (bf16[2,16,512]{2,1,0:T(8,128)(2,1)S(1)}, bf16[2,16,512]{2,1,0:T(8,128)(2,1)S(1)}, u32[]{:S(2)}, u32[]{:S(2)}) collective-permute-start(bf16[2,16,512]{2,1,0:T(8,128)(2,1)S(1)} %get-tuple-element.177.refs_6_), channel_id=1, source_target_pairs={{8,6},{9,7},{10,4},{11,5},{12,2},{13,3},{14,0},{15,1},{24,22},{25,... | collective-permute-start | bytes 98312 | tf_op jit(solution)/shard_map/ppermute | solution.py:88
  83.5 13.0 %collective-permute-start.54 = (bf16[2,16,512]{2,1,0:T(8,128)(2,1)S(1)}, bf16[2,16,512]{2,1,0:T(8,128)(2,1)S(1)}, u32[]{:S(2)}, u32[]{:S(2)}) collective-permute-start(bf16[2,16,512]{2,1,0:T(8,128)(2,1)S(1)} %get-tuple-element.177.refs_6_), channel_id=1, source_target_pairs={{8,4},{9,5},{10,6},{11,7},{12,0},{13,1},{14,2},{15,3},{24,20},{25,... | collective-permute-start | bytes 98312 | tf_op jit(solution)/shard_map/ppermute | solution.py:88
  84.8 13.5 %collective-permute-start.56 = (bf16[2,16,512]{2,1,0:T(8,128)(2,1)S(1)}, bf16[2,16,512]{2,1,0:T(8,128)(2,1)S(1)}, u32[]{:S(2)}, u32[]{:S(2)}) collective-permute-start(bf16[2,16,512]{2,1,0:T(8,128)(2,1)S(1)} %get-tuple-element.177.refs_6_), channel_id=1, source_target_pairs={{8,2},{9,3},{10,0},{11,1},{12,6},{13,7},{14,4},{15,5},{24,18},{25,... | collective-permute-start | bytes 98312 | tf_op jit(solution)/shard_map/ppermute | solution.py:88
  86.1 12.2 %collective-permute-start.57 = (bf16[2,16,512]{2,1,0:T(8,128)(2,1)S(1)}, bf16[2,16,512]{2,1,0:T(8,128)(2,1)S(1)}, u32[]{:S(2)}, u32[]{:S(2)}) collective-permute-start(bf16[2,16,512]{2,1,0:T(8,128)(2,1)S(1)} %get-tuple-element.177.refs_6_), channel_id=1, source_target_pairs={{0,8},{1,9},{2,10},{3,11},{4,12},{5,13},{6,14},{7,15},{8,0},{9,1},... | collective-permute-start | bytes 98312 | tf_op jit(solution)/shard_map/ppermute | solution.py:88
  96.5 1.9 %collective-permute-start.55 = (bf16[2,2,16,512]{3,2,1,0:T(8,128)(2,1)S(1)}, bf16[2,2,16,512]{3,2,1,0:T(8,128)(2,1)S(1)}, u32[]{:S(2)}, u32[]{:S(2)}) collective-permute-start(bf16[2,2,16,512]{3,2,1,0:T(8,128)(2,1)S(1)} %multiply_convert_fusion.5.refs_0_), channel_id=1, source_target_pairs={{0,1},{1,0},{2,3},{3,2},{4,5},{5,4},{6,7},{7,6},{8,9},{9,8},{10,11... | collective-permute-start | bytes 196616 | tf_op jit(solution)/shard_map/ppermute | solution.py:31
  99.6 4.9 %collective-permute-start.59 = (bf16[2,16,512]{2,1,0:T(8,128)(2,1)S(1)}, bf16[2,16,512]{2,1,0:T(8,128)(2,1)S(1)}, u32[]{:S(2)}, u32[]{:S(2)}) collective-permute-start(bf16[2,16,512]{2,1,0:T(8,128)(2,1)S(1)} %get-tuple-element.183.refs_6_), channel_id=1, source_target_pairs={{0,6},{1,7},{2,4},{3,5},{4,2},{5,3},{6,0},{7,1},{8,9},{9,8},{10,11... | collective-permute-start | bytes 98312 | tf_op jit(solution)/shard_map/ppermute | solution.py:31
  100.7 4.0 %collective-permute-start.61 = (bf16[2,16,512]{2,1,0:T(8,128)(2,1)S(1)}, bf16[2,16,512]{2,1,0:T(8,128)(2,1)S(1)}, u32[]{:S(2)}, u32[]{:S(2)}) collective-permute-start(bf16[2,16,512]{2,1,0:T(8,128)(2,1)S(1)} %get-tuple-element.183.refs_6_), channel_id=1, source_target_pairs={{0,4},{1,5},{2,6},{3,7},{4,0},{5,1},{6,2},{7,3},{8,9},{9,8},{10,11... | collective-permute-start | bytes 98312 | tf_op jit(solution)/shard_map/ppermute | solution.py:31
  102.2 3.9 %collective-permute-start.62 = (bf16[2,16,512]{2,1,0:T(8,128)(2,1)S(1)}, bf16[2,16,512]{2,1,0:T(8,128)(2,1)S(1)}, u32[]{:S(2)}, u32[]{:S(2)}) collective-permute-start(bf16[2,16,512]{2,1,0:T(8,128)(2,1)S(1)} %get-tuple-element.183.refs_6_), channel_id=1, source_target_pairs={{0,2},{1,3},{2,0},{3,1},{4,6},{5,7},{6,4},{7,5},{8,9},{9,8},{10,11... | collective-permute-start | bytes 98312 | tf_op jit(solution)/shard_map/ppermute | solution.py:31
  104.5 1.7 %collective-permute-start.60 = (bf16[2,2,16,512]{3,2,1,0:T(8,128)(2,1)S(1)}, bf16[2,2,16,512]{3,2,1,0:T(8,128)(2,1)S(1)}, u32[]{:S(2)}, u32[]{:S(2)}) collective-permute-start(bf16[2,2,16,512]{3,2,1,0:T(8,128)(2,1)S(1)} %pad_maximum_fusion.17.refs_0_), channel_id=1, source_target_pairs={{0,1},{1,0},{2,3},{3,2},{4,5},{5,4},{6,7},{7,6},{8,9},{9,8},{10,11... | collective-permute-start | bytes 196616 | tf_op jit(solution)/shard_map/ppermute | solution.py:31
  107.5 2.2 %collective-permute-start.64 = (bf16[2,16,512]{2,1,0:T(8,128)(2,1)S(1)}, bf16[2,16,512]{2,1,0:T(8,128)(2,1)S(1)}, u32[]{:S(2)}, u32[]{:S(2)}) collective-permute-start(bf16[2,16,512]{2,1,0:T(8,128)(2,1)S(1)} %get-tuple-element.188.refs_6_), channel_id=1, source_target_pairs={{16,14},{17,15},{18,12},{19,13},{20,10},{21,11},{22,8},{23,9}} | collective-permute-start | bytes 98312 | tf_op jit(solution)/shard_map/ppermute | solution.py:88
  108.1 1.6 collective-permute-start.65
  108.8 1.3 collective-permute-start.67
  109.7 1.3 collective-permute-start.66
  115.1 20.7 %collective-permute-start.75 = (bf16[2,16,512]{2,1,0:T(8,128)(2,1)S(1)}, bf16[2,16,512]{2,1,0:T(8,128)(2,1)S(1)}, u32[]{:S(2)}, u32[]{:S(2)}) collective-permute-start(bf16[2,16,512]{2,1,0:T(8,128)(2,1)S(1)} %get-tuple-element.198.refs_6_), channel_id=1, source_target_pairs={{8,6},{9,7},{10,4},{11,5},{12,2},{13,3},{14,0},{15,1},{24,22},{25,... | collective-permute-start | bytes 98312 | tf_op jit(solution)/shard_map/ppermute | solution.py:88
  116.4 20.0 %collective-permute-start.76 = (bf16[2,16,512]{2,1,0:T(8,128)(2,1)S(1)}, bf16[2,16,512]{2,1,0:T(8,128)(2,1)S(1)}, u32[]{:S(2)}, u32[]{:S(2)}) collective-permute-start(bf16[2,16,512]{2,1,0:T(8,128)(2,1)S(1)} %get-tuple-element.198.refs_6_), channel_id=1, source_target_pairs={{8,4},{9,5},{10,6},{11,7},{12,0},{13,1},{14,2},{15,3},{24,20},{25,... | collective-permute-start | bytes 98312 | tf_op jit(solution)/shard_map/ppermute | solution.py:88
  117.7 19.8 %collective-permute-start.78 = (bf16[2,16,512]{2,1,0:T(8,128)(2,1)S(1)}, bf16[2,16,512]{2,1,0:T(8,128)(2,1)S(1)}, u32[]{:S(2)}, u32[]{:S(2)}) collective-permute-start(bf16[2,16,512]{2,1,0:T(8,128)(2,1)S(1)} %get-tuple-element.198.refs_6_), channel_id=1, source_target_pairs={{8,2},{9,3},{10,0},{11,1},{12,6},{13,7},{14,4},{15,5},{24,18},{25,... | collective-permute-start | bytes 98312 | tf_op jit(solution)/shard_map/ppermute | solution.py:88
  119.0 18.5 %collective-permute-start.79 = (bf16[2,16,512]{2,1,0:T(8,128)(2,1)S(1)}, bf16[2,16,512]{2,1,0:T(8,128)(2,1)S(1)}, u32[]{:S(2)}, u32[]{:S(2)}) collective-permute-start(bf16[2,16,512]{2,1,0:T(8,128)(2,1)S(1)} %get-tuple-element.198.refs_6_), channel_id=1, source_target_pairs={{0,8},{1,9},{2,10},{3,11},{4,12},{5,13},{6,14},{7,15},{8,0},{9,1},... | collective-permute-start | bytes 98312 | tf_op jit(solution)/shard_map/ppermute | solution.py:88
  139.3 5.0 %collective-permute-start.81 = (bf16[2,16,512]{2,1,0:T(8,128)(2,1)S(1)}, bf16[2,16,512]{2,1,0:T(8,128)(2,1)S(1)}, u32[]{:S(2)}, u32[]{:S(2)}) collective-permute-start(bf16[2,16,512]{2,1,0:T(8,128)(2,1)S(1)} %get-tuple-element.203), channel_id=1, source_target_pairs={{0,6},{1,7},{2,4},{3,5},{4,2},{5,3},{6,0},{7,1},{8,9},{9,8},{10,11... | collective-permute-start | bytes 98312 | tf_op jit(solution)/shard_map/ppermute | solution.py:31
  141.3 3.9 %collective-permute-start.83 = (bf16[2,16,512]{2,1,0:T(8,128)(2,1)S(1)}, bf16[2,16,512]{2,1,0:T(8,128)(2,1)S(1)}, u32[]{:S(2)}, u32[]{:S(2)}) collective-permute-start(bf16[2,16,512]{2,1,0:T(8,128)(2,1)S(1)} %get-tuple-element.203), channel_id=1, source_target_pairs={{0,4},{1,5},{2,6},{3,7},{4,0},{5,1},{6,2},{7,3},{8,9},{9,8},{10,11... | collective-permute-start | bytes 98312 | tf_op jit(solution)/shard_map/ppermute | solution.py:31
  141.8 3.9 %collective-permute-start.84 = (bf16[2,16,512]{2,1,0:T(8,128)(2,1)S(1)}, bf16[2,16,512]{2,1,0:T(8,128)(2,1)S(1)}, u32[]{:S(2)}, u32[]{:S(2)}) collective-permute-start(bf16[2,16,512]{2,1,0:T(8,128)(2,1)S(1)} %get-tuple-element.203), channel_id=1, source_target_pairs={{0,2},{1,3},{2,0},{3,1},{4,6},{5,7},{6,4},{7,5},{8,9},{9,8},{10,11... | collective-permute-start | bytes 98312 | tf_op jit(solution)/shard_map/ppermute | solution.py:31
  144.3 1.5 collective-permute-start.82
  147.5 5.3 %collective-permute-start.86 = (bf16[2,2,16,512]{3,2,1,0:T(8,128)(2,1)S(1)}, bf16[2,2,16,512]{3,2,1,0:T(8,128)(2,1)S(1)}, u32[]{:S(2)}, u32[]{:S(2)}) collective-permute-start(bf16[2,2,16,512]{3,2,1,0:T(8,128)(2,1)S(1)} %get-tuple-element.209), channel_id=1, source_target_pairs={{0,6},{1,7},{2,4},{3,5},{4,2},{5,3},{6,0},{7,1},{8,14},{9,15},{10,... | collective-permute-start | bytes 196616 | tf_op jit(solution)/shard_map/ppermute | solution.py:31
  149.7 4.5 %collective-permute-start.88 = (bf16[2,2,16,512]{3,2,1,0:T(8,128)(2,1)S(1)}, bf16[2,2,16,512]{3,2,1,0:T(8,128)(2,1)S(1)}, u32[]{:S(2)}, u32[]{:S(2)}) collective-permute-start(bf16[2,2,16,512]{3,2,1,0:T(8,128)(2,1)S(1)} %get-tuple-element.209), channel_id=1, source_target_pairs={{0,4},{1,5},{2,6},{3,7},{4,0},{5,1},{6,2},{7,3},{8,12},{9,13},{10,... | collective-permute-start | bytes 196616 | tf_op jit(solution)/shard_map/ppermute | solution.py:31
  150.2 4.3 %collective-permute-start.89 = (bf16[2,2,16,512]{3,2,1,0:T(8,128)(2,1)S(1)}, bf16[2,2,16,512]{3,2,1,0:T(8,128)(2,1)S(1)}, u32[]{:S(2)}, u32[]{:S(2)}) collective-permute-start(bf16[2,2,16,512]{3,2,1,0:T(8,128)(2,1)S(1)} %get-tuple-element.209), channel_id=1, source_target_pairs={{0,2},{1,3},{2,0},{3,1},{4,6},{5,7},{6,4},{7,5},{8,10},{9,11},{10,... | collective-permute-start | bytes 196616 | tf_op jit(solution)/shard_map/ppermute | solution.py:31
  152.8 2.4 %collective-permute-start.87 = (bf16[2,2,2,16,512]{4,3,2,1,0:T(8,128)(2,1)S(1)}, bf16[2,2,2,16,512]{4,3,2,1,0:T(8,128)(2,1)S(1)}, u32[]{:S(2)}, u32[]{:S(2)}) collective-permute-start(bf16[2,2,2,16,512]{4,3,2,1,0:T(8,128)(2,1)S(1)} %pad_maximum_fusion.refs_0_), channel_id=1, source_target_pairs={{0,1},{1,0},{2,3},{3,2},{4,5},{5,4},{6,7},{7,6},{8,9},{9,8},{10,11... | collective-permute-start | bytes 393224 | tf_op jit(solution)/shard_map/ppermute | solution.py:31
  154.4 1.4 collective-permute-start.90
  (27 other events, 34.5 us)

commit v6 on v5

--- a/solution.py
+++ b/solution.py
@@ -172,39 +172,35 @@
     source_ref, inverse_ref, coupling_ref, rows_ref, link_ref, _ = held
     panel_count, _, side_count, _ = source_ref.shape
     bound, share = sent_ref.shape[1], link_ref.shape[1]
-    copies = []
-    for index, (operand, place) in enumerate(zip(operands, held)):
-        for panel in range(panel_count):
-            copies.append(
-                pltpu.make_async_copy(
-                    operand.at[panel], place.at[panel], sems.at[index * panel_count + panel]
-                )
-            )
-    by_operand = [copies[i * panel_count : (i + 1) * panel_count] for i in range(len(operands))]
-    size_copy = pltpu.make_async_copy(size_in, sizes, sems.at[len(copies)])
-    size_copy.start()
+    ends = []
     for panel in range(panel_count):
-        for index in range(3):
-            by_operand[index][panel].start()
-    for group in by_operand[3:]:
-        for copy in group:
-            copy.start()
+        ends.append((operands[0].at[panel], held[0].at[panel]))
+        for operand, place in zip(operands[1:3], held[1:3]):
+            for part in range(2):
+                ends.append((operand.at[panel, 0, part], place.at[panel, 0, part]))
+    ends += list(zip(operands[3:], held[3:])) + [(size_in, sizes)]
+    copies = [
+        pltpu.make_async_copy(operand, place, sems.at[index])
+        for index, (operand, place) in enumerate(ends)
+    ]
+    for copy in copies:
+        copy.start()
     for panel in range(panel_count):
-        by_operand[0][panel].wait()
-        by_operand[1][panel].wait()
+        for copy in copies[5 * panel : 5 * panel + 3]:
+            copy.wait()
         field = source_ref[panel].astype(jnp.bfloat16).reshape(2 * side_count, -1)
         solved = combined(real_products(field, inverse_ref.at[panel, 0]))
         for part in range(2):
             solved_ref[panel, part] = solved[part]
         field = jnp.concatenate(solved).astype(jnp.bfloat16)
-        by_operand[2][panel].wait()
+        for copy in copies[5 * panel + 3 : 5 * panel + 5]:
+            copy.wait()
         pushed = combined(real_products(field, coupling_ref.at[panel, 0]))
         for part in range(2):
             start = (2 * panel + part) * side_count
             sent_ref[pl.ds(start, side_count), :] = pushed[part].astype(jnp.bfloat16)
-    for group in by_operand[3:]:
-        for copy in group:
-            copy.wait()
+    for copy in copies[5 * panel_count :]:
+        copy.wait()
     tail_ref[...] = jnp.zeros(tail_ref.shape, jnp.float32)
     for panel in range(panel_count):
         rows = rows_ref[pl.ds(panel, 1), :]
@@ -220,7 +216,6 @@
         row += 2
     first = 2 * side_count * panel_count
     sent_ref[pl.ds(first, tail_ref.shape[0]), :] = tail_ref[...].astype(jnp.bfloat16)
-    size_copy.wait()
     me = lax.axis_index("xy")
     masks = [live(sizes, panel, me * share, share) for panel in range(panel_count)]
     for panel in range(panel_count):
@@ -460,12 +455,30 @@
     return found
 
 
+def first_pick_kernel(sources, mine_ref, rows_ref, picked_ref, chosen_ref):
+    (origins, _), (_, lasts) = sources(lax.axis_index("xy"))
+    for panel, value in enumerate(picks(mine_ref, rows_ref, origins, None)):
+        picked_ref[panel] = value
+    panel_count, _, share, bound = chosen_ref.shape
+    for panel in range(panel_count):
+        for index, origin in enumerate(lasts):
+            rows = origin * share + lax.broadcasted_iota(jnp.int32, (share, bound), 0)
+            hits = jnp.where(rows == rows_ref[pl.ds(panel, 1), :], 1.0, 0.0)
+            chosen_ref[panel, index] = hits.astype(jnp.bfloat16)
+
+
 def inner_kernel(
-    sources, picked_ref, last_ref, rows_ref, coupling_ref, inverse_ref, solved_ref, out_ref, inner_ref, sems
+    picked_ref, last_ref, chosen_ref, coupling_ref, inverse_ref, solved_ref, out_ref, inner_ref, sems
 ):
     contract = (((1,), (1,)), ((), ()))
-    origins = sources(lax.axis_index("xy"))[-1][1]
-    picked = picks(last_ref, rows_ref, origins, [picked_ref[p] for p in range(picked_ref.shape[0])])
+    _, panel_count, _, side_count, share = last_ref.shape
+    picked = []
+    for panel in range(panel_count):
+        total = picked_ref[panel]
+        for place in range(last_ref.shape[0]):
+            field = last_ref[place, panel].reshape(2 * side_count, share)
+            total += jnp.dot(field, chosen_ref[panel, place], preferred_element_type=jnp.float32)
+        picked.append(total)
     lifted = [
         combined(
             [
@@ -522,7 +535,7 @@
         scratch=[
             pltpu.SMEM(front_size.shape, jnp.int32),
             pltpu.VMEM((tail_rows, bound), jnp.float32),
-            pltpu.SemaphoreType.DMA((len(taken) * panel_count + 1,)),
+            pltpu.SemaphoreType.DMA((5 * panel_count + 4,)),
         ],
     )
     masks, forward_scales = scales[:panel_count], scales[panel_count : 2 * panel_count]
@@ -534,7 +547,6 @@
             functools.partial(push_kernel, panel, panel_count, len(shards)),
             [((2 * side_count, share), jnp.float32)],
             [resident(value) for value in operands],
-            moved=2**22,
         )[0]
 
     shards, contrib, schurs = gathered_within(
@@ -614,12 +626,23 @@
             moved=2**22,
         )[0]
 
-    pieces, picked, _ = gathered_within(message, None, lambda mine: pick([(0, 0)], [mine]))
+    def first_pick(mine):
+        return in_kernel(
+            functools.partial(first_pick_kernel, within),
+            [
+                ((panel_count, 2 * side_count, bound), jnp.float32),
+                ((panel_count, peers // 2 - mine.shape[0], share, bound), jnp.bfloat16),
+            ],
+            [resident(mine), resident(rows_held)],
+            moved=2**22,
+        )
+
+    pieces, (picked, chosen), _ = gathered_within(message, None, first_pick)
     (_, other), (more, last) = pieces
     picked = pick([(0, 1), (1, 0)], [other, more], picked)
-    operands = [picked, last, rows_held, coupling_held, inverse_held, solved]
+    operands = [picked, last, chosen, coupling_held, inverse_held, solved]
     inner = pl.pallas_call(
-        functools.partial(inner_kernel, within),
+        inner_kernel,
         out_shape=jax.ShapeDtypeStruct(solved.shape, jnp.float32),
         in_specs=[IN_VMEM] * len(operands),
         out_specs=IN_HBM,

time: 158 us -> 158 us (level)
  no operation moved by 1% of the time
where the time goes in v6:
time: 158 us
  starting transfers between devices  88.7 us (56%)
  waiting for transfers between devices  44.4 us (28%)
  Pallas kernels  21.9 us (14%)
  between operations  1.6 us (1%)
    ppermute x24, starting transfers between devices, across(): return lax.ppermute(message, ('gz', 'xy'), pairs)  54.7 us
    ppermute x67, starting transfers between devices, swapped(): return lax.ppermute(shard, ('gz', 'xy'), pairs)  34 us
    ppermute x67, waiting for transfers between devices, swapped(): return lax.ppermute(shard, ('gz', 'xy'), pairs)  31.5 us
    pallas_call x54, Pallas kernels, in_kernel(): pl.pallas_call(body, out_shape=tuple((pltpu.VMEM(shape, dtype) for shape,...  20.2 us
    ppermute x24, waiting for transfers between devices, across(): return lax.ppermute(message, ('gz', 'xy'), pairs)  12.9 us
  transfers between devices with their start and end apart: 91, of which 60 were waited for; matrix products, arithmetic and copies ran while one was open for 1% of the time, Pallas kernels for 9%

profile of v6, /device:TPU:0, one launch (start us, length us, event | category | flops | bytes accessed | tf_op | source)
XLA Modules:
  0.0 157.6 jit_solution(14270526875177645068)
XLA Ops:
  0.6 3.3 %shard_map.95 = (f32[2,2,16,512]{3,2,1,0:T(8,128)S(1)}, bf16[80,256]{1,0:T(8,128)(2,1)S(1)}, f32[2,2,16,512]{3,2,1,0:T(8,128)}, bf16[2,1,2,512,512]{4,3,2,1,0:T(...) custom-call(f32[2,2,16,512]{3,2,1,0:T(8,128)} %refs_0_.1, ...), custom_call_target="tpu_custom_call" | custom-call | tf_op jit(solution)/shard_map/pallas_call | solution.py:109
  3.9 4.0 %collective-permute-start = (bf16[80,256]{1,0:T(8,128)(2,1)S(1)}, bf16[80,256]{1,0:T(8,128)(2,1)S(1)}, u32[]{:S(2)}, u32[]{:S(2)}) collective-permute-start(bf16[80,256]{1,0:T(8,128)(2,1)S(1)} %get-tuple-element.114.after_ref), channel_id=1, source_target_pairs={{0,6},{1,7},{2,4},{3,5},{4,2},{5,3},{6,0},{7,1},{8,14},{9,15},{10,... | collective-permute-start | bytes 122888 | tf_op jit(solution)/shard_map/ppermute | solution.py:31
  8.5 3.5 %shard_map.97.refs_1_.refs_2_.schur_ref = bf16[2,4096,512]{2,1,0:T(8,128)(2,1)S(1)} custom-call(bf16[2,2,4096,512]{3,2,1,0:T(8,128)(2,1)} %refs_4_.3, bf16[80,256]{1,0:T(8,128)(2,1)S(1)} %get-tuple-element.114.after_ref), custom_call_target="tpu_custom_call" | custom-call | bytes 8388608 | tf_op jit(solution)/shard_map/pallas_call | solution.py:109
  12.9 0.7 collective-permute-done.1.refs_0_.refs_1_
  14.0 0.9 shard_map.99
  14.9 2.8 %collective-permute-start.7 = (bf16[2,16,512]{2,1,0:T(8,128)(2,1)S(1)}, bf16[2,16,512]{2,1,0:T(8,128)(2,1)S(1)}, u32[]{:S(2)}, u32[]{:S(2)}) collective-permute-start(bf16[2,16,512]{2,1,0:T(8,128)(2,1)S(1)} %get-tuple-element.119.refs_5_.refs_7_), channel_id=1, source_target_pairs={{0,6},{1,7},{2,4},{3,5},{4,2},{5,3},{6,0},{7,1},{8,14},{9,15},{10,... | collective-permute-start | bytes 98312 | tf_op jit(solution)/shard_map/ppermute | solution.py:31
  18.5 3.8 %shard_map.101 = (f32[2,16,512]{2,1,0:T(8,128)S(1)}, bf16[2,4096,512]{2,1,0:T(8,128)(2,1)S(1)}) custom-call(f32[1,512]{1,0:T(1,128)S(1)} %get-tuple-element.121.mask_ref.refs_3_, f32[2,2,16,512]{3,2,1,0:T(8,128)S(1)} %get-tuple-element.118.source_ref, bf16[2,80,256]{2,1,0:T(8,128)(2,1)S(1)} %pad_maximum_fusion.3.refs_0_.one_ref, ...), custom_call_target="tpu_custom_call" | custom-call | bytes 8388608 | tf_op jit(solution)/shard_map/pallas_call | solution.py:109
  23.6 0.8 shard_map.103.refs_0_
  25.0 2.9 %collective-permute-start.10 = (bf16[2,16,512]{2,1,0:T(8,128)(2,1)S(1)}, bf16[2,16,512]{2,1,0:T(8,128)(2,1)S(1)}, u32[]{:S(2)}, u32[]{:S(2)}) collective-permute-start(bf16[2,16,512]{2,1,0:T(8,128)(2,1)S(1)} %get-tuple-element.137.refs_5_), channel_id=1, source_target_pairs={{0,6},{1,7},{2,4},{3,5},{4,2},{5,3},{6,0},{7,1},{8,9},{9,8},{10,11... | collective-permute-start | bytes 98312 | tf_op jit(solution)/shard_map/ppermute | solution.py:31
  28.5 1.3 collective-permute-done.10
  30.4 1.4 collective-permute-done.12
  32.4 0.8 shard_map.106.refs_0_
  34.1 1.3 collective-permute-start.15
  35.4 1.3 collective-permute-start.16
  36.7 1.3 collective-permute-start.18
  38.4 1.2 collective-permute-done.18
  39.6 2.4 %collective-permute-done.19 = bf16[2,16,512]{2,1,0:T(8,128)(2,1)S(1)} collective-permute-done((bf16[2,16,512]{2,1,0:T(8,128)(2,1)S(1)}, bf16[2,16,512]{2,1,0:T(8,128)(2,1)S(1)}, u32[]{:S(2)}, u32[]{:S(2)}) %collective-permute-start.19) | collective-permute-done | bytes 32800 | tf_op jit(solution)/shard_map/ppermute | solution.py:88
  42.1 1.2 collective-permute-done.20.refs_1_
  46.4 0.7 collective-permute-start.26
  47.1 0.7 collective-permute-start.27
  47.7 0.7 collective-permute-start.29
  50.0 1.0 collective-permute-done.31.refs_1_
  51.0 1.5 collective-permute-start.32
  52.8 1.7 %collective-permute-start.35 = (bf16[2,16,512]{2,1,0:T(8,128)(2,1)S(1)}, bf16[2,16,512]{2,1,0:T(8,128)(2,1)S(1)}, u32[]{:S(2)}, u32[]{:S(2)}) collective-permute-start(bf16[2,16,512]{2,1,0:T(8,128)(2,1)S(1)} %get-tuple-element.158.refs_5_), channel_id=1, source_target_pairs={{0,2},{1,3},{2,0},{3,1},{4,6},{5,7},{6,4},{7,5},{8,9},{9,8},{10,11... | collective-permute-start | bytes 98312 | tf_op jit(solution)/shard_map/ppermute | solution.py:31
  54.5 1.3 collective-permute-done.32
  57.2 0.9 collective-permute-done.36.refs_1_
  58.0 10.1 %collective-permute-start.37 = (bf16[2,16,512]{2,1,0:T(8,128)(2,1)S(1)}, bf16[2,16,512]{2,1,0:T(8,128)(2,1)S(1)}, u32[]{:S(2)}, u32[]{:S(2)}) collective-permute-start(bf16[2,16,512]{2,1,0:T(8,128)(2,1)S(1)} %get-tuple-element.163.refs_7_), channel_id=1, source_target_pairs={{0,14},{1,15},{2,12},{3,13},{4,10},{5,11},{6,8},{7,9},{16,30},{17,... | collective-permute-start | bytes 98312 | tf_op jit(solution)/shard_map/ppermute | solution.py:88
  68.1 1.3 collective-permute-start.38
  69.4 1.3 collective-permute-start.40
  71.1 1.2 collective-permute-done.40
  72.3 2.4 %collective-permute-done.41 = bf16[2,16,512]{2,1,0:T(8,128)(2,1)S(1)} collective-permute-done((bf16[2,16,512]{2,1,0:T(8,128)(2,1)S(1)}, bf16[2,16,512]{2,1,0:T(8,128)(2,1)S(1)}, u32[]{:S(2)}, u32[]{:S(2)}) %collective-permute-start.41) | collective-permute-done | bytes 32800 | tf_op jit(solution)/shard_map/ppermute | solution.py:88
  74.8 1.2 collective-permute-done.42.refs_1_
  82.1 1.3 collective-permute-start.53
  83.4 1.3 collective-permute-start.54
  84.8 1.3 collective-permute-start.56
  86.1 9.9 %collective-permute-start.57 = (bf16[2,16,512]{2,1,0:T(8,128)(2,1)S(1)}, bf16[2,16,512]{2,1,0:T(8,128)(2,1)S(1)}, u32[]{:S(2)}, u32[]{:S(2)}) collective-permute-start(bf16[2,16,512]{2,1,0:T(8,128)(2,1)S(1)} %get-tuple-element.180.refs_6_), channel_id=1, source_target_pairs={{0,8},{1,9},{2,10},{3,11},{4,12},{5,13},{6,14},{7,15},{8,0},{9,1},... | collective-permute-start | bytes 98312 | tf_op jit(solution)/shard_map/ppermute | solution.py:88
  96.5 1.7 %collective-permute-done.56 = bf16[2,16,512]{2,1,0:T(8,128)(2,1)S(1)} collective-permute-done((bf16[2,16,512]{2,1,0:T(8,128)(2,1)S(1)}, bf16[2,16,512]{2,1,0:T(8,128)(2,1)S(1)}, u32[]{:S(2)}, u32[]{:S(2)}) %collective-permute-start.56) | collective-permute-done | bytes 32800 | tf_op jit(solution)/shard_map/ppermute | solution.py:88
  98.4 1.2 collective-permute-done.58.refs_1_
  99.6 1.1 collective-permute-start.59
  100.7 1.5 collective-permute-start.61
  102.2 0.9 collective-permute-start.62
  103.1 1.4 collective-permute-done.59
  104.8 1.3 collective-permute-done.62
  106.2 1.2 collective-permute-done.63.refs_1_
  107.4 0.7 collective-permute-start.64
  108.1 0.7 collective-permute-start.65
  108.8 0.7 collective-permute-start.67
  111.0 1.0 collective-permute-done.69.refs_1_
  115.1 1.3 collective-permute-start.75
  116.4 1.3 collective-permute-start.76
  117.7 1.3 collective-permute-start.78
  119.0 16.0 %collective-permute-start.79 = (bf16[2,16,512]{2,1,0:T(8,128)(2,1)S(1)}, bf16[2,16,512]{2,1,0:T(8,128)(2,1)S(1)}, u32[]{:S(2)}, u32[]{:S(2)}) collective-permute-start(bf16[2,16,512]{2,1,0:T(8,128)(2,1)S(1)} %get-tuple-element.201.refs_6_), channel_id=1, source_target_pairs={{0,8},{1,9},{2,10},{3,11},{4,12},{5,13},{6,14},{7,15},{8,0},{9,1},... | collective-permute-start | bytes 98312 | tf_op jit(solution)/shard_map/ppermute | solution.py:88
  135.0 0.9 collective-permute-done.75
  137.8 0.8 shard_map.142.refs_0_
  139.3 1.9 %collective-permute-start.81 = (bf16[2,16,512]{2,1,0:T(8,128)(2,1)S(1)}, bf16[2,16,512]{2,1,0:T(8,128)(2,1)S(1)}, u32[]{:S(2)}, u32[]{:S(2)}) collective-permute-start(bf16[2,16,512]{2,1,0:T(8,128)(2,1)S(1)} %get-tuple-element.206), channel_id=1, source_target_pairs={{0,6},{1,7},{2,4},{3,5},{4,2},{5,3},{6,0},{7,1},{8,9},{9,8},{10,11... | collective-permute-start | bytes 98312 | tf_op jit(solution)/shard_map/ppermute | solution.py:31
  141.7 1.1 collective-permute-start.84
  142.9 1.4 collective-permute-done.81
  145.8 0.8 shard_map.145.products_ref
  147.5 2.1 %collective-permute-start.86 = (bf16[2,2,16,512]{3,2,1,0:T(8,128)(2,1)S(1)}, bf16[2,2,16,512]{3,2,1,0:T(8,128)(2,1)S(1)}, u32[]{:S(2)}, u32[]{:S(2)}) collective-permute-start(bf16[2,2,16,512]{3,2,1,0:T(8,128)(2,1)S(1)} %get-tuple-element.212), channel_id=1, source_target_pairs={{0,6},{1,7},{2,4},{3,5},{4,2},{5,3},{6,0},{7,1},{8,14},{9,15},{10,... | collective-permute-start | bytes 196616 | tf_op jit(solution)/shard_map/ppermute | solution.py:31
  150.1 0.9 collective-permute-start.89
  151.0 1.7 %collective-permute-done.86 = bf16[2,2,16,512]{3,2,1,0:T(8,128)(2,1)S(1)} collective-permute-done((bf16[2,2,16,512]{3,2,1,0:T(8,128)(2,1)S(1)}, bf16[2,2,16,512]{3,2,1,0:T(8,128)(2,1)S(1)}, u32[]{:S(2)}, u32[]{:S(2)}) %collective-permute-start.86) | collective-permute-done | bytes 65568 | tf_op jit(solution)/shard_map/ppermute | solution.py:31
  153.3 0.8 collective-permute-done.88
  154.5 0.7 pad_maximum_fusion.2
  155.8 1.6 %shard_map.149 = f32[2,2,16,512]{3,2,1,0:T(8,128)} custom-call(f32[2,32,256]{2,1,0:T(8,128)S(1)} %shard_map.148.picked_ref, bf16[2,2,2,16,512]{4,3,2,1,0:T(8,128)(2,1)S(1)} %collective-permute-done.90.last_ref, bf16[2,2,512,256]{3,2,1,0:T(8,128)(2,1)S(1)} %get-tuple-element.219.chosen_ref, bf16[2,1,2,512,256]{4,3,2,1,0:T(8,128)(2,1)S(1)} %get-tuple-element.220.coupling_ref, ...), custom_call_target="tpu_custom_call" | custom-call | tf_op jit(solution)/shard_map/pallas_call | solution.py:644
  (214 shorter events, 33.5 us)
Async XLA Ops:
  3.9 8.1 %collective-permute-start = (bf16[80,256]{1,0:T(8,128)(2,1)S(1)}, bf16[80,256]{1,0:T(8,128)(2,1)S(1)}, u32[]{:S(2)}, u32[]{:S(2)}) collective-permute-start(bf16[80,256]{1,0:T(8,128)(2,1)S(1)} %get-tuple-element.114.after_ref), channel_id=1, source_target_pairs={{0,6},{1,7},{2,4},{3,5},{4,2},{5,3},{6,0},{7,1},{8,14},{9,15},{10,... | collective-permute-start | bytes 122888 | tf_op jit(solution)/shard_map/ppermute | solution.py:31
  7.9 4.4 %collective-permute-start.2 = (bf16[80,256]{1,0:T(8,128)(2,1)S(1)}, bf16[80,256]{1,0:T(8,128)(2,1)S(1)}, u32[]{:S(2)}, u32[]{:S(2)}) collective-permute-start(bf16[80,256]{1,0:T(8,128)(2,1)S(1)} %get-tuple-element.114.after_ref), channel_id=1, source_target_pairs={{0,4},{1,5},{2,6},{3,7},{4,0},{5,1},{6,2},{7,3},{8,12},{9,13},{10,... | collective-permute-start | bytes 122888 | tf_op jit(solution)/shard_map/ppermute | solution.py:31
  8.4 4.0 %collective-permute-start.3 = (bf16[80,256]{1,0:T(8,128)(2,1)S(1)}, bf16[80,256]{1,0:T(8,128)(2,1)S(1)}, u32[]{:S(2)}, u32[]{:S(2)}) collective-permute-start(bf16[80,256]{1,0:T(8,128)(2,1)S(1)} %get-tuple-element.114.after_ref), channel_id=1, source_target_pairs={{0,2},{1,3},{2,0},{3,1},{4,6},{5,7},{6,4},{7,5},{8,10},{9,11},{10,... | collective-permute-start | bytes 122888 | tf_op jit(solution)/shard_map/ppermute | solution.py:31
  12.4 1.6 %collective-permute-start.4 = (bf16[2,80,256]{2,1,0:T(8,128)(2,1)S(1)}, bf16[2,80,256]{2,1,0:T(8,128)(2,1)S(1)}, u32[]{:S(2)}, u32[]{:S(2)}) collective-permute-start(bf16[2,80,256]{2,1,0:T(8,128)(2,1)S(1)} %pad_maximum_fusion.4.refs_1_.refs_2_.two_ref), channel_id=1, source_target_pairs={{0,1},{1,0},{2,3},{3,2},{4,5},{5,4},{6,7},{7,6},{8,9},{9,8},{10,11... | collective-permute-start | bytes 245768 | tf_op jit(solution)/shard_map/ppermute | solution.py:31
  14.9 7.4 %collective-permute-start.7 = (bf16[2,16,512]{2,1,0:T(8,128)(2,1)S(1)}, bf16[2,16,512]{2,1,0:T(8,128)(2,1)S(1)}, u32[]{:S(2)}, u32[]{:S(2)}) collective-permute-start(bf16[2,16,512]{2,1,0:T(8,128)(2,1)S(1)} %get-tuple-element.119.refs_5_.refs_7_), channel_id=1, source_target_pairs={{0,6},{1,7},{2,4},{3,5},{4,2},{5,3},{6,0},{7,1},{8,14},{9,15},{10,... | collective-permute-start | bytes 98312 | tf_op jit(solution)/shard_map/ppermute | solution.py:31
  17.8 5.1 %collective-permute-start.5 = (bf16[2,16,512]{2,1,0:T(8,128)(2,1)S(1)}, bf16[2,16,512]{2,1,0:T(8,128)(2,1)S(1)}, u32[]{:S(2)}, u32[]{:S(2)}) collective-permute-start(bf16[2,16,512]{2,1,0:T(8,128)(2,1)S(1)} %get-tuple-element.119.refs_5_.refs_7_), channel_id=1, source_target_pairs={{0,4},{1,5},{2,6},{3,7},{4,0},{5,1},{6,2},{7,3},{8,12},{9,13},{10,... | collective-permute-start | bytes 98312 | tf_op jit(solution)/shard_map/ppermute | solution.py:31
  18.4 4.5 %collective-permute-start.6 = (bf16[2,16,512]{2,1,0:T(8,128)(2,1)S(1)}, bf16[2,16,512]{2,1,0:T(8,128)(2,1)S(1)}, u32[]{:S(2)}, u32[]{:S(2)}) collective-permute-start(bf16[2,16,512]{2,1,0:T(8,128)(2,1)S(1)} %get-tuple-element.119.refs_5_.refs_7_), channel_id=1, source_target_pairs={{0,2},{1,3},{2,0},{3,1},{4,6},{5,7},{6,4},{7,5},{8,10},{9,11},{10,... | collective-permute-start | bytes 98312 | tf_op jit(solution)/shard_map/ppermute | solution.py:31
  22.3 1.3 collective-permute-start.8
  22.9 1.6 collective-permute-start.9
  25.0 4.9 %collective-permute-start.10 = (bf16[2,16,512]{2,1,0:T(8,128)(2,1)S(1)}, bf16[2,16,512]{2,1,0:T(8,128)(2,1)S(1)}, u32[]{:S(2)}, u32[]{:S(2)}) collective-permute-start(bf16[2,16,512]{2,1,0:T(8,128)(2,1)S(1)} %get-tuple-element.137.refs_5_), channel_id=1, source_target_pairs={{0,6},{1,7},{2,4},{3,5},{4,2},{5,3},{6,0},{7,1},{8,9},{9,8},{10,11... | collective-permute-start | bytes 98312 | tf_op jit(solution)/shard_map/ppermute | solution.py:31
  27.9 3.9 %collective-permute-start.12 = (bf16[2,16,512]{2,1,0:T(8,128)(2,1)S(1)}, bf16[2,16,512]{2,1,0:T(8,128)(2,1)S(1)}, u32[]{:S(2)}, u32[]{:S(2)}) collective-permute-start(bf16[2,16,512]{2,1,0:T(8,128)(2,1)S(1)} %get-tuple-element.137.refs_5_), channel_id=1, source_target_pairs={{0,4},{1,5},{2,6},{3,7},{4,0},{5,1},{6,2},{7,3},{8,9},{9,8},{10,11... | collective-permute-start | bytes 98312 | tf_op jit(solution)/shard_map/ppermute | solution.py:31
  28.4 3.9 %collective-permute-start.13 = (bf16[2,16,512]{2,1,0:T(8,128)(2,1)S(1)}, bf16[2,16,512]{2,1,0:T(8,128)(2,1)S(1)}, u32[]{:S(2)}, u32[]{:S(2)}) collective-permute-start(bf16[2,16,512]{2,1,0:T(8,128)(2,1)S(1)} %get-tuple-element.137.refs_5_), channel_id=1, source_target_pairs={{0,2},{1,3},{2,0},{3,1},{4,6},{5,7},{6,4},{7,5},{8,9},{9,8},{10,11... | collective-permute-start | bytes 98312 | tf_op jit(solution)/shard_map/ppermute | solution.py:31
  29.9 2.5 %collective-permute-start.11 = (bf16[2,2,16,512]{3,2,1,0:T(8,128)(2,1)S(1)}, bf16[2,2,16,512]{3,2,1,0:T(8,128)(2,1)S(1)}, u32[]{:S(2)}, u32[]{:S(2)}) collective-permute-start(bf16[2,2,16,512]{3,2,1,0:T(8,128)(2,1)S(1)} %pad_maximum_fusion.7.refs_0_), channel_id=1, source_target_pairs={{0,1},{1,0},{2,3},{3,2},{4,5},{5,4},{6,7},{7,6},{8,9},{9,8},{10,11... | collective-permute-start | bytes 196616 | tf_op jit(solution)/shard_map/ppermute | solution.py:31
  32.3 1.3 collective-permute-start.14
  34.1 4.0 %collective-permute-start.15 = (bf16[2,16,512]{2,1,0:T(8,128)(2,1)S(1)}, bf16[2,16,512]{2,1,0:T(8,128)(2,1)S(1)}, u32[]{:S(2)}, u32[]{:S(2)}) collective-permute-start(bf16[2,16,512]{2,1,0:T(8,128)(2,1)S(1)} %get-tuple-element.142.refs_7_), channel_id=1, source_target_pairs={{0,14},{1,15},{2,12},{3,13},{4,10},{5,11},{6,8},{7,9},{16,30},{17,... | collective-permute-start | bytes 98312 | tf_op jit(solution)/shard_map/ppermute | solution.py:88
  35.4 2.9 %collective-permute-start.16 = (bf16[2,16,512]{2,1,0:T(8,128)(2,1)S(1)}, bf16[2,16,512]{2,1,0:T(8,128)(2,1)S(1)}, u32[]{:S(2)}, u32[]{:S(2)}) collective-permute-start(bf16[2,16,512]{2,1,0:T(8,128)(2,1)S(1)} %get-tuple-element.142.refs_7_), channel_id=1, source_target_pairs={{0,12},{1,13},{2,14},{3,15},{4,8},{5,9},{6,10},{7,11},{16,28},{17,... | collective-permute-start | bytes 98312 | tf_op jit(solution)/shard_map/ppermute | solution.py:88
  36.7 2.9 %collective-permute-start.18 = (bf16[2,16,512]{2,1,0:T(8,128)(2,1)S(1)}, bf16[2,16,512]{2,1,0:T(8,128)(2,1)S(1)}, u32[]{:S(2)}, u32[]{:S(2)}) collective-permute-start(bf16[2,16,512]{2,1,0:T(8,128)(2,1)S(1)} %get-tuple-element.142.refs_7_), channel_id=1, source_target_pairs={{0,10},{1,11},{2,8},{3,9},{4,14},{5,15},{6,12},{7,13},{16,26},{17,... | collective-permute-start | bytes 98312 | tf_op jit(solution)/shard_map/ppermute | solution.py:88
  38.0 4.0 %collective-permute-start.19 = (bf16[2,16,512]{2,1,0:T(8,128)(2,1)S(1)}, bf16[2,16,512]{2,1,0:T(8,128)(2,1)S(1)}, u32[]{:S(2)}, u32[]{:S(2)}) collective-permute-start(bf16[2,16,512]{2,1,0:T(8,128)(2,1)S(1)} %get-tuple-element.142.refs_7_), channel_id=1, source_target_pairs={{0,8},{1,9},{2,10},{3,11},{4,12},{5,13},{6,14},{7,15},{8,0},{9,1},... | collective-permute-start | bytes 98312 | tf_op jit(solution)/shard_map/ppermute | solution.py:88
  38.3 3.8 %collective-permute-start.17 = (bf16[2,2,16,512]{3,2,1,0:T(8,128)(2,1)S(1)}, bf16[2,2,16,512]{3,2,1,0:T(8,128)(2,1)S(1)}, u32[]{:S(2)}, u32[]{:S(2)}) collective-permute-start(bf16[2,2,16,512]{3,2,1,0:T(8,128)(2,1)S(1)} %multiply_convert_fusion.11.refs_0_), channel_id=1, source_target_pairs={{0,1},{1,0},{2,3},{3,2},{4,5},{5,4},{6,7},{7,6},{8,9},{9,8},{10,11... | collective-permute-start | bytes 196616 | tf_op jit(solution)/shard_map/ppermute | solution.py:31
  42.0 1.3 collective-permute-start.20
  44.6 1.3 collective-permute-start.22
  45.1 1.3 collective-permute-start.25
  46.4 2.2 %collective-permute-start.26 = (bf16[2,16,512]{2,1,0:T(8,128)(2,1)S(1)}, bf16[2,16,512]{2,1,0:T(8,128)(2,1)S(1)}, u32[]{:S(2)}, u32[]{:S(2)}) collective-permute-start(bf16[2,16,512]{2,1,0:T(8,128)(2,1)S(1)} %get-tuple-element.153.refs_7_), channel_id=1, source_target_pairs={{8,22},{9,23},{10,20},{11,21},{12,18},{13,19},{14,16},{15,17}} | collective-permute-start | bytes 98312 | tf_op jit(solution)/shard_map/ppermute | solution.py:88
  47.1 1.6 collective-permute-start.27
  47.7 1.3 collective-permute-start.29
  48.7 1.3 collective-permute-start.28
  49.7 1.3 collective-permute-start.31
  51.0 4.8 %collective-permute-start.32 = (bf16[2,16,512]{2,1,0:T(8,128)(2,1)S(1)}, bf16[2,16,512]{2,1,0:T(8,128)(2,1)S(1)}, u32[]{:S(2)}, u32[]{:S(2)}) collective-permute-start(bf16[2,16,512]{2,1,0:T(8,128)(2,1)S(1)} %get-tuple-element.158.refs_5_), channel_id=1, source_target_pairs={{0,6},{1,7},{2,4},{3,5},{4,2},{5,3},{6,0},{7,1},{8,9},{9,8},{10,11... | collective-permute-start | bytes 98312 | tf_op jit(solution)/shard_map/ppermute | solution.py:31
  52.5 3.9 %collective-permute-start.34 = (bf16[2,16,512]{2,1,0:T(8,128)(2,1)S(1)}, bf16[2,16,512]{2,1,0:T(8,128)(2,1)S(1)}, u32[]{:S(2)}, u32[]{:S(2)}) collective-permute-start(bf16[2,16,512]{2,1,0:T(8,128)(2,1)S(1)} %get-tuple-element.158.refs_5_), channel_id=1, source_target_pairs={{0,4},{1,5},{2,6},{3,7},{4,0},{5,1},{6,2},{7,3},{8,9},{9,8},{10,11... | collective-permute-start | bytes 98312 | tf_op jit(solution)/shard_map/ppermute | solution.py:31
  52.8 3.9 %collective-permute-start.35 = (bf16[2,16,512]{2,1,0:T(8,128)(2,1)S(1)}, bf16[2,16,512]{2,1,0:T(8,128)(2,1)S(1)}, u32[]{:S(2)}, u32[]{:S(2)}) collective-permute-start(bf16[2,16,512]{2,1,0:T(8,128)(2,1)S(1)} %get-tuple-element.158.refs_5_), channel_id=1, source_target_pairs={{0,2},{1,3},{2,0},{3,1},{4,6},{5,7},{6,4},{7,5},{8,9},{9,8},{10,11... | collective-permute-start | bytes 98312 | tf_op jit(solution)/shard_map/ppermute | solution.py:31
  55.8 1.3 collective-permute-start.33
  56.7 1.3 collective-permute-start.36
  58.0 12.8 %collective-permute-start.37 = (bf16[2,16,512]{2,1,0:T(8,128)(2,1)S(1)}, bf16[2,16,512]{2,1,0:T(8,128)(2,1)S(1)}, u32[]{:S(2)}, u32[]{:S(2)}) collective-permute-start(bf16[2,16,512]{2,1,0:T(8,128)(2,1)S(1)} %get-tuple-element.163.refs_7_), channel_id=1, source_target_pairs={{0,14},{1,15},{2,12},{3,13},{4,10},{5,11},{6,8},{7,9},{16,30},{17,... | collective-permute-start | bytes 98312 | tf_op jit(solution)/shard_map/ppermute | solution.py:88
  68.1 2.9 %collective-permute-start.38 = (bf16[2,16,512]{2,1,0:T(8,128)(2,1)S(1)}, bf16[2,16,512]{2,1,0:T(8,128)(2,1)S(1)}, u32[]{:S(2)}, u32[]{:S(2)}) collective-permute-start(bf16[2,16,512]{2,1,0:T(8,128)(2,1)S(1)} %get-tuple-element.163.refs_7_), channel_id=1, source_target_pairs={{0,12},{1,13},{2,14},{3,15},{4,8},{5,9},{6,10},{7,11},{16,28},{17,... | collective-permute-start | bytes 98312 | tf_op jit(solution)/shard_map/ppermute | solution.py:88
  69.4 2.9 %collective-permute-start.40 = (bf16[2,16,512]{2,1,0:T(8,128)(2,1)S(1)}, bf16[2,16,512]{2,1,0:T(8,128)(2,1)S(1)}, u32[]{:S(2)}, u32[]{:S(2)}) collective-permute-start(bf16[2,16,512]{2,1,0:T(8,128)(2,1)S(1)} %get-tuple-element.163.refs_7_), channel_id=1, source_target_pairs={{0,10},{1,11},{2,8},{3,9},{4,14},{5,15},{6,12},{7,13},{16,26},{17,... | collective-permute-start | bytes 98312 | tf_op jit(solution)/shard_map/ppermute | solution.py:88
  70.7 4.0 %collective-permute-start.41 = (bf16[2,16,512]{2,1,0:T(8,128)(2,1)S(1)}, bf16[2,16,512]{2,1,0:T(8,128)(2,1)S(1)}, u32[]{:S(2)}, u32[]{:S(2)}) collective-permute-start(bf16[2,16,512]{2,1,0:T(8,128)(2,1)S(1)} %get-tuple-element.163.refs_7_), channel_id=1, source_target_pairs={{0,8},{1,9},{2,10},{3,11},{4,12},{5,13},{6,14},{7,15},{8,0},{9,1},... | collective-permute-start | bytes 98312 | tf_op jit(solution)/shard_map/ppermute | solution.py:88
  71.0 3.8 %collective-permute-start.39 = (bf16[2,2,16,512]{3,2,1,0:T(8,128)(2,1)S(1)}, bf16[2,2,16,512]{3,2,1,0:T(8,128)(2,1)S(1)}, u32[]{:S(2)}, u32[]{:S(2)}) collective-permute-start(bf16[2,2,16,512]{3,2,1,0:T(8,128)(2,1)S(1)} %multiply_convert_fusion.7.refs_0_), channel_id=1, source_target_pairs={{0,1},{1,0},{2,3},{3,2},{4,5},{5,4},{6,7},{7,6},{8,9},{9,8},{10,11... | collective-permute-start | bytes 196616 | tf_op jit(solution)/shard_map/ppermute | solution.py:31
  74.7 1.3 collective-permute-start.42
  82.1 13.8 %collective-permute-start.53 = (bf16[2,16,512]{2,1,0:T(8,128)(2,1)S(1)}, bf16[2,16,512]{2,1,0:T(8,128)(2,1)S(1)}, u32[]{:S(2)}, u32[]{:S(2)}) collective-permute-start(bf16[2,16,512]{2,1,0:T(8,128)(2,1)S(1)} %get-tuple-element.180.refs_6_), channel_id=1, source_target_pairs={{8,6},{9,7},{10,4},{11,5},{12,2},{13,3},{14,0},{15,1},{24,22},{25,... | collective-permute-start | bytes 98312 | tf_op jit(solution)/shard_map/ppermute | solution.py:88
  83.4 13.0 %collective-permute-start.54 = (bf16[2,16,512]{2,1,0:T(8,128)(2,1)S(1)}, bf16[2,16,512]{2,1,0:T(8,128)(2,1)S(1)}, u32[]{:S(2)}, u32[]{:S(2)}) collective-permute-start(bf16[2,16,512]{2,1,0:T(8,128)(2,1)S(1)} %get-tuple-element.180.refs_6_), channel_id=1, source_target_pairs={{8,4},{9,5},{10,6},{11,7},{12,0},{13,1},{14,2},{15,3},{24,20},{25,... | collective-permute-start | bytes 98312 | tf_op jit(solution)/shard_map/ppermute | solution.py:88
  84.8 13.5 %collective-permute-start.56 = (bf16[2,16,512]{2,1,0:T(8,128)(2,1)S(1)}, bf16[2,16,512]{2,1,0:T(8,128)(2,1)S(1)}, u32[]{:S(2)}, u32[]{:S(2)}) collective-permute-start(bf16[2,16,512]{2,1,0:T(8,128)(2,1)S(1)} %get-tuple-element.180.refs_6_), channel_id=1, source_target_pairs={{8,2},{9,3},{10,0},{11,1},{12,6},{13,7},{14,4},{15,5},{24,18},{25,... | collective-permute-start | bytes 98312 | tf_op jit(solution)/shard_map/ppermute | solution.py:88
  86.1 12.2 %collective-permute-start.57 = (bf16[2,16,512]{2,1,0:T(8,128)(2,1)S(1)}, bf16[2,16,512]{2,1,0:T(8,128)(2,1)S(1)}, u32[]{:S(2)}, u32[]{:S(2)}) collective-permute-start(bf16[2,16,512]{2,1,0:T(8,128)(2,1)S(1)} %get-tuple-element.180.refs_6_), channel_id=1, source_target_pairs={{0,8},{1,9},{2,10},{3,11},{4,12},{5,13},{6,14},{7,15},{8,0},{9,1},... | collective-permute-start | bytes 98312 | tf_op jit(solution)/shard_map/ppermute | solution.py:88
  96.4 1.9 %collective-permute-start.55 = (bf16[2,2,16,512]{3,2,1,0:T(8,128)(2,1)S(1)}, bf16[2,2,16,512]{3,2,1,0:T(8,128)(2,1)S(1)}, u32[]{:S(2)}, u32[]{:S(2)}) collective-permute-start(bf16[2,2,16,512]{3,2,1,0:T(8,128)(2,1)S(1)} %multiply_convert_fusion.5.refs_0_), channel_id=1, source_target_pairs={{0,1},{1,0},{2,3},{3,2},{4,5},{5,4},{6,7},{7,6},{8,9},{9,8},{10,11... | collective-permute-start | bytes 196616 | tf_op jit(solution)/shard_map/ppermute | solution.py:31
  99.6 4.9 %collective-permute-start.59 = (bf16[2,16,512]{2,1,0:T(8,128)(2,1)S(1)}, bf16[2,16,512]{2,1,0:T(8,128)(2,1)S(1)}, u32[]{:S(2)}, u32[]{:S(2)}) collective-permute-start(bf16[2,16,512]{2,1,0:T(8,128)(2,1)S(1)} %get-tuple-element.186.refs_6_), channel_id=1, source_target_pairs={{0,6},{1,7},{2,4},{3,5},{4,2},{5,3},{6,0},{7,1},{8,9},{9,8},{10,11... | collective-permute-start | bytes 98312 | tf_op jit(solution)/shard_map/ppermute | solution.py:31
  100.7 4.0 %collective-permute-start.61 = (bf16[2,16,512]{2,1,0:T(8,128)(2,1)S(1)}, bf16[2,16,512]{2,1,0:T(8,128)(2,1)S(1)}, u32[]{:S(2)}, u32[]{:S(2)}) collective-permute-start(bf16[2,16,512]{2,1,0:T(8,128)(2,1)S(1)} %get-tuple-element.186.refs_6_), channel_id=1, source_target_pairs={{0,4},{1,5},{2,6},{3,7},{4,0},{5,1},{6,2},{7,3},{8,9},{9,8},{10,11... | collective-permute-start | bytes 98312 | tf_op jit(solution)/shard_map/ppermute | solution.py:31
  102.2 3.9 %collective-permute-start.62 = (bf16[2,16,512]{2,1,0:T(8,128)(2,1)S(1)}, bf16[2,16,512]{2,1,0:T(8,128)(2,1)S(1)}, u32[]{:S(2)}, u32[]{:S(2)}) collective-permute-start(bf16[2,16,512]{2,1,0:T(8,128)(2,1)S(1)} %get-tuple-element.186.refs_6_), channel_id=1, source_target_pairs={{0,2},{1,3},{2,0},{3,1},{4,6},{5,7},{6,4},{7,5},{8,9},{9,8},{10,11... | collective-permute-start | bytes 98312 | tf_op jit(solution)/shard_map/ppermute | solution.py:31
  104.5 1.7 %collective-permute-start.60 = (bf16[2,2,16,512]{3,2,1,0:T(8,128)(2,1)S(1)}, bf16[2,2,16,512]{3,2,1,0:T(8,128)(2,1)S(1)}, u32[]{:S(2)}, u32[]{:S(2)}) collective-permute-start(bf16[2,2,16,512]{3,2,1,0:T(8,128)(2,1)S(1)} %pad_maximum_fusion.17.refs_0_), channel_id=1, source_target_pairs={{0,1},{1,0},{2,3},{3,2},{4,5},{5,4},{6,7},{7,6},{8,9},{9,8},{10,11... | collective-permute-start | bytes 196616 | tf_op jit(solution)/shard_map/ppermute | solution.py:31
  107.4 2.2 %collective-permute-start.64 = (bf16[2,16,512]{2,1,0:T(8,128)(2,1)S(1)}, bf16[2,16,512]{2,1,0:T(8,128)(2,1)S(1)}, u32[]{:S(2)}, u32[]{:S(2)}) collective-permute-start(bf16[2,16,512]{2,1,0:T(8,128)(2,1)S(1)} %get-tuple-element.191.refs_6_), channel_id=1, source_target_pairs={{16,14},{17,15},{18,12},{19,13},{20,10},{21,11},{22,8},{23,9}} | collective-permute-start | bytes 98312 | tf_op jit(solution)/shard_map/ppermute | solution.py:88
  108.1 1.6 collective-permute-start.65
  108.8 1.3 collective-permute-start.67
  109.7 1.3 collective-permute-start.66
  115.1 20.7 %collective-permute-start.75 = (bf16[2,16,512]{2,1,0:T(8,128)(2,1)S(1)}, bf16[2,16,512]{2,1,0:T(8,128)(2,1)S(1)}, u32[]{:S(2)}, u32[]{:S(2)}) collective-permute-start(bf16[2,16,512]{2,1,0:T(8,128)(2,1)S(1)} %get-tuple-element.201.refs_6_), channel_id=1, source_target_pairs={{8,6},{9,7},{10,4},{11,5},{12,2},{13,3},{14,0},{15,1},{24,22},{25,... | collective-permute-start | bytes 98312 | tf_op jit(solution)/shard_map/ppermute | solution.py:88
  116.4 20.0 %collective-permute-start.76 = (bf16[2,16,512]{2,1,0:T(8,128)(2,1)S(1)}, bf16[2,16,512]{2,1,0:T(8,128)(2,1)S(1)}, u32[]{:S(2)}, u32[]{:S(2)}) collective-permute-start(bf16[2,16,512]{2,1,0:T(8,128)(2,1)S(1)} %get-tuple-element.201.refs_6_), channel_id=1, source_target_pairs={{8,4},{9,5},{10,6},{11,7},{12,0},{13,1},{14,2},{15,3},{24,20},{25,... | collective-permute-start | bytes 98312 | tf_op jit(solution)/shard_map/ppermute | solution.py:88
  117.7 19.8 %collective-permute-start.78 = (bf16[2,16,512]{2,1,0:T(8,128)(2,1)S(1)}, bf16[2,16,512]{2,1,0:T(8,128)(2,1)S(1)}, u32[]{:S(2)}, u32[]{:S(2)}) collective-permute-start(bf16[2,16,512]{2,1,0:T(8,128)(2,1)S(1)} %get-tuple-element.201.refs_6_), channel_id=1, source_target_pairs={{8,2},{9,3},{10,0},{11,1},{12,6},{13,7},{14,4},{15,5},{24,18},{25,... | collective-permute-start | bytes 98312 | tf_op jit(solution)/shard_map/ppermute | solution.py:88
  119.0 18.5 %collective-permute-start.79 = (bf16[2,16,512]{2,1,0:T(8,128)(2,1)S(1)}, bf16[2,16,512]{2,1,0:T(8,128)(2,1)S(1)}, u32[]{:S(2)}, u32[]{:S(2)}) collective-permute-start(bf16[2,16,512]{2,1,0:T(8,128)(2,1)S(1)} %get-tuple-element.201.refs_6_), channel_id=1, source_target_pairs={{0,8},{1,9},{2,10},{3,11},{4,12},{5,13},{6,14},{7,15},{8,0},{9,1},... | collective-permute-start | bytes 98312 | tf_op jit(solution)/shard_map/ppermute | solution.py:88
  139.3 5.0 %collective-permute-start.81 = (bf16[2,16,512]{2,1,0:T(8,128)(2,1)S(1)}, bf16[2,16,512]{2,1,0:T(8,128)(2,1)S(1)}, u32[]{:S(2)}, u32[]{:S(2)}) collective-permute-start(bf16[2,16,512]{2,1,0:T(8,128)(2,1)S(1)} %get-tuple-element.206), channel_id=1, source_target_pairs={{0,6},{1,7},{2,4},{3,5},{4,2},{5,3},{6,0},{7,1},{8,9},{9,8},{10,11... | collective-permute-start | bytes 98312 | tf_op jit(solution)/shard_map/ppermute | solution.py:31
  141.2 3.9 %collective-permute-start.83 = (bf16[2,16,512]{2,1,0:T(8,128)(2,1)S(1)}, bf16[2,16,512]{2,1,0:T(8,128)(2,1)S(1)}, u32[]{:S(2)}, u32[]{:S(2)}) collective-permute-start(bf16[2,16,512]{2,1,0:T(8,128)(2,1)S(1)} %get-tuple-element.206), channel_id=1, source_target_pairs={{0,4},{1,5},{2,6},{3,7},{4,0},{5,1},{6,2},{7,3},{8,9},{9,8},{10,11... | collective-permute-start | bytes 98312 | tf_op jit(solution)/shard_map/ppermute | solution.py:31
  141.7 3.9 %collective-permute-start.84 = (bf16[2,16,512]{2,1,0:T(8,128)(2,1)S(1)}, bf16[2,16,512]{2,1,0:T(8,128)(2,1)S(1)}, u32[]{:S(2)}, u32[]{:S(2)}) collective-permute-start(bf16[2,16,512]{2,1,0:T(8,128)(2,1)S(1)} %get-tuple-element.206), channel_id=1, source_target_pairs={{0,2},{1,3},{2,0},{3,1},{4,6},{5,7},{6,4},{7,5},{8,9},{9,8},{10,11... | collective-permute-start | bytes 98312 | tf_op jit(solution)/shard_map/ppermute | solution.py:31
  144.3 1.4 collective-permute-start.82
  147.5 5.3 %collective-permute-start.86 = (bf16[2,2,16,512]{3,2,1,0:T(8,128)(2,1)S(1)}, bf16[2,2,16,512]{3,2,1,0:T(8,128)(2,1)S(1)}, u32[]{:S(2)}, u32[]{:S(2)}) collective-permute-start(bf16[2,2,16,512]{3,2,1,0:T(8,128)(2,1)S(1)} %get-tuple-element.212), channel_id=1, source_target_pairs={{0,6},{1,7},{2,4},{3,5},{4,2},{5,3},{6,0},{7,1},{8,14},{9,15},{10,... | collective-permute-start | bytes 196616 | tf_op jit(solution)/shard_map/ppermute | solution.py:31
  149.6 4.5 %collective-permute-start.88 = (bf16[2,2,16,512]{3,2,1,0:T(8,128)(2,1)S(1)}, bf16[2,2,16,512]{3,2,1,0:T(8,128)(2,1)S(1)}, u32[]{:S(2)}, u32[]{:S(2)}) collective-permute-start(bf16[2,2,16,512]{3,2,1,0:T(8,128)(2,1)S(1)} %get-tuple-element.212), channel_id=1, source_target_pairs={{0,4},{1,5},{2,6},{3,7},{4,0},{5,1},{6,2},{7,3},{8,12},{9,13},{10,... | collective-permute-start | bytes 196616 | tf_op jit(solution)/shard_map/ppermute | solution.py:31
  150.1 4.3 %collective-permute-start.89 = (bf16[2,2,16,512]{3,2,1,0:T(8,128)(2,1)S(1)}, bf16[2,2,16,512]{3,2,1,0:T(8,128)(2,1)S(1)}, u32[]{:S(2)}, u32[]{:S(2)}) collective-permute-start(bf16[2,2,16,512]{3,2,1,0:T(8,128)(2,1)S(1)} %get-tuple-element.212), channel_id=1, source_target_pairs={{0,2},{1,3},{2,0},{3,1},{4,6},{5,7},{6,4},{7,5},{8,10},{9,11},{10,... | collective-permute-start | bytes 196616 | tf_op jit(solution)/shard_map/ppermute | solution.py:31
  152.8 2.4 %collective-permute-start.87 = (bf16[2,2,2,16,512]{4,3,2,1,0:T(8,128)(2,1)S(1)}, bf16[2,2,2,16,512]{4,3,2,1,0:T(8,128)(2,1)S(1)}, u32[]{:S(2)}, u32[]{:S(2)}) collective-permute-start(bf16[2,2,2,16,512]{4,3,2,1,0:T(8,128)(2,1)S(1)} %pad_maximum_fusion.mine_ref), channel_id=1, source_target_pairs={{0,1},{1,0},{2,3},{3,2},{4,5},{5,4},{6,7},{7,6},{8,9},{9,8},{10,11... | collective-permute-start | bytes 393224 | tf_op jit(solution)/shard_map/ppermute | solution.py:31
  154.4 1.4 collective-permute-start.90
  (27 other events, 34.5 us)

commit v7 on v6

--- a/solution.py
+++ b/solution.py
@@ -455,7 +455,14 @@
     return found
 
 
-def first_pick_kernel(sources, mine_ref, rows_ref, picked_ref, chosen_ref):
+def first_pick_kernel(sources, mine_ref, rows_ref, *refs):
+    kepts, (picked_ref, chosen_ref, fronts_ref, sems) = refs[:-4], refs[-4:]
+    copies = [
+        pltpu.make_async_copy(kept_ref, fronts_ref.at[panel], sems.at[panel])
+        for panel, kept_ref in enumerate(kepts)
+    ]
+    for copy in copies:
+        copy.start()
     (origins, _), (_, lasts) = sources(lax.axis_index("xy"))
     for panel, value in enumerate(picks(mine_ref, rows_ref, origins, None)):
         picked_ref[panel] = value
@@ -465,6 +472,8 @@
             rows = origin * share + lax.broadcasted_iota(jnp.int32, (share, bound), 0)
             hits = jnp.where(rows == rows_ref[pl.ds(panel, 1), :], 1.0, 0.0)
             chosen_ref[panel, index] = hits.astype(jnp.bfloat16)
+    for copy in copies:
+        copy.wait()
 
 
 def inner_kernel(
@@ -616,7 +625,6 @@
                 mask=masks[panel], scale=scale, addend=addend,
             )
 
-    fronts = jnp.stack(kept)
 
     def pick(which, parts, *picked):
         return in_kernel(
@@ -627,17 +635,23 @@
         )[0]
 
     def first_pick(mine):
-        return in_kernel(
+        last_count = peers // 2 - mine.shape[0]
+        operands = [mine, rows_held, *kept]
+        return pl.pallas_call(
             functools.partial(first_pick_kernel, within),
-            [
-                ((panel_count, 2 * side_count, bound), jnp.float32),
-                ((panel_count, peers // 2 - mine.shape[0], share, bound), jnp.bfloat16),
-            ],
-            [resident(mine), resident(rows_held)],
-            moved=2**22,
-        )
-
-    pieces, (picked, chosen), _ = gathered_within(message, None, first_pick)
+            out_shape=(
+                pltpu.VMEM((panel_count, 2 * side_count, bound), jnp.float32),
+                pltpu.VMEM((panel_count, last_count, share, bound), jnp.bfloat16),
+                jax.ShapeDtypeStruct((panel_count, 2, side_count, share), jnp.float32),
+            ),
+            in_specs=[IN_VMEM] * len(operands),
+            out_specs=(IN_VMEM, IN_VMEM, IN_HBM),
+            scratch_shapes=[pltpu.SemaphoreType.DMA((panel_count,))],
+            compiler_params=pltpu.CompilerParams(vmem_limit_bytes=16 * 2**20),
+            cost_estimate=pl.CostEstimate(flops=0, bytes_accessed=2**22, transcendentals=0),
+        )(*[resident(value) for value in operands])
+
+    pieces, (picked, chosen, fronts), _ = gathered_within(message, None, first_pick)
     (_, other), (more, last) = pieces
     picked = pick([(0, 1), (1, 0)], [other, more], picked)
     operands = [picked, last, chosen, coupling_held, inverse_held, solved]

time: 158 us -> 158 us (level)
    pallas_call x54 -> x53, Pallas kernels: 20.2 us -> 19.8 us  [in_kernel(): pl.pallas_call(body, out_shape=tuple((pltpu.VMEM(shape, dtype) for shape,...]
  transfers between devices with their start and end apart: 91 -> 91, of which waited for: 60 -> 61; matrix products, arithmetic and copies ran while one was open for 1% -> 0% of each run, Pallas kernels for 9% -> 9%
where the time goes in v7:
time: 158 us
  starting transfers between devices  88.7 us (56%)
  waiting for transfers between devices  44.5 us (28%)
  Pallas kernels  22.4 us (14%)
  between operations  1.61 us (1%)
    ppermute x24, starting transfers between devices, across(): return lax.ppermute(message, ('gz', 'xy'), pairs)  54.7 us
    ppermute x67, starting transfers between devices, swapped(): return lax.ppermute(shard, ('gz', 'xy'), pairs)  34 us
    ppermute x67, waiting for transfers between devices, swapped(): return lax.ppermute(shard, ('gz', 'xy'), pairs)  31.6 us
    pallas_call x53, Pallas kernels, in_kernel(): pl.pallas_call(body, out_shape=tuple((pltpu.VMEM(shape, dtype) for shape,...  19.8 us
    ppermute x24, waiting for transfers between devices, across(): return lax.ppermute(message, ('gz', 'xy'), pairs)  12.9 us
  transfers between devices with their start and end apart: 91, of which 61 were waited for; matrix products, arithmetic and copies ran while one was open for 0% of the time, Pallas kernels for 9%

profile of v7, /device:TPU:0, one launch (start us, length us, event | category | flops | bytes accessed | tf_op | source)
XLA Modules:
  0.0 157.6 jit_solution(2150609812312310194)
XLA Ops:
  0.6 3.3 %shard_map.95 = (f32[2,2,16,512]{3,2,1,0:T(8,128)S(1)}, bf16[80,256]{1,0:T(8,128)(2,1)S(1)}, f32[2,2,16,512]{3,2,1,0:T(8,128)}, bf16[2,1,2,512,512]{4,3,2,1,0:T(...) custom-call(f32[2,2,16,512]{3,2,1,0:T(8,128)} %refs_0_.1, ...), custom_call_target="tpu_custom_call" | custom-call | tf_op jit(solution)/shard_map/pallas_call | solution.py:109
  3.9 4.0 %collective-permute-start = (bf16[80,256]{1,0:T(8,128)(2,1)S(1)}, bf16[80,256]{1,0:T(8,128)(2,1)S(1)}, u32[]{:S(2)}, u32[]{:S(2)}) collective-permute-start(bf16[80,256]{1,0:T(8,128)(2,1)S(1)} %get-tuple-element.116.after_ref), channel_id=1, source_target_pairs={{0,6},{1,7},{2,4},{3,5},{4,2},{5,3},{6,0},{7,1},{8,14},{9,15},{10,... | collective-permute-start | bytes 122888 | tf_op jit(solution)/shard_map/ppermute | solution.py:31
  8.5 3.5 %shard_map.97.refs_1_.refs_2_.schur_ref = bf16[2,4096,512]{2,1,0:T(8,128)(2,1)S(1)} custom-call(bf16[2,2,4096,512]{3,2,1,0:T(8,128)(2,1)} %refs_4_.3, bf16[80,256]{1,0:T(8,128)(2,1)S(1)} %get-tuple-element.116.after_ref), custom_call_target="tpu_custom_call" | custom-call | bytes 8388608 | tf_op jit(solution)/shard_map/pallas_call | solution.py:109
  12.9 0.7 collective-permute-done.1.refs_0_.refs_1_
  14.0 0.9 shard_map.99
  14.9 2.8 %collective-permute-start.7 = (bf16[2,16,512]{2,1,0:T(8,128)(2,1)S(1)}, bf16[2,16,512]{2,1,0:T(8,128)(2,1)S(1)}, u32[]{:S(2)}, u32[]{:S(2)}) collective-permute-start(bf16[2,16,512]{2,1,0:T(8,128)(2,1)S(1)} %get-tuple-element.121.refs_5_.refs_7_), channel_id=1, source_target_pairs={{0,6},{1,7},{2,4},{3,5},{4,2},{5,3},{6,0},{7,1},{8,14},{9,15},{10,... | collective-permute-start | bytes 98312 | tf_op jit(solution)/shard_map/ppermute | solution.py:31
  18.5 3.8 %shard_map.101 = (f32[2,16,512]{2,1,0:T(8,128)S(1)}, bf16[2,4096,512]{2,1,0:T(8,128)(2,1)S(1)}) custom-call(f32[1,512]{1,0:T(1,128)S(1)} %get-tuple-element.123.mask_ref.refs_3_, f32[2,2,16,512]{3,2,1,0:T(8,128)S(1)} %get-tuple-element.120.source_ref, bf16[2,80,256]{2,1,0:T(8,128)(2,1)S(1)} %pad_maximum_fusion.2.refs_0_.one_ref, ...), custom_call_target="tpu_custom_call" | custom-call | bytes 8388608 | tf_op jit(solution)/shard_map/pallas_call | solution.py:109
  23.6 0.8 shard_map.103.refs_0_
  25.0 2.9 %collective-permute-start.10 = (bf16[2,16,512]{2,1,0:T(8,128)(2,1)S(1)}, bf16[2,16,512]{2,1,0:T(8,128)(2,1)S(1)}, u32[]{:S(2)}, u32[]{:S(2)}) collective-permute-start(bf16[2,16,512]{2,1,0:T(8,128)(2,1)S(1)} %get-tuple-element.139.refs_5_), channel_id=1, source_target_pairs={{0,6},{1,7},{2,4},{3,5},{4,2},{5,3},{6,0},{7,1},{8,9},{9,8},{10,11... | collective-permute-start | bytes 98312 | tf_op jit(solution)/shard_map/ppermute | solution.py:31
  28.5 1.3 collective-permute-done.10
  30.4 1.4 collective-permute-done.12
  32.4 0.8 shard_map.106.refs_0_
  34.1 1.3 collective-permute-start.15
  35.4 1.3 collective-permute-start.16
  36.7 1.3 collective-permute-start.18
  38.4 1.2 collective-permute-done.18
  39.6 2.4 %collective-permute-done.19 = bf16[2,16,512]{2,1,0:T(8,128)(2,1)S(1)} collective-permute-done((bf16[2,16,512]{2,1,0:T(8,128)(2,1)S(1)}, bf16[2,16,512]{2,1,0:T(8,128)(2,1)S(1)}, u32[]{:S(2)}, u32[]{:S(2)}) %collective-permute-start.19) | collective-permute-done | bytes 32800 | tf_op jit(solution)/shard_map/ppermute | solution.py:88
  42.1 1.2 collective-permute-done.20.refs_1_
  46.4 0.7 collective-permute-start.26
  47.1 0.7 collective-permute-start.27
  47.7 0.7 collective-permute-start.29
  50.0 1.0 collective-permute-done.31.refs_1_
  51.0 1.5 collective-permute-start.32
  52.8 1.7 %collective-permute-start.35 = (bf16[2,16,512]{2,1,0:T(8,128)(2,1)S(1)}, bf16[2,16,512]{2,1,0:T(8,128)(2,1)S(1)}, u32[]{:S(2)}, u32[]{:S(2)}) collective-permute-start(bf16[2,16,512]{2,1,0:T(8,128)(2,1)S(1)} %get-tuple-element.160.refs_5_), channel_id=1, source_target_pairs={{0,2},{1,3},{2,0},{3,1},{4,6},{5,7},{6,4},{7,5},{8,9},{9,8},{10,11... | collective-permute-start | bytes 98312 | tf_op jit(solution)/shard_map/ppermute | solution.py:31
  54.5 1.3 collective-permute-done.32
  57.2 0.9 collective-permute-done.36.refs_1_
  58.0 10.1 %collective-permute-start.37 = (bf16[2,16,512]{2,1,0:T(8,128)(2,1)S(1)}, bf16[2,16,512]{2,1,0:T(8,128)(2,1)S(1)}, u32[]{:S(2)}, u32[]{:S(2)}) collective-permute-start(bf16[2,16,512]{2,1,0:T(8,128)(2,1)S(1)} %get-tuple-element.165.refs_7_), channel_id=1, source_target_pairs={{0,14},{1,15},{2,12},{3,13},{4,10},{5,11},{6,8},{7,9},{16,30},{17,... | collective-permute-start | bytes 98312 | tf_op jit(solution)/shard_map/ppermute | solution.py:88
  68.1 1.3 collective-permute-start.38
  69.4 1.3 collective-permute-start.40
  71.1 1.2 collective-permute-done.40
  72.3 2.4 %collective-permute-done.41 = bf16[2,16,512]{2,1,0:T(8,128)(2,1)S(1)} collective-permute-done((bf16[2,16,512]{2,1,0:T(8,128)(2,1)S(1)}, bf16[2,16,512]{2,1,0:T(8,128)(2,1)S(1)}, u32[]{:S(2)}, u32[]{:S(2)}) %collective-permute-start.41) | collective-permute-done | bytes 32800 | tf_op jit(solution)/shard_map/ppermute | solution.py:88
  74.8 1.2 collective-permute-done.42.refs_1_
  82.1 1.3 collective-permute-start.53
  83.4 1.3 collective-permute-start.54
  84.7 1.3 collective-permute-start.56
  86.0 9.9 %collective-permute-start.57 = (bf16[2,16,512]{2,1,0:T(8,128)(2,1)S(1)}, bf16[2,16,512]{2,1,0:T(8,128)(2,1)S(1)}, u32[]{:S(2)}, u32[]{:S(2)}) collective-permute-start(bf16[2,16,512]{2,1,0:T(8,128)(2,1)S(1)} %get-tuple-element.182.refs_6_), channel_id=1, source_target_pairs={{0,8},{1,9},{2,10},{3,11},{4,12},{5,13},{6,14},{7,15},{8,0},{9,1},... | collective-permute-start | bytes 98312 | tf_op jit(solution)/shard_map/ppermute | solution.py:88
  96.5 1.7 %collective-permute-done.56 = bf16[2,16,512]{2,1,0:T(8,128)(2,1)S(1)} collective-permute-done((bf16[2,16,512]{2,1,0:T(8,128)(2,1)S(1)}, bf16[2,16,512]{2,1,0:T(8,128)(2,1)S(1)}, u32[]{:S(2)}, u32[]{:S(2)}) %collective-permute-start.56) | collective-permute-done | bytes 32800 | tf_op jit(solution)/shard_map/ppermute | solution.py:88
  98.4 1.2 collective-permute-done.58.refs_1_
  99.6 1.1 collective-permute-start.59
  100.7 1.5 collective-permute-start.61
  102.2 0.9 collective-permute-start.62
  103.1 1.4 collective-permute-done.59
  104.8 1.3 collective-permute-done.62
  106.2 1.2 collective-permute-done.63.refs_1_
  107.4 0.7 collective-permute-start.64
  108.1 0.7 collective-permute-start.65
  108.7 0.7 collective-permute-start.67
  111.0 1.0 collective-permute-done.69.refs_1_
  115.1 1.3 collective-permute-start.75
  116.4 1.3 collective-permute-start.76
  117.7 1.3 collective-permute-start.78
  119.0 16.0 %collective-permute-start.79 = (bf16[2,16,512]{2,1,0:T(8,128)(2,1)S(1)}, bf16[2,16,512]{2,1,0:T(8,128)(2,1)S(1)}, u32[]{:S(2)}, u32[]{:S(2)}) collective-permute-start(bf16[2,16,512]{2,1,0:T(8,128)(2,1)S(1)} %get-tuple-element.203.refs_6_), channel_id=1, source_target_pairs={{0,8},{1,9},{2,10},{3,11},{4,12},{5,13},{6,14},{7,15},{8,0},{9,1},... | collective-permute-start | bytes 98312 | tf_op jit(solution)/shard_map/ppermute | solution.py:88
  134.9 0.8 collective-permute-done.75
  137.8 0.8 shard_map.142.refs_0_
  139.3 1.9 %collective-permute-start.81 = (bf16[2,16,512]{2,1,0:T(8,128)(2,1)S(1)}, bf16[2,16,512]{2,1,0:T(8,128)(2,1)S(1)}, u32[]{:S(2)}, u32[]{:S(2)}) collective-permute-start(bf16[2,16,512]{2,1,0:T(8,128)(2,1)S(1)} %get-tuple-element.208), channel_id=1, source_target_pairs={{0,6},{1,7},{2,4},{3,5},{4,2},{5,3},{6,0},{7,1},{8,9},{9,8},{10,11... | collective-permute-start | bytes 98312 | tf_op jit(solution)/shard_map/ppermute | solution.py:31
  141.7 1.1 collective-permute-start.84
  142.8 1.4 collective-permute-done.81
  145.8 0.8 shard_map.145.products_ref
  147.5 2.1 %collective-permute-start.86 = (bf16[2,2,16,512]{3,2,1,0:T(8,128)(2,1)S(1)}, bf16[2,2,16,512]{3,2,1,0:T(8,128)(2,1)S(1)}, u32[]{:S(2)}, u32[]{:S(2)}) collective-permute-start(bf16[2,2,16,512]{3,2,1,0:T(8,128)(2,1)S(1)} %get-tuple-element.214), channel_id=1, source_target_pairs={{0,6},{1,7},{2,4},{3,5},{4,2},{5,3},{6,0},{7,1},{8,14},{9,15},{10,... | collective-permute-start | bytes 196616 | tf_op jit(solution)/shard_map/ppermute | solution.py:31
  150.1 0.9 collective-permute-start.89
  151.0 1.7 %collective-permute-done.86 = bf16[2,2,16,512]{3,2,1,0:T(8,128)(2,1)S(1)} collective-permute-done((bf16[2,2,16,512]{3,2,1,0:T(8,128)(2,1)S(1)}, bf16[2,2,16,512]{3,2,1,0:T(8,128)(2,1)S(1)}, u32[]{:S(2)}, u32[]{:S(2)}) %collective-permute-start.86) | collective-permute-done | bytes 65568 | tf_op jit(solution)/shard_map/ppermute | solution.py:31
  152.9 1.0 shard_map.147
  155.0 0.8 collective-permute-done.90.last_ref
  155.8 1.6 %shard_map.149 = f32[2,2,16,512]{3,2,1,0:T(8,128)} custom-call(f32[2,32,256]{2,1,0:T(8,128)S(1)} %shard_map.148.picked_ref, bf16[2,2,2,16,512]{4,3,2,1,0:T(8,128)(2,1)S(1)} %collective-permute-done.90.last_ref, bf16[2,2,512,256]{3,2,1,0:T(8,128)(2,1)S(1)} %get-tuple-element.223.chosen_ref, bf16[2,1,2,512,256]{4,3,2,1,0:T(8,128)(2,1)S(1)} %get-tuple-element.224.coupling_ref, ...), custom_call_target="tpu_custom_call" | custom-call | tf_op jit(solution)/shard_map/pallas_call | solution.py:658
  (213 shorter events, 33.1 us)
Async XLA Ops:
  3.9 8.1 %collective-permute-start = (bf16[80,256]{1,0:T(8,128)(2,1)S(1)}, bf16[80,256]{1,0:T(8,128)(2,1)S(1)}, u32[]{:S(2)}, u32[]{:S(2)}) collective-permute-start(bf16[80,256]{1,0:T(8,128)(2,1)S(1)} %get-tuple-element.116.after_ref), channel_id=1, source_target_pairs={{0,6},{1,7},{2,4},{3,5},{4,2},{5,3},{6,0},{7,1},{8,14},{9,15},{10,... | collective-permute-start | bytes 122888 | tf_op jit(solution)/shard_map/ppermute | solution.py:31
  7.9 4.4 %collective-permute-start.2 = (bf16[80,256]{1,0:T(8,128)(2,1)S(1)}, bf16[80,256]{1,0:T(8,128)(2,1)S(1)}, u32[]{:S(2)}, u32[]{:S(2)}) collective-permute-start(bf16[80,256]{1,0:T(8,128)(2,1)S(1)} %get-tuple-element.116.after_ref), channel_id=1, source_target_pairs={{0,4},{1,5},{2,6},{3,7},{4,0},{5,1},{6,2},{7,3},{8,12},{9,13},{10,... | collective-permute-start | bytes 122888 | tf_op jit(solution)/shard_map/ppermute | solution.py:31
  8.4 4.0 %collective-permute-start.3 = (bf16[80,256]{1,0:T(8,128)(2,1)S(1)}, bf16[80,256]{1,0:T(8,128)(2,1)S(1)}, u32[]{:S(2)}, u32[]{:S(2)}) collective-permute-start(bf16[80,256]{1,0:T(8,128)(2,1)S(1)} %get-tuple-element.116.after_ref), channel_id=1, source_target_pairs={{0,2},{1,3},{2,0},{3,1},{4,6},{5,7},{6,4},{7,5},{8,10},{9,11},{10,... | collective-permute-start | bytes 122888 | tf_op jit(solution)/shard_map/ppermute | solution.py:31
  12.4 1.6 %collective-permute-start.4 = (bf16[2,80,256]{2,1,0:T(8,128)(2,1)S(1)}, bf16[2,80,256]{2,1,0:T(8,128)(2,1)S(1)}, u32[]{:S(2)}, u32[]{:S(2)}) collective-permute-start(bf16[2,80,256]{2,1,0:T(8,128)(2,1)S(1)} %pad_maximum_fusion.3.refs_1_.refs_2_.two_ref), channel_id=1, source_target_pairs={{0,1},{1,0},{2,3},{3,2},{4,5},{5,4},{6,7},{7,6},{8,9},{9,8},{10,11... | collective-permute-start | bytes 245768 | tf_op jit(solution)/shard_map/ppermute | solution.py:31
  14.9 7.4 %collective-permute-start.7 = (bf16[2,16,512]{2,1,0:T(8,128)(2,1)S(1)}, bf16[2,16,512]{2,1,0:T(8,128)(2,1)S(1)}, u32[]{:S(2)}, u32[]{:S(2)}) collective-permute-start(bf16[2,16,512]{2,1,0:T(8,128)(2,1)S(1)} %get-tuple-element.121.refs_5_.refs_7_), channel_id=1, source_target_pairs={{0,6},{1,7},{2,4},{3,5},{4,2},{5,3},{6,0},{7,1},{8,14},{9,15},{10,... | collective-permute-start | bytes 98312 | tf_op jit(solution)/shard_map/ppermute | solution.py:31
  17.8 5.1 %collective-permute-start.5 = (bf16[2,16,512]{2,1,0:T(8,128)(2,1)S(1)}, bf16[2,16,512]{2,1,0:T(8,128)(2,1)S(1)}, u32[]{:S(2)}, u32[]{:S(2)}) collective-permute-start(bf16[2,16,512]{2,1,0:T(8,128)(2,1)S(1)} %get-tuple-element.121.refs_5_.refs_7_), channel_id=1, source_target_pairs={{0,4},{1,5},{2,6},{3,7},{4,0},{5,1},{6,2},{7,3},{8,12},{9,13},{10,... | collective-permute-start | bytes 98312 | tf_op jit(solution)/shard_map/ppermute | solution.py:31
  18.4 4.5 %collective-permute-start.6 = (bf16[2,16,512]{2,1,0:T(8,128)(2,1)S(1)}, bf16[2,16,512]{2,1,0:T(8,128)(2,1)S(1)}, u32[]{:S(2)}, u32[]{:S(2)}) collective-permute-start(bf16[2,16,512]{2,1,0:T(8,128)(2,1)S(1)} %get-tuple-element.121.refs_5_.refs_7_), channel_id=1, source_target_pairs={{0,2},{1,3},{2,0},{3,1},{4,6},{5,7},{6,4},{7,5},{8,10},{9,11},{10,... | collective-permute-start | bytes 98312 | tf_op jit(solution)/shard_map/ppermute | solution.py:31
  22.3 1.3 collective-permute-start.8
  22.9 1.6 collective-permute-start.9
  25.0 4.9 %collective-permute-start.10 = (bf16[2,16,512]{2,1,0:T(8,128)(2,1)S(1)}, bf16[2,16,512]{2,1,0:T(8,128)(2,1)S(1)}, u32[]{:S(2)}, u32[]{:S(2)}) collective-permute-start(bf16[2,16,512]{2,1,0:T(8,128)(2,1)S(1)} %get-tuple-element.139.refs_5_), channel_id=1, source_target_pairs={{0,6},{1,7},{2,4},{3,5},{4,2},{5,3},{6,0},{7,1},{8,9},{9,8},{10,11... | collective-permute-start | bytes 98312 | tf_op jit(solution)/shard_map/ppermute | solution.py:31
  27.9 3.9 %collective-permute-start.12 = (bf16[2,16,512]{2,1,0:T(8,128)(2,1)S(1)}, bf16[2,16,512]{2,1,0:T(8,128)(2,1)S(1)}, u32[]{:S(2)}, u32[]{:S(2)}) collective-permute-start(bf16[2,16,512]{2,1,0:T(8,128)(2,1)S(1)} %get-tuple-element.139.refs_5_), channel_id=1, source_target_pairs={{0,4},{1,5},{2,6},{3,7},{4,0},{5,1},{6,2},{7,3},{8,9},{9,8},{10,11... | collective-permute-start | bytes 98312 | tf_op jit(solution)/shard_map/ppermute | solution.py:31
  28.4 3.9 %collective-permute-start.13 = (bf16[2,16,512]{2,1,0:T(8,128)(2,1)S(1)}, bf16[2,16,512]{2,1,0:T(8,128)(2,1)S(1)}, u32[]{:S(2)}, u32[]{:S(2)}) collective-permute-start(bf16[2,16,512]{2,1,0:T(8,128)(2,1)S(1)} %get-tuple-element.139.refs_5_), channel_id=1, source_target_pairs={{0,2},{1,3},{2,0},{3,1},{4,6},{5,7},{6,4},{7,5},{8,9},{9,8},{10,11... | collective-permute-start | bytes 98312 | tf_op jit(solution)/shard_map/ppermute | solution.py:31
  29.9 2.5 %collective-permute-start.11 = (bf16[2,2,16,512]{3,2,1,0:T(8,128)(2,1)S(1)}, bf16[2,2,16,512]{3,2,1,0:T(8,128)(2,1)S(1)}, u32[]{:S(2)}, u32[]{:S(2)}) collective-permute-start(bf16[2,2,16,512]{3,2,1,0:T(8,128)(2,1)S(1)} %pad_maximum_fusion.6.refs_0_), channel_id=1, source_target_pairs={{0,1},{1,0},{2,3},{3,2},{4,5},{5,4},{6,7},{7,6},{8,9},{9,8},{10,11... | collective-permute-start | bytes 196616 | tf_op jit(solution)/shard_map/ppermute | solution.py:31
  32.3 1.3 collective-permute-start.14
  34.1 4.0 %collective-permute-start.15 = (bf16[2,16,512]{2,1,0:T(8,128)(2,1)S(1)}, bf16[2,16,512]{2,1,0:T(8,128)(2,1)S(1)}, u32[]{:S(2)}, u32[]{:S(2)}) collective-permute-start(bf16[2,16,512]{2,1,0:T(8,128)(2,1)S(1)} %get-tuple-element.144.refs_7_), channel_id=1, source_target_pairs={{0,14},{1,15},{2,12},{3,13},{4,10},{5,11},{6,8},{7,9},{16,30},{17,... | collective-permute-start | bytes 98312 | tf_op jit(solution)/shard_map/ppermute | solution.py:88
  35.4 2.9 %collective-permute-start.16 = (bf16[2,16,512]{2,1,0:T(8,128)(2,1)S(1)}, bf16[2,16,512]{2,1,0:T(8,128)(2,1)S(1)}, u32[]{:S(2)}, u32[]{:S(2)}) collective-permute-start(bf16[2,16,512]{2,1,0:T(8,128)(2,1)S(1)} %get-tuple-element.144.refs_7_), channel_id=1, source_target_pairs={{0,12},{1,13},{2,14},{3,15},{4,8},{5,9},{6,10},{7,11},{16,28},{17,... | collective-permute-start | bytes 98312 | tf_op jit(solution)/shard_map/ppermute | solution.py:88
  36.7 2.9 %collective-permute-start.18 = (bf16[2,16,512]{2,1,0:T(8,128)(2,1)S(1)}, bf16[2,16,512]{2,1,0:T(8,128)(2,1)S(1)}, u32[]{:S(2)}, u32[]{:S(2)}) collective-permute-start(bf16[2,16,512]{2,1,0:T(8,128)(2,1)S(1)} %get-tuple-element.144.refs_7_), channel_id=1, source_target_pairs={{0,10},{1,11},{2,8},{3,9},{4,14},{5,15},{6,12},{7,13},{16,26},{17,... | collective-permute-start | bytes 98312 | tf_op jit(solution)/shard_map/ppermute | solution.py:88
  38.0 4.0 %collective-permute-start.19 = (bf16[2,16,512]{2,1,0:T(8,128)(2,1)S(1)}, bf16[2,16,512]{2,1,0:T(8,128)(2,1)S(1)}, u32[]{:S(2)}, u32[]{:S(2)}) collective-permute-start(bf16[2,16,512]{2,1,0:T(8,128)(2,1)S(1)} %get-tuple-element.144.refs_7_), channel_id=1, source_target_pairs={{0,8},{1,9},{2,10},{3,11},{4,12},{5,13},{6,14},{7,15},{8,0},{9,1},... | collective-permute-start | bytes 98312 | tf_op jit(solution)/shard_map/ppermute | solution.py:88
  38.3 3.8 %collective-permute-start.17 = (bf16[2,2,16,512]{3,2,1,0:T(8,128)(2,1)S(1)}, bf16[2,2,16,512]{3,2,1,0:T(8,128)(2,1)S(1)}, u32[]{:S(2)}, u32[]{:S(2)}) collective-permute-start(bf16[2,2,16,512]{3,2,1,0:T(8,128)(2,1)S(1)} %multiply_convert_fusion.11.refs_0_), channel_id=1, source_target_pairs={{0,1},{1,0},{2,3},{3,2},{4,5},{5,4},{6,7},{7,6},{8,9},{9,8},{10,11... | collective-permute-start | bytes 196616 | tf_op jit(solution)/shard_map/ppermute | solution.py:31
  42.0 1.3 collective-permute-start.20
  44.6 1.3 collective-permute-start.22
  45.1 1.3 collective-permute-start.25
  46.4 2.2 %collective-permute-start.26 = (bf16[2,16,512]{2,1,0:T(8,128)(2,1)S(1)}, bf16[2,16,512]{2,1,0:T(8,128)(2,1)S(1)}, u32[]{:S(2)}, u32[]{:S(2)}) collective-permute-start(bf16[2,16,512]{2,1,0:T(8,128)(2,1)S(1)} %get-tuple-element.155.refs_7_), channel_id=1, source_target_pairs={{8,22},{9,23},{10,20},{11,21},{12,18},{13,19},{14,16},{15,17}} | collective-permute-start | bytes 98312 | tf_op jit(solution)/shard_map/ppermute | solution.py:88
  47.1 1.6 collective-permute-start.27
  47.7 1.3 collective-permute-start.29
  48.6 1.3 collective-permute-start.28
  49.7 1.3 collective-permute-start.31
  51.0 4.8 %collective-permute-start.32 = (bf16[2,16,512]{2,1,0:T(8,128)(2,1)S(1)}, bf16[2,16,512]{2,1,0:T(8,128)(2,1)S(1)}, u32[]{:S(2)}, u32[]{:S(2)}) collective-permute-start(bf16[2,16,512]{2,1,0:T(8,128)(2,1)S(1)} %get-tuple-element.160.refs_5_), channel_id=1, source_target_pairs={{0,6},{1,7},{2,4},{3,5},{4,2},{5,3},{6,0},{7,1},{8,9},{9,8},{10,11... | collective-permute-start | bytes 98312 | tf_op jit(solution)/shard_map/ppermute | solution.py:31
  52.5 3.9 %collective-permute-start.34 = (bf16[2,16,512]{2,1,0:T(8,128)(2,1)S(1)}, bf16[2,16,512]{2,1,0:T(8,128)(2,1)S(1)}, u32[]{:S(2)}, u32[]{:S(2)}) collective-permute-start(bf16[2,16,512]{2,1,0:T(8,128)(2,1)S(1)} %get-tuple-element.160.refs_5_), channel_id=1, source_target_pairs={{0,4},{1,5},{2,6},{3,7},{4,0},{5,1},{6,2},{7,3},{8,9},{9,8},{10,11... | collective-permute-start | bytes 98312 | tf_op jit(solution)/shard_map/ppermute | solution.py:31
  52.8 3.9 %collective-permute-start.35 = (bf16[2,16,512]{2,1,0:T(8,128)(2,1)S(1)}, bf16[2,16,512]{2,1,0:T(8,128)(2,1)S(1)}, u32[]{:S(2)}, u32[]{:S(2)}) collective-permute-start(bf16[2,16,512]{2,1,0:T(8,128)(2,1)S(1)} %get-tuple-element.160.refs_5_), channel_id=1, source_target_pairs={{0,2},{1,3},{2,0},{3,1},{4,6},{5,7},{6,4},{7,5},{8,9},{9,8},{10,11... | collective-permute-start | bytes 98312 | tf_op jit(solution)/shard_map/ppermute | solution.py:31
  55.8 1.3 collective-permute-start.33
  56.7 1.3 collective-permute-start.36
  58.0 12.8 %collective-permute-start.37 = (bf16[2,16,512]{2,1,0:T(8,128)(2,1)S(1)}, bf16[2,16,512]{2,1,0:T(8,128)(2,1)S(1)}, u32[]{:S(2)}, u32[]{:S(2)}) collective-permute-start(bf16[2,16,512]{2,1,0:T(8,128)(2,1)S(1)} %get-tuple-element.165.refs_7_), channel_id=1, source_target_pairs={{0,14},{1,15},{2,12},{3,13},{4,10},{5,11},{6,8},{7,9},{16,30},{17,... | collective-permute-start | bytes 98312 | tf_op jit(solution)/shard_map/ppermute | solution.py:88
  68.1 2.9 %collective-permute-start.38 = (bf16[2,16,512]{2,1,0:T(8,128)(2,1)S(1)}, bf16[2,16,512]{2,1,0:T(8,128)(2,1)S(1)}, u32[]{:S(2)}, u32[]{:S(2)}) collective-permute-start(bf16[2,16,512]{2,1,0:T(8,128)(2,1)S(1)} %get-tuple-element.165.refs_7_), channel_id=1, source_target_pairs={{0,12},{1,13},{2,14},{3,15},{4,8},{5,9},{6,10},{7,11},{16,28},{17,... | collective-permute-start | bytes 98312 | tf_op jit(solution)/shard_map/ppermute | solution.py:88
  69.4 2.9 %collective-permute-start.40 = (bf16[2,16,512]{2,1,0:T(8,128)(2,1)S(1)}, bf16[2,16,512]{2,1,0:T(8,128)(2,1)S(1)}, u32[]{:S(2)}, u32[]{:S(2)}) collective-permute-start(bf16[2,16,512]{2,1,0:T(8,128)(2,1)S(1)} %get-tuple-element.165.refs_7_), channel_id=1, source_target_pairs={{0,10},{1,11},{2,8},{3,9},{4,14},{5,15},{6,12},{7,13},{16,26},{17,... | collective-permute-start | bytes 98312 | tf_op jit(solution)/shard_map/ppermute | solution.py:88
  70.7 4.0 %collective-permute-start.41 = (bf16[2,16,512]{2,1,0:T(8,128)(2,1)S(1)}, bf16[2,16,512]{2,1,0:T(8,128)(2,1)S(1)}, u32[]{:S(2)}, u32[]{:S(2)}) collective-permute-start(bf16[2,16,512]{2,1,0:T(8,128)(2,1)S(1)} %get-tuple-element.165.refs_7_), channel_id=1, source_target_pairs={{0,8},{1,9},{2,10},{3,11},{4,12},{5,13},{6,14},{7,15},{8,0},{9,1},... | collective-permute-start | bytes 98312 | tf_op jit(solution)/shard_map/ppermute | solution.py:88
  71.0 3.8 %collective-permute-start.39 = (bf16[2,2,16,512]{3,2,1,0:T(8,128)(2,1)S(1)}, bf16[2,2,16,512]{3,2,1,0:T(8,128)(2,1)S(1)}, u32[]{:S(2)}, u32[]{:S(2)}) collective-permute-start(bf16[2,2,16,512]{3,2,1,0:T(8,128)(2,1)S(1)} %multiply_convert_fusion.7.refs_0_), channel_id=1, source_target_pairs={{0,1},{1,0},{2,3},{3,2},{4,5},{5,4},{6,7},{7,6},{8,9},{9,8},{10,11... | collective-permute-start | bytes 196616 | tf_op jit(solution)/shard_map/ppermute | solution.py:31
  74.7 1.3 collective-permute-start.42
  82.1 13.8 %collective-permute-start.53 = (bf16[2,16,512]{2,1,0:T(8,128)(2,1)S(1)}, bf16[2,16,512]{2,1,0:T(8,128)(2,1)S(1)}, u32[]{:S(2)}, u32[]{:S(2)}) collective-permute-start(bf16[2,16,512]{2,1,0:T(8,128)(2,1)S(1)} %get-tuple-element.182.refs_6_), channel_id=1, source_target_pairs={{8,6},{9,7},{10,4},{11,5},{12,2},{13,3},{14,0},{15,1},{24,22},{25,... | collective-permute-start | bytes 98312 | tf_op jit(solution)/shard_map/ppermute | solution.py:88
  83.4 13.0 %collective-permute-start.54 = (bf16[2,16,512]{2,1,0:T(8,128)(2,1)S(1)}, bf16[2,16,512]{2,1,0:T(8,128)(2,1)S(1)}, u32[]{:S(2)}, u32[]{:S(2)}) collective-permute-start(bf16[2,16,512]{2,1,0:T(8,128)(2,1)S(1)} %get-tuple-element.182.refs_6_), channel_id=1, source_target_pairs={{8,4},{9,5},{10,6},{11,7},{12,0},{13,1},{14,2},{15,3},{24,20},{25,... | collective-permute-start | bytes 98312 | tf_op jit(solution)/shard_map/ppermute | solution.py:88
  84.7 13.5 %collective-permute-start.56 = (bf16[2,16,512]{2,1,0:T(8,128)(2,1)S(1)}, bf16[2,16,512]{2,1,0:T(8,128)(2,1)S(1)}, u32[]{:S(2)}, u32[]{:S(2)}) collective-permute-start(bf16[2,16,512]{2,1,0:T(8,128)(2,1)S(1)} %get-tuple-element.182.refs_6_), channel_id=1, source_target_pairs={{8,2},{9,3},{10,0},{11,1},{12,6},{13,7},{14,4},{15,5},{24,18},{25,... | collective-permute-start | bytes 98312 | tf_op jit(solution)/shard_map/ppermute | solution.py:88
  86.0 12.2 %collective-permute-start.57 = (bf16[2,16,512]{2,1,0:T(8,128)(2,1)S(1)}, bf16[2,16,512]{2,1,0:T(8,128)(2,1)S(1)}, u32[]{:S(2)}, u32[]{:S(2)}) collective-permute-start(bf16[2,16,512]{2,1,0:T(8,128)(2,1)S(1)} %get-tuple-element.182.refs_6_), channel_id=1, source_target_pairs={{0,8},{1,9},{2,10},{3,11},{4,12},{5,13},{6,14},{7,15},{8,0},{9,1},... | collective-permute-start | bytes 98312 | tf_op jit(solution)/shard_map/ppermute | solution.py:88
  96.4 1.9 %collective-permute-start.55 = (bf16[2,2,16,512]{3,2,1,0:T(8,128)(2,1)S(1)}, bf16[2,2,16,512]{3,2,1,0:T(8,128)(2,1)S(1)}, u32[]{:S(2)}, u32[]{:S(2)}) collective-permute-start(bf16[2,2,16,512]{3,2,1,0:T(8,128)(2,1)S(1)} %multiply_convert_fusion.5.refs_0_), channel_id=1, source_target_pairs={{0,1},{1,0},{2,3},{3,2},{4,5},{5,4},{6,7},{7,6},{8,9},{9,8},{10,11... | collective-permute-start | bytes 196616 | tf_op jit(solution)/shard_map/ppermute | solution.py:31
  99.6 4.9 %collective-permute-start.59 = (bf16[2,16,512]{2,1,0:T(8,128)(2,1)S(1)}, bf16[2,16,512]{2,1,0:T(8,128)(2,1)S(1)}, u32[]{:S(2)}, u32[]{:S(2)}) collective-permute-start(bf16[2,16,512]{2,1,0:T(8,128)(2,1)S(1)} %get-tuple-element.188.refs_6_), channel_id=1, source_target_pairs={{0,6},{1,7},{2,4},{3,5},{4,2},{5,3},{6,0},{7,1},{8,9},{9,8},{10,11... | collective-permute-start | bytes 98312 | tf_op jit(solution)/shard_map/ppermute | solution.py:31
  100.7 4.0 %collective-permute-start.61 = (bf16[2,16,512]{2,1,0:T(8,128)(2,1)S(1)}, bf16[2,16,512]{2,1,0:T(8,128)(2,1)S(1)}, u32[]{:S(2)}, u32[]{:S(2)}) collective-permute-start(bf16[2,16,512]{2,1,0:T(8,128)(2,1)S(1)} %get-tuple-element.188.refs_6_), channel_id=1, source_target_pairs={{0,4},{1,5},{2,6},{3,7},{4,0},{5,1},{6,2},{7,3},{8,9},{9,8},{10,11... | collective-permute-start | bytes 98312 | tf_op jit(solution)/shard_map/ppermute | solution.py:31
  102.2 3.9 %collective-permute-start.62 = (bf16[2,16,512]{2,1,0:T(8,128)(2,1)S(1)}, bf16[2,16,512]{2,1,0:T(8,128)(2,1)S(1)}, u32[]{:S(2)}, u32[]{:S(2)}) collective-permute-start(bf16[2,16,512]{2,1,0:T(8,128)(2,1)S(1)} %get-tuple-element.188.refs_6_), channel_id=1, source_target_pairs={{0,2},{1,3},{2,0},{3,1},{4,6},{5,7},{6,4},{7,5},{8,9},{9,8},{10,11... | collective-permute-start | bytes 98312 | tf_op jit(solution)/shard_map/ppermute | solution.py:31
  104.5 1.7 %collective-permute-start.60 = (bf16[2,2,16,512]{3,2,1,0:T(8,128)(2,1)S(1)}, bf16[2,2,16,512]{3,2,1,0:T(8,128)(2,1)S(1)}, u32[]{:S(2)}, u32[]{:S(2)}) collective-permute-start(bf16[2,2,16,512]{3,2,1,0:T(8,128)(2,1)S(1)} %pad_maximum_fusion.16.refs_0_), channel_id=1, source_target_pairs={{0,1},{1,0},{2,3},{3,2},{4,5},{5,4},{6,7},{7,6},{8,9},{9,8},{10,11... | collective-permute-start | bytes 196616 | tf_op jit(solution)/shard_map/ppermute | solution.py:31
  107.4 2.2 %collective-permute-start.64 = (bf16[2,16,512]{2,1,0:T(8,128)(2,1)S(1)}, bf16[2,16,512]{2,1,0:T(8,128)(2,1)S(1)}, u32[]{:S(2)}, u32[]{:S(2)}) collective-permute-start(bf16[2,16,512]{2,1,0:T(8,128)(2,1)S(1)} %get-tuple-element.193.refs_6_), channel_id=1, source_target_pairs={{16,14},{17,15},{18,12},{19,13},{20,10},{21,11},{22,8},{23,9}} | collective-permute-start | bytes 98312 | tf_op jit(solution)/shard_map/ppermute | solution.py:88
  108.1 1.6 collective-permute-start.65
  108.7 1.3 collective-permute-start.67
  109.7 1.3 collective-permute-start.66
  115.1 20.7 %collective-permute-start.75 = (bf16[2,16,512]{2,1,0:T(8,128)(2,1)S(1)}, bf16[2,16,512]{2,1,0:T(8,128)(2,1)S(1)}, u32[]{:S(2)}, u32[]{:S(2)}) collective-permute-start(bf16[2,16,512]{2,1,0:T(8,128)(2,1)S(1)} %get-tuple-element.203.refs_6_), channel_id=1, source_target_pairs={{8,6},{9,7},{10,4},{11,5},{12,2},{13,3},{14,0},{15,1},{24,22},{25,... | collective-permute-start | bytes 98312 | tf_op jit(solution)/shard_map/ppermute | solution.py:88
  116.4 20.0 %collective-permute-start.76 = (bf16[2,16,512]{2,1,0:T(8,128)(2,1)S(1)}, bf16[2,16,512]{2,1,0:T(8,128)(2,1)S(1)}, u32[]{:S(2)}, u32[]{:S(2)}) collective-permute-start(bf16[2,16,512]{2,1,0:T(8,128)(2,1)S(1)} %get-tuple-element.203.refs_6_), channel_id=1, source_target_pairs={{8,4},{9,5},{10,6},{11,7},{12,0},{13,1},{14,2},{15,3},{24,20},{25,... | collective-permute-start | bytes 98312 | tf_op jit(solution)/shard_map/ppermute | solution.py:88
  117.7 19.8 %collective-permute-start.78 = (bf16[2,16,512]{2,1,0:T(8,128)(2,1)S(1)}, bf16[2,16,512]{2,1,0:T(8,128)(2,1)S(1)}, u32[]{:S(2)}, u32[]{:S(2)}) collective-permute-start(bf16[2,16,512]{2,1,0:T(8,128)(2,1)S(1)} %get-tuple-element.203.refs_6_), channel_id=1, source_target_pairs={{8,2},{9,3},{10,0},{11,1},{12,6},{13,7},{14,4},{15,5},{24,18},{25,... | collective-permute-start | bytes 98312 | tf_op jit(solution)/shard_map/ppermute | solution.py:88
  119.0 18.5 %collective-permute-start.79 = (bf16[2,16,512]{2,1,0:T(8,128)(2,1)S(1)}, bf16[2,16,512]{2,1,0:T(8,128)(2,1)S(1)}, u32[]{:S(2)}, u32[]{:S(2)}) collective-permute-start(bf16[2,16,512]{2,1,0:T(8,128)(2,1)S(1)} %get-tuple-element.203.refs_6_), channel_id=1, source_target_pairs={{0,8},{1,9},{2,10},{3,11},{4,12},{5,13},{6,14},{7,15},{8,0},{9,1},... | collective-permute-start | bytes 98312 | tf_op jit(solution)/shard_map/ppermute | solution.py:88
  139.3 5.0 %collective-permute-start.81 = (bf16[2,16,512]{2,1,0:T(8,128)(2,1)S(1)}, bf16[2,16,512]{2,1,0:T(8,128)(2,1)S(1)}, u32[]{:S(2)}, u32[]{:S(2)}) collective-permute-start(bf16[2,16,512]{2,1,0:T(8,128)(2,1)S(1)} %get-tuple-element.208), channel_id=1, source_target_pairs={{0,6},{1,7},{2,4},{3,5},{4,2},{5,3},{6,0},{7,1},{8,9},{9,8},{10,11... | collective-permute-start | bytes 98312 | tf_op jit(solution)/shard_map/ppermute | solution.py:31
  141.2 3.9 %collective-permute-start.83 = (bf16[2,16,512]{2,1,0:T(8,128)(2,1)S(1)}, bf16[2,16,512]{2,1,0:T(8,128)(2,1)S(1)}, u32[]{:S(2)}, u32[]{:S(2)}) collective-permute-start(bf16[2,16,512]{2,1,0:T(8,128)(2,1)S(1)} %get-tuple-element.208), channel_id=1, source_target_pairs={{0,4},{1,5},{2,6},{3,7},{4,0},{5,1},{6,2},{7,3},{8,9},{9,8},{10,11... | collective-permute-start | bytes 98312 | tf_op jit(solution)/shard_map/ppermute | solution.py:31
  141.7 3.9 %collective-permute-start.84 = (bf16[2,16,512]{2,1,0:T(8,128)(2,1)S(1)}, bf16[2,16,512]{2,1,0:T(8,128)(2,1)S(1)}, u32[]{:S(2)}, u32[]{:S(2)}) collective-permute-start(bf16[2,16,512]{2,1,0:T(8,128)(2,1)S(1)} %get-tuple-element.208), channel_id=1, source_target_pairs={{0,2},{1,3},{2,0},{3,1},{4,6},{5,7},{6,4},{7,5},{8,9},{9,8},{10,11... | collective-permute-start | bytes 98312 | tf_op jit(solution)/shard_map/ppermute | solution.py:31
  144.3 1.4 collective-permute-start.82
  147.5 5.3 %collective-permute-start.86 = (bf16[2,2,16,512]{3,2,1,0:T(8,128)(2,1)S(1)}, bf16[2,2,16,512]{3,2,1,0:T(8,128)(2,1)S(1)}, u32[]{:S(2)}, u32[]{:S(2)}) collective-permute-start(bf16[2,2,16,512]{3,2,1,0:T(8,128)(2,1)S(1)} %get-tuple-element.214), channel_id=1, source_target_pairs={{0,6},{1,7},{2,4},{3,5},{4,2},{5,3},{6,0},{7,1},{8,14},{9,15},{10,... | collective-permute-start | bytes 196616 | tf_op jit(solution)/shard_map/ppermute | solution.py:31
  149.6 4.5 %collective-permute-start.88 = (bf16[2,2,16,512]{3,2,1,0:T(8,128)(2,1)S(1)}, bf16[2,2,16,512]{3,2,1,0:T(8,128)(2,1)S(1)}, u32[]{:S(2)}, u32[]{:S(2)}) collective-permute-start(bf16[2,2,16,512]{3,2,1,0:T(8,128)(2,1)S(1)} %get-tuple-element.214), channel_id=1, source_target_pairs={{0,4},{1,5},{2,6},{3,7},{4,0},{5,1},{6,2},{7,3},{8,12},{9,13},{10,... | collective-permute-start | bytes 196616 | tf_op jit(solution)/shard_map/ppermute | solution.py:31
  150.1 4.3 %collective-permute-start.89 = (bf16[2,2,16,512]{3,2,1,0:T(8,128)(2,1)S(1)}, bf16[2,2,16,512]{3,2,1,0:T(8,128)(2,1)S(1)}, u32[]{:S(2)}, u32[]{:S(2)}) collective-permute-start(bf16[2,2,16,512]{3,2,1,0:T(8,128)(2,1)S(1)} %get-tuple-element.214), channel_id=1, source_target_pairs={{0,2},{1,3},{2,0},{3,1},{4,6},{5,7},{6,4},{7,5},{8,10},{9,11},{10,... | collective-permute-start | bytes 196616 | tf_op jit(solution)/shard_map/ppermute | solution.py:31
  152.8 1.7 %collective-permute-start.87 = (bf16[2,2,2,16,512]{4,3,2,1,0:T(8,128)(2,1)S(1)}, bf16[2,2,2,16,512]{4,3,2,1,0:T(8,128)(2,1)S(1)}, u32[]{:S(2)}, u32[]{:S(2)}) collective-permute-start(bf16[2,2,2,16,512]{4,3,2,1,0:T(8,128)(2,1)S(1)} %pad_maximum_fusion.mine_ref), channel_id=1, source_target_pairs={{0,1},{1,0},{2,3},{3,2},{4,5},{5,4},{6,7},{7,6},{8,9},{9,8},{10,11... | collective-permute-start | bytes 393224 | tf_op jit(solution)/shard_map/ppermute | solution.py:31
  154.4 1.4 collective-permute-start.90
  (27 other events, 34.5 us)

commit v8 on v6

--- a/solution.py
+++ b/solution.py
@@ -26,7 +26,7 @@
     peers, groups = lax.axis_size("xy"), lax.axis_size("gz")
     pairs = []
     for group in range(groups):
-        used = mask if turn is None or (group - turn) % 2 == 0 else 1
+        used = mask if turn is None or group == turn else 1
         pairs += [(group * peers + peer, group * peers + (peer ^ used)) for peer in range(peers)]
     return lax.ppermute(shard, ("gz", "xy"), pairs)
 

time: 158 us -> 158 us (level)
  starting transfers between devices: 88.7 us -> 92.5 us
  waiting for transfers between devices: 44.4 us -> 40.7 us
    ppermute x24, starting transfers between devices: 54.7 us -> 63.6 us  [across(): return lax.ppermute(message, ('gz', 'xy'), pairs)]
    ppermute x67, starting transfers between devices: 34 us -> 29 us  [swapped(): return lax.ppermute(shard, ('gz', 'xy'), pairs)]
    ppermute x67, waiting for transfers between devices: 31.5 us -> 27.9 us  [swapped(): return lax.ppermute(shard, ('gz', 'xy'), pairs)]
  transfers between devices with their start and end apart: 91 -> 91, of which waited for: 60 -> 61; matrix products, arithmetic and copies ran while one was open for 1% -> 1% of each run, Pallas kernels for 9% -> 9%
where the time goes in v8:
time: 158 us
  starting transfers between devices  92.5 us (59%)
  waiting for transfers between devices  40.7 us (26%)
  Pallas kernels  21.8 us (14%)
    ppermute x24, starting transfers between devices, across(): return lax.ppermute(message, ('gz', 'xy'), pairs)  63.6 us
    ppermute x67, starting transfers between devices, swapped(): return lax.ppermute(shard, ('gz', 'xy'), pairs)  29 us
    ppermute x67, waiting for transfers between devices, swapped(): return lax.ppermute(shard, ('gz', 'xy'), pairs)  27.9 us
    pallas_call x54, Pallas kernels, in_kernel(): pl.pallas_call(body, out_shape=tuple((pltpu.VMEM(shape, dtype) for shape,...  20.2 us
    ppermute x24, waiting for transfers between devices, across(): return lax.ppermute(message, ('gz', 'xy'), pairs)  12.8 us
  transfers between devices with their start and end apart: 91, of which 61 were waited for; matrix products, arithmetic and copies ran while one was open for 1% of the time, Pallas kernels for 9%

profile of v8, /device:TPU:0, one launch (start us, length us, event | category | flops | bytes accessed | tf_op | source)
XLA Modules:
  0.0 157.6 jit_solution(9330546683564031761)
XLA Ops:
  0.6 3.3 %shard_map.95 = (f32[2,2,16,512]{3,2,1,0:T(8,128)S(1)}, bf16[80,256]{1,0:T(8,128)(2,1)S(1)}, f32[2,2,16,512]{3,2,1,0:T(8,128)}, bf16[2,1,2,512,512]{4,3,2,1,0:T(...) custom-call(f32[2,2,16,512]{3,2,1,0:T(8,128)} %refs_0_.1, ...), custom_call_target="tpu_custom_call" | custom-call | tf_op jit(solution)/shard_map/pallas_call | solution.py:109
  3.9 4.0 %collective-permute-start = (bf16[80,256]{1,0:T(8,128)(2,1)S(1)}, bf16[80,256]{1,0:T(8,128)(2,1)S(1)}, u32[]{:S(2)}, u32[]{:S(2)}) collective-permute-start(bf16[80,256]{1,0:T(8,128)(2,1)S(1)} %get-tuple-element.114.after_ref), channel_id=1, source_target_pairs={{0,6},{1,7},{2,4},{3,5},{4,2},{5,3},{6,0},{7,1},{8,14},{9,15},{10,... | collective-permute-start | bytes 122888 | tf_op jit(solution)/shard_map/ppermute | solution.py:31
  8.5 3.5 %shard_map.97.refs_1_.refs_2_.schur_ref = bf16[2,4096,512]{2,1,0:T(8,128)(2,1)S(1)} custom-call(bf16[2,2,4096,512]{3,2,1,0:T(8,128)(2,1)} %refs_4_.3, bf16[80,256]{1,0:T(8,128)(2,1)S(1)} %get-tuple-element.114.after_ref), custom_call_target="tpu_custom_call" | custom-call | bytes 8388608 | tf_op jit(solution)/shard_map/pallas_call | solution.py:109
  12.9 0.7 collective-permute-done.1.refs_0_.refs_1_
  14.0 0.9 shard_map.99
  14.9 2.8 %collective-permute-start.7 = (bf16[2,16,512]{2,1,0:T(8,128)(2,1)S(1)}, bf16[2,16,512]{2,1,0:T(8,128)(2,1)S(1)}, u32[]{:S(2)}, u32[]{:S(2)}) collective-permute-start(bf16[2,16,512]{2,1,0:T(8,128)(2,1)S(1)} %get-tuple-element.119.refs_5_.refs_7_), channel_id=1, source_target_pairs={{0,6},{1,7},{2,4},{3,5},{4,2},{5,3},{6,0},{7,1},{8,14},{9,15},{10,... | collective-permute-start | bytes 98312 | tf_op jit(solution)/shard_map/ppermute | solution.py:31
  18.5 3.8 %shard_map.101 = (f32[2,16,512]{2,1,0:T(8,128)S(1)}, bf16[2,4096,512]{2,1,0:T(8,128)(2,1)S(1)}) custom-call(f32[1,512]{1,0:T(1,128)S(1)} %get-tuple-element.121.mask_ref.refs_3_, f32[2,2,16,512]{3,2,1,0:T(8,128)S(1)} %get-tuple-element.118.source_ref, bf16[2,80,256]{2,1,0:T(8,128)(2,1)S(1)} %pad_maximum_fusion.3.refs_0_.one_ref, ...), custom_call_target="tpu_custom_call" | custom-call | bytes 8388608 | tf_op jit(solution)/shard_map/pallas_call | solution.py:109
  23.6 0.8 shard_map.103.refs_0_
  25.0 2.9 %collective-permute-start.10 = (bf16[2,16,512]{2,1,0:T(8,128)(2,1)S(1)}, bf16[2,16,512]{2,1,0:T(8,128)(2,1)S(1)}, u32[]{:S(2)}, u32[]{:S(2)}) collective-permute-start(bf16[2,16,512]{2,1,0:T(8,128)(2,1)S(1)} %get-tuple-element.137.refs_5_), channel_id=1, source_target_pairs={{0,6},{1,7},{2,4},{3,5},{4,2},{5,3},{6,0},{7,1},{8,9},{9,8},{10,11... | collective-permute-start | bytes 98312 | tf_op jit(solution)/shard_map/ppermute | solution.py:31
  28.5 1.3 collective-permute-done.10
  30.4 1.4 collective-permute-done.12
  32.4 0.8 shard_map.106.refs_0_
  34.1 1.3 collective-permute-start.15
  35.4 1.3 collective-permute-start.16
  36.7 1.3 collective-permute-start.18
  38.4 1.2 collective-permute-done.18
  39.6 2.4 %collective-permute-done.19 = bf16[2,16,512]{2,1,0:T(8,128)(2,1)S(1)} collective-permute-done((bf16[2,16,512]{2,1,0:T(8,128)(2,1)S(1)}, bf16[2,16,512]{2,1,0:T(8,128)(2,1)S(1)}, u32[]{:S(2)}, u32[]{:S(2)}) %collective-permute-start.19) | collective-permute-done | bytes 32800 | tf_op jit(solution)/shard_map/ppermute | solution.py:88
  42.1 1.2 collective-permute-done.20.refs_1_
  45.3 0.6 collective-permute-done.22.refs_0_
  46.4 0.7 collective-permute-start.26
  47.1 0.7 collective-permute-start.27
  47.7 0.7 collective-permute-start.29
  49.1 0.6 collective-permute-done.30
  50.0 1.0 collective-permute-done.31.refs_1_
  53.0 0.6 collective-permute-done.33.refs_0_
  54.1 14.0 %collective-permute-start.37 = (bf16[2,16,512]{2,1,0:T(8,128)(2,1)S(1)}, bf16[2,16,512]{2,1,0:T(8,128)(2,1)S(1)}, u32[]{:S(2)}, u32[]{:S(2)}) collective-permute-start(bf16[2,16,512]{2,1,0:T(8,128)(2,1)S(1)} %get-tuple-element.163.refs_7_), channel_id=1, source_target_pairs={{0,14},{1,15},{2,12},{3,13},{4,10},{5,11},{6,8},{7,9},{16,30},{17,... | collective-permute-start | bytes 98312 | tf_op jit(solution)/shard_map/ppermute | solution.py:88
  68.1 1.3 collective-permute-start.38
  69.4 1.3 collective-permute-start.40
  71.1 1.2 collective-permute-done.40
  72.3 2.4 %collective-permute-done.41 = bf16[2,16,512]{2,1,0:T(8,128)(2,1)S(1)} collective-permute-done((bf16[2,16,512]{2,1,0:T(8,128)(2,1)S(1)}, bf16[2,16,512]{2,1,0:T(8,128)(2,1)S(1)}, u32[]{:S(2)}, u32[]{:S(2)}) %collective-permute-start.41) | collective-permute-done | bytes 32800 | tf_op jit(solution)/shard_map/ppermute | solution.py:88
  74.8 1.2 collective-permute-done.42.refs_1_
  78.0 0.6 collective-permute-done.44.refs_0_
  81.0 0.6 collective-permute-done.49.refs_0_
  82.1 1.3 collective-permute-start.53
  83.4 1.3 collective-permute-start.54
  84.8 1.3 collective-permute-start.56
  86.1 3.3 %collective-permute-start.57 = (bf16[2,16,512]{2,1,0:T(8,128)(2,1)S(1)}, bf16[2,16,512]{2,1,0:T(8,128)(2,1)S(1)}, u32[]{:S(2)}, u32[]{:S(2)}) collective-permute-start(bf16[2,16,512]{2,1,0:T(8,128)(2,1)S(1)} %get-tuple-element.180.refs_6_), channel_id=1, source_target_pairs={{0,8},{1,9},{2,10},{3,11},{4,12},{5,13},{6,14},{7,15},{8,0},{9,1},... | collective-permute-start | bytes 98312 | tf_op jit(solution)/shard_map/ppermute | solution.py:88
  89.3 0.6 collective-permute-done.53
  89.9 0.7 collective-permute-done.54
  90.8 0.6 collective-permute-done.56
  92.0 0.8 collective-permute-done.58.refs_1_
  94.8 0.6 collective-permute-done.60.refs_0_
  95.9 0.7 collective-permute-start.64
  96.5 0.7 collective-permute-start.65
  97.2 0.7 collective-permute-start.67
  98.5 0.6 collective-permute-done.68
  99.4 1.0 collective-permute-done.69.refs_1_
  103.5 1.3 collective-permute-start.75
  104.8 1.3 collective-permute-start.76
  106.1 1.3 collective-permute-start.78
  107.4 27.5 %collective-permute-start.79 = (bf16[2,16,512]{2,1,0:T(8,128)(2,1)S(1)}, bf16[2,16,512]{2,1,0:T(8,128)(2,1)S(1)}, u32[]{:S(2)}, u32[]{:S(2)}) collective-permute-start(bf16[2,16,512]{2,1,0:T(8,128)(2,1)S(1)} %get-tuple-element.201.refs_6_), channel_id=1, source_target_pairs={{0,8},{1,9},{2,10},{3,11},{4,12},{5,13},{6,14},{7,15},{8,0},{9,1},... | collective-permute-start | bytes 98312 | tf_op jit(solution)/shard_map/ppermute | solution.py:88
  135.0 0.9 collective-permute-done.75
  135.8 0.6 collective-permute-done.76
  137.8 0.8 shard_map.142.refs_0_
  139.3 1.9 %collective-permute-start.81 = (bf16[2,16,512]{2,1,0:T(8,128)(2,1)S(1)}, bf16[2,16,512]{2,1,0:T(8,128)(2,1)S(1)}, u32[]{:S(2)}, u32[]{:S(2)}) collective-permute-start(bf16[2,16,512]{2,1,0:T(8,128)(2,1)S(1)} %get-tuple-element.206), channel_id=1, source_target_pairs={{0,6},{1,7},{2,4},{3,5},{4,2},{5,3},{6,0},{7,1},{8,9},{9,8},{10,11... | collective-permute-start | bytes 98312 | tf_op jit(solution)/shard_map/ppermute | solution.py:31
  141.7 1.1 collective-permute-start.84
  142.9 1.4 collective-permute-done.81
  145.8 0.8 shard_map.145.products_ref
  147.5 2.1 %collective-permute-start.86 = (bf16[2,2,16,512]{3,2,1,0:T(8,128)(2,1)S(1)}, bf16[2,2,16,512]{3,2,1,0:T(8,128)(2,1)S(1)}, u32[]{:S(2)}, u32[]{:S(2)}) collective-permute-start(bf16[2,2,16,512]{3,2,1,0:T(8,128)(2,1)S(1)} %get-tuple-element.212), channel_id=1, source_target_pairs={{0,6},{1,7},{2,4},{3,5},{4,2},{5,3},{6,0},{7,1},{8,14},{9,15},{10,... | collective-permute-start | bytes 196616 | tf_op jit(solution)/shard_map/ppermute | solution.py:31
  150.1 0.9 collective-permute-start.89
  151.0 1.7 %collective-permute-done.86 = bf16[2,2,16,512]{3,2,1,0:T(8,128)(2,1)S(1)} collective-permute-done((bf16[2,2,16,512]{3,2,1,0:T(8,128)(2,1)S(1)}, bf16[2,2,16,512]{3,2,1,0:T(8,128)(2,1)S(1)}, u32[]{:S(2)}, u32[]{:S(2)}) %collective-permute-start.86) | collective-permute-done | bytes 65568 | tf_op jit(solution)/shard_map/ppermute | solution.py:31
  153.3 0.8 collective-permute-done.88
  154.5 0.7 pad_maximum_fusion.2
  155.8 1.6 %shard_map.149 = f32[2,2,16,512]{3,2,1,0:T(8,128)} custom-call(f32[2,32,256]{2,1,0:T(8,128)S(1)} %shard_map.148.picked_ref, bf16[2,2,2,16,512]{4,3,2,1,0:T(8,128)(2,1)S(1)} %collective-permute-done.90.last_ref, bf16[2,2,512,256]{3,2,1,0:T(8,128)(2,1)S(1)} %get-tuple-element.219.chosen_ref, bf16[2,1,2,512,256]{4,3,2,1,0:T(8,128)(2,1)S(1)} %get-tuple-element.220.coupling_ref, ...), custom_call_target="tpu_custom_call" | custom-call | tf_op jit(solution)/shard_map/pallas_call | solution.py:644
  (214 shorter events, 32.9 us)
Async XLA Ops:
  3.9 8.1 %collective-permute-start = (bf16[80,256]{1,0:T(8,128)(2,1)S(1)}, bf16[80,256]{1,0:T(8,128)(2,1)S(1)}, u32[]{:S(2)}, u32[]{:S(2)}) collective-permute-start(bf16[80,256]{1,0:T(8,128)(2,1)S(1)} %get-tuple-element.114.after_ref), channel_id=1, source_target_pairs={{0,6},{1,7},{2,4},{3,5},{4,2},{5,3},{6,0},{7,1},{8,14},{9,15},{10,... | collective-permute-start | bytes 122888 | tf_op jit(solution)/shard_map/ppermute | solution.py:31
  7.9 4.4 %collective-permute-start.2 = (bf16[80,256]{1,0:T(8,128)(2,1)S(1)}, bf16[80,256]{1,0:T(8,128)(2,1)S(1)}, u32[]{:S(2)}, u32[]{:S(2)}) collective-permute-start(bf16[80,256]{1,0:T(8,128)(2,1)S(1)} %get-tuple-element.114.after_ref), channel_id=1, source_target_pairs={{0,4},{1,5},{2,6},{3,7},{4,0},{5,1},{6,2},{7,3},{8,12},{9,13},{10,... | collective-permute-start | bytes 122888 | tf_op jit(solution)/shard_map/ppermute | solution.py:31
  8.4 4.0 %collective-permute-start.3 = (bf16[80,256]{1,0:T(8,128)(2,1)S(1)}, bf16[80,256]{1,0:T(8,128)(2,1)S(1)}, u32[]{:S(2)}, u32[]{:S(2)}) collective-permute-start(bf16[80,256]{1,0:T(8,128)(2,1)S(1)} %get-tuple-element.114.after_ref), channel_id=1, source_target_pairs={{0,2},{1,3},{2,0},{3,1},{4,6},{5,7},{6,4},{7,5},{8,10},{9,11},{10,... | collective-permute-start | bytes 122888 | tf_op jit(solution)/shard_map/ppermute | solution.py:31
  12.4 1.6 %collective-permute-start.4 = (bf16[2,80,256]{2,1,0:T(8,128)(2,1)S(1)}, bf16[2,80,256]{2,1,0:T(8,128)(2,1)S(1)}, u32[]{:S(2)}, u32[]{:S(2)}) collective-permute-start(bf16[2,80,256]{2,1,0:T(8,128)(2,1)S(1)} %pad_maximum_fusion.4.refs_1_.refs_2_.two_ref), channel_id=1, source_target_pairs={{0,1},{1,0},{2,3},{3,2},{4,5},{5,4},{6,7},{7,6},{8,9},{9,8},{10,11... | collective-permute-start | bytes 245768 | tf_op jit(solution)/shard_map/ppermute | solution.py:31
  14.9 7.4 %collective-permute-start.7 = (bf16[2,16,512]{2,1,0:T(8,128)(2,1)S(1)}, bf16[2,16,512]{2,1,0:T(8,128)(2,1)S(1)}, u32[]{:S(2)}, u32[]{:S(2)}) collective-permute-start(bf16[2,16,512]{2,1,0:T(8,128)(2,1)S(1)} %get-tuple-element.119.refs_5_.refs_7_), channel_id=1, source_target_pairs={{0,6},{1,7},{2,4},{3,5},{4,2},{5,3},{6,0},{7,1},{8,14},{9,15},{10,... | collective-permute-start | bytes 98312 | tf_op jit(solution)/shard_map/ppermute | solution.py:31
  17.8 5.1 %collective-permute-start.5 = (bf16[2,16,512]{2,1,0:T(8,128)(2,1)S(1)}, bf16[2,16,512]{2,1,0:T(8,128)(2,1)S(1)}, u32[]{:S(2)}, u32[]{:S(2)}) collective-permute-start(bf16[2,16,512]{2,1,0:T(8,128)(2,1)S(1)} %get-tuple-element.119.refs_5_.refs_7_), channel_id=1, source_target_pairs={{0,4},{1,5},{2,6},{3,7},{4,0},{5,1},{6,2},{7,3},{8,12},{9,13},{10,... | collective-permute-start | bytes 98312 | tf_op jit(solution)/shard_map/ppermute | solution.py:31
  18.4 4.5 %collective-permute-start.6 = (bf16[2,16,512]{2,1,0:T(8,128)(2,1)S(1)}, bf16[2,16,512]{2,1,0:T(8,128)(2,1)S(1)}, u32[]{:S(2)}, u32[]{:S(2)}) collective-permute-start(bf16[2,16,512]{2,1,0:T(8,128)(2,1)S(1)} %get-tuple-element.119.refs_5_.refs_7_), channel_id=1, source_target_pairs={{0,2},{1,3},{2,0},{3,1},{4,6},{5,7},{6,4},{7,5},{8,10},{9,11},{10,... | collective-permute-start | bytes 98312 | tf_op jit(solution)/shard_map/ppermute | solution.py:31
  22.3 1.3 collective-permute-start.8
  22.9 1.6 collective-permute-start.9
  25.0 4.9 %collective-permute-start.10 = (bf16[2,16,512]{2,1,0:T(8,128)(2,1)S(1)}, bf16[2,16,512]{2,1,0:T(8,128)(2,1)S(1)}, u32[]{:S(2)}, u32[]{:S(2)}) collective-permute-start(bf16[2,16,512]{2,1,0:T(8,128)(2,1)S(1)} %get-tuple-element.137.refs_5_), channel_id=1, source_target_pairs={{0,6},{1,7},{2,4},{3,5},{4,2},{5,3},{6,0},{7,1},{8,9},{9,8},{10,11... | collective-permute-start | bytes 98312 | tf_op jit(solution)/shard_map/ppermute | solution.py:31
  27.9 3.9 %collective-permute-start.12 = (bf16[2,16,512]{2,1,0:T(8,128)(2,1)S(1)}, bf16[2,16,512]{2,1,0:T(8,128)(2,1)S(1)}, u32[]{:S(2)}, u32[]{:S(2)}) collective-permute-start(bf16[2,16,512]{2,1,0:T(8,128)(2,1)S(1)} %get-tuple-element.137.refs_5_), channel_id=1, source_target_pairs={{0,4},{1,5},{2,6},{3,7},{4,0},{5,1},{6,2},{7,3},{8,9},{9,8},{10,11... | collective-permute-start | bytes 98312 | tf_op jit(solution)/shard_map/ppermute | solution.py:31
  28.4 3.9 %collective-permute-start.13 = (bf16[2,16,512]{2,1,0:T(8,128)(2,1)S(1)}, bf16[2,16,512]{2,1,0:T(8,128)(2,1)S(1)}, u32[]{:S(2)}, u32[]{:S(2)}) collective-permute-start(bf16[2,16,512]{2,1,0:T(8,128)(2,1)S(1)} %get-tuple-element.137.refs_5_), channel_id=1, source_target_pairs={{0,2},{1,3},{2,0},{3,1},{4,6},{5,7},{6,4},{7,5},{8,9},{9,8},{10,11... | collective-permute-start | bytes 98312 | tf_op jit(solution)/shard_map/ppermute | solution.py:31
  29.9 2.5 %collective-permute-start.11 = (bf16[2,2,16,512]{3,2,1,0:T(8,128)(2,1)S(1)}, bf16[2,2,16,512]{3,2,1,0:T(8,128)(2,1)S(1)}, u32[]{:S(2)}, u32[]{:S(2)}) collective-permute-start(bf16[2,2,16,512]{3,2,1,0:T(8,128)(2,1)S(1)} %pad_maximum_fusion.7.refs_0_), channel_id=1, source_target_pairs={{0,1},{1,0},{2,3},{3,2},{4,5},{5,4},{6,7},{7,6},{8,9},{9,8},{10,11... | collective-permute-start | bytes 196616 | tf_op jit(solution)/shard_map/ppermute | solution.py:31
  32.3 1.3 collective-permute-start.14
  34.1 4.0 %collective-permute-start.15 = (bf16[2,16,512]{2,1,0:T(8,128)(2,1)S(1)}, bf16[2,16,512]{2,1,0:T(8,128)(2,1)S(1)}, u32[]{:S(2)}, u32[]{:S(2)}) collective-permute-start(bf16[2,16,512]{2,1,0:T(8,128)(2,1)S(1)} %get-tuple-element.142.refs_7_), channel_id=1, source_target_pairs={{0,14},{1,15},{2,12},{3,13},{4,10},{5,11},{6,8},{7,9},{16,30},{17,... | collective-permute-start | bytes 98312 | tf_op jit(solution)/shard_map/ppermute | solution.py:88
  35.4 2.9 %collective-permute-start.16 = (bf16[2,16,512]{2,1,0:T(8,128)(2,1)S(1)}, bf16[2,16,512]{2,1,0:T(8,128)(2,1)S(1)}, u32[]{:S(2)}, u32[]{:S(2)}) collective-permute-start(bf16[2,16,512]{2,1,0:T(8,128)(2,1)S(1)} %get-tuple-element.142.refs_7_), channel_id=1, source_target_pairs={{0,12},{1,13},{2,14},{3,15},{4,8},{5,9},{6,10},{7,11},{16,28},{17,... | collective-permute-start | bytes 98312 | tf_op jit(solution)/shard_map/ppermute | solution.py:88
  36.7 2.9 %collective-permute-start.18 = (bf16[2,16,512]{2,1,0:T(8,128)(2,1)S(1)}, bf16[2,16,512]{2,1,0:T(8,128)(2,1)S(1)}, u32[]{:S(2)}, u32[]{:S(2)}) collective-permute-start(bf16[2,16,512]{2,1,0:T(8,128)(2,1)S(1)} %get-tuple-element.142.refs_7_), channel_id=1, source_target_pairs={{0,10},{1,11},{2,8},{3,9},{4,14},{5,15},{6,12},{7,13},{16,26},{17,... | collective-permute-start | bytes 98312 | tf_op jit(solution)/shard_map/ppermute | solution.py:88
  38.0 4.0 %collective-permute-start.19 = (bf16[2,16,512]{2,1,0:T(8,128)(2,1)S(1)}, bf16[2,16,512]{2,1,0:T(8,128)(2,1)S(1)}, u32[]{:S(2)}, u32[]{:S(2)}) collective-permute-start(bf16[2,16,512]{2,1,0:T(8,128)(2,1)S(1)} %get-tuple-element.142.refs_7_), channel_id=1, source_target_pairs={{0,8},{1,9},{2,10},{3,11},{4,12},{5,13},{6,14},{7,15},{8,0},{9,1},... | collective-permute-start | bytes 98312 | tf_op jit(solution)/shard_map/ppermute | solution.py:88
  38.3 3.8 %collective-permute-start.17 = (bf16[2,2,16,512]{3,2,1,0:T(8,128)(2,1)S(1)}, bf16[2,2,16,512]{3,2,1,0:T(8,128)(2,1)S(1)}, u32[]{:S(2)}, u32[]{:S(2)}) collective-permute-start(bf16[2,2,16,512]{3,2,1,0:T(8,128)(2,1)S(1)} %multiply_convert_fusion.11.refs_0_), channel_id=1, source_target_pairs={{0,1},{1,0},{2,3},{3,2},{4,5},{5,4},{6,7},{7,6},{8,9},{9,8},{10,11... | collective-permute-start | bytes 196616 | tf_op jit(solution)/shard_map/ppermute | solution.py:31
  42.0 1.3 collective-permute-start.20
  44.6 1.3 collective-permute-start.22
  45.1 1.3 collective-permute-start.25
  46.4 2.2 %collective-permute-start.26 = (bf16[2,16,512]{2,1,0:T(8,128)(2,1)S(1)}, bf16[2,16,512]{2,1,0:T(8,128)(2,1)S(1)}, u32[]{:S(2)}, u32[]{:S(2)}) collective-permute-start(bf16[2,16,512]{2,1,0:T(8,128)(2,1)S(1)} %get-tuple-element.153.refs_7_), channel_id=1, source_target_pairs={{8,22},{9,23},{10,20},{11,21},{12,18},{13,19},{14,16},{15,17}} | collective-permute-start | bytes 98312 | tf_op jit(solution)/shard_map/ppermute | solution.py:88
  47.1 1.6 collective-permute-start.27
  47.7 1.3 collective-permute-start.29
  48.7 1.3 collective-permute-start.28
  49.7 1.3 collective-permute-start.31
  52.2 1.3 collective-permute-start.33
  52.7 1.3 collective-permute-start.36
  54.1 16.7 %collective-permute-start.37 = (bf16[2,16,512]{2,1,0:T(8,128)(2,1)S(1)}, bf16[2,16,512]{2,1,0:T(8,128)(2,1)S(1)}, u32[]{:S(2)}, u32[]{:S(2)}) collective-permute-start(bf16[2,16,512]{2,1,0:T(8,128)(2,1)S(1)} %get-tuple-element.163.refs_7_), channel_id=1, source_target_pairs={{0,14},{1,15},{2,12},{3,13},{4,10},{5,11},{6,8},{7,9},{16,30},{17,... | collective-permute-start | bytes 98312 | tf_op jit(solution)/shard_map/ppermute | solution.py:88
  68.1 2.9 %collective-permute-start.38 = (bf16[2,16,512]{2,1,0:T(8,128)(2,1)S(1)}, bf16[2,16,512]{2,1,0:T(8,128)(2,1)S(1)}, u32[]{:S(2)}, u32[]{:S(2)}) collective-permute-start(bf16[2,16,512]{2,1,0:T(8,128)(2,1)S(1)} %get-tuple-element.163.refs_7_), channel_id=1, source_target_pairs={{0,12},{1,13},{2,14},{3,15},{4,8},{5,9},{6,10},{7,11},{16,28},{17,... | collective-permute-start | bytes 98312 | tf_op jit(solution)/shard_map/ppermute | solution.py:88
  69.4 2.9 %collective-permute-start.40 = (bf16[2,16,512]{2,1,0:T(8,128)(2,1)S(1)}, bf16[2,16,512]{2,1,0:T(8,128)(2,1)S(1)}, u32[]{:S(2)}, u32[]{:S(2)}) collective-permute-start(bf16[2,16,512]{2,1,0:T(8,128)(2,1)S(1)} %get-tuple-element.163.refs_7_), channel_id=1, source_target_pairs={{0,10},{1,11},{2,8},{3,9},{4,14},{5,15},{6,12},{7,13},{16,26},{17,... | collective-permute-start | bytes 98312 | tf_op jit(solution)/shard_map/ppermute | solution.py:88
  70.7 4.0 %collective-permute-start.41 = (bf16[2,16,512]{2,1,0:T(8,128)(2,1)S(1)}, bf16[2,16,512]{2,1,0:T(8,128)(2,1)S(1)}, u32[]{:S(2)}, u32[]{:S(2)}) collective-permute-start(bf16[2,16,512]{2,1,0:T(8,128)(2,1)S(1)} %get-tuple-element.163.refs_7_), channel_id=1, source_target_pairs={{0,8},{1,9},{2,10},{3,11},{4,12},{5,13},{6,14},{7,15},{8,0},{9,1},... | collective-permute-start | bytes 98312 | tf_op jit(solution)/shard_map/ppermute | solution.py:88
  71.0 3.8 %collective-permute-start.39 = (bf16[2,2,16,512]{3,2,1,0:T(8,128)(2,1)S(1)}, bf16[2,2,16,512]{3,2,1,0:T(8,128)(2,1)S(1)}, u32[]{:S(2)}, u32[]{:S(2)}) collective-permute-start(bf16[2,2,16,512]{3,2,1,0:T(8,128)(2,1)S(1)} %multiply_convert_fusion.7.refs_0_), channel_id=1, source_target_pairs={{0,1},{1,0},{2,3},{3,2},{4,5},{5,4},{6,7},{7,6},{8,9},{9,8},{10,11... | collective-permute-start | bytes 196616 | tf_op jit(solution)/shard_map/ppermute | solution.py:31
  74.7 1.3 collective-permute-start.42
  77.3 1.3 collective-permute-start.44
  77.8 1.3 collective-permute-start.47
  80.3 1.3 collective-permute-start.49
  80.8 1.3 collective-permute-start.52
  82.1 7.8 %collective-permute-start.53 = (bf16[2,16,512]{2,1,0:T(8,128)(2,1)S(1)}, bf16[2,16,512]{2,1,0:T(8,128)(2,1)S(1)}, u32[]{:S(2)}, u32[]{:S(2)}) collective-permute-start(bf16[2,16,512]{2,1,0:T(8,128)(2,1)S(1)} %get-tuple-element.180.refs_6_), channel_id=1, source_target_pairs={{8,6},{9,7},{10,4},{11,5},{12,2},{13,3},{14,0},{15,1},{24,22},{25,... | collective-permute-start | bytes 98312 | tf_op jit(solution)/shard_map/ppermute | solution.py:88
  83.4 7.3 %collective-permute-start.54 = (bf16[2,16,512]{2,1,0:T(8,128)(2,1)S(1)}, bf16[2,16,512]{2,1,0:T(8,128)(2,1)S(1)}, u32[]{:S(2)}, u32[]{:S(2)}) collective-permute-start(bf16[2,16,512]{2,1,0:T(8,128)(2,1)S(1)} %get-tuple-element.180.refs_6_), channel_id=1, source_target_pairs={{8,4},{9,5},{10,6},{11,7},{12,0},{13,1},{14,2},{15,3},{24,20},{25,... | collective-permute-start | bytes 98312 | tf_op jit(solution)/shard_map/ppermute | solution.py:88
  84.8 6.7 %collective-permute-start.56 = (bf16[2,16,512]{2,1,0:T(8,128)(2,1)S(1)}, bf16[2,16,512]{2,1,0:T(8,128)(2,1)S(1)}, u32[]{:S(2)}, u32[]{:S(2)}) collective-permute-start(bf16[2,16,512]{2,1,0:T(8,128)(2,1)S(1)} %get-tuple-element.180.refs_6_), channel_id=1, source_target_pairs={{8,2},{9,3},{10,0},{11,1},{12,6},{13,7},{14,4},{15,5},{24,18},{25,... | collective-permute-start | bytes 98312 | tf_op jit(solution)/shard_map/ppermute | solution.py:88
  86.1 5.4 %collective-permute-start.57 = (bf16[2,16,512]{2,1,0:T(8,128)(2,1)S(1)}, bf16[2,16,512]{2,1,0:T(8,128)(2,1)S(1)}, u32[]{:S(2)}, u32[]{:S(2)}) collective-permute-start(bf16[2,16,512]{2,1,0:T(8,128)(2,1)S(1)} %get-tuple-element.180.refs_6_), channel_id=1, source_target_pairs={{0,8},{1,9},{2,10},{3,11},{4,12},{5,13},{6,14},{7,15},{8,0},{9,1},... | collective-permute-start | bytes 98312 | tf_op jit(solution)/shard_map/ppermute | solution.py:88
  90.7 1.3 collective-permute-start.55
  91.5 1.3 collective-permute-start.58
  94.0 1.3 collective-permute-start.60
  94.5 1.3 collective-permute-start.63
  95.9 2.2 %collective-permute-start.64 = (bf16[2,16,512]{2,1,0:T(8,128)(2,1)S(1)}, bf16[2,16,512]{2,1,0:T(8,128)(2,1)S(1)}, u32[]{:S(2)}, u32[]{:S(2)}) collective-permute-start(bf16[2,16,512]{2,1,0:T(8,128)(2,1)S(1)} %get-tuple-element.191.refs_6_), channel_id=1, source_target_pairs={{16,14},{17,15},{18,12},{19,13},{20,10},{21,11},{22,8},{23,9}} | collective-permute-start | bytes 98312 | tf_op jit(solution)/shard_map/ppermute | solution.py:88
  96.5 1.6 collective-permute-start.65
  97.2 1.3 collective-permute-start.67
  98.1 1.3 collective-permute-start.66
  103.5 32.3 %collective-permute-start.75 = (bf16[2,16,512]{2,1,0:T(8,128)(2,1)S(1)}, bf16[2,16,512]{2,1,0:T(8,128)(2,1)S(1)}, u32[]{:S(2)}, u32[]{:S(2)}) collective-permute-start(bf16[2,16,512]{2,1,0:T(8,128)(2,1)S(1)} %get-tuple-element.201.refs_6_), channel_id=1, source_target_pairs={{8,6},{9,7},{10,4},{11,5},{12,2},{13,3},{14,0},{15,1},{24,22},{25,... | collective-permute-start | bytes 98312 | tf_op jit(solution)/shard_map/ppermute | solution.py:88
  104.8 31.6 %collective-permute-start.76 = (bf16[2,16,512]{2,1,0:T(8,128)(2,1)S(1)}, bf16[2,16,512]{2,1,0:T(8,128)(2,1)S(1)}, u32[]{:S(2)}, u32[]{:S(2)}) collective-permute-start(bf16[2,16,512]{2,1,0:T(8,128)(2,1)S(1)} %get-tuple-element.201.refs_6_), channel_id=1, source_target_pairs={{8,4},{9,5},{10,6},{11,7},{12,0},{13,1},{14,2},{15,3},{24,20},{25,... | collective-permute-start | bytes 98312 | tf_op jit(solution)/shard_map/ppermute | solution.py:88
  106.1 31.4 %collective-permute-start.78 = (bf16[2,16,512]{2,1,0:T(8,128)(2,1)S(1)}, bf16[2,16,512]{2,1,0:T(8,128)(2,1)S(1)}, u32[]{:S(2)}, u32[]{:S(2)}) collective-permute-start(bf16[2,16,512]{2,1,0:T(8,128)(2,1)S(1)} %get-tuple-element.201.refs_6_), channel_id=1, source_target_pairs={{8,2},{9,3},{10,0},{11,1},{12,6},{13,7},{14,4},{15,5},{24,18},{25,... | collective-permute-start | bytes 98312 | tf_op jit(solution)/shard_map/ppermute | solution.py:88
  107.4 30.1 %collective-permute-start.79 = (bf16[2,16,512]{2,1,0:T(8,128)(2,1)S(1)}, bf16[2,16,512]{2,1,0:T(8,128)(2,1)S(1)}, u32[]{:S(2)}, u32[]{:S(2)}) collective-permute-start(bf16[2,16,512]{2,1,0:T(8,128)(2,1)S(1)} %get-tuple-element.201.refs_6_), channel_id=1, source_target_pairs={{0,8},{1,9},{2,10},{3,11},{4,12},{5,13},{6,14},{7,15},{8,0},{9,1},... | collective-permute-start | bytes 98312 | tf_op jit(solution)/shard_map/ppermute | solution.py:88
  139.3 5.0 %collective-permute-start.81 = (bf16[2,16,512]{2,1,0:T(8,128)(2,1)S(1)}, bf16[2,16,512]{2,1,0:T(8,128)(2,1)S(1)}, u32[]{:S(2)}, u32[]{:S(2)}) collective-permute-start(bf16[2,16,512]{2,1,0:T(8,128)(2,1)S(1)} %get-tuple-element.206), channel_id=1, source_target_pairs={{0,6},{1,7},{2,4},{3,5},{4,2},{5,3},{6,0},{7,1},{8,9},{9,8},{10,11... | collective-permute-start | bytes 98312 | tf_op jit(solution)/shard_map/ppermute | solution.py:31
  141.2 3.9 %collective-permute-start.83 = (bf16[2,16,512]{2,1,0:T(8,128)(2,1)S(1)}, bf16[2,16,512]{2,1,0:T(8,128)(2,1)S(1)}, u32[]{:S(2)}, u32[]{:S(2)}) collective-permute-start(bf16[2,16,512]{2,1,0:T(8,128)(2,1)S(1)} %get-tuple-element.206), channel_id=1, source_target_pairs={{0,4},{1,5},{2,6},{3,7},{4,0},{5,1},{6,2},{7,3},{8,9},{9,8},{10,11... | collective-permute-start | bytes 98312 | tf_op jit(solution)/shard_map/ppermute | solution.py:31
  141.7 3.9 %collective-permute-start.84 = (bf16[2,16,512]{2,1,0:T(8,128)(2,1)S(1)}, bf16[2,16,512]{2,1,0:T(8,128)(2,1)S(1)}, u32[]{:S(2)}, u32[]{:S(2)}) collective-permute-start(bf16[2,16,512]{2,1,0:T(8,128)(2,1)S(1)} %get-tuple-element.206), channel_id=1, source_target_pairs={{0,2},{1,3},{2,0},{3,1},{4,6},{5,7},{6,4},{7,5},{8,9},{9,8},{10,11... | collective-permute-start | bytes 98312 | tf_op jit(solution)/shard_map/ppermute | solution.py:31
  144.3 1.4 collective-permute-start.82
  147.5 5.3 %collective-permute-start.86 = (bf16[2,2,16,512]{3,2,1,0:T(8,128)(2,1)S(1)}, bf16[2,2,16,512]{3,2,1,0:T(8,128)(2,1)S(1)}, u32[]{:S(2)}, u32[]{:S(2)}) collective-permute-start(bf16[2,2,16,512]{3,2,1,0:T(8,128)(2,1)S(1)} %get-tuple-element.212), channel_id=1, source_target_pairs={{0,6},{1,7},{2,4},{3,5},{4,2},{5,3},{6,0},{7,1},{8,14},{9,15},{10,... | collective-permute-start | bytes 196616 | tf_op jit(solution)/shard_map/ppermute | solution.py:31
  149.6 4.5 %collective-permute-start.88 = (bf16[2,2,16,512]{3,2,1,0:T(8,128)(2,1)S(1)}, bf16[2,2,16,512]{3,2,1,0:T(8,128)(2,1)S(1)}, u32[]{:S(2)}, u32[]{:S(2)}) collective-permute-start(bf16[2,2,16,512]{3,2,1,0:T(8,128)(2,1)S(1)} %get-tuple-element.212), channel_id=1, source_target_pairs={{0,4},{1,5},{2,6},{3,7},{4,0},{5,1},{6,2},{7,3},{8,12},{9,13},{10,... | collective-permute-start | bytes 196616 | tf_op jit(solution)/shard_map/ppermute | solution.py:31
  150.1 4.3 %collective-permute-start.89 = (bf16[2,2,16,512]{3,2,1,0:T(8,128)(2,1)S(1)}, bf16[2,2,16,512]{3,2,1,0:T(8,128)(2,1)S(1)}, u32[]{:S(2)}, u32[]{:S(2)}) collective-permute-start(bf16[2,2,16,512]{3,2,1,0:T(8,128)(2,1)S(1)} %get-tuple-element.212), channel_id=1, source_target_pairs={{0,2},{1,3},{2,0},{3,1},{4,6},{5,7},{6,4},{7,5},{8,10},{9,11},{10,... | collective-permute-start | bytes 196616 | tf_op jit(solution)/shard_map/ppermute | solution.py:31
  152.8 2.4 %collective-permute-start.87 = (bf16[2,2,2,16,512]{4,3,2,1,0:T(8,128)(2,1)S(1)}, bf16[2,2,2,16,512]{4,3,2,1,0:T(8,128)(2,1)S(1)}, u32[]{:S(2)}, u32[]{:S(2)}) collective-permute-start(bf16[2,2,2,16,512]{4,3,2,1,0:T(8,128)(2,1)S(1)} %pad_maximum_fusion.mine_ref), channel_id=1, source_target_pairs={{0,1},{1,0},{2,3},{3,2},{4,5},{5,4},{6,7},{7,6},{8,9},{9,8},{10,11... | collective-permute-start | bytes 393224 | tf_op jit(solution)/shard_map/ppermute | solution.py:31
  154.4 1.4 collective-permute-start.90
  (27 other events, 34.0 us)
